TPU v7x, 32 devices: a whole 2x2x4 slice. The times are simulated.
32 devices in a mesh: seq: 4 (over z), exp: 8 (over y, x, core).
Axes of the slice: x: 2, y: 2, z: 4, core: 2. Of those that a mesh axis runs over, the one named last changes fastest.
Arguments:
- byte_embed: bfloat16 [8, 512, 1024], P('exp', 'seq'), may hold values from -16 to 16
- score_weight: float32 [1024], replicated, may hold values from -1 to 1
- norm_gain: float32 [1024], replicated, may hold values from 0.25 to 1.75
- router: bfloat16 [1024, 8], replicated, may hold values from -0.1875 to 0.1875
- routes: int32 [8, 128, 2], P('exp', 'seq'), may hold values from 0 to 7, all different within a row; in each aligned block of 32 rows (0 to 31, 32 to 63, ..., all dimensions but the last counted through in order) at most 12 rows name the same one
- expert_in: bfloat16 [8, 1024, 4096], P('exp', None, 'seq'), may hold values from -0.1875 to 0.1875
- expert_out: bfloat16 [8, 4096, 1024], P('exp', 'seq'), may hold values from -0.09375 to 0.09375
- cotangent: bfloat16 [8, 128, 1024], P('exp', 'seq'), may hold values from -6 to 6
Outputs:
- grad_embed: bfloat16 [8, 512, 1024], P('exp', 'seq')
- grad_in: float32 [8, 1024, 4096], P('exp', None, 'seq')
- grad_out: float32 [8, 4096, 1024], P('exp', 'seq')
Inputs may be any that keep to these rules, and one draw needn't show every extreme that they name: `routes`: among the 32 tokens of one device, at most 12 pairs name the same expert, and some device reaches 12 for some expert. The two experts of a token differ.
All inputs are finite; a program needn't handle non-finite values.
Results may differ from a plain program's by a relative error of at most 0.014.
Values may be sent and summed in bfloat16 or wider, within the bound.
No kernel may reach another device: no remote copies, remote signals or barrier semaphores. Data moves between devices by JAX's collectives and lax.ppermute only.
A program may use at most 64 MiB of HBM per device.

v0:
```python
import jax
import jax.numpy as jnp
from jax import lax
from jax.sharding import PartitionSpec as P

SQRT_HALF = 0.7071067811865476
INV_ROOT_TWO_PI = 0.3989422804014327


def front(inputs, norm_gain, score_weight, router, routes):
    batches, length, features = inputs.shape
    highest = lax.Precision.HIGHEST
    quartets = inputs.reshape(batches, length // 4, 4, features)
    pair_means = quartets.reshape(batches, length // 4, 2, 2, features).mean(axis=3)
    quad_mean = quartets.mean(axis=2)
    score_one = jnp.einsum("btqd,d->btq", quartets, score_weight, precision=highest)
    score_two = jnp.repeat(
        jnp.einsum("btpd,d->btp", pair_means, score_weight, precision=highest), 2, axis=2
    )
    score_four = jnp.broadcast_to(
        jnp.einsum("btd,d->bt", quad_mean, score_weight, precision=highest)[:, :, None],
        score_one.shape,
    )
    largest = jnp.maximum(jnp.maximum(score_one, score_two), score_four)
    weight_one = jnp.exp(score_one - largest)
    weight_two = jnp.exp(score_two - largest)
    weight_four = jnp.exp(score_four - largest)
    denominator = weight_one + weight_two + weight_four
    pair_full = jnp.repeat(pair_means, 2, axis=2)
    blended = (
        weight_one[..., None] * quartets
        + weight_two[..., None] * pair_full
        + weight_four[..., None] * quad_mean[:, :, None, :]
    ) / denominator[..., None]
    tokens = blended.mean(axis=2)
    mean_square = jnp.mean(tokens * tokens, axis=-1, keepdims=True)
    normed = tokens * lax.rsqrt(mean_square + 1e-06) * norm_gain
    logits = jnp.einsum("btd,de->bte", normed, router.astype(jnp.float32), precision=highest)
    experts = logits.shape[-1]
    sigmoid_all = 1.0 / (1.0 + jnp.exp(-logits))
    chosen = (routes[..., None] == jnp.arange(experts, dtype=jnp.int32)).astype(jnp.float32)
    picked = jnp.sum(chosen * sigmoid_all[:, :, None, :], axis=-1)
    gate_values = picked / jnp.sum(picked, axis=-1, keepdims=True)
    return (tokens, normed, gate_values)


def deliver(row_stack, gates_in):
    owned_rows, owned_gates = (
        lax.all_to_all(row_stack, "exp", split_axis=1, concat_axis=1, tiled=True),
        lax.all_to_all(gates_in, "exp", split_axis=1, concat_axis=1, tiled=True),
    )
    return (
        lax.all_gather(owned_rows, "seq", axis=1, tiled=True),
        lax.all_gather(owned_gates, "seq", axis=1, tiled=True),
    )


def per_device(
    byte_embed, score_weight, norm_gain, router, routes, expert_in, expert_out, cotangent
):
    experts_all = router.shape[1]
    token_count = routes.shape[1]
    width_model = byte_embed.shape[2]
    capacity = max(2, 3 * token_count // experts_all)
    owners = lax.axis_size("exp")
    slot_count = lax.axis_size("seq") * owners * capacity
    highest = lax.Precision.HIGHEST
    contract_rows = (((0,), (0,)), ((), ()))
    contract_cols = (((1,), (1,)), ((), ()))

    def local_front(values):
        return front(values, norm_gain, score_weight, router, routes)

    (tokens, normed, gate_values), pullback = jax.vjp(local_front, byte_embed.astype(jnp.float32))
    normed_rows = normed[0].astype(jnp.bfloat16)
    route_rows = routes[0]
    onehot = (route_rows[:, :, None] == jnp.arange(experts_all, dtype=jnp.int32)).astype(jnp.int32)
    running = jnp.cumsum(onehot.reshape(2 * token_count, experts_all), axis=0)
    running = running.reshape(token_count, 2, experts_all)
    position = jnp.sum(onehot * (running - 1), axis=2)
    slot_index = route_rows * capacity + position
    matches = (
        slot_index[:, :, None] == jnp.arange(experts_all * capacity, dtype=jnp.int32)
    ).astype(jnp.float32)
    picker = jnp.sum(matches, axis=1).astype(jnp.bfloat16)
    token_buffer = lax.dot_general(
        picker, normed_rows, contract_rows, preferred_element_type=jnp.float32
    )
    cot_buffer = lax.dot_general(
        picker, cotangent[0], contract_rows, preferred_element_type=jnp.float32
    )
    row_buffer = (
        jnp.stack([token_buffer, cot_buffer])
        .astype(jnp.bfloat16)
        .reshape(2, experts_all, capacity, width_model)
    )
    gate_buffer = jnp.einsum("tks,tk->s", matches, gate_values[0], precision=highest)
    gate_buffer = gate_buffer.astype(jnp.bfloat16).reshape(1, experts_all, capacity)
    weight_in = expert_in[0]
    weight_out = expert_out[0]
    both_rows, slot_gates = deliver(row_buffer, gate_buffer)
    token_rows = both_rows[0].reshape(slot_count, width_model)
    cot_rows = both_rows[1].reshape(slot_count, width_model)
    gate_first = slot_gates.reshape(slot_count).astype(jnp.float32)
    preact = jnp.dot(token_rows, weight_in, preferred_element_type=jnp.float32)
    normal_cdf = 0.5 * (1.0 + jax.scipy.special.erf(preact * SQRT_HALF))
    normal_pdf = INV_ROOT_TWO_PI * jnp.exp(-0.5 * preact * preact)
    hidden = preact * normal_cdf
    upstream = lax.dot_general(
        cot_rows, weight_out, contract_cols, preferred_element_type=jnp.float32
    )
    gate_terms = jnp.sum(hidden * upstream, axis=1)
    hidden_grad = (gate_first[:, None] * upstream * (normal_cdf + preact * normal_pdf)).astype(
        jnp.bfloat16
    )
    gated_hidden = (gate_first[:, None] * hidden).astype(jnp.bfloat16)
    grad_out = lax.dot_general(
        gated_hidden, cot_rows, contract_rows, preferred_element_type=jnp.float32
    )
    grad_in = lax.dot_general(
        token_rows, hidden_grad, contract_rows, preferred_element_type=jnp.float32
    )
    own_slots = owners * capacity
    summed_rows = lax.psum_scatter(
        lax.dot_general(
            hidden_grad, weight_in, contract_cols, preferred_element_type=jnp.float32
        ).astype(jnp.bfloat16),
        "seq",
        scatter_dimension=0,
        tiled=True,
    )
    every_term = lax.psum(gate_terms, "seq")
    own_terms = lax.dynamic_slice_in_dim(
        every_term, lax.axis_index("seq") * own_slots, own_slots, 0
    )
    returned_rows, returned_gates = (
        lax.all_to_all(
            summed_rows.reshape(owners, capacity, width_model),
            "exp",
            split_axis=0,
            concat_axis=0,
            tiled=True,
        ),
        lax.all_to_all(
            own_terms.astype(jnp.bfloat16).reshape(owners, capacity),
            "exp",
            split_axis=0,
            concat_axis=0,
            tiled=True,
        ),
    )
    normed_grad = jnp.dot(
        picker,
        returned_rows.reshape(experts_all * capacity, width_model),
        preferred_element_type=jnp.float32,
    )
    gate_grad = jnp.einsum(
        "tks,s->tk", matches, returned_gates.reshape(-1).astype(jnp.float32), precision=highest
    )
    (embed_grad,) = pullback((cotangent.astype(jnp.float32), normed_grad[None], gate_grad[None]))
    return (embed_grad.astype(jnp.bfloat16), grad_in[None], grad_out[None])


def solution(mesh):
    in_specs = (
        P("exp", "seq", None),
        P(),
        P(),
        P(),
        P("exp", "seq", None),
        P("exp", None, "seq"),
        P("exp", "seq", None),
        P("exp", "seq", None),
    )
    out_specs = (P("exp", "seq", None), P("exp", None, "seq"), P("exp", "seq", None))
    return jax.shard_map(
        per_device, mesh=mesh, in_specs=in_specs, out_specs=out_specs, check_vma=False
    )
```

profile of v0, /device:TPU:0, one launch (start us, length us, event | category | flops | bytes accessed | tf_op | source)
XLA Modules:
  0.0 176.0 jit_solution(9342809860289236321)
XLA Ops:
  7.3 1.9 %reshape.707 = bf16[32,4,1024]{2,1,0:T(4,128)(2,1)} reshape(bf16[1,128,1024]{2,1,0:T(8,128)(2,1)} %param.8) | data formatting | bytes 524288 | tf_op jit(solution)/shard_map/reshape
  9.2 1.1 reshape.709
  10.3 1.3 reshape.708
  11.6 1.0 reshape.710
  14.6 1.6 fusion.26
  17.4 1.5 reduce_sum.182
  18.9 1.1 broadcast_multiply_fusion
  21.1 1.2 broadcast_in_dim.94
  23.0 1.8 %fusion.25 = f32[32,1024]{1,0:T(8,128)S(1)} fusion(f32[1,32,4,1024]{3,2,1,0:T(4,128)} %broadcast_in_dim.94, f32[1,32,4,1024]{3,2,1,0:T(4,128)} %reshape.710, f32[32,4]{1,0:T(8,128)S(1)} %get-tuple-element.14, f32[32,1024]{1,0:T(8,128)S(1)} %broadcast_multiply_fusion.1, f32[32,4]{1,0:T(8,128)S(1)} %get-tuple-element.22, f32[32,4]{1,0:T(8,128)S(1)} %get-tuple-element.21, ...), kind=kLoop, calls=%fused_computation.46 | loop fusion | flops 884736 | bytes 1312768 | tf_op jit(solution)/shard_map/jvp()/reduce_sum | solution.py:35
  26.0 0.9 convolution_convert_fusion.1
  27.0 1.0 stack.7
  27.9 1.1 fusion.15
  29.6 13.4 %all_to_all.25 = bf16[2,8,12,1024]{3,0,2,1:T(2,128)(2,1)} all-to-all(bf16[2,8,12,1024]{3,0,2,1:T(2,128)(2,1)S(1)} %copy.147), channel_id=1, replica_groups=mesh['seq'=4,'exp'=8] {'exp'}, dimensions={1} | all-to-all | bytes 786432 | tf_op jit(solution)/shard_map/all_to_all | solution.py:49
  43.1 0.9 add_divide_fusion.1
  44.3 7.0 %all_to_all.26 = bf16[1,8,12]{2,0,1:T(2,128)(2,1)S(1)} all-to-all(bf16[1,8,12]{2,0,1:T(2,128)(2,1)S(1)} %reshape.729), channel_id=1, replica_groups=mesh['seq'=4,'exp'=8] {'exp'}, dimensions={1} | all-to-all | bytes 384 | tf_op jit(solution)/shard_map/all_to_all | solution.py:50
  51.3 12.6 %all_gather.6 = bf16[1,32,12]{2,1,0:T(8,128)(2,1)S(1)} all-gather(bf16[1,8,12]{2,1,0:T(8,128)(2,1)S(1)} %copy.145), channel_id=1, replica_groups=mesh['seq'=4,'exp'=8] {'seq'}, dimensions={1}, use_global_device_ids=true | all-gather | bytes 960 | tf_op jit(solution)/shard_map/all_gather | solution.py:54
  64.5 15.2 %all-gather.2.cloned.1.call-done = bf16[2,32,12,1024]{3,0,2,1:T(2,128)(2,1)} async-done(((bf16[2,8,12,1024]{3,0,2,1:T(2,128)(2,1)}), bf16[2,32,12,1024]{3,0,2,1:T(2,128)(2,1)}) %all-gather.2.cloned.1.call-update) | async-done | bytes 1572880 | tf_op jit(solution)/shard_map/all_gather | solution.py:53
  79.7 9.8 %slice_reduce_fusion = (bf16[32,12,1024]{2,1,0:T(8,128)(2,1)}, bf16[32,12,1024]{2,1,0:T(8,128)(2,1)}) fusion(bf16[2,32,12,1024]{3,0,2,1:T(2,128)(2,1)} %all-gather.2.cloned.1.call-done), kind=kLoop, calls=%fused_computation.15 | loop fusion | bytes 3145728 | tf_op jit(solution)/shard_map/slice | solution.py:102
  89.6 1.3 reshape_squeeze.7
  90.9 2.1 %reshape_squeeze.6 = bf16[384,1024]{1,0:T(8,128)(2,1)} reshape(bf16[32,12,1024]{2,1,0:T(8,128)(2,1)} %get-tuple-element.4) | data formatting | bytes 1572864 | tf_op jit(solution)/shard_map/reshape;squeeze | solution.py:103
  93.0 2.8 %fusion.4 = f32[384,1024]{1,0:T(8,128)S(1)} fusion(bf16[384,1024]{1,0:T(8,128)(2,1)} %reshape_squeeze.6, bf16[1,1024,1024]{2,1,0:T(8,128)(2,1)} %param.14), kind=kOutput, calls=%fused_computation.7 | convolution fusion | flops 805306368 | bytes 4456448 | tf_op jit(solution)/shard_map/dot_general | solution.py:109
  95.9 3.3 %fusion.11 = (bf16[384,1024]{1,0:T(8,128)(2,1)S(1)}, f32[384]{0:T(512)}, f32[384,1024]{1,0:T(8,128)}) fusion(f32[384,1024]{1,0:T(8,128)S(1)} %fusion.4, f32[384]{0:T(512)S(1)} %copy-done.29, bf16[384,1024]{1,0:T(8,128)(2,1)S(1)} %reshape_squeeze.7, bf16[1,1024,1024]{2,1,0:T(8,128)(2,1)S(1)} %copy-done), kind=kOutput, calls=%fused_computation.14 | convolution fusion | flops 810811008 | bytes 6818816 | tf_op jit(solution)/shard_map/dot_general | solution.py:105
  99.2 0.9 copy-done.8
  100.1 1.9 %fusion.12 = bf16[384,1024]{1,0:T(8,128)(2,1)} fusion(bf16[384,1024]{1,0:T(8,128)(2,1)S(1)} %get-tuple-element.15, bf16[1,1024,1024]{2,1,0:T(8,128)(2,1)S(1)} %copy-done), kind=kOutput, calls=%fused_computation.20 | convolution fusion | flops 805699584 | bytes 3670016 | tf_op jit(solution)/shard_map/dot_general | solution.py:125
  102.0 1.4 mul.503
  103.4 1.3 mul.506
  104.7 1.4 mul.509
  106.8 1.4 copy.154
  108.8 0.8 copy.150
  109.6 2.2 %broadcast_in_dim.102 = f32[1,128,1024]{2,1,0:T(8,128)} reshape(f32[32,2,2,1024]{3,2,1,0:T(2,128)} %copy-done.2) | data formatting | bytes 1048576 | tf_op jit(solution)/shard_map/jvp()/broadcast_in_dim | solution.py:29
  111.8 1.8 %mul.511 = f32[32,4,1024]{2,1,0:T(4,128)} broadcast(f32[32,1024]{1,0:T(8,128)} %copy-done.4), dimensions={0,2} | broadcast | bytes 655360 | tf_op jit(solution)/shard_map/jvp()/mul | solution.py:33
  113.6 2.0 %mul.512 = f32[1,128,1024]{2,1,0:T(8,128)} reshape(f32[32,4,1024]{2,1,0:T(4,128)} %mul.511) | data formatting | bytes 1048576 | tf_op jit(solution)/shard_map/jvp()/mul | solution.py:33
  116.8 9.8 %psum.7 = bf16[384]{0:T(512)(128)(2,1)S(1)} all-reduce(f32[384]{0:T(512)S(1)} %copy-done.43), channel_id=1, replica_groups=mesh['seq'=4,'exp'=8] {'seq'}, use_global_device_ids=true, to_apply=%region_11.12 | all-reduce | flops 384 | bytes 2304 | tf_op jit(solution)/shard_map/psum | solution.py:132
  127.4 3.6 %all-to-all-start.3 = ((bf16[8,1,12]{2,1,0:T(2,128)(2,1)}), bf16[8,1,12]{2,1,0:T(2,128)(2,1)S(1)}, u32[]{:S(2)}, u32[]{:S(2)}) async-start(bf16[8,1,12]{2,1,0:T(2,128)(2,1)} %all_to_all.20), calls=%async_computation.4 | async-start | bytes 8192 | tf_op jit(solution)/shard_map/all_to_all | solution.py:144
  131.0 5.1 %convolution_bitcast_fusion = f32[1,1024,1024]{2,1,0:T(8,128)} fusion(bf16[384,1024]{1,0:T(8,128)(2,1)} %reshape_squeeze.6, f32[384]{0:T(512)S(1)} %copy-done.30, f32[384,1024]{1,0:T(8,128)} %get-tuple-element.27), kind=kOutput, calls=%fused_computation.1 | convolution fusion | flops 807665664 | bytes 6555136 | tf_op jit(solution)/shard_map/dot_general | solution.py:117
  136.1 3.3 %convolution_bitcast_fusion.1 = f32[1,1024,1024]{2,1,0:T(8,128)} fusion(bf16[384,1024]{1,0:T(8,128)(2,1)S(1)} %reshape_squeeze.7, bf16[384,1024]{1,0:T(8,128)(2,1)S(1)} %copy-done.9), kind=kOutput, calls=%fused_computation.2 | convolution fusion | flops 805306368 | bytes 5767168 | tf_op jit(solution)/shard_map/dot_general | solution.py:120
  141.9 1.7 reshape.713
  143.6 4.2 %all-to-all-start.2 = ((bf16[8,12,1024]{2,1,0:T(8,128)(2,1)}), bf16[8,12,1024]{2,1,0:T(8,128)(2,1)S(1)}, u32[]{:S(2)}, u32[]{:S(2)}) async-start(bf16[8,12,1024]{2,1,0:T(8,128)(2,1)} %reshape.713), calls=%async_computation.3 | async-start | bytes 524288 | tf_op jit(solution)/shard_map/all_to_all | solution.py:137
  147.8 1.0 fusion.43
  148.8 5.9 %all-to-all-done.2 = bf16[8,12,1024]{2,1,0:T(8,128)(2,1)S(1)} async-done(((bf16[8,12,1024]{2,1,0:T(8,128)(2,1)}), bf16[8,12,1024]{2,1,0:T(8,128)(2,1)S(1)}, u32[]{:S(2)}, u32[]{:S(2)}) %all-to-all-start.2) | async-done | bytes 196640 | tf_op jit(solution)/shard_map/all_to_all | solution.py:137
  155.1 1.0 fusion.30
  156.1 1.9 %multiply_reduce_fusion.2 = (f32[32,1024]{1,0:T(8,128)S(1)}, f32[32,4]{1,0:T(8,128)}) fusion(f32[32,4]{1,0:T(8,128)S(1)} %get-tuple-element.14, f32[32,1024]{1,0:T(8,128)S(1)} %fusion.30, f32[32,4]{1,0:T(8,128)} %copy-done.12, f32[32,1024]{1,0:T(8,128)S(1)} %copy-done.5), kind=kLoop, calls=%fused_computation.39 | loop fusion | flops 622464 | bytes 394752 | tf_op jit(solution)/shard_map/transpose(jvp())/reduce_sum | solution.py:33
  158.0 1.6 multiply_reduce_fusion.3
  159.7 1.0 broadcast_in_dim.98
  160.7 2.1 %broadcast_in_dim.99 = f32[1,128,1024]{2,1,0:T(8,128)} reshape(f32[32,4,1024]{2,1,0:T(4,128)} %broadcast_in_dim.98) | data formatting | bytes 1048576 | tf_op jit(solution)/shard_map/transpose(jvp())/broadcast_in_dim | solution.py:35
  162.7 1.6 multiply_reduce_fusion.5
  165.3 1.1 broadcast_in_dim.108
  166.4 1.5 broadcast_in_dim.109
  (155 shorter events, 16.1 us)
Async XLA Ops:
  7.2 88.7 %copy-start = (bf16[1,1024,1024]{2,1,0:T(8,128)(2,1)S(1)}, bf16[1,1024,1024]{2,1,0:T(8,128)(2,1)}, u32[]{:S(2)}) copy-start(bf16[1,1024,1024]{2,1,0:T(8,128)(2,1)} %param.13) | copy-start | bytes 6291460
  7.2 4.4 %copy-start.1 = (bf16[1,128,1024]{2,1,0:T(8,128)(2,1)S(1)}, bf16[1,128,1024]{2,1,0:T(8,128)(2,1)}, u32[]{:S(2)}) copy-start(bf16[1,128,1024]{2,1,0:T(8,128)(2,1)} %param.8) | copy-start | bytes 786436
  7.2 5.4 %copy-start.31 = (s32[1,32,2]{1,2,0:T(2,128)S(1)}, s32[1,32,2]{1,2,0:T(2,128)}, u32[]{:S(2)}) copy-start(s32[1,32,2]{1,2,0:T(2,128)} %param.12) | copy-start | bytes 772
  7.2 7.4 %copy-start.21 = (f32[1024]{0:T(1024)S(1)}, f32[1024]{0:T(1024)}, u32[]{:S(2)}) copy-start(f32[1024]{0:T(1024)} %param.9) | copy-start | bytes 12292
  7.2 72.5 %all-gather.2.cloned.1.call-start = ((), (), s32[]{:S(2)}) async-start(), calls=%async_computation.5 | async-start | bytes 1966080 | tf_op jit(solution)/shard_map/all_gather | solution.py:53
  13.9 2.3 %copy-start.18 = (bf16[32,96]{1,0:T(8,128)(2,1)}, bf16[32,96]{1,0:T(8,128)(2,1)S(1)}, u32[]{:S(2)}) copy-start(bf16[32,96]{1,0:T(8,128)(2,1)S(1)} %convert_reduce_fusion) | copy-start | bytes 18436
  17.2 5.8 %copy-start.4 = (f32[32,1024]{1,0:T(8,128)}, f32[32,1024]{1,0:T(8,128)S(1)}, u32[]{:S(2)}) copy-start(f32[32,1024]{1,0:T(8,128)S(1)} %broadcast_multiply_fusion.1) | copy-start | bytes 393220
  17.4 4.9 %copy-start.34 = (f32[32]{0:T(128)}, f32[32]{0:T(128)S(1)}, u32[]{:S(2)}) copy-start(f32[32]{0:T(128)S(1)} %convolution_bitcast_fusion.3) | copy-start | bytes 388
  17.4 4.9 %copy-start.14 = (f32[1,32,4]{2,1,0:T(8,128)S(1)}, f32[1,32,4]{2,1,0:T(8,128)}, u32[]{:S(2)}) copy-start(f32[1,32,4]{2,1,0:T(8,128)} %copy.161) | copy-start | bytes 1540
  20.7 4.1 %copy-start.16 = (f32[32,4]{1,0:T(8,128)}, f32[32,4]{1,0:T(8,128)S(1)}, u32[]{:S(2)}) copy-start(f32[32,4]{1,0:T(8,128)S(1)} %copy.140) | copy-start | bytes 1540
  20.7 5.3 %copy-start.19 = (bf16[32,96]{1,0:T(8,128)(2,1)S(1)}, bf16[32,96]{1,0:T(8,128)(2,1)}, u32[]{:S(2)}) copy-start(bf16[32,96]{1,0:T(8,128)(2,1)} %copy-done.18) | copy-start | bytes 18436
  20.7 5.3 %copy-start.26 = (f32[1024]{0:T(1024)S(1)}, f32[1024]{0:T(1024)}, u32[]{:S(2)}) copy-start(f32[1024]{0:T(1024)} %param.10) | copy-start | bytes 12292
  21.1 6.9 %copy-start.2 = (f32[32,2,2,1024]{3,2,1,0:T(2,128)}, f32[32,2,2,1024]{3,2,1,0:T(2,128)S(1)}, u32[]{:S(2)}) copy-start(f32[32,2,2,1024]{3,2,1,0:T(2,128)S(1)} %broadcast_in_dim.93) | copy-start | bytes 1572868
  23.0 2.5 %copy-start.10 = (f32[32,4]{1,0:T(8,128)}, f32[32,4]{1,0:T(8,128)S(1)}, u32[]{:S(2)}) copy-start(f32[32,4]{1,0:T(8,128)S(1)} %get-tuple-element.20) | copy-start | bytes 1540
  23.0 2.5 %copy-start.12 = (f32[32,4]{1,0:T(8,128)}, f32[32,4]{1,0:T(8,128)S(1)}, u32[]{:S(2)}) copy-start(f32[32,4]{1,0:T(8,128)S(1)} %get-tuple-element.22) | copy-start | bytes 1540
  23.0 2.5 %copy-start.13 = (f32[32,4]{1,0:T(8,128)}, f32[32,4]{1,0:T(8,128)S(1)}, u32[]{:S(2)}) copy-start(f32[32,4]{1,0:T(8,128)S(1)} %get-tuple-element.21) | copy-start | bytes 1540
  24.9 0.6 copy-start.44
  29.0 14.0 %copy-start.24 = (bf16[1024,8]{0,1:T(8,128)(2,1)S(1)}, bf16[1024,8]{0,1:T(8,128)(2,1)}, u32[]{:S(2)}) copy-start(bf16[1024,8]{0,1:T(8,128)(2,1)} %param.11) | copy-start | bytes 49156
  29.0 14.0 %copy-start.27 = (f32[1024]{0:T(1024)S(1)}, f32[1024]{0:T(1024)}, u32[]{:S(2)}) copy-start(f32[1024]{0:T(1024)} %param.10) | copy-start | bytes 12292
  29.0 14.0 %copy-start.42 = (f32[32]{0:T(128)S(1)}, f32[32]{0:T(128)}, u32[]{:S(2)}) copy-start(f32[32]{0:T(128)} %copy-done.41) | copy-start | bytes 388
  29.0 14.9 %copy-start.32 = (s32[1,32,2]{1,2,0:T(2,128)S(1)}, s32[1,32,2]{1,2,0:T(2,128)}, u32[]{:S(2)}) copy-start(s32[1,32,2]{1,2,0:T(2,128)} %param.12) | copy-start | bytes 772
  29.1 14.9 %copy-start.39 = (s32[32,2]{0,1:T(2,128)S(1)}, s32[32,2]{0,1:T(2,128)}, u32[]{:S(2)}) copy-start(s32[32,2]{0,1:T(2,128)} %copy-done.38) | copy-start | bytes 772
  43.0 98.9 %reduce-scatter.2.cloned.1.call-start = ((), (), s32[]{:S(2)}) async-start(), calls=%async_computation.6 | async-start | bytes 983040 | tf_op jit(solution)/shard_map/reduce_scatter | solution.py:124
  44.0 45.6 %copy-start.33 = (f32[32,2]{0,1:T(2,128)}, f32[32,2]{0,1:T(2,128)S(1)}, u32[]{:S(2)}) copy-start(f32[32,2]{0,1:T(2,128)S(1)} %get-tuple-element.12) | copy-start | bytes 772
  44.0 45.6 %copy-start.36 = (f32[32]{0:T(128)}, f32[32]{0:T(128)S(1)}, u32[]{:S(2)}) copy-start(f32[32]{0:T(128)S(1)} %get-tuple-element.11) | copy-start | bytes 388
  93.0 2.9 %copy-start.29 = (f32[384]{0:T(512)S(1)}, f32[384]{0:T(512)}, u32[]{:S(2)}) copy-start(f32[384]{0:T(512)} %reshape.717) | copy-start | bytes 4612
  99.2 0.9 copy-start.8
  109.6 6.1 %copy-start.25 = (f32[32,4]{1,0:T(8,128)S(1)}, f32[32,4]{1,0:T(8,128)}, u32[]{:S(2)}) copy-start(f32[32,4]{1,0:T(8,128)} %get-tuple-element.13) | copy-start | bytes 1540
  109.6 6.7 %copy-start.37 = (f32[32]{0:T(128)S(1)}, f32[32]{0:T(128)}, u32[]{:S(2)}) copy-start(f32[32]{0:T(128)} %copy-done.36) | copy-start | bytes 388
  109.6 7.3 %copy-start.43 = (f32[384]{0:T(512)S(1)}, f32[384]{0:T(512)}, u32[]{:S(2)}) copy-start(f32[384]{0:T(512)} %get-tuple-element.16) | copy-start | bytes 4612
  109.6 21.5 %copy-start.30 = (f32[384]{0:T(512)S(1)}, f32[384]{0:T(512)}, u32[]{:S(2)}) copy-start(f32[384]{0:T(512)} %reshape.717) | copy-start | bytes 4612
  127.4 12.1 %all-to-all-start.3 = ((bf16[8,1,12]{2,1,0:T(2,128)(2,1)}), bf16[8,1,12]{2,1,0:T(2,128)(2,1)S(1)}, u32[]{:S(2)}, u32[]{:S(2)}) async-start(bf16[8,1,12]{2,1,0:T(2,128)(2,1)} %all_to_all.20), calls=%async_computation.4 | async-start | bytes 8192 | tf_op jit(solution)/shard_map/all_to_all | solution.py:144
  131.0 5.1 %copy-start.9 = (bf16[384,1024]{1,0:T(8,128)(2,1)S(1)}, bf16[384,1024]{1,0:T(8,128)(2,1)}, u32[]{:S(2)}) copy-start(bf16[384,1024]{1,0:T(8,128)(2,1)} %copy-done.8) | copy-start | bytes 2359300
  136.1 3.5 %copy-start.40 = (s32[32,2]{0,1:T(2,128)S(1)}, s32[32,2]{0,1:T(2,128)}, u32[]{:S(2)}) copy-start(s32[32,2]{0,1:T(2,128)} %copy-done.38) | copy-start | bytes 772
  139.4 15.3 %copy-start.20 = (bf16[32,96]{1,0:T(8,128)(2,1)S(1)}, bf16[32,96]{1,0:T(8,128)(2,1)}, u32[]{:S(2)}) copy-start(bf16[32,96]{1,0:T(8,128)(2,1)} %copy-done.18) | copy-start | bytes 18436
  139.4 15.3 %copy-start.28 = (f32[1024]{0:T(1024)S(1)}, f32[1024]{0:T(1024)}, u32[]{:S(2)}) copy-start(f32[1024]{0:T(1024)} %param.10) | copy-start | bytes 12292
  139.4 15.6 %copy-start.45 = (f32[32]{0:T(128)S(1)}, f32[32]{0:T(128)}, u32[]{:S(2)}) copy-start(f32[32]{0:T(128)} %copy-done.44) | copy-start | bytes 388
  139.4 16.6 %copy-start.5 = (f32[32,1024]{1,0:T(8,128)S(1)}, f32[32,1024]{1,0:T(8,128)}, u32[]{:S(2)}) copy-start(f32[32,1024]{1,0:T(8,128)} %copy-done.4) | copy-start | bytes 393220
  139.8 18.2 %copy-start.6 = (f32[32,2,1024]{2,0,1:T(8,128)S(1)}, f32[32,2,1024]{2,0,1:T(8,128)}, u32[]{:S(2)}) copy-start(f32[32,2,1024]{2,0,1:T(8,128)} %copy.150) | copy-start | bytes 786436
  143.6 11.1 %all-to-all-start.2 = ((bf16[8,12,1024]{2,1,0:T(8,128)(2,1)}), bf16[8,12,1024]{2,1,0:T(8,128)(2,1)S(1)}, u32[]{:S(2)}, u32[]{:S(2)}) async-start(bf16[8,12,1024]{2,1,0:T(8,128)(2,1)} %reshape.713), calls=%async_computation.3 | async-start | bytes 524288 | tf_op jit(solution)/shard_map/all_to_all | solution.py:137
  155.1 7.7 %copy-start.3 = (f32[1,128,1024]{2,1,0:T(8,128)S(1)}, f32[1,128,1024]{2,1,0:T(8,128)}, u32[]{:S(2)}) copy-start(f32[1,128,1024]{2,1,0:T(8,128)} %broadcast_in_dim.102) | copy-start | bytes 1572868
  160.6 3.9 %copy-start.15 = (f32[1,32,4]{2,1,0:T(8,128)S(1)}, f32[1,32,4]{2,1,0:T(8,128)}, u32[]{:S(2)}) copy-start(f32[1,32,4]{2,1,0:T(8,128)} %copy.161) | copy-start | bytes 1540
  160.6 3.9 %copy-start.17 = (f32[32,4]{1,0:T(8,128)S(1)}, f32[32,4]{1,0:T(8,128)}, u32[]{:S(2)}) copy-start(f32[32,4]{1,0:T(8,128)} %copy-done.16) | copy-start | bytes 1540
  160.6 3.9 %copy-start.23 = (f32[32,4]{1,0:T(8,128)S(1)}, f32[32,4]{1,0:T(8,128)}, u32[]{:S(2)}) copy-start(f32[32,4]{1,0:T(8,128)} %get-tuple-element.8) | copy-start | bytes 1540
  160.6 4.0 %copy-start.35 = (f32[32]{0:T(128)S(1)}, f32[32]{0:T(128)}, u32[]{:S(2)}) copy-start(f32[32]{0:T(128)} %copy-done.34) | copy-start | bytes 388
  160.7 4.3 %copy-start.7 = (f32[32,2,1024]{2,0,1:T(8,128)S(1)}, f32[32,2,1024]{2,0,1:T(8,128)}, u32[]{:S(2)}) copy-start(f32[32,2,1024]{2,0,1:T(8,128)} %get-tuple-element.10) | copy-start | bytes 786436
  160.7 4.3 %copy-start.22 = (f32[1024]{0:T(1024)S(1)}, f32[1024]{0:T(1024)}, u32[]{:S(2)}) copy-start(f32[1024]{0:T(1024)} %param.9) | copy-start | bytes 12292
  164.3 3.7 %copy-start.11 = (f32[32,4]{1,0:T(8,128)S(1)}, f32[32,4]{1,0:T(8,128)}, u32[]{:S(2)}) copy-start(f32[32,4]{1,0:T(8,128)} %copy-done.10) | copy-start | bytes 1540
  (2 other events, 1.1 us)
Sparse Core Ops, SparseCore 0:
  43.1 36.5 all-gather.1
  102.1 22.1 reduce-scatter.1
where the time goes:
time: 177 us; the launch traced here: 176 us
  local copies, waits for them, and re-layouts  49.8 us (28%)
  blocking collectives  42.8 us (24%)
  matrix products  23.3 us (13%)
  waiting for transfers between devices  21.2 us (12%)
  other arithmetic  16.4 us (9%)
  between operations  14.6 us (8%)
  starting transfers between devices  7.9 us (4%)
    all_gather x1, waiting for transfers between devices, deliver(): lax.all_gather(owned_rows, 'seq', axis=1, tiled=True)  15.2 us
    all_to_all x1, blocking collectives, deliver(): lax.all_to_all(row_stack, 'exp', split_axis=1, concat_axis=1, tiled=True)  13.4 us
    all_gather x1, blocking collectives, deliver(): lax.all_gather(owned_gates, 'seq', axis=1, tiled=True)  12.6 us
    slice x1, local copies, waits for them, and re-layouts, per_device(): token_rows = both_rows[0].reshape(slot_count, width_model)  9.82 us
    psum x1, blocking collectives, per_device(): every_term = lax.psum(gate_terms, 'seq')  9.8 us
    all_to_all x1, blocking collectives, deliver(): lax.all_to_all(gates_in, 'exp', split_axis=1, concat_axis=1, tiled=True)  7.04 us
    all_to_all x1, waiting for transfers between devices, per_device(): lax.all_to_all(summed_rows.reshape(owners, capacity, width_model), 'exp',...  5.95 us
    mul x3, local copies, waits for them, and re-layouts, front(): weight_four[..., None] * quad_mean[:, :, None, :]  5.22 us
  transfers between devices with their start and end apart: 4, of which 2 were waited for; matrix products, arithmetic and copies ran while one was open for 16% of the time, Pallas kernels for 0%

commit v1 on v0

v1 whole, which is shorter than its diff:
```python
import functools
import jax
import jax.numpy as jnp
from jax import lax
from jax.experimental import pallas as pl
from jax.experimental.pallas import tpu as pltpu
from jax.sharding import PartitionSpec as P

SQRT_HALF = 0.7071067811865476
INV_ROOT_TWO_PI = 0.3989422804014327
LANES = 128
HALF = LANES // 2
BF = jnp.bfloat16
F32 = jnp.float32
HIGHEST = lax.Precision.HIGHEST
ROWS_T = (((0,), (0,)), ((), ()))
COLS = (((1,), (1,)), ((), ()))
VMEM_LIMIT = 56 * 1024 * 1024


def call(body, name, outs, args, scratch=(), flops=0, nbytes=0, **kwargs):
    return pl.pallas_call(
        body,
        name=name,
        out_shape=outs,
        scratch_shapes=list(scratch),
        compiler_params=pltpu.CompilerParams(vmem_limit_bytes=VMEM_LIMIT),
        cost_estimate=pl.CostEstimate(flops=flops, bytes_accessed=nbytes, transcendentals=0),
        **kwargs,
    )(*args)


def route_mask(routes_t, k, wrap):
    count = routes_t.shape[1]
    lane = lax.broadcasted_iota(jnp.int32, (LANES, count), 0)
    if wrap:
        lane = lane & (HALF - 1)
    mask_t = (lane == routes_t[k : k + 1, :]).astype(F32).astype(BF)
    row = lax.broadcasted_iota(jnp.int32, (count, count), 0)
    col = lax.broadcasted_iota(jnp.int32, (count, count), 1)
    eye = (row == col).astype(F32).astype(BF)
    return lax.dot_general(eye, mask_t, COLS, preferred_element_type=F32)


def cot_payload_kernel(cot_ref, routes_ref, out_ref):
    width = cot_ref.shape[1]
    routes_t = routes_ref[...]
    mask = route_mask(routes_t, 0, False) + route_mask(routes_t, 1, False)
    out_ref[:, :width] = cot_ref[...]
    out_ref[:, width:] = mask.astype(BF)


def quartet_order(count):
    row = lax.broadcasted_iota(jnp.int32, (4 * count, 4 * count), 0)
    col = lax.broadcasted_iota(jnp.int32, (4 * count, 4 * count), 1)
    return (4 * (row % count) + row // count == col).astype(F32).astype(BF)


def quartet_values(embed, count):
    ordered = jnp.dot(quartet_order(count), embed, preferred_element_type=F32)
    return [ordered[q * count : (q + 1) * count, :] for q in range(4)]


def quartet_scores(values, weight):
    ones = [jnp.sum(v * weight, axis=1, keepdims=True) for v in values]
    pairs = [0.5 * (ones[0] + ones[1]), 0.5 * (ones[2] + ones[3])]
    four = 0.5 * (pairs[0] + pairs[1])
    shares = []
    for q in range(4):
        scores = (ones[q], pairs[q // 2], four)
        largest = jnp.maximum(jnp.maximum(scores[0], scores[1]), scores[2])
        weights = [jnp.exp(s - largest) for s in scores]
        denominator = weights[0] + weights[1] + weights[2]
        shares.append([w / denominator for w in weights])
    return shares


def front_kernel(embed_ref, score_ref, gain_ref, router_ref, routes_ref, pay_ref, tok_ref, keep_ref, logit):
    count, width = tok_ref.shape
    experts = router_ref.shape[0]
    values = quartet_values(embed_ref[...], count)
    shares = quartet_scores(values, score_ref[...])
    whole = 0.25 * (shares[0][2] + shares[1][2] + shares[2][2] + shares[3][2])
    coefs = []
    for q in range(4):
        pair = 0.5 * (shares[q][1] + shares[q ^ 1][1])
        coefs.append(0.25 * (shares[q][0] + pair + whole))
    tokens = coefs[0] * values[0] + coefs[1] * values[1] + coefs[2] * values[2] + coefs[3] * values[3]
    tok_ref[...] = tokens
    scale = lax.rsqrt(jnp.mean(tokens * tokens, axis=1, keepdims=True) + 1e-06)
    normed = tokens * scale * gain_ref[...]
    logit[...] = jnp.zeros_like(logit)
    logit[:, :experts] = lax.dot_general(
        normed, router_ref[...].astype(F32), COLS, precision=HIGHEST, preferred_element_type=F32
    )
    logits = logit[...]
    sigmoid = 1.0 / (1.0 + jnp.exp(-logits))
    rest = 1.0 / (1.0 + jnp.exp(logits))
    routes_t = routes_ref[...]
    masks = [route_mask(routes_t, k, False) for k in range(2)]
    picked = [jnp.sum(m * sigmoid, axis=1, keepdims=True) for m in masks]
    others = [jnp.sum(m * rest, axis=1, keepdims=True) for m in masks]
    total = picked[0] + picked[1]
    gates = [p / total for p in picked]
    pay_ref[:, :width] = normed.astype(BF)
    pay_ref[:, width:] = (masks[0] * gates[0] + masks[1] * gates[1]).astype(BF)
    lane = lax.broadcasted_iota(jnp.int32, keep_ref.shape, 1)
    columns = coefs + [s for share in shares for s in share] + [scale] + gates + others
    kept = jnp.zeros(keep_ref.shape, F32)
    for i, column in enumerate(columns):
        kept = jnp.where(lane == i, column, kept)
    keep_ref[...] = kept


def cot_pick_kernel(pieces, chunks, rows, capacity, my_ref, *refs):
    ins, outs, pick_ref = refs[:pieces], refs[pieces : pieces + chunks], refs[pieces + chunks]
    count, full = ins[0].shape
    width = full - LANES
    tokens = pieces * count
    stacked = jnp.concatenate([r[...] for r in ins], axis=0)
    lane_row = lax.broadcasted_iota(jnp.int32, (LANES, LANES), 0)
    lane_col = lax.broadcasted_iota(jnp.int32, (LANES, LANES), 1)
    order = ((lane_row == (lane_col ^ my_ref[0])) & (lane_col < chunks)).astype(F32).astype(BF)
    named = jnp.dot(stacked[:, width:], order, preferred_element_type=F32).astype(BF)
    row = lax.broadcasted_iota(jnp.int32, (tokens, tokens), 0)
    col = lax.broadcasted_iota(jnp.int32, (tokens, tokens), 1)
    eye = (row == col).astype(F32).astype(BF)
    before = ((row < col) & (row // count == col // count)).astype(F32).astype(BF)
    named_t = lax.dot_general(named, eye, ROWS_T, preferred_element_type=F32)
    place_t = lax.dot_general(named, before, ROWS_T, preferred_element_type=F32)
    block = lax.broadcasted_iota(jnp.int32, (LANES, tokens), 1) // count
    place_t = jnp.where(named_t > 0.5, place_t + (block * capacity).astype(F32), -1.0)
    slot = lax.broadcasted_iota(jnp.int32, (rows, tokens), 0).astype(F32)
    for m in range(chunks):
        pick = (place_t[m : m + 1, :] == slot).astype(F32).astype(BF)
        pick_ref[m * rows : (m + 1) * rows, :] = pick
    chosen = jnp.dot(pick_ref[...], stacked[:, :width], preferred_element_type=F32).astype(BF)
    for m in range(chunks):
        outs[m][...] = chosen[m * rows : (m + 1) * rows, :]


def token_pick_kernel(pieces, chunks, rows, pick_ref, *refs):
    ins, outs = refs[:pieces], refs[pieces:]
    stacked = jnp.concatenate([r[...] for r in ins], axis=0)
    chosen = jnp.dot(pick_ref[...], stacked, preferred_element_type=F32).astype(BF)
    for m in range(chunks):
        outs[m][...] = chosen[m * rows : (m + 1) * rows, :]


def upstream_kernel(chunks, rows, *refs):
    ins, weight_ref, out_ref, rows_ref = refs[:chunks], refs[chunks], refs[chunks + 1], refs[chunks + 2]

    @pl.when(pl.program_id(0) == 0)
    def _():
        for m in range(chunks):
            rows_ref[m * rows : (m + 1) * rows, :] = ins[m][...]

    out_ref[...] = lax.dot_general(rows_ref[...], weight_ref[...], COLS, preferred_element_type=F32)


def expert_kernel(chunks, rows, my_ref, *refs):
    ins = refs[:chunks]
    upstream_ref, weight_ref = refs[chunks : chunks + 2]
    outs = refs[chunks + 2 : 2 * chunks + 2]
    rows_ref, gated_ref, grad_ref, total, terms, gate = refs[2 * chunks + 2 :]
    step = pl.program_id(0)
    width = rows_ref.shape[1]
    lane = lax.broadcasted_iota(jnp.int32, (rows, LANES), 1)

    @pl.when(step == 0)
    def _():
        for m in range(chunks):
            at = slice(m * rows, (m + 1) * rows)
            rows_ref[at, :] = ins[m][:, :width]
            tail = ins[m][:, width:].astype(F32)
            gate[at, :] = jnp.sum(jnp.where(lane == my_ref[0], tail, 0.0), axis=1, keepdims=True)

    preact = jnp.dot(rows_ref[...], weight_ref[...], preferred_element_type=F32)
    upstream = upstream_ref[...]
    normal_cdf = 0.5 * (1.0 + lax.erf(preact * SQRT_HALF))
    normal_pdf = INV_ROOT_TWO_PI * jnp.exp(-0.5 * preact * preact)
    hidden = preact * normal_cdf
    scale = gate[...]
    term = jnp.sum(hidden * upstream, axis=1, keepdims=True)
    hidden_grad = (scale * upstream * (normal_cdf + preact * normal_pdf)).astype(BF)
    grad_ref[...] = hidden_grad
    gated_ref[...] = (scale * hidden).astype(BF)
    part = lax.dot_general(hidden_grad, weight_ref[...], COLS, preferred_element_type=F32)

    @pl.when(step == 0)
    def _():
        total[...] = part
        terms[...] = term

    @pl.when(step > 0)
    def _():
        total[...] += part
        terms[...] += term

    @pl.when(step == pl.num_programs(0) - 1)
    def _():
        for m in range(chunks):
            at = slice(m * rows, (m + 1) * rows)
            outs[m][:, :width] = total[at, :].astype(BF)
            exact = terms[at, :]
            high = exact.astype(BF).astype(F32)
            tail = jnp.where(lane == my_ref[0], high, 0.0)
            tail = jnp.where(lane == my_ref[0] + HALF, exact - high, tail)
            outs[m][:, width:] = tail.astype(BF)


def combine_kernel(pieces, chunks, pick_ref, *refs):
    ins, outs = refs[:chunks], refs[chunks:]
    stacked = jnp.concatenate([r[...] for r in ins], axis=0)
    back = lax.dot_general(pick_ref[...], stacked, ROWS_T, preferred_element_type=F32).astype(BF)
    count = back.shape[0] // pieces
    for k in range(pieces):
        outs[k][...] = back[k * count : (k + 1) * count, :]


def back_kernel(pieces, embed_ref, score_ref, gain_ref, router_ref, routes_ref, tok_ref, keep_ref, cot_ref, *refs):
    parts, out_ref = refs[:pieces], refs[pieces]
    count, width = tok_ref.shape
    experts = router_ref.shape[0]
    values = quartet_values(embed_ref[...], count)
    kept = keep_ref[...]
    column = [kept[:, i : i + 1] for i in range(21)]
    coefs = column[:4]
    shares = [column[4 + 3 * q : 7 + 3 * q] for q in range(4)]
    scale, gates, others = column[16], column[17:19], column[19:21]
    summed = parts[0][...].astype(F32)
    for part in parts[1:]:
        summed = summed + part[...].astype(F32)
    routes_t = routes_ref[...]
    masks = [route_mask(routes_t, k, True) for k in range(2)]
    tail = summed[:, width:]
    gate_grad = [jnp.sum(m * tail, axis=1, keepdims=True) for m in masks]
    pull = gates[0] * gates[1] * (gate_grad[0] - gate_grad[1])
    logit_grad = pull * (masks[0] * others[0] - masks[1] * others[1])
    normed_grad = summed[:, :width] + jnp.dot(
        logit_grad[:, :experts], router_ref[...].astype(F32), precision=HIGHEST, preferred_element_type=F32
    )
    tokens = tok_ref[...]
    scaled = gain_ref[...] * normed_grad
    inner = jnp.mean(tokens * scaled, axis=1, keepdims=True)
    token_grad = cot_ref[...].astype(F32) + scale * scaled - tokens * (scale * scale * scale * inner)
    dots = [jnp.sum(token_grad * v, axis=1, keepdims=True) for v in values]
    pairs = [dots[0] + dots[1], dots[2] + dots[3]]
    four = 0.0625 * (pairs[0] + pairs[1])
    score_grads = []
    for q in range(4):
        share = shares[q]
        grads = (0.25 * dots[q], 0.125 * pairs[q // 2], four)
        average = share[0] * grads[0] + share[1] * grads[1] + share[2] * grads[2]
        score_grads.append([s * (g - average) for s, g in zip(share, grads)])
    all_four = 0.25 * (score_grads[0][2] + score_grads[1][2] + score_grads[2][2] + score_grads[3][2])
    weight = score_ref[...]
    ordered = []
    for q in range(4):
        pair = 0.5 * (score_grads[q][1] + score_grads[q ^ 1][1])
        slope = score_grads[q][0] + pair + all_four
        ordered.append((coefs[q] * token_grad + slope * weight).astype(BF))
    out_ref[...] = lax.dot_general(
        quartet_order(count), jnp.concatenate(ordered, axis=0), ROWS_T, preferred_element_type=F32
    ).astype(BF)


def per_device(byte_embed, score_weight, norm_gain, router, routes, expert_in, expert_out, cotangent):
    experts = router.shape[1]
    count = routes.shape[1]
    width = byte_embed.shape[2]
    full = width + LANES
    capacity = max(2, 3 * count // experts)
    pieces = lax.axis_size("seq")
    chunks = lax.axis_size("exp")
    rows = pieces * capacity
    slots = chunks * rows
    tokens = pieces * count
    hidden = expert_in.shape[2]
    tile = min(256, hidden)
    steps = hidden // tile
    my = lax.axis_index("exp").astype(jnp.int32).reshape(1)
    embed = byte_embed[0]
    cot = cotangent[0]
    score_row = score_weight.reshape(1, width)
    gain_row = norm_gain.reshape(1, width)
    router_t = router.T
    routes_t = routes[0].T
    weight_in = expert_in[0]
    weight_out = expert_out[0]
    smem = pl.BlockSpec(memory_space=pltpu.SMEM)
    vmem = pl.BlockSpec()

    def shape(*dims, dtype=BF):
        return jax.ShapeDtypeStruct(dims, dtype)

    def over_seq(values, sign):
        moved = [values[0]]
        for k in range(1, pieces):
            pairs = [(i, (i + sign * k) % pieces) for i in range(pieces)]
            moved.append(lax.ppermute(values[k], "seq", pairs))
        return moved

    def over_exp(values):
        moved = [values[0]]
        for m in range(1, chunks):
            moved.append(lax.ppermute(values[m], "exp", [(i, i ^ m) for i in range(chunks)]))
        return moved

    cot_pay = call(cot_payload_kernel, "cot_payload", shape(count, full), (cot, routes_t))
    cot_all = over_seq([cot_pay] * pieces, 1)
    pay, tok, keep = call(
        front_kernel,
        "front",
        (shape(count, full), shape(count, width, dtype=F32), shape(count, LANES, dtype=F32)),
        (embed, score_row, gain_row, router_t, routes_t),
        scratch=[pltpu.VMEM((count, LANES), F32)],
    )
    pay_all = over_seq([pay] * pieces, 1)
    *cot_chunks, pick = call(
        functools.partial(cot_pick_kernel, pieces, chunks, rows, capacity),
        "cot_pick",
        [shape(rows, width)] * chunks + [shape(slots, tokens)],
        (my, *cot_all),
        in_specs=[smem] + [vmem] * pieces,
    )
    cot_rows = over_exp(cot_chunks)
    pay_chunks = call(
        functools.partial(token_pick_kernel, pieces, chunks, rows),
        "token_pick",
        [shape(rows, full)] * chunks,
        (pick, *pay_all),
    )
    pay_rows = over_exp(pay_chunks)

    def fixed(*dims):
        return pl.BlockSpec(dims, lambda i: (0, 0))

    upstream, cot_slots = call(
        functools.partial(upstream_kernel, chunks, rows),
        "upstream",
        (shape(slots, hidden, dtype=F32), shape(slots, width)),
        (*cot_rows, weight_out),
        grid=(steps,),
        in_specs=[fixed(rows, width)] * chunks + [pl.BlockSpec((tile, width), lambda i: (i, 0))],
        out_specs=(pl.BlockSpec((slots, tile), lambda i: (0, i)), fixed(slots, width)),
    )
    *back_chunks, token_slots, gated_hidden, hidden_grad = call(
        functools.partial(expert_kernel, chunks, rows),
        "expert",
        [shape(rows, full)] * chunks + [shape(slots, width), shape(slots, hidden), shape(slots, hidden)],
        (my, *pay_rows, upstream, weight_in),
        scratch=[pltpu.VMEM((slots, width), F32), pltpu.VMEM((slots, 1), F32), pltpu.VMEM((slots, 1), F32)],
        grid=(steps,),
        in_specs=[smem]
        + [fixed(rows, full)] * chunks
        + [pl.BlockSpec((slots, tile), lambda i: (0, i)), pl.BlockSpec((width, tile), lambda i: (0, i))],
        out_specs=[fixed(rows, full)] * chunks
        + [fixed(slots, width)]
        + [pl.BlockSpec((slots, tile), lambda i: (0, i))] * 2,
    )
    returned = over_exp(back_chunks)
    grad_out = lax.dot_general(gated_hidden, cot_slots, ROWS_T, preferred_element_type=F32)
    grad_in = lax.dot_general(token_slots, hidden_grad, ROWS_T, preferred_element_type=F32)
    partial_rows = call(
        functools.partial(combine_kernel, pieces, chunks),
        "combine",
        [shape(count, full)] * pieces,
        (pick, *returned),
    )
    parts = over_seq(partial_rows, -1)
    embed_grad = call(
        functools.partial(back_kernel, pieces),
        "back",
        shape(4 * count, width),
        (embed, score_row, gain_row, router_t, routes_t, tok, keep, cot, *parts),
    )
    return (embed_grad[None], grad_in[None], grad_out[None])


def solution(mesh):
    in_specs = (
        P("exp", "seq", None),
        P(),
        P(),
        P(),
        P("exp", "seq", None),
        P("exp", None, "seq"),
        P("exp", "seq", None),
        P("exp", "seq", None),
    )
    out_specs = (P("exp", "seq", None), P("exp", None, "seq"), P("exp", "seq", None))
    return jax.shard_map(
        per_device, mesh=mesh, in_specs=in_specs, out_specs=out_specs, check_vma=False
    )
```

time: 177 us -> 93.3 us (0.53)
  local copies, waits for them, and re-layouts: 49.8 us -> 3.34 us
  blocking collectives: 42.8 us -> 0 us
  Pallas kernels: 0 us -> 27.7 us
  starting transfers between devices: 7.9 us -> 31.2 us
  other arithmetic: 16.4 us -> 0 us
  matrix products: 23.3 us -> 7.74 us
  between operations: 14.6 us -> 0.88 us
    ppermute x0 -> x30, starting transfers between devices: none -> 31.2 us  [the longest x21 18.9 us: over_exp(): lax.ppermute(values[m], 'exp', [(i, i ^ m) for i in range(chunks)])]
    pallas_call x0 -> x8, Pallas kernels: none -> 27.7 us  [call(): pl.pallas_call(body, name=name, out_shape=outs, scratch_shapes=list(scrat...]
    ppermute x0 -> x30, waiting for transfers between devices: none -> 22 us  [the longest x21 12.1 us: over_exp(): lax.ppermute(values[m], 'exp', [(i, i ^ m) for i in range(chunks)])]
    all_to_all x2 -> x0, blocking collectives: 20.4 us -> none  [the longest x1 13.4 us: deliver(): lax.all_to_all(row_stack, 'exp', split_axis=1, concat_axis=1, tiled=True)]
    dot_general x15 -> x2, matrix products: 23.3 us -> 7.74 us  [the longest x1 4.44 us: per_device(): lax.dot_general(gated_hidden, cot_slots, ROWS_T, preferred_element_type=F32)]
    all_gather x1 -> x0, waiting for transfers between devices: 15.2 us -> none  [deliver(): lax.all_gather(owned_rows, 'seq', axis=1, tiled=True)]
    all_gather x1 -> x0, blocking collectives: 12.6 us -> none  [deliver(): lax.all_gather(owned_gates, 'seq', axis=1, tiled=True)]
    reduce_sum x13 -> x0, other arithmetic: 10.6 us -> none  [the longest x1 1.86 us: front(): weight_four[..., None] * quad_mean[:, :, None, :]]
  transfers between devices with their start and end apart: 4 -> 30, of which waited for: 2 -> 9; matrix products, arithmetic and copies ran while one was open for 16% -> 8% of each run, Pallas kernels for 0% -> 13%
where the time goes in v1:
time: 93.3 us; the launch traced here: 92.9 us
  starting transfers between devices  31.2 us (33%)
  Pallas kernels  27.7 us (30%)
  waiting for transfers between devices  22 us (24%)
  matrix products  7.74 us (8%)
  local copies, waits for them, and re-layouts  3.34 us (4%)
    pallas_call x8, Pallas kernels, call(): pl.pallas_call(body, name=name, out_shape=outs, scratch_shapes=list(scrat...  27.7 us
    ppermute x21, starting transfers between devices, over_exp(): lax.ppermute(values[m], 'exp', [(i, i ^ m) for i in range(chunks)])  18.9 us
    ppermute x9, starting transfers between devices, over_seq(): moved.append(lax.ppermute(values[k], 'seq', pairs))  12.3 us
    ppermute x21, waiting for transfers between devices, over_exp(): lax.ppermute(values[m], 'exp', [(i, i ^ m) for i in range(chunks)])  12.1 us
    ppermute x9, waiting for transfers between devices, over_seq(): moved.append(lax.ppermute(values[k], 'seq', pairs))  9.95 us
    dot_general x1, matrix products, per_device(): lax.dot_general(gated_hidden, cot_slots, ROWS_T, preferred_element_type=F32)  4.44 us
    unnamed x66, local copies, waits for them, and re-layouts  3.34 us
    dot_general x1, matrix products, per_device(): lax.dot_general(token_slots, hidden_grad, ROWS_T, preferred_element_type=...  3.3 us
  transfers between devices with their start and end apart: 30, of which 9 were waited for; matrix products, arithmetic and copies ran while one was open for 8% of the time, Pallas kernels for 13%

profile of v1, /device:TPU:0, one launch (start us, length us, event | category | flops | bytes accessed | tf_op | source)
XLA Modules:
  0.0 92.9 jit_solution(17955482499222054074)
XLA Ops:
  0.6 1.6 %cot_payload.1.refs_0_ = bf16[32,1152]{1,0:T(8,128)(2,1)} custom-call(bf16[32,1024]{1,0:T(8,128)(2,1)} %bitcast.25, s32[2,32]{1,0:T(2,128)} %bitcast.33), custom_call_target="tpu_custom_call" | custom-call | tf_op jit(solution)/shard_map/cot_payload/pallas_call | solution.py:22
  2.3 5.0 %collective-permute-start.2 = (bf16[32,1152]{1,0:T(8,128)(2,1)}, bf16[32,1152]{1,0:T(8,128)(2,1)S(1)}, u32[]{:S(2)}, u32[]{:S(2)}) collective-permute-start(bf16[32,1152]{1,0:T(8,128)(2,1)} %cot_payload.1.refs_0_), channel_id=1, source_target_pairs={{0,24},{8,0},{16,8},{24,16},{1,25},{9,1},{17,9},{25,17},{2,26},{10... | collective-permute-start | bytes 221192 | tf_op jit(solution)/shard_map/ppermute | solution.py:301
  7.3 1.0 %collective-permute-start = (bf16[32,1152]{1,0:T(8,128)(2,1)}, bf16[32,1152]{1,0:T(8,128)(2,1)S(1)}, u32[]{:S(2)}, u32[]{:S(2)}) collective-permute-start(bf16[32,1152]{1,0:T(8,128)(2,1)} %cot_payload.1.refs_0_), channel_id=1, source_target_pairs={{0,8},{8,16},{16,24},{24,0},{1,9},{9,17},{17,25},{25,1},{2,10},{10... | collective-permute-start | bytes 221192 | tf_op jit(solution)/shard_map/ppermute | solution.py:301
  8.3 2.6 %front.1 = (bf16[32,1152]{1,0:T(8,128)(2,1)}, f32[32,1024]{1,0:T(8,128)}, f32[32,128]{1,0:T(8,128)}) custom-call(bf16[128,1024]{1,0:T(8,128)(2,1)} %bitcast.22, f32[1,1024]{1,0:T(1,128)} %bitcast.29, f32[1,1024]{1,0:T(1,128)} %bitcast.31, bf16[8,1024]{1,0:T(8,128)(2,1)} %bitcast.27, s32[2,32]{1,0:T(2,128)} %bitcast.34), custom_call_target="tpu_custom_call" | custom-call | tf_op jit(solution)/shard_map/front/pallas_call | solution.py:22
  10.9 2.8 %collective-permute-start.5 = (bf16[32,1152]{1,0:T(8,128)(2,1)}, bf16[32,1152]{1,0:T(8,128)(2,1)S(1)}, u32[]{:S(2)}, u32[]{:S(2)}) collective-permute-start(bf16[32,1152]{1,0:T(8,128)(2,1)} %get-tuple-element.43.refs_0_), channel_id=1, source_target_pairs={{0,24},{8,0},{16,8},{24,16},{1,25},{9,1},{17,9},{25,17},{2,26},{10... | collective-permute-start | bytes 221192 | tf_op jit(solution)/shard_map/ppermute | solution.py:301
  13.7 1.1 %collective-permute-start.4 = (bf16[32,1152]{1,0:T(8,128)(2,1)}, bf16[32,1152]{1,0:T(8,128)(2,1)S(1)}, u32[]{:S(2)}, u32[]{:S(2)}) collective-permute-start(bf16[32,1152]{1,0:T(8,128)(2,1)} %get-tuple-element.43.refs_0_), channel_id=1, source_target_pairs={{0,16},{8,24},{16,0},{24,8},{1,17},{9,25},{17,1},{25,9},{2,18},{10... | collective-permute-start | bytes 221192 | tf_op jit(solution)/shard_map/ppermute | solution.py:301
  14.9 0.6 copy-done.29
  15.5 2.5 %cot_pick.1 = (bf16[48,1024]{1,0:T(8,128)(2,1)}, bf16[48,1024]{1,0:T(8,128)(2,1)}, bf16[48,1024]{1,0:T(8,128)(2,1)}, bf16[48,1024]{1,0:T(8,128)(2,1)}, bf16[48,1...) custom-call(s32[1]{0:T(128)} %bitcast.8.my_ref, ...), custom_call_target="tpu_custom_call" | custom-call | tf_op jit(solution)/shard_map/cot_pick/pallas_call | solution.py:22
  18.0 1.5 %collective-permute-start.14 = (bf16[48,1024]{1,0:T(8,128)(2,1)}, bf16[48,1024]{1,0:T(8,128)(2,1)S(1)}, u32[]{:S(2)}, u32[]{:S(2)}) collective-permute-start(bf16[48,1024]{1,0:T(8,128)(2,1)} %get-tuple-element.54), channel_id=1, source_target_pairs={{0,2},{1,3},{2,0},{3,1},{4,6},{5,7},{6,4},{7,5},{8,10},{9,11},{10,... | collective-permute-start | bytes 294920 | tf_op jit(solution)/shard_map/ppermute | solution.py:307
  19.5 0.3 collective-permute-start.15
  19.9 1.5 %collective-permute-start.16 = (bf16[48,1024]{1,0:T(8,128)(2,1)}, bf16[48,1024]{1,0:T(8,128)(2,1)S(1)}, u32[]{:S(2)}, u32[]{:S(2)}) collective-permute-start(bf16[48,1024]{1,0:T(8,128)(2,1)} %get-tuple-element.56), channel_id=1, source_target_pairs={{0,4},{1,5},{2,6},{3,7},{4,0},{5,1},{6,2},{7,3},{8,12},{9,13},{10,... | collective-permute-start | bytes 294920 | tf_op jit(solution)/shard_map/ppermute | solution.py:307
  21.4 0.2 collective-permute-start.3
  21.6 6.2 %collective-permute-done.3.refs_1_ = bf16[32,1152]{1,0:T(8,128)(2,1)S(1)} collective-permute-done((bf16[32,1152]{1,0:T(8,128)(2,1)}, bf16[32,1152]{1,0:T(8,128)(2,1)S(1)}, u32[]{:S(2)}, u32[]{:S(2)}) %collective-permute-start.3) | collective-permute-done | bytes 73760 | tf_op jit(solution)/shard_map/ppermute | solution.py:301
  27.8 0.6 copy-done.32
  28.4 2.3 %token_pick.1 = (bf16[48,1152]{1,0:T(8,128)(2,1)}, bf16[48,1152]{1,0:T(8,128)(2,1)}, bf16[48,1152]{1,0:T(8,128)(2,1)}, bf16[48,1152]{1,0:T(8,128)(2,1)}, bf16[48...) custom-call(bf16[384,128]{1,0:T(8,128)(2,1)} %get-tuple-element.42.pick_ref, ...), custom_call_target="tpu_custom_call" | custom-call | tf_op jit(solution)/shard_map/token_pick/pallas_call | solution.py:22
  30.7 1.6 %collective-permute-start.7 = (bf16[48,1152]{1,0:T(8,128)(2,1)}, bf16[48,1152]{1,0:T(8,128)(2,1)S(1)}, u32[]{:S(2)}, u32[]{:S(2)}) collective-permute-start(bf16[48,1152]{1,0:T(8,128)(2,1)} %get-tuple-element.46), channel_id=1, source_target_pairs={{0,2},{1,3},{2,0},{3,1},{4,6},{5,7},{6,4},{7,5},{8,10},{9,11},{10,... | collective-permute-start | bytes 331784 | tf_op jit(solution)/shard_map/ppermute | solution.py:307
  32.2 0.3 collective-permute-start.17
  32.5 1.5 %collective-permute-start.18 = (bf16[48,1024]{1,0:T(8,128)(2,1)}, bf16[48,1024]{1,0:T(8,128)(2,1)S(1)}, u32[]{:S(2)}, u32[]{:S(2)}) collective-permute-start(bf16[48,1024]{1,0:T(8,128)(2,1)} %get-tuple-element.58), channel_id=1, source_target_pairs={{0,6},{1,7},{2,4},{3,5},{4,2},{5,3},{6,0},{7,1},{8,14},{9,15},{10,... | collective-permute-start | bytes 294920 | tf_op jit(solution)/shard_map/ppermute | solution.py:307
  34.0 1.1 %collective-permute-start.19 = (bf16[48,1024]{1,0:T(8,128)(2,1)}, bf16[48,1024]{1,0:T(8,128)(2,1)S(1)}, u32[]{:S(2)}, u32[]{:S(2)}) collective-permute-start(bf16[48,1024]{1,0:T(8,128)(2,1)} %get-tuple-element.59), channel_id=1, source_target_pairs={{0,7},{1,6},{2,5},{3,4},{4,3},{5,2},{6,1},{7,0},{8,15},{9,14},{10,... | collective-permute-start | bytes 294920 | tf_op jit(solution)/shard_map/ppermute | solution.py:307
  35.1 6.4 %collective-permute-done.17.refs_5_ = bf16[48,1024]{1,0:T(8,128)(2,1)S(1)} collective-permute-done((bf16[48,1024]{1,0:T(8,128)(2,1)}, bf16[48,1024]{1,0:T(8,128)(2,1)S(1)}, u32[]{:S(2)}, u32[]{:S(2)}) %collective-permute-start.17) | collective-permute-done | bytes 98336 | tf_op jit(solution)/shard_map/ppermute | solution.py:307
  41.5 0.2 collective-permute-start.8
  41.7 1.3 %collective-permute-start.10 = (bf16[48,1152]{1,0:T(8,128)(2,1)}, bf16[48,1152]{1,0:T(8,128)(2,1)S(1)}, u32[]{:S(2)}, u32[]{:S(2)}) collective-permute-start(bf16[48,1152]{1,0:T(8,128)(2,1)} %get-tuple-element.49), channel_id=1, source_target_pairs={{0,5},{1,4},{2,7},{3,6},{4,1},{5,0},{6,3},{7,2},{8,13},{9,12},{10,... | collective-permute-start | bytes 331784 | tf_op jit(solution)/shard_map/ppermute | solution.py:307
  43.1 1.8 %collective-permute-start.11 = (bf16[48,1152]{1,0:T(8,128)(2,1)}, bf16[48,1152]{1,0:T(8,128)(2,1)S(1)}, u32[]{:S(2)}, u32[]{:S(2)}) collective-permute-start(bf16[48,1152]{1,0:T(8,128)(2,1)} %get-tuple-element.50), channel_id=1, source_target_pairs={{0,6},{1,7},{2,4},{3,5},{4,2},{5,3},{6,0},{7,1},{8,14},{9,15},{10,... | collective-permute-start | bytes 331784 | tf_op jit(solution)/shard_map/ppermute | solution.py:307
  44.9 1.3 %collective-permute-start.12 = (bf16[48,1152]{1,0:T(8,128)(2,1)}, bf16[48,1152]{1,0:T(8,128)(2,1)S(1)}, u32[]{:S(2)}, u32[]{:S(2)}) collective-permute-start(bf16[48,1152]{1,0:T(8,128)(2,1)} %get-tuple-element.51), channel_id=1, source_target_pairs={{0,7},{1,6},{2,5},{3,4},{4,3},{5,2},{6,1},{7,0},{8,15},{9,14},{10,... | collective-permute-start | bytes 331784 | tf_op jit(solution)/shard_map/ppermute | solution.py:307
  46.2 4.7 %upstream.1 = (f32[384,1024]{1,0:T(8,128)}, bf16[384,1024]{1,0:T(8,128)(2,1)}) custom-call(bf16[48,1024]{1,0:T(8,128)(2,1)} %get-tuple-element.52.refs_0_, bf16[48,1024]{1,0:T(8,128)(2,1)} %copy-done.17, bf16[48,1024]{1,0:T(8,128)(2,1)} %copy-done.18, bf16[48,1024]{1,0:T(8,128)(2,1)} %copy-done.19, bf16[48,1024]{1,0:T(8,128)(2,1)} %copy-done.20, ...), custom_call_target="tpu_custom_call" | custom-call | tf_op jit(solution)/shard_map/upstream/pallas_call | solution.py:22
  50.9 1.7 %collective-permute-done.9.refs_4_ = bf16[48,1152]{1,0:T(8,128)(2,1)S(1)} collective-permute-done((bf16[48,1152]{1,0:T(8,128)(2,1)}, bf16[48,1152]{1,0:T(8,128)(2,1)S(1)}, u32[]{:S(2)}, u32[]{:S(2)}) %collective-permute-start.9) | collective-permute-done | bytes 110624 | tf_op jit(solution)/shard_map/ppermute | solution.py:307
  52.6 0.4 collective-permute-done.10.refs_5_
  53.1 0.2 copy-done.6
  53.2 0.4 copy-done.7
  53.7 8.3 %expert.1 = (bf16[48,1152]{1,0:T(8,128)(2,1)}, bf16[48,1152]{1,0:T(8,128)(2,1)}, bf16[48,1152]{1,0:T(8,128)(2,1)}, bf16[48,1152]{1,0:T(8,128)(2,1)}, bf16[48,115...) custom-call(s32[1]{0:T(128)} %bitcast.8.my_ref, ...), custom_call_target="tpu_custom_call" | custom-call | tf_op jit(solution)/shard_map/expert/pallas_call | solution.py:22
  62.1 0.9 collective-permute-start.20
  63.0 2.0 %collective-permute-start.21 = (bf16[48,1152]{1,0:T(8,128)(2,1)}, bf16[48,1152]{1,0:T(8,128)(2,1)S(1)}, u32[]{:S(2)}, u32[]{:S(2)}) collective-permute-start(bf16[48,1152]{1,0:T(8,128)(2,1)} %get-tuple-element.63), channel_id=1, source_target_pairs={{0,2},{1,3},{2,0},{3,1},{4,6},{5,7},{6,4},{7,5},{8,10},{9,11},{10,... | collective-permute-start | bytes 331784 | tf_op jit(solution)/shard_map/ppermute | solution.py:307
  65.0 0.3 collective-permute-start.23
  65.3 1.2 %collective-permute-start.24 = (bf16[48,1152]{1,0:T(8,128)(2,1)}, bf16[48,1152]{1,0:T(8,128)(2,1)S(1)}, u32[]{:S(2)}, u32[]{:S(2)}) collective-permute-start(bf16[48,1152]{1,0:T(8,128)(2,1)} %get-tuple-element.66), channel_id=1, source_target_pairs={{0,5},{1,4},{2,7},{3,6},{4,1},{5,0},{6,3},{7,2},{8,13},{9,12},{10,... | collective-permute-start | bytes 331784 | tf_op jit(solution)/shard_map/ppermute | solution.py:307
  66.5 1.7 %collective-permute-start.25 = (bf16[48,1152]{1,0:T(8,128)(2,1)}, bf16[48,1152]{1,0:T(8,128)(2,1)S(1)}, u32[]{:S(2)}, u32[]{:S(2)}) collective-permute-start(bf16[48,1152]{1,0:T(8,128)(2,1)} %get-tuple-element.67), channel_id=1, source_target_pairs={{0,6},{1,7},{2,4},{3,5},{4,2},{5,3},{6,0},{7,1},{8,14},{9,15},{10,... | collective-permute-start | bytes 331784 | tf_op jit(solution)/shard_map/ppermute | solution.py:307
  68.2 0.8 collective-permute-done.21.refs_2_
  69.0 0.4 collective-permute-start.26
  69.4 4.4 %convolution_bitcast_fusion = f32[1,1024,1024]{2,1,0:T(8,128)} fusion(bf16[384,1024]{1,0:T(8,128)(2,1)} %get-tuple-element.75, bf16[384,1024]{1,0:T(8,128)(2,1)S(1)} %copy-done.2), kind=kOutput, calls=%fused_computation | convolution fusion | flops 805306368 | bytes 5767168 | tf_op jit(solution)/shard_map/dot_general | solution.py:363
  73.8 2.0 %collective-permute-done.23.refs_4_ = bf16[48,1152]{1,0:T(8,128)(2,1)S(1)} collective-permute-done((bf16[48,1152]{1,0:T(8,128)(2,1)}, bf16[48,1152]{1,0:T(8,128)(2,1)S(1)}, u32[]{:S(2)}, u32[]{:S(2)}) %collective-permute-start.23) | collective-permute-done | bytes 110624 | tf_op jit(solution)/shard_map/ppermute | solution.py:307
  75.8 0.8 collective-permute-done.24.refs_5_
  76.7 0.6 copy-done.14
  77.3 2.3 %combine.1 = (bf16[32,1152]{1,0:T(8,128)(2,1)}, bf16[32,1152]{1,0:T(8,128)(2,1)}, bf16[32,1152]{1,0:T(8,128)(2,1)}, bf16[32,1152]{1,0:T(8,128)(2,1)}) custom-call(bf16[384,128]{1,0:T(8,128)(2,1)} %get-tuple-element.42.pick_ref, bf16[48,1152]{1,0:T(8,128)(2,1)} %get-tuple-element.61.refs_0_, bf16[48,1152]{1,0:T(8,128)(2,1)} %copy-done.10, ...), custom_call_target="tpu_custom_call" | custom-call | tf_op jit(solution)/shard_map/combine/pallas_call | solution.py:22
  79.7 2.0 %collective-permute-start.29 = (bf16[32,1152]{1,0:T(8,128)(2,1)}, bf16[32,1152]{1,0:T(8,128)(2,1)S(1)}, u32[]{:S(2)}, u32[]{:S(2)}) collective-permute-start(bf16[32,1152]{1,0:T(8,128)(2,1)} %get-tuple-element.72), channel_id=1, source_target_pairs={{0,8},{8,16},{16,24},{24,0},{1,9},{9,17},{17,25},{25,1},{2,10},{10... | collective-permute-start | bytes 221192 | tf_op jit(solution)/shard_map/ppermute | solution.py:301
  81.7 3.3 %convolution_bitcast_fusion.1 = f32[1,1024,1024]{2,1,0:T(8,128)} fusion(bf16[384,1024]{1,0:T(8,128)(2,1)S(1)} %copy-done, bf16[384,1024]{1,0:T(8,128)(2,1)S(1)} %copy-done.1), kind=kOutput, calls=%fused_computation.1 | convolution fusion | flops 805306368 | bytes 5767168 | tf_op jit(solution)/shard_map/dot_general | solution.py:364
  85.0 0.8 collective-permute-done.27.refs_1_
  85.8 3.0 %collective-permute-done.28.refs_2_ = bf16[32,1152]{1,0:T(8,128)(2,1)S(1)} collective-permute-done((bf16[32,1152]{1,0:T(8,128)(2,1)}, bf16[32,1152]{1,0:T(8,128)(2,1)S(1)}, u32[]{:S(2)}, u32[]{:S(2)}) %collective-permute-start.28) | collective-permute-done | bytes 73760 | tf_op jit(solution)/shard_map/ppermute | solution.py:301
  88.8 0.6 copy-done.25
  89.5 3.4 %back.1 = bf16[128,1024]{1,0:T(8,128)(2,1)} custom-call(bf16[128,1024]{1,0:T(8,128)(2,1)} %bitcast.23, f32[1,1024]{1,0:T(1,128)} %bitcast.30, f32[1,1024]{1,0:T(1,128)} %bitcast.32, bf16[8,1024]{1,0:T(8,128)(2,1)} %bitcast.28, s32[2,32]{1,0:T(2,128)} %bitcast.35, f32[32,1024]{1,0:T(8,128)} %get-tuple-element.40.tok_ref, ...), custom_call_target="tpu_custom_call" | custom-call | tf_op jit(solution)/shard_map/back/pallas_call | solution.py:22
  (88 shorter events, 0.6 us)
Async XLA Ops:
  2.3 12.6 %collective-permute-start.2 = (bf16[32,1152]{1,0:T(8,128)(2,1)}, bf16[32,1152]{1,0:T(8,128)(2,1)S(1)}, u32[]{:S(2)}, u32[]{:S(2)}) collective-permute-start(bf16[32,1152]{1,0:T(8,128)(2,1)} %cot_payload.1.refs_0_), channel_id=1, source_target_pairs={{0,24},{8,0},{16,8},{24,16},{1,25},{9,1},{17,9},{25,17},{2,26},{10... | collective-permute-start | bytes 221192 | tf_op jit(solution)/shard_map/ppermute | solution.py:301
  7.3 7.5 %collective-permute-start.1 = (bf16[32,1152]{1,0:T(8,128)(2,1)}, bf16[32,1152]{1,0:T(8,128)(2,1)S(1)}, u32[]{:S(2)}, u32[]{:S(2)}) collective-permute-start(bf16[32,1152]{1,0:T(8,128)(2,1)} %cot_payload.1.refs_0_), channel_id=1, source_target_pairs={{0,16},{8,24},{16,0},{24,8},{1,17},{9,25},{17,1},{25,9},{2,18},{10... | collective-permute-start | bytes 221192 | tf_op jit(solution)/shard_map/ppermute | solution.py:301
  7.3 7.6 %collective-permute-start = (bf16[32,1152]{1,0:T(8,128)(2,1)}, bf16[32,1152]{1,0:T(8,128)(2,1)S(1)}, u32[]{:S(2)}, u32[]{:S(2)}) collective-permute-start(bf16[32,1152]{1,0:T(8,128)(2,1)} %cot_payload.1.refs_0_), channel_id=1, source_target_pairs={{0,8},{8,16},{16,24},{24,0},{1,9},{9,17},{17,25},{25,1},{2,10},{10... | collective-permute-start | bytes 221192 | tf_op jit(solution)/shard_map/ppermute | solution.py:301
  10.9 9.0 %collective-permute-start.5 = (bf16[32,1152]{1,0:T(8,128)(2,1)}, bf16[32,1152]{1,0:T(8,128)(2,1)S(1)}, u32[]{:S(2)}, u32[]{:S(2)}) collective-permute-start(bf16[32,1152]{1,0:T(8,128)(2,1)} %get-tuple-element.43.refs_0_), channel_id=1, source_target_pairs={{0,24},{8,0},{16,8},{24,16},{1,25},{9,1},{17,9},{25,17},{2,26},{10... | collective-permute-start | bytes 221192 | tf_op jit(solution)/shard_map/ppermute | solution.py:301
  13.7 7.7 %collective-permute-start.4 = (bf16[32,1152]{1,0:T(8,128)(2,1)}, bf16[32,1152]{1,0:T(8,128)(2,1)S(1)}, u32[]{:S(2)}, u32[]{:S(2)}) collective-permute-start(bf16[32,1152]{1,0:T(8,128)(2,1)} %get-tuple-element.43.refs_0_), channel_id=1, source_target_pairs={{0,16},{8,24},{16,0},{24,8},{1,17},{9,25},{17,1},{25,9},{2,18},{10... | collective-permute-start | bytes 221192 | tf_op jit(solution)/shard_map/ppermute | solution.py:301
  18.0 12.6 %collective-permute-start.13 = (bf16[48,1024]{1,0:T(8,128)(2,1)}, bf16[48,1024]{1,0:T(8,128)(2,1)S(1)}, u32[]{:S(2)}, u32[]{:S(2)}) collective-permute-start(bf16[48,1024]{1,0:T(8,128)(2,1)} %get-tuple-element.53), channel_id=1, source_target_pairs={{0,1},{1,0},{2,3},{3,2},{4,5},{5,4},{6,7},{7,6},{8,9},{9,8},{10,11... | collective-permute-start | bytes 294920 | tf_op jit(solution)/shard_map/ppermute | solution.py:307
  18.0 14.2 %collective-permute-start.14 = (bf16[48,1024]{1,0:T(8,128)(2,1)}, bf16[48,1024]{1,0:T(8,128)(2,1)S(1)}, u32[]{:S(2)}, u32[]{:S(2)}) collective-permute-start(bf16[48,1024]{1,0:T(8,128)(2,1)} %get-tuple-element.54), channel_id=1, source_target_pairs={{0,2},{1,3},{2,0},{3,1},{4,6},{5,7},{6,4},{7,5},{8,10},{9,11},{10,... | collective-permute-start | bytes 294920 | tf_op jit(solution)/shard_map/ppermute | solution.py:307
  19.5 13.0 %collective-permute-start.15 = (bf16[48,1024]{1,0:T(8,128)(2,1)}, bf16[48,1024]{1,0:T(8,128)(2,1)S(1)}, u32[]{:S(2)}, u32[]{:S(2)}) collective-permute-start(bf16[48,1024]{1,0:T(8,128)(2,1)} %get-tuple-element.55), channel_id=1, source_target_pairs={{0,3},{1,2},{2,1},{3,0},{4,7},{5,6},{6,5},{7,4},{8,11},{9,10},{10,... | collective-permute-start | bytes 294920 | tf_op jit(solution)/shard_map/ppermute | solution.py:307
  19.9 7.9 %copy-start.27 = (bf16[32,1152]{1,0:T(8,128)(2,1)}, bf16[32,1152]{1,0:T(8,128)(2,1)S(1)}, u32[]{:S(2)}) copy-start(bf16[32,1152]{1,0:T(8,128)(2,1)S(1)} %collective-permute-done.5.refs_3_) | copy-start | bytes 221188
  19.9 14.1 %collective-permute-start.16 = (bf16[48,1024]{1,0:T(8,128)(2,1)}, bf16[48,1024]{1,0:T(8,128)(2,1)S(1)}, u32[]{:S(2)}, u32[]{:S(2)}) collective-permute-start(bf16[48,1024]{1,0:T(8,128)(2,1)} %get-tuple-element.56), channel_id=1, source_target_pairs={{0,4},{1,5},{2,6},{3,7},{4,0},{5,1},{6,2},{7,3},{8,12},{9,13},{10,... | collective-permute-start | bytes 294920 | tf_op jit(solution)/shard_map/ppermute | solution.py:307
  21.4 6.4 %copy-start.28 = (bf16[32,1152]{1,0:T(8,128)(2,1)}, bf16[32,1152]{1,0:T(8,128)(2,1)S(1)}, u32[]{:S(2)}) copy-start(bf16[32,1152]{1,0:T(8,128)(2,1)S(1)} %collective-permute-done.4.refs_2_) | copy-start | bytes 221188
  21.4 6.4 %collective-permute-start.3 = (bf16[32,1152]{1,0:T(8,128)(2,1)}, bf16[32,1152]{1,0:T(8,128)(2,1)S(1)}, u32[]{:S(2)}, u32[]{:S(2)}) collective-permute-start(bf16[32,1152]{1,0:T(8,128)(2,1)} %get-tuple-element.43.refs_0_), channel_id=1, source_target_pairs={{0,8},{8,16},{16,24},{24,0},{1,9},{9,17},{17,25},{25,1},{2,10},{10... | collective-permute-start | bytes 221192 | tf_op jit(solution)/shard_map/ppermute | solution.py:301
  30.7 12.4 %collective-permute-start.6 = (bf16[48,1152]{1,0:T(8,128)(2,1)}, bf16[48,1152]{1,0:T(8,128)(2,1)S(1)}, u32[]{:S(2)}, u32[]{:S(2)}) collective-permute-start(bf16[48,1152]{1,0:T(8,128)(2,1)} %get-tuple-element.45), channel_id=1, source_target_pairs={{0,1},{1,0},{2,3},{3,2},{4,5},{5,4},{6,7},{7,6},{8,9},{9,8},{10,11... | collective-permute-start | bytes 331784 | tf_op jit(solution)/shard_map/ppermute | solution.py:307
  30.7 15.5 %copy-start.17 = (bf16[48,1024]{1,0:T(8,128)(2,1)}, bf16[48,1024]{1,0:T(8,128)(2,1)S(1)}, u32[]{:S(2)}) copy-start(bf16[48,1024]{1,0:T(8,128)(2,1)S(1)} %collective-permute-done.13.refs_1_) | copy-start | bytes 294916
  30.7 14.2 %collective-permute-start.7 = (bf16[48,1152]{1,0:T(8,128)(2,1)}, bf16[48,1152]{1,0:T(8,128)(2,1)S(1)}, u32[]{:S(2)}, u32[]{:S(2)}) collective-permute-start(bf16[48,1152]{1,0:T(8,128)(2,1)} %get-tuple-element.46), channel_id=1, source_target_pairs={{0,2},{1,3},{2,0},{3,1},{4,6},{5,7},{6,4},{7,5},{8,10},{9,11},{10,... | collective-permute-start | bytes 331784 | tf_op jit(solution)/shard_map/ppermute | solution.py:307
  32.2 13.9 %copy-start.18 = (bf16[48,1024]{1,0:T(8,128)(2,1)}, bf16[48,1024]{1,0:T(8,128)(2,1)S(1)}, u32[]{:S(2)}) copy-start(bf16[48,1024]{1,0:T(8,128)(2,1)S(1)} %collective-permute-done.14.refs_2_) | copy-start | bytes 294916
  32.2 9.3 %collective-permute-start.17 = (bf16[48,1024]{1,0:T(8,128)(2,1)}, bf16[48,1024]{1,0:T(8,128)(2,1)S(1)}, u32[]{:S(2)}, u32[]{:S(2)}) collective-permute-start(bf16[48,1024]{1,0:T(8,128)(2,1)} %get-tuple-element.57), channel_id=1, source_target_pairs={{0,5},{1,4},{2,7},{3,6},{4,1},{5,0},{6,3},{7,2},{8,13},{9,12},{10,... | collective-permute-start | bytes 294920 | tf_op jit(solution)/shard_map/ppermute | solution.py:307
  32.5 13.6 %copy-start.19 = (bf16[48,1024]{1,0:T(8,128)(2,1)}, bf16[48,1024]{1,0:T(8,128)(2,1)S(1)}, u32[]{:S(2)}) copy-start(bf16[48,1024]{1,0:T(8,128)(2,1)S(1)} %collective-permute-done.15.refs_3_) | copy-start | bytes 294916
  32.5 9.2 %collective-permute-start.18 = (bf16[48,1024]{1,0:T(8,128)(2,1)}, bf16[48,1024]{1,0:T(8,128)(2,1)S(1)}, u32[]{:S(2)}, u32[]{:S(2)}) collective-permute-start(bf16[48,1024]{1,0:T(8,128)(2,1)} %get-tuple-element.58), channel_id=1, source_target_pairs={{0,6},{1,7},{2,4},{3,5},{4,2},{5,3},{6,0},{7,1},{8,14},{9,15},{10,... | collective-permute-start | bytes 294920 | tf_op jit(solution)/shard_map/ppermute | solution.py:307
  34.0 12.1 %copy-start.20 = (bf16[48,1024]{1,0:T(8,128)(2,1)}, bf16[48,1024]{1,0:T(8,128)(2,1)S(1)}, u32[]{:S(2)}) copy-start(bf16[48,1024]{1,0:T(8,128)(2,1)S(1)} %collective-permute-done.16.refs_4_) | copy-start | bytes 294916
  34.0 7.7 %collective-permute-start.19 = (bf16[48,1024]{1,0:T(8,128)(2,1)}, bf16[48,1024]{1,0:T(8,128)(2,1)S(1)}, u32[]{:S(2)}, u32[]{:S(2)}) collective-permute-start(bf16[48,1024]{1,0:T(8,128)(2,1)} %get-tuple-element.59), channel_id=1, source_target_pairs={{0,7},{1,6},{2,5},{3,4},{4,3},{5,2},{6,1},{7,0},{8,15},{9,14},{10,... | collective-permute-start | bytes 294920 | tf_op jit(solution)/shard_map/ppermute | solution.py:307
  41.5 4.6 %copy-start.21 = (bf16[48,1024]{1,0:T(8,128)(2,1)}, bf16[48,1024]{1,0:T(8,128)(2,1)S(1)}, u32[]{:S(2)}) copy-start(bf16[48,1024]{1,0:T(8,128)(2,1)S(1)} %collective-permute-done.17.refs_5_) | copy-start | bytes 294916
  41.5 9.4 %collective-permute-start.8 = (bf16[48,1152]{1,0:T(8,128)(2,1)}, bf16[48,1152]{1,0:T(8,128)(2,1)S(1)}, u32[]{:S(2)}, u32[]{:S(2)}) collective-permute-start(bf16[48,1152]{1,0:T(8,128)(2,1)} %get-tuple-element.47), channel_id=1, source_target_pairs={{0,3},{1,2},{2,1},{3,0},{4,7},{5,6},{6,5},{7,4},{8,11},{9,10},{10,... | collective-permute-start | bytes 331784 | tf_op jit(solution)/shard_map/ppermute | solution.py:307
  41.7 4.4 %copy-start.22 = (bf16[48,1024]{1,0:T(8,128)(2,1)}, bf16[48,1024]{1,0:T(8,128)(2,1)S(1)}, u32[]{:S(2)}) copy-start(bf16[48,1024]{1,0:T(8,128)(2,1)S(1)} %collective-permute-done.18.refs_6_) | copy-start | bytes 294916
  41.7 10.9 %collective-permute-start.9 = (bf16[48,1152]{1,0:T(8,128)(2,1)}, bf16[48,1152]{1,0:T(8,128)(2,1)S(1)}, u32[]{:S(2)}, u32[]{:S(2)}) collective-permute-start(bf16[48,1152]{1,0:T(8,128)(2,1)} %get-tuple-element.48), channel_id=1, source_target_pairs={{0,4},{1,5},{2,6},{3,7},{4,0},{5,1},{6,2},{7,3},{8,12},{9,13},{10,... | collective-permute-start | bytes 331784 | tf_op jit(solution)/shard_map/ppermute | solution.py:307
  41.7 4.4 %copy-start.23 = (bf16[48,1024]{1,0:T(8,128)(2,1)}, bf16[48,1024]{1,0:T(8,128)(2,1)S(1)}, u32[]{:S(2)}) copy-start(bf16[48,1024]{1,0:T(8,128)(2,1)S(1)} %collective-permute-done.19.refs_7_) | copy-start | bytes 294916
  41.7 11.3 %collective-permute-start.10 = (bf16[48,1152]{1,0:T(8,128)(2,1)}, bf16[48,1152]{1,0:T(8,128)(2,1)S(1)}, u32[]{:S(2)}, u32[]{:S(2)}) collective-permute-start(bf16[48,1152]{1,0:T(8,128)(2,1)} %get-tuple-element.49), channel_id=1, source_target_pairs={{0,5},{1,4},{2,7},{3,6},{4,1},{5,0},{6,3},{7,2},{8,13},{9,12},{10,... | collective-permute-start | bytes 331784 | tf_op jit(solution)/shard_map/ppermute | solution.py:307
  43.1 10.0 %copy-start.3 = (bf16[48,1152]{1,0:T(8,128)(2,1)}, bf16[48,1152]{1,0:T(8,128)(2,1)S(1)}, u32[]{:S(2)}) copy-start(bf16[48,1152]{1,0:T(8,128)(2,1)S(1)} %collective-permute-done.6.refs_1_) | copy-start | bytes 331780
  43.1 9.9 %collective-permute-start.11 = (bf16[48,1152]{1,0:T(8,128)(2,1)}, bf16[48,1152]{1,0:T(8,128)(2,1)S(1)}, u32[]{:S(2)}, u32[]{:S(2)}) collective-permute-start(bf16[48,1152]{1,0:T(8,128)(2,1)} %get-tuple-element.50), channel_id=1, source_target_pairs={{0,6},{1,7},{2,4},{3,5},{4,2},{5,3},{6,0},{7,1},{8,14},{9,15},{10,... | collective-permute-start | bytes 331784 | tf_op jit(solution)/shard_map/ppermute | solution.py:307
  44.9 8.2 %copy-start.4 = (bf16[48,1152]{1,0:T(8,128)(2,1)}, bf16[48,1152]{1,0:T(8,128)(2,1)S(1)}, u32[]{:S(2)}) copy-start(bf16[48,1152]{1,0:T(8,128)(2,1)S(1)} %collective-permute-done.7.refs_2_) | copy-start | bytes 331780
  44.9 8.2 %collective-permute-start.12 = (bf16[48,1152]{1,0:T(8,128)(2,1)}, bf16[48,1152]{1,0:T(8,128)(2,1)S(1)}, u32[]{:S(2)}, u32[]{:S(2)}) collective-permute-start(bf16[48,1152]{1,0:T(8,128)(2,1)} %get-tuple-element.51), channel_id=1, source_target_pairs={{0,7},{1,6},{2,5},{3,4},{4,3},{5,2},{6,1},{7,0},{8,15},{9,14},{10,... | collective-permute-start | bytes 331784 | tf_op jit(solution)/shard_map/ppermute | solution.py:307
  50.9 18.5 %copy-start.2 = (bf16[384,1024]{1,0:T(8,128)(2,1)S(1)}, bf16[384,1024]{1,0:T(8,128)(2,1)}, u32[]{:S(2)}) copy-start(bf16[384,1024]{1,0:T(8,128)(2,1)} %get-tuple-element.76) | copy-start | bytes 2359300
  62.1 19.6 %copy-start = (bf16[384,1024]{1,0:T(8,128)(2,1)S(1)}, bf16[384,1024]{1,0:T(8,128)(2,1)}, u32[]{:S(2)}) copy-start(bf16[384,1024]{1,0:T(8,128)(2,1)} %get-tuple-element.73) | copy-start | bytes 2359300
  62.1 19.6 %copy-start.1 = (bf16[384,1024]{1,0:T(8,128)(2,1)S(1)}, bf16[384,1024]{1,0:T(8,128)(2,1)}, u32[]{:S(2)}) copy-start(bf16[384,1024]{1,0:T(8,128)(2,1)} %get-tuple-element.74) | copy-start | bytes 2359300
  62.1 4.4 %collective-permute-start.20 = (bf16[48,1152]{1,0:T(8,128)(2,1)}, bf16[48,1152]{1,0:T(8,128)(2,1)S(1)}, u32[]{:S(2)}, u32[]{:S(2)}) collective-permute-start(bf16[48,1152]{1,0:T(8,128)(2,1)} %get-tuple-element.62), channel_id=1, source_target_pairs={{0,1},{1,0},{2,3},{3,2},{4,5},{5,4},{6,7},{7,6},{8,9},{9,8},{10,11... | collective-permute-start | bytes 331784 | tf_op jit(solution)/shard_map/ppermute | solution.py:307
  63.0 6.0 %collective-permute-start.21 = (bf16[48,1152]{1,0:T(8,128)(2,1)}, bf16[48,1152]{1,0:T(8,128)(2,1)S(1)}, u32[]{:S(2)}, u32[]{:S(2)}) collective-permute-start(bf16[48,1152]{1,0:T(8,128)(2,1)} %get-tuple-element.63), channel_id=1, source_target_pairs={{0,2},{1,3},{2,0},{3,1},{4,6},{5,7},{6,4},{7,5},{8,10},{9,11},{10,... | collective-permute-start | bytes 331784 | tf_op jit(solution)/shard_map/ppermute | solution.py:307
  65.0 8.9 %collective-permute-start.22 = (bf16[48,1152]{1,0:T(8,128)(2,1)}, bf16[48,1152]{1,0:T(8,128)(2,1)S(1)}, u32[]{:S(2)}, u32[]{:S(2)}) collective-permute-start(bf16[48,1152]{1,0:T(8,128)(2,1)} %get-tuple-element.64), channel_id=1, source_target_pairs={{0,3},{1,2},{2,1},{3,0},{4,7},{5,6},{6,5},{7,4},{8,11},{9,10},{10,... | collective-permute-start | bytes 331784 | tf_op jit(solution)/shard_map/ppermute | solution.py:307
  65.0 10.9 %collective-permute-start.23 = (bf16[48,1152]{1,0:T(8,128)(2,1)}, bf16[48,1152]{1,0:T(8,128)(2,1)S(1)}, u32[]{:S(2)}, u32[]{:S(2)}) collective-permute-start(bf16[48,1152]{1,0:T(8,128)(2,1)} %get-tuple-element.65), channel_id=1, source_target_pairs={{0,4},{1,5},{2,6},{3,7},{4,0},{5,1},{6,2},{7,3},{8,12},{9,13},{10,... | collective-permute-start | bytes 331784 | tf_op jit(solution)/shard_map/ppermute | solution.py:307
  65.3 11.4 %collective-permute-start.24 = (bf16[48,1152]{1,0:T(8,128)(2,1)}, bf16[48,1152]{1,0:T(8,128)(2,1)S(1)}, u32[]{:S(2)}, u32[]{:S(2)}) collective-permute-start(bf16[48,1152]{1,0:T(8,128)(2,1)} %get-tuple-element.66), channel_id=1, source_target_pairs={{0,5},{1,4},{2,7},{3,6},{4,1},{5,0},{6,3},{7,2},{8,13},{9,12},{10,... | collective-permute-start | bytes 331784 | tf_op jit(solution)/shard_map/ppermute | solution.py:307
  66.5 10.2 %copy-start.10 = (bf16[48,1152]{1,0:T(8,128)(2,1)}, bf16[48,1152]{1,0:T(8,128)(2,1)S(1)}, u32[]{:S(2)}) copy-start(bf16[48,1152]{1,0:T(8,128)(2,1)S(1)} %collective-permute-done.20.refs_1_) | copy-start | bytes 331780
  66.5 10.1 %collective-permute-start.25 = (bf16[48,1152]{1,0:T(8,128)(2,1)}, bf16[48,1152]{1,0:T(8,128)(2,1)S(1)}, u32[]{:S(2)}, u32[]{:S(2)}) collective-permute-start(bf16[48,1152]{1,0:T(8,128)(2,1)} %get-tuple-element.67), channel_id=1, source_target_pairs={{0,6},{1,7},{2,4},{3,5},{4,2},{5,3},{6,0},{7,1},{8,14},{9,15},{10,... | collective-permute-start | bytes 331784 | tf_op jit(solution)/shard_map/ppermute | solution.py:307
  69.0 7.7 %copy-start.11 = (bf16[48,1152]{1,0:T(8,128)(2,1)}, bf16[48,1152]{1,0:T(8,128)(2,1)S(1)}, u32[]{:S(2)}) copy-start(bf16[48,1152]{1,0:T(8,128)(2,1)S(1)} %collective-permute-done.21.refs_2_) | copy-start | bytes 331780
  69.0 7.6 %collective-permute-start.26 = (bf16[48,1152]{1,0:T(8,128)(2,1)}, bf16[48,1152]{1,0:T(8,128)(2,1)S(1)}, u32[]{:S(2)}, u32[]{:S(2)}) collective-permute-start(bf16[48,1152]{1,0:T(8,128)(2,1)} %get-tuple-element.68), channel_id=1, source_target_pairs={{0,7},{1,6},{2,5},{3,4},{4,3},{5,2},{6,1},{7,0},{8,15},{9,14},{10,... | collective-permute-start | bytes 331784 | tf_op jit(solution)/shard_map/ppermute | solution.py:307
  73.8 2.8 %copy-start.12 = (bf16[48,1152]{1,0:T(8,128)(2,1)}, bf16[48,1152]{1,0:T(8,128)(2,1)S(1)}, u32[]{:S(2)}) copy-start(bf16[48,1152]{1,0:T(8,128)(2,1)S(1)} %collective-permute-done.22.refs_3_) | copy-start | bytes 331780
  79.7 6.2 %collective-permute-start.27 = (bf16[32,1152]{1,0:T(8,128)(2,1)}, bf16[32,1152]{1,0:T(8,128)(2,1)S(1)}, u32[]{:S(2)}, u32[]{:S(2)}) collective-permute-start(bf16[32,1152]{1,0:T(8,128)(2,1)} %get-tuple-element.70), channel_id=1, source_target_pairs={{0,24},{8,0},{16,8},{24,16},{1,25},{9,1},{17,9},{25,17},{2,26},{10... | collective-permute-start | bytes 221192 | tf_op jit(solution)/shard_map/ppermute | solution.py:301
  79.7 9.1 %collective-permute-start.28 = (bf16[32,1152]{1,0:T(8,128)(2,1)}, bf16[32,1152]{1,0:T(8,128)(2,1)S(1)}, u32[]{:S(2)}, u32[]{:S(2)}) collective-permute-start(bf16[32,1152]{1,0:T(8,128)(2,1)} %get-tuple-element.71), channel_id=1, source_target_pairs={{0,16},{8,24},{16,0},{24,8},{1,17},{9,25},{17,1},{25,9},{2,18},{10... | collective-permute-start | bytes 221192 | tf_op jit(solution)/shard_map/ppermute | solution.py:301
  79.7 9.1 %collective-permute-start.29 = (bf16[32,1152]{1,0:T(8,128)(2,1)}, bf16[32,1152]{1,0:T(8,128)(2,1)S(1)}, u32[]{:S(2)}, u32[]{:S(2)}) collective-permute-start(bf16[32,1152]{1,0:T(8,128)(2,1)} %get-tuple-element.72), channel_id=1, source_target_pairs={{0,8},{8,16},{16,24},{24,0},{1,9},{9,17},{17,25},{25,1},{2,10},{10... | collective-permute-start | bytes 221192 | tf_op jit(solution)/shard_map/ppermute | solution.py:301
  85.8 3.0 %copy-start.24 = (bf16[32,1152]{1,0:T(8,128)(2,1)}, bf16[32,1152]{1,0:T(8,128)(2,1)S(1)}, u32[]{:S(2)}) copy-start(bf16[32,1152]{1,0:T(8,128)(2,1)S(1)} %collective-permute-done.27.refs_1_) | copy-start | bytes 221188
  (15 other events, 11.5 us)

commit v2 on v1

v2 whole, which is shorter than its diff:
```python
import functools
import jax
import jax.numpy as jnp
from jax import lax
from jax.experimental import pallas as pl
from jax.experimental.pallas import tpu as pltpu
from jax.sharding import PartitionSpec as P

SQRT_HALF = 0.7071067811865476
INV_ROOT_TWO_PI = 0.3989422804014327
LANES = 128
HALF = LANES // 2
BF = jnp.bfloat16
F32 = jnp.float32
HIGHEST = lax.Precision.HIGHEST
ROWS_T = (((0,), (0,)), ((), ()))
COLS = (((1,), (1,)), ((), ()))
MIB = 1024 * 1024
BYTES_PER_US = 0


def call(body, name, outs, args, us, scratch=(), limit=8, scalars=0, held=True):
    vmem = pl.BlockSpec(memory_space=pltpu.VMEM)
    smem = pl.BlockSpec(memory_space=pltpu.SMEM)
    rest = vmem if held else pl.BlockSpec(memory_space=pltpu.HBM)
    return pl.pallas_call(
        body,
        name=name,
        out_shape=outs,
        in_specs=[smem] * scalars + [rest] * (len(args) - scalars),
        out_specs=jax.tree.map(lambda _: vmem, outs),
        scratch_shapes=list(scratch),
        compiler_params=pltpu.CompilerParams(vmem_limit_bytes=limit * MIB),
        cost_estimate=pl.CostEstimate(flops=0, bytes_accessed=int(us * BYTES_PER_US), transcendentals=0),
    )(*args)


def route_mask(routes_t, k, wrap):
    count = routes_t.shape[1]
    lane = lax.broadcasted_iota(jnp.int32, (LANES, count), 0)
    if wrap:
        lane = lane & (HALF - 1)
    mask_t = (lane == routes_t[k : k + 1, :]).astype(F32).astype(BF)
    row = lax.broadcasted_iota(jnp.int32, (count, count), 0)
    col = lax.broadcasted_iota(jnp.int32, (count, count), 1)
    eye = (row == col).astype(F32).astype(BF)
    return lax.dot_general(eye, mask_t, COLS, preferred_element_type=F32)


def quartet_order(count):
    row = lax.broadcasted_iota(jnp.int32, (4 * count, 4 * count), 0)
    col = lax.broadcasted_iota(jnp.int32, (4 * count, 4 * count), 1)
    return (4 * (row % count) + row // count == col).astype(F32).astype(BF)


def quartet_values(embed, count):
    ordered = jnp.dot(quartet_order(count), embed, preferred_element_type=F32)
    return [ordered[q * count : (q + 1) * count, :] for q in range(4)]


def quartet_scores(values, weight):
    ones = [jnp.sum(v * weight, axis=1, keepdims=True) for v in values]
    pairs = [0.5 * (ones[0] + ones[1]), 0.5 * (ones[2] + ones[3])]
    four = 0.5 * (pairs[0] + pairs[1])
    shares = []
    for q in range(4):
        scores = (ones[q], pairs[q // 2], four)
        largest = jnp.maximum(jnp.maximum(scores[0], scores[1]), scores[2])
        weights = [jnp.exp(s - largest) for s in scores]
        denominator = weights[0] + weights[1] + weights[2]
        shares.append([w / denominator for w in weights])
    return shares


def front_kernel(*refs):
    far, outs, near, logit, arrived = refs[:6], refs[6:10], refs[10:16], refs[16], refs[17]
    copies = [pltpu.make_async_copy(a, b, arrived.at[i]) for i, (a, b) in enumerate(zip(far, near))]
    for copy in copies:
        copy.start()
    embed_ref, score_ref, gain_ref, router_ref, routes_ref, cot_ref = near
    both_ref, pay_ref, tok_ref, keep_ref = outs
    for copy in copies:
        copy.wait()
    count, width = tok_ref.shape
    experts = router_ref.shape[0]
    values = quartet_values(embed_ref[...], count)
    shares = quartet_scores(values, score_ref[...])
    whole = 0.25 * (shares[0][2] + shares[1][2] + shares[2][2] + shares[3][2])
    coefs = []
    for q in range(4):
        pair = 0.5 * (shares[q][1] + shares[q ^ 1][1])
        coefs.append(0.25 * (shares[q][0] + pair + whole))
    tokens = coefs[0] * values[0] + coefs[1] * values[1] + coefs[2] * values[2] + coefs[3] * values[3]
    tok_ref[...] = tokens
    scale = lax.rsqrt(jnp.mean(tokens * tokens, axis=1, keepdims=True) + 1e-06)
    normed = tokens * scale * gain_ref[...]
    logit[...] = jnp.zeros_like(logit)
    logit[:, :experts] = lax.dot_general(
        normed, router_ref[...].astype(F32), COLS, precision=HIGHEST, preferred_element_type=F32
    )
    logits = logit[...]
    sigmoid = 1.0 / (1.0 + jnp.exp(-logits))
    rest = 1.0 / (1.0 + jnp.exp(logits))
    routes_t = routes_ref[...]
    masks = [route_mask(routes_t, k, False) for k in range(2)]
    picked = [jnp.sum(m * sigmoid, axis=1, keepdims=True) for m in masks]
    others = [jnp.sum(m * rest, axis=1, keepdims=True) for m in masks]
    total = picked[0] + picked[1]
    gates = [p / total for p in picked]
    named = masks[0] + masks[1]
    wide_masks = [route_mask(routes_t, k, True) for k in range(2)]
    gated = wide_masks[0] * gates[0] + wide_masks[1] * gates[1]
    first_half = lax.broadcasted_iota(jnp.int32, named.shape, 1) < HALF
    pay_ref[:, :width] = normed.astype(BF)
    pay_ref[:, width:] = jnp.where(first_half, named, gated).astype(BF)
    both_ref[:, :width] = cot_ref[...]
    both_ref[:, width:] = pay_ref[...]
    lane = lax.broadcasted_iota(jnp.int32, keep_ref.shape, 1)
    columns = coefs + [s for share in shares for s in share] + [scale] + gates + others
    kept = jnp.zeros(keep_ref.shape, F32)
    for i, column in enumerate(columns):
        kept = jnp.where(lane == i, column, kept)
    keep_ref[...] = kept


def gather_kernel(*refs):
    ins, out_ref = refs[:-1], refs[-1]
    at = 0
    for r in ins:
        out_ref[at : at + r.shape[0], :] = r[...]
        at += r.shape[0]


def slot_places(tail, chunks, capacity, count, blocks, halves, my):
    tokens = tail.shape[0]
    lane_row = lax.broadcasted_iota(jnp.int32, (LANES, LANES), 0)
    lane_col = lax.broadcasted_iota(jnp.int32, (LANES, LANES), 1)
    named_lane = (2 * lane_col) ^ my
    live = lane_col < chunks
    order = ((lane_row == named_lane) & live).astype(F32).astype(BF)
    gate_order = ((lane_row == named_lane + HALF) & live).astype(F32).astype(BF)
    named = jnp.dot(tail, order, preferred_element_type=F32).astype(BF)
    gates = jnp.dot(tail, gate_order, preferred_element_type=F32).astype(BF)
    row = lax.broadcasted_iota(jnp.int32, (tokens, tokens), 0)
    col = lax.broadcasted_iota(jnp.int32, (tokens, tokens), 1)
    eye = (row == col).astype(F32).astype(BF)
    before = ((row < col) & (row // count == col // count)).astype(F32).astype(BF)
    named_t = lax.dot_general(named, eye, ROWS_T, preferred_element_type=F32)
    gates_t = lax.dot_general(gates, eye, ROWS_T, preferred_element_type=F32)
    place_t = lax.dot_general(named, before, ROWS_T, preferred_element_type=F32)
    block = lax.broadcasted_iota(jnp.int32, (LANES, tokens), 1) // count
    share = blocks // halves
    doc, block = block // blocks, block % blocks
    base = ((block // share * 2 + doc) * share + block % share) * capacity
    return jnp.where(named_t > 0.5, place_t + base.astype(F32), -1.0), gates_t


def near_gather_kernel(*refs):
    ins, out_ref = refs[:-1], refs[-1]
    count = ins[0].shape[0]
    full = out_ref.shape[1]
    width = full - LANES
    shared = len(ins) // 2
    for i, r in enumerate(ins[:shared]):
        cot_at = slice(i * count, (i + 1) * count)
        token_at = slice((shared + i) * count, (shared + i + 1) * count)
        out_ref[cot_at, :width] = r[:, :width]
        out_ref[cot_at, width:] = r[:, 2 * width :]
        out_ref[token_at, :] = r[:, width:]
    for i, r in enumerate(ins[shared:]):
        at = (2 * shared + i) * count
        out_ref[at : at + count, :] = r[...]


def pick_kernel(blocks, chunks, rows, capacity, my_ref, own_ref, other_ref, *refs):
    cot_outs, outs, pick_ref = refs[:chunks], refs[chunks : 2 * chunks], refs[2 * chunks]
    width = outs[0].shape[1]
    count = own_ref.shape[0] // (blocks + blocks // 2)
    cots = blocks // 2 * count
    half = rows // 2
    for first, last, held, halves in ((0, cots, half, 1), (cots, own_ref.shape[0], rows, 2)):
        stacked = jnp.concatenate([own_ref[first:last, :], other_ref[first:last, :]], axis=0)
        share = blocks // (3 - halves)
        places, gates = slot_places(stacked[:, width:], chunks, capacity, count, share, halves, my_ref[0])
        slot = lax.broadcasted_iota(jnp.int32, (held, stacked.shape[0]), 0).astype(F32)
        picks = []
        for m in range(chunks):
            value = gates[m : m + 1, :] if halves == 1 else jnp.ones_like(gates[m : m + 1, :])
            picks.append(jnp.where(places[m : m + 1, :] == slot, value, 0.0).astype(BF))
        picks = jnp.concatenate(picks, axis=0)
        chosen = jnp.dot(picks, stacked[:, :width], preferred_element_type=F32).astype(BF)
        for m in range(chunks):
            (cot_outs if halves == 1 else outs)[m][...] = chosen[m * held : (m + 1) * held, :]
    pick_ref[...] = picks


def upstream_kernel(rows_ref, weight_ref, out_ref):
    out_ref[...] = lax.dot_general(rows_ref[...], weight_ref[...], COLS, preferred_element_type=F32)


def expert_kernel(chunks, rows, tile, my_ref, *refs):
    ins = refs[:chunks]
    upstream_refs, weight_ref = refs[chunks : chunks + 2], refs[chunks + 2]
    outs = refs[chunks + 3 : 2 * chunks + 3]
    rows_ref, hidden_ref, grad_ref = refs[2 * chunks + 3 :]
    slots, width = rows_ref.shape
    half = rows // 2
    for m in range(chunks):
        rows_ref[m * rows : (m + 1) * rows, :] = ins[m][...]
    token_rows = rows_ref[...]
    terms = jnp.zeros((slots, LANES), F32)
    for f in range(weight_ref.shape[1] // tile):
        part = slice(f * tile, (f + 1) * tile)
        preact = jnp.dot(token_rows, weight_ref[:, part], preferred_element_type=F32)
        upstream = jnp.concatenate(
            [r[m * half : (m + 1) * half, part] for m in range(chunks) for r in upstream_refs], axis=0
        )
        normal_cdf = 0.5 * (1.0 + lax.erf(preact * SQRT_HALF))
        normal_pdf = INV_ROOT_TWO_PI * jnp.exp(-0.5 * preact * preact)
        hidden = preact * normal_cdf
        products = hidden * upstream
        for k in range(tile // LANES):
            terms = terms + products[:, k * LANES : (k + 1) * LANES]
        grad_ref[:, part] = (upstream * (normal_cdf + preact * normal_pdf)).astype(BF)
        hidden_ref[:, part] = hidden.astype(BF)
    back = lax.dot_general(grad_ref[...], weight_ref[...], COLS, preferred_element_type=F32).astype(BF)
    exact = jnp.sum(terms, axis=1, keepdims=True)
    high = exact.astype(BF).astype(F32)
    lane = lax.broadcasted_iota(jnp.int32, (slots, LANES), 1)
    tail = jnp.where(lane == my_ref[0], high, 0.0)
    tail = jnp.where(lane == my_ref[0] + HALF, exact - high, tail).astype(BF)
    for m in range(chunks):
        outs[m][:, :width] = back[m * rows : (m + 1) * rows, :]
        outs[m][:, width:] = tail[m * rows : (m + 1) * rows, :]


def cot_order_kernel(chunks, cot_a_ref, cot_b_ref, out_ref):
    half = cot_a_ref.shape[0] // chunks
    for m in range(chunks):
        for i, r in enumerate((cot_a_ref, cot_b_ref)):
            at = (2 * m + i) * half
            out_ref[at : at + half, :] = r[m * half : (m + 1) * half, :]


def combine_other_kernel(chunks, rows, pick_ref, *refs):
    ins, out_ref = refs[:chunks], refs[chunks]
    tokens = out_ref.shape[0]
    stacked = jnp.concatenate([r[...] for r in ins], axis=0)
    out_ref[...] = lax.dot_general(
        pick_ref[:, tokens:], stacked, ROWS_T, preferred_element_type=F32
    ).astype(BF)


def combine_own_kernel(pieces, chunks, pick_ref, *refs):
    ins, other_ref, outs = refs[:chunks], refs[chunks], refs[chunks + 1 :]
    tokens = other_ref.shape[0]
    count = tokens // pieces
    stacked = jnp.concatenate([r[...] for r in ins], axis=0)
    back = lax.dot_general(pick_ref[:, :tokens], stacked, ROWS_T, preferred_element_type=F32)
    back = (back + other_ref[...].astype(F32)).astype(BF)
    for k in range(pieces):
        outs[k][...] = back[k * count : (k + 1) * count, :]


def back_kernel(pieces, embed_ref, score_ref, gain_ref, router_ref, routes_ref, tok_ref, keep_ref, cot_ref, *refs):
    parts, out_ref = refs[:pieces], refs[pieces]
    count, width = tok_ref.shape
    experts = router_ref.shape[0]
    values = quartet_values(embed_ref[...], count)
    kept = keep_ref[...]
    column = [kept[:, i : i + 1] for i in range(21)]
    coefs = column[:4]
    shares = [column[4 + 3 * q : 7 + 3 * q] for q in range(4)]
    scale, gates, others = column[16], column[17:19], column[19:21]
    summed = parts[0][...].astype(F32)
    for part in parts[1:]:
        summed = summed + part[...].astype(F32)
    routes_t = routes_ref[...]
    masks = [route_mask(routes_t, k, True) for k in range(2)]
    tail = summed[:, width:]
    gate_grad = [jnp.sum(m * tail, axis=1, keepdims=True) for m in masks]
    pull = gate_grad[0] * gates[1] - gate_grad[1] * gates[0]
    logit_grad = pull * (masks[0] * others[0] - masks[1] * others[1])
    normed_grad = summed[:, :width] + jnp.dot(
        logit_grad[:, :experts], router_ref[...].astype(F32), precision=HIGHEST, preferred_element_type=F32
    )
    tokens = tok_ref[...]
    scaled = gain_ref[...] * normed_grad
    inner = jnp.mean(tokens * scaled, axis=1, keepdims=True)
    token_grad = cot_ref[...].astype(F32) + scale * scaled - tokens * (scale * scale * scale * inner)
    dots = [jnp.sum(token_grad * v, axis=1, keepdims=True) for v in values]
    pairs = [dots[0] + dots[1], dots[2] + dots[3]]
    four = 0.0625 * (pairs[0] + pairs[1])
    score_grads = []
    for q in range(4):
        share = shares[q]
        grads = (0.25 * dots[q], 0.125 * pairs[q // 2], four)
        average = share[0] * grads[0] + share[1] * grads[1] + share[2] * grads[2]
        score_grads.append([s * (g - average) for s, g in zip(share, grads)])
    all_four = 0.25 * (score_grads[0][2] + score_grads[1][2] + score_grads[2][2] + score_grads[3][2])
    weight = score_ref[...]
    ordered = []
    for q in range(4):
        pair = 0.5 * (score_grads[q][1] + score_grads[q ^ 1][1])
        slope = score_grads[q][0] + pair + all_four
        ordered.append((coefs[q] * token_grad + slope * weight).astype(BF))
    out_ref[...] = lax.dot_general(
        quartet_order(count), jnp.concatenate(ordered, axis=0), ROWS_T, preferred_element_type=F32
    ).astype(BF)


def per_device(byte_embed, score_weight, norm_gain, router, routes, expert_in, expert_out, cotangent):
    experts = router.shape[1]
    count = routes.shape[1]
    width = byte_embed.shape[2]
    full = width + LANES
    capacity = max(2, 3 * count // experts)
    pieces = lax.axis_size("seq")
    owners = lax.axis_size("exp")
    chunks = owners // 2
    rows = 2 * pieces * capacity
    slots = chunks * rows
    tokens = pieces * count
    hidden = expert_in.shape[2]
    tile = min(256, hidden)
    my = lax.axis_index("exp").astype(jnp.int32).reshape(1)
    embed = byte_embed[0]
    cot = cotangent[0]
    score_row = score_weight.reshape(1, width)
    gain_row = norm_gain.reshape(1, width)
    router_t = router.T
    routes_t = routes[0].T
    weight_in = expert_in[0]
    weight_out = expert_out[0]

    def shape(*dims, dtype=BF):
        return jax.ShapeDtypeStruct(dims, dtype)

    def over_seq(value, k):
        return lax.ppermute(value, "seq", [(i, i ^ k) for i in range(pieces)])

    def over_cores(value):
        return lax.ppermute(value, "exp", [(i, i ^ 1) for i in range(owners)])

    def over_chips(values):
        moved = [values[0]]
        for m in range(1, chunks):
            moved.append(lax.ppermute(values[m], "exp", [(i, i ^ (2 * m)) for i in range(owners)]))
        return moved

    half = pieces // 2
    places = list(range(0, pieces, 2)) + list(range(1, pieces, 2))
    front_args = (embed, score_row, gain_row, router_t, routes_t, cot)
    both, pay, tok, keep = call(
        front_kernel,
        "front",
        (
            shape(count, full + width),
            shape(count, full),
            shape(count, width, dtype=F32),
            shape(count, LANES, dtype=F32),
        ),
        front_args,
        2.0,
        scratch=[pltpu.VMEM(a.shape, a.dtype) for a in front_args]
        + [pltpu.VMEM((count, LANES), F32), pltpu.SemaphoreType.DMA((len(front_args),))],
        limit=56,
        held=False,
    )
    near = [both] + [over_seq(both, k) for k in places[1:half]] + [over_seq(pay, k) for k in places[half:]]
    own = call(near_gather_kernel, "near_gather", shape(half * count + tokens, full), near, 0.3)
    *chosen, pick = call(
        functools.partial(pick_kernel, pieces, chunks, rows, capacity),
        "pick",
        [shape(rows // 2, width)] * chunks + [shape(rows, width)] * chunks + [shape(slots, 2 * tokens)],
        (my, own, over_cores(own)),
        1.0,
        scalars=1,
        limit=16,
    )
    cot_a = call(gather_kernel, "cot_slots", shape(slots // 2, width), over_chips(chosen[:chunks]), 0.3)
    cot_b = over_seq(cot_a, 1)
    pay_rows = over_chips(chosen[chunks:])

    upstream_a, upstream_b = [
        call(upstream_kernel, "upstream", shape(slots // 2, hidden, dtype=F32), (c, weight_out), 1.5, limit=16)
        for c in (cot_a, cot_b)
    ]
    *back_chunks, token_slots, hidden_rows, hidden_grad = call(
        functools.partial(expert_kernel, chunks, rows, tile),
        "expert",
        [shape(rows, full)] * chunks + [shape(slots, width), shape(slots, hidden), shape(slots, hidden)],
        (my, *pay_rows, upstream_a, upstream_b, weight_in),
        4.0,
        scalars=1,
        limit=24,
    )
    cot_slots = call(
        functools.partial(cot_order_kernel, chunks), "cot_order", shape(slots, width), (cot_a, cot_b), 0.5
    )
    grad_out = lax.dot_general(hidden_rows, cot_slots, ROWS_T, preferred_element_type=F32)
    grad_in = lax.dot_general(token_slots, hidden_grad, ROWS_T, preferred_element_type=F32)
    *returned, grad_out = lax.optimization_barrier((*over_chips(back_chunks), grad_out))
    other_rows = over_cores(
        call(
            functools.partial(combine_other_kernel, chunks, rows),
            "combine_other",
            shape(tokens, full),
            (pick, *returned),
            1.0,
            limit=16,
        )
    )
    partial_rows = call(
        functools.partial(combine_own_kernel, pieces, chunks),
        "combine_own",
        [shape(count, full)] * pieces,
        (pick, *returned, other_rows),
        1.0,
        limit=16,
    )
    parts = list(partial_rows[:1]) + [over_seq(v, k) for v, k in zip(partial_rows[1:], places[1:])]
    embed_grad = call(
        functools.partial(back_kernel, pieces),
        "back",
        shape(4 * count, width),
        (embed, score_row, gain_row, router_t, routes_t, tok, keep, cot, *parts),
        2.0,
    )
    return (embed_grad[None], grad_in[None], grad_out[None])


def solution(mesh):
    in_specs = (
        P("exp", "seq", None),
        P(),
        P(),
        P(),
        P("exp", "seq", None),
        P("exp", None, "seq"),
        P("exp", "seq", None),
        P("exp", "seq", None),
    )
    out_specs = (P("exp", "seq", None), P("exp", None, "seq"), P("exp", "seq", None))
    return jax.shard_map(
        per_device, mesh=mesh, in_specs=in_specs, out_specs=out_specs, check_vma=False
    )
```

time: 93.3 us -> 69.5 us (0.74)
  Pallas kernels: 27.7 us -> 11.1 us
  starting transfers between devices: 31.2 us -> 22.9 us
  waiting for transfers between devices: 22 us -> 26.9 us
  local copies, waits for them, and re-layouts: 3.34 us -> 0.96 us
  matrix products: 7.74 us -> 6.62 us
    pallas_call x8 -> x11, Pallas kernels: 27.7 us -> 11.1 us  [call(): pl.pallas_call(body, name=name, out_shape=outs, in_specs=[smem] * scalars...]
    ppermute x30 -> x18, starting transfers between devices: 31.2 us -> 22.9 us  [the longest x7 12.2 us: over_seq(): return lax.ppermute(value, 'seq', [(i, i ^ k) for i in range(pieces)])]
    ppermute x30 -> x18, waiting for transfers between devices: 22 us -> 26.9 us  [the longest x7 13.2 us: over_seq(): return lax.ppermute(value, 'seq', [(i, i ^ k) for i in range(pieces)])]
    unnamed x66 -> x22, local copies, waits for them, and re-layouts: 3.34 us -> 0.96 us
    dot_general x1, matrix products: 4.44 us -> 3.32 us  [per_device(): lax.dot_general(hidden_rows, cot_slots, ROWS_T, preferred_element_type=F32)]
  transfers between devices with their start and end apart: 30 -> 18, of which waited for: 9 -> 13; matrix products, arithmetic and copies ran while one was open for 8% -> 10% of each run, Pallas kernels for 13% -> 2%
where the time goes in v2:
time: 69.5 us; the launch traced here: 69.3 us
  waiting for transfers between devices  26.9 us (39%)
  starting transfers between devices  22.9 us (33%)
  Pallas kernels  11.1 us (16%)
  matrix products  6.62 us (10%)
  local copies, waits for them, and re-layouts  0.96 us (1%)
  between operations  0.83 us (1%)
    ppermute x7, waiting for transfers between devices, over_seq(): return lax.ppermute(value, 'seq', [(i, i ^ k) for i in range(pieces)])  13.2 us
    ppermute x7, starting transfers between devices, over_seq(): return lax.ppermute(value, 'seq', [(i, i ^ k) for i in range(pieces)])  12.2 us
    pallas_call x11, Pallas kernels, call(): pl.pallas_call(body, name=name, out_shape=outs, in_specs=[smem] * scalars...  11.1 us
    ppermute x9, starting transfers between devices, over_chips(): lax.ppermute(values[m], 'exp', [(i, i ^ 2 * m) for i in range(owners)])  10.6 us
    ppermute x9, waiting for transfers between devices, over_chips(): lax.ppermute(values[m], 'exp', [(i, i ^ 2 * m) for i in range(owners)])  10.3 us
    ppermute x2, waiting for transfers between devices, over_cores(): return lax.ppermute(value, 'exp', [(i, i ^ 1) for i in range(owners)])  3.33 us
    dot_general x1, matrix products, per_device(): lax.dot_general(hidden_rows, cot_slots, ROWS_T, preferred_element_type=F32)  3.32 us
    dot_general x1, matrix products, per_device(): lax.dot_general(token_slots, hidden_grad, ROWS_T, preferred_element_type=...  3.3 us
  transfers between devices with their start and end apart: 18, of which 13 were waited for; matrix products, arithmetic and copies ran while one was open for 10% of the time, Pallas kernels for 2%

profile of v2, /device:TPU:0, one launch (start us, length us, event | category | flops | bytes accessed | tf_op | source)
XLA Modules:
  0.0 69.3 jit_solution(13670221518172175765)
XLA Ops:
  0.6 2.9 %front.1 = (bf16[32,2176]{1,0:T(8,128)(2,1)}, bf16[32,1152]{1,0:T(8,128)(2,1)}, f32[32,1024]{1,0:T(8,128)}, f32[32,128]{1,0:T(8,128)}) custom-call(bf16[128,1024]{1,0:T(8,128)(2,1)} %bitcast.22, f32[1,1024]{1,0:T(1,128)} %bitcast.28, f32[1,1024]{1,0:T(1,128)} %bitcast.30, bf16[8,1024]{1,0:T(8,128)(2,1)} %bitcast.26, s32[2,32]{1,0:T(2,128)} %bitcast.32, ...), custom_call_target="tpu_custom_call" | custom-call | tf_op jit(solution)/shard_map/front/pallas_call | solution.py:26
  3.5 4.1 %collective-permute-start = (bf16[32,2176]{1,0:T(8,128)(2,1)}, bf16[32,2176]{1,0:T(8,128)(2,1)S(1)}, u32[]{:S(2)}, u32[]{:S(2)}) collective-permute-start(bf16[32,2176]{1,0:T(8,128)(2,1)} %get-tuple-element.34.refs_0_), channel_id=1, source_target_pairs={{0,16},{8,24},{16,0},{24,8},{1,17},{9,25},{17,1},{25,9},{2,18},{10... | collective-permute-start | bytes 417800 | tf_op jit(solution)/shard_map/ppermute | solution.py:340
  7.6 1.3 %collective-permute-start.2 = (bf16[32,1152]{1,0:T(8,128)(2,1)}, bf16[32,1152]{1,0:T(8,128)(2,1)S(1)}, u32[]{:S(2)}, u32[]{:S(2)}) collective-permute-start(bf16[32,1152]{1,0:T(8,128)(2,1)} %get-tuple-element.35), channel_id=1, source_target_pairs={{0,24},{8,16},{16,8},{24,0},{1,25},{9,17},{17,9},{25,1},{2,26},{10... | collective-permute-start | bytes 221192 | tf_op jit(solution)/shard_map/ppermute | solution.py:340
  9.0 0.2 collective-permute-start.1
  9.2 5.8 %collective-permute-done.2.refs_3_ = bf16[32,1152]{1,0:T(8,128)(2,1)S(1)} collective-permute-done((bf16[32,1152]{1,0:T(8,128)(2,1)}, bf16[32,1152]{1,0:T(8,128)(2,1)S(1)}, u32[]{:S(2)}, u32[]{:S(2)}) %collective-permute-start.2) | collective-permute-done | bytes 73760 | tf_op jit(solution)/shard_map/ppermute | solution.py:340
  15.0 1.0 %collective-permute-done.1.refs_2_ = bf16[32,1152]{1,0:T(8,128)(2,1)S(1)} collective-permute-done((bf16[32,1152]{1,0:T(8,128)(2,1)}, bf16[32,1152]{1,0:T(8,128)(2,1)S(1)}, u32[]{:S(2)}, u32[]{:S(2)}) %collective-permute-start.1) | collective-permute-done | bytes 73760 | tf_op jit(solution)/shard_map/ppermute | solution.py:340
  16.0 0.9 %collective-permute-done.refs_1_ = bf16[32,2176]{1,0:T(8,128)(2,1)S(1)} collective-permute-done((bf16[32,2176]{1,0:T(8,128)(2,1)}, bf16[32,2176]{1,0:T(8,128)(2,1)S(1)}, u32[]{:S(2)}, u32[]{:S(2)}) %collective-permute-start) | collective-permute-done | bytes 139296 | tf_op jit(solution)/shard_map/ppermute | solution.py:340
  16.9 0.9 %copy-done.4 = bf16[32,2176]{1,0:T(8,128)(2,1)S(1)} copy-done((bf16[32,2176]{1,0:T(8,128)(2,1)S(1)}, bf16[32,2176]{1,0:T(8,128)(2,1)}, u32[]{:S(2)}) %copy-start.4) | copy-done | bytes 139288
  17.8 0.1 collective-permute-start.3
  17.9 0.0 copy-start.1
  17.9 1.8 %collective-permute-done.3.other_ref = bf16[192,1152]{1,0:T(8,128)(2,1)S(1)} collective-permute-done((bf16[192,1152]{1,0:T(8,128)(2,1)S(1)}, bf16[192,1152]{1,0:T(8,128)(2,1)S(1)}, u32[]{:S(2)}, u32[]{:S(2)}) %collective-permute-start.3) | collective-permute-done | bytes 442400 | tf_op jit(solution)/shard_map/ppermute | solution.py:343
  19.7 1.1 %pick.1 = (bf16[48,1024]{1,0:T(8,128)(2,1)S(1)}, bf16[48,1024]{1,0:T(8,128)(2,1)S(1)}, bf16[48,1024]{1,0:T(8,128)(2,1)S(1)}, bf16[48,1024]{1,0:T(8,128)(2,1)S(1)...) custom-call(s32[1]{0:T(128)} %bitcast.8.my_ref, ...), custom_call_target="tpu_custom_call" | custom-call | tf_op jit(solution)/shard_map/pick/pallas_call | solution.py:26
  20.8 1.6 %collective-permute-start.7 = (bf16[48,1024]{1,0:T(8,128)(2,1)S(1)}, bf16[48,1024]{1,0:T(8,128)(2,1)S(1)}, u32[]{:S(2)}, u32[]{:S(2)}) collective-permute-start(bf16[48,1024]{1,0:T(8,128)(2,1)S(1)} %get-tuple-element.42), channel_id=1, source_target_pairs={{0,2},{1,3},{2,0},{3,1},{4,6},{5,7},{6,4},{7,5},{8,10},{9,11},{10,... | collective-permute-start | bytes 294920 | tf_op jit(solution)/shard_map/ppermute | solution.py:348
  22.4 1.5 %collective-permute-start.8 = (bf16[48,1024]{1,0:T(8,128)(2,1)S(1)}, bf16[48,1024]{1,0:T(8,128)(2,1)S(1)}, u32[]{:S(2)}, u32[]{:S(2)}) collective-permute-start(bf16[48,1024]{1,0:T(8,128)(2,1)S(1)} %get-tuple-element.43), channel_id=1, source_target_pairs={{0,4},{1,5},{2,6},{3,7},{4,0},{5,1},{6,2},{7,3},{8,12},{9,13},{10,... | collective-permute-start | bytes 294920 | tf_op jit(solution)/shard_map/ppermute | solution.py:348
  24.0 0.4 collective-permute-start.9
  24.4 1.4 %collective-permute-done.7.refs_1_ = bf16[48,1024]{1,0:T(8,128)(2,1)S(1)} collective-permute-done((bf16[48,1024]{1,0:T(8,128)(2,1)S(1)}, bf16[48,1024]{1,0:T(8,128)(2,1)S(1)}, u32[]{:S(2)}, u32[]{:S(2)}) %collective-permute-start.7) | collective-permute-done | bytes 98336 | tf_op jit(solution)/shard_map/ppermute | solution.py:348
  25.7 2.5 %collective-permute-done.8.refs_2_ = bf16[48,1024]{1,0:T(8,128)(2,1)S(1)} collective-permute-done((bf16[48,1024]{1,0:T(8,128)(2,1)S(1)}, bf16[48,1024]{1,0:T(8,128)(2,1)S(1)}, u32[]{:S(2)}, u32[]{:S(2)}) %collective-permute-start.8) | collective-permute-done | bytes 98336 | tf_op jit(solution)/shard_map/ppermute | solution.py:348
  28.2 1.3 %collective-permute-done.9.refs_3_ = bf16[48,1024]{1,0:T(8,128)(2,1)S(1)} collective-permute-done((bf16[48,1024]{1,0:T(8,128)(2,1)S(1)}, bf16[48,1024]{1,0:T(8,128)(2,1)S(1)}, u32[]{:S(2)}, u32[]{:S(2)}) %collective-permute-start.9) | collective-permute-done | bytes 98336 | tf_op jit(solution)/shard_map/ppermute | solution.py:348
  29.5 1.6 %collective-permute-start.10 = (bf16[192,1024]{1,0:T(8,128)(2,1)S(1)}, bf16[192,1024]{1,0:T(8,128)(2,1)S(1)}, u32[]{:S(2)}, u32[]{:S(2)}) collective-permute-start(bf16[192,1024]{1,0:T(8,128)(2,1)S(1)} %cot_slots.1.rows_ref.cot_a_ref), channel_id=1, source_target_pairs={{0,8},{8,0},{16,24},{24,16},{1,9},{9,1},{17,25},{25,17},{2,10},{10... | collective-permute-start | bytes 1179656 | tf_op jit(solution)/shard_map/ppermute | solution.py:340
  31.1 0.9 %collective-permute-start.4 = (bf16[96,1024]{1,0:T(8,128)(2,1)S(1)}, bf16[96,1024]{1,0:T(8,128)(2,1)S(1)}, u32[]{:S(2)}, u32[]{:S(2)}) collective-permute-start(bf16[96,1024]{1,0:T(8,128)(2,1)S(1)} %get-tuple-element.38), channel_id=1, source_target_pairs={{0,2},{1,3},{2,0},{3,1},{4,6},{5,7},{6,4},{7,5},{8,10},{9,11},{10,... | collective-permute-start | bytes 589832 | tf_op jit(solution)/shard_map/ppermute | solution.py:348
  32.0 0.9 %collective-permute-start.5 = (bf16[96,1024]{1,0:T(8,128)(2,1)S(1)}, bf16[96,1024]{1,0:T(8,128)(2,1)S(1)}, u32[]{:S(2)}, u32[]{:S(2)}) collective-permute-start(bf16[96,1024]{1,0:T(8,128)(2,1)S(1)} %get-tuple-element.39), channel_id=1, source_target_pairs={{0,4},{1,5},{2,6},{3,7},{4,0},{5,1},{6,2},{7,3},{8,12},{9,13},{10,... | collective-permute-start | bytes 589832 | tf_op jit(solution)/shard_map/ppermute | solution.py:348
  32.9 1.7 %collective-permute-start.6 = (bf16[96,1024]{1,0:T(8,128)(2,1)S(1)}, bf16[96,1024]{1,0:T(8,128)(2,1)S(1)}, u32[]{:S(2)}, u32[]{:S(2)}) collective-permute-start(bf16[96,1024]{1,0:T(8,128)(2,1)S(1)} %get-tuple-element.40), channel_id=1, source_target_pairs={{0,6},{1,7},{2,4},{3,5},{4,2},{5,3},{6,0},{7,1},{8,14},{9,15},{10,... | collective-permute-start | bytes 589832 | tf_op jit(solution)/shard_map/ppermute | solution.py:348
  34.6 0.8 %upstream.2.refs_4_ = f32[192,1024]{1,0:T(8,128)S(1)} custom-call(bf16[192,1024]{1,0:T(8,128)(2,1)S(1)} %cot_slots.1.rows_ref.cot_a_ref, bf16[1024,1024]{1,0:T(8,128)(2,1)S(1)} %bitcast.19), custom_call_target="tpu_custom_call" | custom-call | tf_op jit(solution)/shard_map/upstream/pallas_call | solution.py:26
  35.5 3.6 %collective-permute-done.10.rows_ref.cot_b_ref = bf16[192,1024]{1,0:T(8,128)(2,1)S(1)} collective-permute-done((bf16[192,1024]{1,0:T(8,128)(2,1)S(1)}, bf16[192,1024]{1,0:T(8,128)(2,1)S(1)}, u32[]{:S(2)}, u32[]{:S(2)}) %collective-permute-start.10) | collective-permute-done | bytes 393248 | tf_op jit(solution)/shard_map/ppermute | solution.py:340
  39.1 0.8 %upstream.3.refs_5_ = f32[192,1024]{1,0:T(8,128)S(1)} custom-call(bf16[192,1024]{1,0:T(8,128)(2,1)S(1)} %collective-permute-done.10.rows_ref.cot_b_ref, bf16[1024,1024]{1,0:T(8,128)(2,1)S(1)} %bitcast.20), custom_call_target="tpu_custom_call" | custom-call | tf_op jit(solution)/shard_map/upstream/pallas_call | solution.py:26
  39.9 1.9 %collective-permute-done.5.refs_2_ = bf16[96,1024]{1,0:T(8,128)(2,1)S(1)} collective-permute-done((bf16[96,1024]{1,0:T(8,128)(2,1)S(1)}, bf16[96,1024]{1,0:T(8,128)(2,1)S(1)}, u32[]{:S(2)}, u32[]{:S(2)}) %collective-permute-start.5) | collective-permute-done | bytes 196640 | tf_op jit(solution)/shard_map/ppermute | solution.py:348
  41.8 2.3 %expert.1 = (bf16[96,1152]{1,0:T(8,128)(2,1)S(1)}, bf16[96,1152]{1,0:T(8,128)(2,1)S(1)}, bf16[96,1152]{1,0:T(8,128)(2,1)S(1)}, bf16[96,1152]{1,0:T(8,128)(2,1)S(...) custom-call(s32[1]{0:T(128)} %bitcast.8.my_ref, ...), custom_call_target="tpu_custom_call" | custom-call | tf_op jit(solution)/shard_map/expert/pallas_call | solution.py:26
  44.1 0.7 collective-permute-start.11
  44.8 1.6 %collective-permute-start.12 = (bf16[96,1152]{1,0:T(8,128)(2,1)S(1)}, bf16[96,1152]{1,0:T(8,128)(2,1)S(1)}, u32[]{:S(2)}, u32[]{:S(2)}) collective-permute-start(bf16[96,1152]{1,0:T(8,128)(2,1)S(1)} %get-tuple-element.47), channel_id=1, source_target_pairs={{0,4},{1,5},{2,6},{3,7},{4,0},{5,1},{6,2},{7,3},{8,12},{9,13},{10,... | collective-permute-start | bytes 663560 | tf_op jit(solution)/shard_map/ppermute | solution.py:348
  46.4 1.3 %collective-permute-start.13 = (bf16[96,1152]{1,0:T(8,128)(2,1)S(1)}, bf16[96,1152]{1,0:T(8,128)(2,1)S(1)}, u32[]{:S(2)}, u32[]{:S(2)}) collective-permute-start(bf16[96,1152]{1,0:T(8,128)(2,1)S(1)} %get-tuple-element.48), channel_id=1, source_target_pairs={{0,6},{1,7},{2,4},{3,5},{4,2},{5,3},{6,0},{7,1},{8,14},{9,15},{10,... | collective-permute-start | bytes 663560 | tf_op jit(solution)/shard_map/ppermute | solution.py:348
  47.7 0.1 cot_order.1
  47.8 3.3 %fusion = f32[1024,1024]{1,0:T(8,128)} fusion(bf16[384,1024]{1,0:T(8,128)(2,1)S(1)} %get-tuple-element.49, bf16[384,1024]{1,0:T(8,128)(2,1)S(1)} %cot_order.1), kind=kOutput, calls=%fused_computation.1 | convolution fusion | flops 805306368 | bytes 5767168 | tf_op jit(solution)/shard_map/dot_general | solution.py:401
  51.1 3.3 %collective-permute-done.12.refs_2_ = bf16[96,1152]{1,0:T(8,128)(2,1)S(1)} collective-permute-done((bf16[96,1152]{1,0:T(8,128)(2,1)S(1)}, bf16[96,1152]{1,0:T(8,128)(2,1)S(1)}, u32[]{:S(2)}, u32[]{:S(2)}) %collective-permute-start.12) | collective-permute-done | bytes 221216 | tf_op jit(solution)/shard_map/ppermute | solution.py:348
  54.4 0.0 copy-start.6
  54.4 0.0 copy-start.8
  54.4 0.0 copy-start.9
  54.4 0.0 copy-start.10
  54.5 0.4 combine_other.1
  54.8 0.1 collective-permute-start.14
  54.9 1.6 %collective-permute-done.14.refs_4_ = bf16[128,1152]{1,0:T(8,128)(2,1)S(1)} collective-permute-done((bf16[128,1152]{1,0:T(8,128)(2,1)S(1)}, bf16[128,1152]{1,0:T(8,128)(2,1)S(1)}, u32[]{:S(2)}, u32[]{:S(2)}) %collective-permute-start.14) | collective-permute-done | bytes 294944 | tf_op jit(solution)/shard_map/ppermute | solution.py:343
  56.5 0.4 combine_own.1
  56.8 3.4 %collective-permute-start.15 = (bf16[32,1152]{1,0:T(8,128)(2,1)S(1)}, bf16[32,1152]{1,0:T(8,128)(2,1)S(1)}, u32[]{:S(2)}, u32[]{:S(2)}) collective-permute-start(bf16[32,1152]{1,0:T(8,128)(2,1)S(1)} %get-tuple-element.55), channel_id=1, source_target_pairs={{0,16},{8,24},{16,0},{24,8},{1,17},{9,25},{17,1},{25,9},{2,18},{10... | collective-permute-start | bytes 221192 | tf_op jit(solution)/shard_map/ppermute | solution.py:340
  60.2 0.6 collective-permute-start.16
  60.8 1.0 %collective-permute-start.17 = (bf16[32,1152]{1,0:T(8,128)(2,1)S(1)}, bf16[32,1152]{1,0:T(8,128)(2,1)S(1)}, u32[]{:S(2)}, u32[]{:S(2)}) collective-permute-start(bf16[32,1152]{1,0:T(8,128)(2,1)S(1)} %get-tuple-element.57), channel_id=1, source_target_pairs={{0,24},{8,16},{16,8},{24,0},{1,25},{9,17},{17,9},{25,1},{2,26},{10... | collective-permute-start | bytes 221192 | tf_op jit(solution)/shard_map/ppermute | solution.py:340
  61.7 3.3 %convolution_bitcast_fusion = f32[1,1024,1024]{2,1,0:T(8,128)} fusion(bf16[384,1024]{1,0:T(8,128)(2,1)S(1)} %get-tuple-element.58, bf16[384,1024]{1,0:T(8,128)(2,1)S(1)} %get-tuple-element.59), kind=kOutput, calls=%fused_computation | convolution fusion | flops 805306368 | bytes 5767168 | tf_op jit(solution)/shard_map/dot_general | solution.py:402
  65.0 1.2 %collective-permute-done.16.refs_2_ = bf16[32,1152]{1,0:T(8,128)(2,1)S(1)} collective-permute-done((bf16[32,1152]{1,0:T(8,128)(2,1)S(1)}, bf16[32,1152]{1,0:T(8,128)(2,1)S(1)}, u32[]{:S(2)}, u32[]{:S(2)}) %collective-permute-start.16) | collective-permute-done | bytes 73760 | tf_op jit(solution)/shard_map/ppermute | solution.py:340
  66.2 0.8 %collective-permute-done.17.refs_3_ = bf16[32,1152]{1,0:T(8,128)(2,1)S(1)} collective-permute-done((bf16[32,1152]{1,0:T(8,128)(2,1)S(1)}, bf16[32,1152]{1,0:T(8,128)(2,1)S(1)}, u32[]{:S(2)}, u32[]{:S(2)}) %collective-permute-start.17) | collective-permute-done | bytes 73760 | tf_op jit(solution)/shard_map/ppermute | solution.py:340
  67.1 2.3 %back.1 = bf16[128,1024]{1,0:T(8,128)(2,1)} custom-call(bf16[128,1024]{1,0:T(8,128)(2,1)S(1)} %bitcast.23, f32[1,1024]{1,0:T(1,128)S(1)} %bitcast.29, f32[1,1024]{1,0:T(1,128)S(1)} %bitcast.31, bf16[8,1024]{1,0:T(8,128)(2,1)S(1)} %bitcast.27, s32[2,32]{1,0:T(2,128)S(1)} %bitcast.33, f32[32,1024]{1,0:T(8,128)S(1)} %copy-done.5, f32[32,128]{1,0:T(8,128)S(1)} %copy-done.7, ...), custom_call_target="tpu_custom_call" | custom-call | tf_op jit(solution)/shard_map/back/pallas_call | solution.py:26
  (23 shorter events, 0.1 us)
Async XLA Ops:
  0.6 34.0 %copy-start = (bf16[1,1024,1024]{2,1,0:T(8,128)(2,1)S(1)}, bf16[1,1024,1024]{2,1,0:T(8,128)(2,1)}, u32[]{:S(2)}) copy-start(bf16[1,1024,1024]{2,1,0:T(8,128)(2,1)} %param.14) | copy-start | bytes 6291460
  3.5 13.4 %collective-permute-start = (bf16[32,2176]{1,0:T(8,128)(2,1)}, bf16[32,2176]{1,0:T(8,128)(2,1)S(1)}, u32[]{:S(2)}, u32[]{:S(2)}) collective-permute-start(bf16[32,2176]{1,0:T(8,128)(2,1)} %get-tuple-element.34.refs_0_), channel_id=1, source_target_pairs={{0,16},{8,24},{16,0},{24,8},{1,17},{9,25},{17,1},{25,9},{2,18},{10... | collective-permute-start | bytes 417800 | tf_op jit(solution)/shard_map/ppermute | solution.py:340
  7.6 7.4 %collective-permute-start.2 = (bf16[32,1152]{1,0:T(8,128)(2,1)}, bf16[32,1152]{1,0:T(8,128)(2,1)S(1)}, u32[]{:S(2)}, u32[]{:S(2)}) collective-permute-start(bf16[32,1152]{1,0:T(8,128)(2,1)} %get-tuple-element.35), channel_id=1, source_target_pairs={{0,24},{8,16},{16,8},{24,0},{1,25},{9,17},{17,9},{25,1},{2,26},{10... | collective-permute-start | bytes 221192 | tf_op jit(solution)/shard_map/ppermute | solution.py:340
  9.0 7.0 %collective-permute-start.1 = (bf16[32,1152]{1,0:T(8,128)(2,1)}, bf16[32,1152]{1,0:T(8,128)(2,1)S(1)}, u32[]{:S(2)}, u32[]{:S(2)}) collective-permute-start(bf16[32,1152]{1,0:T(8,128)(2,1)} %get-tuple-element.35), channel_id=1, source_target_pairs={{0,8},{8,0},{16,24},{24,16},{1,9},{9,1},{17,25},{25,17},{2,10},{10... | collective-permute-start | bytes 221192 | tf_op jit(solution)/shard_map/ppermute | solution.py:340
  16.9 0.9 %copy-start.4 = (bf16[32,2176]{1,0:T(8,128)(2,1)S(1)}, bf16[32,2176]{1,0:T(8,128)(2,1)}, u32[]{:S(2)}) copy-start(bf16[32,2176]{1,0:T(8,128)(2,1)} %get-tuple-element.34.refs_0_) | copy-start | bytes 417796
  17.8 1.9 %collective-permute-start.3 = (bf16[192,1152]{1,0:T(8,128)(2,1)S(1)}, bf16[192,1152]{1,0:T(8,128)(2,1)S(1)}, u32[]{:S(2)}, u32[]{:S(2)}) collective-permute-start(bf16[192,1152]{1,0:T(8,128)(2,1)S(1)} %near_gather.1.own_ref), channel_id=1, source_target_pairs={{0,1},{1,0},{2,3},{3,2},{4,5},{5,4},{6,7},{7,6},{8,9},{9,8},{10,11... | collective-permute-start | bytes 1327112 | tf_op jit(solution)/shard_map/ppermute | solution.py:343
  17.9 23.9 %copy-start.1 = (bf16[1,1024,1024]{2,1,0:T(8,128)(2,1)S(1)}, bf16[1,1024,1024]{2,1,0:T(8,128)(2,1)}, u32[]{:S(2)}) copy-start(bf16[1,1024,1024]{2,1,0:T(8,128)(2,1)} %param.13) | copy-start | bytes 6291460
  20.8 4.9 %collective-permute-start.7 = (bf16[48,1024]{1,0:T(8,128)(2,1)S(1)}, bf16[48,1024]{1,0:T(8,128)(2,1)S(1)}, u32[]{:S(2)}, u32[]{:S(2)}) collective-permute-start(bf16[48,1024]{1,0:T(8,128)(2,1)S(1)} %get-tuple-element.42), channel_id=1, source_target_pairs={{0,2},{1,3},{2,0},{3,1},{4,6},{5,7},{6,4},{7,5},{8,10},{9,11},{10,... | collective-permute-start | bytes 294920 | tf_op jit(solution)/shard_map/ppermute | solution.py:348
  22.4 5.8 %collective-permute-start.8 = (bf16[48,1024]{1,0:T(8,128)(2,1)S(1)}, bf16[48,1024]{1,0:T(8,128)(2,1)S(1)}, u32[]{:S(2)}, u32[]{:S(2)}) collective-permute-start(bf16[48,1024]{1,0:T(8,128)(2,1)S(1)} %get-tuple-element.43), channel_id=1, source_target_pairs={{0,4},{1,5},{2,6},{3,7},{4,0},{5,1},{6,2},{7,3},{8,12},{9,13},{10,... | collective-permute-start | bytes 294920 | tf_op jit(solution)/shard_map/ppermute | solution.py:348
  24.0 5.5 %collective-permute-start.9 = (bf16[48,1024]{1,0:T(8,128)(2,1)S(1)}, bf16[48,1024]{1,0:T(8,128)(2,1)S(1)}, u32[]{:S(2)}, u32[]{:S(2)}) collective-permute-start(bf16[48,1024]{1,0:T(8,128)(2,1)S(1)} %get-tuple-element.44), channel_id=1, source_target_pairs={{0,6},{1,7},{2,4},{3,5},{4,2},{5,3},{6,0},{7,1},{8,14},{9,15},{10,... | collective-permute-start | bytes 294920 | tf_op jit(solution)/shard_map/ppermute | solution.py:348
  29.5 9.5 %collective-permute-start.10 = (bf16[192,1024]{1,0:T(8,128)(2,1)S(1)}, bf16[192,1024]{1,0:T(8,128)(2,1)S(1)}, u32[]{:S(2)}, u32[]{:S(2)}) collective-permute-start(bf16[192,1024]{1,0:T(8,128)(2,1)S(1)} %cot_slots.1.rows_ref.cot_a_ref), channel_id=1, source_target_pairs={{0,8},{8,0},{16,24},{24,16},{1,9},{9,1},{17,25},{25,17},{2,10},{10... | collective-permute-start | bytes 1179656 | tf_op jit(solution)/shard_map/ppermute | solution.py:340
  31.1 8.8 %collective-permute-start.4 = (bf16[96,1024]{1,0:T(8,128)(2,1)S(1)}, bf16[96,1024]{1,0:T(8,128)(2,1)S(1)}, u32[]{:S(2)}, u32[]{:S(2)}) collective-permute-start(bf16[96,1024]{1,0:T(8,128)(2,1)S(1)} %get-tuple-element.38), channel_id=1, source_target_pairs={{0,2},{1,3},{2,0},{3,1},{4,6},{5,7},{6,4},{7,5},{8,10},{9,11},{10,... | collective-permute-start | bytes 589832 | tf_op jit(solution)/shard_map/ppermute | solution.py:348
  32.0 9.8 %collective-permute-start.5 = (bf16[96,1024]{1,0:T(8,128)(2,1)S(1)}, bf16[96,1024]{1,0:T(8,128)(2,1)S(1)}, u32[]{:S(2)}, u32[]{:S(2)}) collective-permute-start(bf16[96,1024]{1,0:T(8,128)(2,1)S(1)} %get-tuple-element.39), channel_id=1, source_target_pairs={{0,4},{1,5},{2,6},{3,7},{4,0},{5,1},{6,2},{7,3},{8,12},{9,13},{10,... | collective-permute-start | bytes 589832 | tf_op jit(solution)/shard_map/ppermute | solution.py:348
  32.9 8.9 %collective-permute-start.6 = (bf16[96,1024]{1,0:T(8,128)(2,1)S(1)}, bf16[96,1024]{1,0:T(8,128)(2,1)S(1)}, u32[]{:S(2)}, u32[]{:S(2)}) collective-permute-start(bf16[96,1024]{1,0:T(8,128)(2,1)S(1)} %get-tuple-element.40), channel_id=1, source_target_pairs={{0,6},{1,7},{2,4},{3,5},{4,2},{5,3},{6,0},{7,1},{8,14},{9,15},{10,... | collective-permute-start | bytes 589832 | tf_op jit(solution)/shard_map/ppermute | solution.py:348
  44.1 6.9 %collective-permute-start.11 = (bf16[96,1152]{1,0:T(8,128)(2,1)S(1)}, bf16[96,1152]{1,0:T(8,128)(2,1)S(1)}, u32[]{:S(2)}, u32[]{:S(2)}) collective-permute-start(bf16[96,1152]{1,0:T(8,128)(2,1)S(1)} %get-tuple-element.46), channel_id=1, source_target_pairs={{0,2},{1,3},{2,0},{3,1},{4,6},{5,7},{6,4},{7,5},{8,10},{9,11},{10,... | collective-permute-start | bytes 663560 | tf_op jit(solution)/shard_map/ppermute | solution.py:348
  44.8 9.6 %collective-permute-start.12 = (bf16[96,1152]{1,0:T(8,128)(2,1)S(1)}, bf16[96,1152]{1,0:T(8,128)(2,1)S(1)}, u32[]{:S(2)}, u32[]{:S(2)}) collective-permute-start(bf16[96,1152]{1,0:T(8,128)(2,1)S(1)} %get-tuple-element.47), channel_id=1, source_target_pairs={{0,4},{1,5},{2,6},{3,7},{4,0},{5,1},{6,2},{7,3},{8,12},{9,13},{10,... | collective-permute-start | bytes 663560 | tf_op jit(solution)/shard_map/ppermute | solution.py:348
  46.4 8.0 %collective-permute-start.13 = (bf16[96,1152]{1,0:T(8,128)(2,1)S(1)}, bf16[96,1152]{1,0:T(8,128)(2,1)S(1)}, u32[]{:S(2)}, u32[]{:S(2)}) collective-permute-start(bf16[96,1152]{1,0:T(8,128)(2,1)S(1)} %get-tuple-element.48), channel_id=1, source_target_pairs={{0,6},{1,7},{2,4},{3,5},{4,2},{5,3},{6,0},{7,1},{8,14},{9,15},{10,... | collective-permute-start | bytes 663560 | tf_op jit(solution)/shard_map/ppermute | solution.py:348
  54.4 12.6 %copy-start.2 = (bf16[1,128,1024]{2,1,0:T(8,128)(2,1)S(1)}, bf16[1,128,1024]{2,1,0:T(8,128)(2,1)}, u32[]{:S(2)}) copy-start(bf16[1,128,1024]{2,1,0:T(8,128)(2,1)} %param.8) | copy-start | bytes 786436
  54.4 12.6 %copy-start.3 = (bf16[1,32,1024]{2,1,0:T(8,128)(2,1)S(1)}, bf16[1,32,1024]{2,1,0:T(8,128)(2,1)}, u32[]{:S(2)}) copy-start(bf16[1,32,1024]{2,1,0:T(8,128)(2,1)} %param.15) | copy-start | bytes 196612
  54.4 12.6 %copy-start.5 = (f32[32,1024]{1,0:T(8,128)S(1)}, f32[32,1024]{1,0:T(8,128)}, u32[]{:S(2)}) copy-start(f32[32,1024]{1,0:T(8,128)} %get-tuple-element.32.tok_ref) | copy-start | bytes 393220
  54.4 12.6 %copy-start.6 = (bf16[1024,8]{0,1:T(8,128)(2,1)S(1)}, bf16[1024,8]{0,1:T(8,128)(2,1)}, u32[]{:S(2)}) copy-start(bf16[1024,8]{0,1:T(8,128)(2,1)} %param.11) | copy-start | bytes 49156
  54.4 12.6 %copy-start.7 = (f32[32,128]{1,0:T(8,128)S(1)}, f32[32,128]{1,0:T(8,128)}, u32[]{:S(2)}) copy-start(f32[32,128]{1,0:T(8,128)} %get-tuple-element.33.keep_ref) | copy-start | bytes 49156
  54.4 12.6 %copy-start.8 = (f32[1024]{0:T(1024)S(1)}, f32[1024]{0:T(1024)}, u32[]{:S(2)}) copy-start(f32[1024]{0:T(1024)} %param.9) | copy-start | bytes 12292
  54.4 12.6 %copy-start.9 = (f32[1024]{0:T(1024)S(1)}, f32[1024]{0:T(1024)}, u32[]{:S(2)}) copy-start(f32[1024]{0:T(1024)} %param.10) | copy-start | bytes 12292
  54.4 12.6 %copy-start.10 = (s32[1,32,2]{1,2,0:T(2,128)S(1)}, s32[1,32,2]{1,2,0:T(2,128)}, u32[]{:S(2)}) copy-start(s32[1,32,2]{1,2,0:T(2,128)} %param.12) | copy-start | bytes 772
  54.8 1.6 %collective-permute-start.14 = (bf16[128,1152]{1,0:T(8,128)(2,1)S(1)}, bf16[128,1152]{1,0:T(8,128)(2,1)S(1)}, u32[]{:S(2)}, u32[]{:S(2)}) collective-permute-start(bf16[128,1152]{1,0:T(8,128)(2,1)S(1)} %combine_other.1), channel_id=1, source_target_pairs={{0,1},{1,0},{2,3},{3,2},{4,5},{5,4},{6,7},{7,6},{8,9},{9,8},{10,11... | collective-permute-start | bytes 884744 | tf_op jit(solution)/shard_map/ppermute | solution.py:343
  56.8 8.2 %collective-permute-start.15 = (bf16[32,1152]{1,0:T(8,128)(2,1)S(1)}, bf16[32,1152]{1,0:T(8,128)(2,1)S(1)}, u32[]{:S(2)}, u32[]{:S(2)}) collective-permute-start(bf16[32,1152]{1,0:T(8,128)(2,1)S(1)} %get-tuple-element.55), channel_id=1, source_target_pairs={{0,16},{8,24},{16,0},{24,8},{1,17},{9,25},{17,1},{25,9},{2,18},{10... | collective-permute-start | bytes 221192 | tf_op jit(solution)/shard_map/ppermute | solution.py:340
  60.2 6.0 %collective-permute-start.16 = (bf16[32,1152]{1,0:T(8,128)(2,1)S(1)}, bf16[32,1152]{1,0:T(8,128)(2,1)S(1)}, u32[]{:S(2)}, u32[]{:S(2)}) collective-permute-start(bf16[32,1152]{1,0:T(8,128)(2,1)S(1)} %get-tuple-element.56), channel_id=1, source_target_pairs={{0,8},{8,0},{16,24},{24,16},{1,9},{9,1},{17,25},{25,17},{2,10},{10... | collective-permute-start | bytes 221192 | tf_op jit(solution)/shard_map/ppermute | solution.py:340
  60.8 6.3 %collective-permute-start.17 = (bf16[32,1152]{1,0:T(8,128)(2,1)S(1)}, bf16[32,1152]{1,0:T(8,128)(2,1)S(1)}, u32[]{:S(2)}, u32[]{:S(2)}) collective-permute-start(bf16[32,1152]{1,0:T(8,128)(2,1)S(1)} %get-tuple-element.57), channel_id=1, source_target_pairs={{0,24},{8,16},{16,8},{24,0},{1,25},{9,17},{17,9},{25,1},{2,26},{10... | collective-permute-start | bytes 221192 | tf_op jit(solution)/shard_map/ppermute | solution.py:340

commit v3 on v2

v3 whole, which is shorter than its diff:
```python
import functools
import jax
import jax.numpy as jnp
from jax import lax
from jax.experimental import pallas as pl
from jax.experimental.pallas import tpu as pltpu
from jax.sharding import PartitionSpec as P

SQRT_HALF = 0.7071067811865476
INV_ROOT_TWO_PI = 0.3989422804014327
LANES = 128
GROUP = LANES // 4
BF = jnp.bfloat16
F32 = jnp.float32
HIGHEST = lax.Precision.HIGHEST
ROWS_T = (((0,), (0,)), ((), ()))
COLS = (((1,), (1,)), ((), ()))
MIB = 1024 * 1024
BYTES_PER_US = 3_000_000


def call(body, name, outs, args, us=0.0, scratch=(), limit=8, scalars=0, held=True):
    vmem = pl.BlockSpec(memory_space=pltpu.VMEM)
    smem = pl.BlockSpec(memory_space=pltpu.SMEM)
    rest = vmem if held else pl.BlockSpec(memory_space=pltpu.HBM)
    return pl.pallas_call(
        body,
        name=name,
        out_shape=outs,
        in_specs=[smem] * scalars + [rest] * (len(args) - scalars),
        out_specs=jax.tree.map(lambda _: vmem, outs),
        scratch_shapes=list(scratch),
        compiler_params=pltpu.CompilerParams(vmem_limit_bytes=limit * MIB),
        cost_estimate=pl.CostEstimate(flops=0, bytes_accessed=int(us * BYTES_PER_US), transcendentals=0),
    )(*args)


def route_mask(routes_t, k):
    count = routes_t.shape[1]
    lane = lax.broadcasted_iota(jnp.int32, (LANES, count), 0) % GROUP
    mask_t = (lane == routes_t[k : k + 1, :]).astype(F32).astype(BF)
    row = lax.broadcasted_iota(jnp.int32, (count, count), 0)
    col = lax.broadcasted_iota(jnp.int32, (count, count), 1)
    eye = (row == col).astype(F32).astype(BF)
    return lax.dot_general(eye, mask_t, COLS, preferred_element_type=F32)


def quartet_order(count):
    row = lax.broadcasted_iota(jnp.int32, (4 * count, 4 * count), 0)
    col = lax.broadcasted_iota(jnp.int32, (4 * count, 4 * count), 1)
    return (4 * (row % count) + row // count == col).astype(F32).astype(BF)


def quartet_values(embed, count):
    ordered = jnp.dot(quartet_order(count), embed, preferred_element_type=F32)
    return [ordered[q * count : (q + 1) * count, :] for q in range(4)]


def quartet_scores(values, weight):
    ones = [jnp.sum(v * weight, axis=1, keepdims=True) for v in values]
    pairs = [0.5 * (ones[0] + ones[1]), 0.5 * (ones[2] + ones[3])]
    four = 0.5 * (pairs[0] + pairs[1])
    shares = []
    for q in range(4):
        scores = (ones[q], pairs[q // 2], four)
        largest = jnp.maximum(jnp.maximum(scores[0], scores[1]), scores[2])
        weights = [jnp.exp(s - largest) for s in scores]
        denominator = weights[0] + weights[1] + weights[2]
        shares.append([w / denominator for w in weights])
    return shares


def front_kernel(*refs):
    far, outs, near, logit, arrived = refs[:5], refs[5:8], refs[8:13], refs[13], refs[14]
    copies = [pltpu.make_async_copy(a, b, arrived.at[i]) for i, (a, b) in enumerate(zip(far, near))]
    for copy in copies:
        copy.start()
    embed_ref, score_ref, gain_ref, router_ref, routes_ref = near
    pay_ref, tok_ref, keep_ref = outs
    for copy in copies:
        copy.wait()
    count, width = tok_ref.shape
    experts = router_ref.shape[0]
    values = quartet_values(embed_ref[...], count)
    shares = quartet_scores(values, score_ref[...])
    whole = 0.25 * (shares[0][2] + shares[1][2] + shares[2][2] + shares[3][2])
    coefs = []
    for q in range(4):
        pair = 0.5 * (shares[q][1] + shares[q ^ 1][1])
        coefs.append(0.25 * (shares[q][0] + pair + whole))
    tokens = coefs[0] * values[0] + coefs[1] * values[1] + coefs[2] * values[2] + coefs[3] * values[3]
    tok_ref[...] = tokens
    scale = lax.rsqrt(jnp.mean(tokens * tokens, axis=1, keepdims=True) + 1e-06)
    normed = tokens * scale * gain_ref[...]
    logit[...] = jnp.zeros_like(logit)
    logit[:, :experts] = lax.dot_general(
        normed, router_ref[...].astype(F32), COLS, precision=HIGHEST, preferred_element_type=F32
    )
    logits = logit[...]
    sigmoid = 1.0 / (1.0 + jnp.exp(-logits))
    rest = 1.0 / (1.0 + jnp.exp(logits))
    routes_t = routes_ref[...]
    masks = [route_mask(routes_t, k) for k in range(2)]
    group = lax.broadcasted_iota(jnp.int32, masks[0].shape, 1) // GROUP
    once = [jnp.where(group == 0, m, 0.0) for m in masks]
    picked = [jnp.sum(m * sigmoid, axis=1, keepdims=True) for m in once]
    others = [jnp.sum(m * rest, axis=1, keepdims=True) for m in once]
    total = picked[0] + picked[1]
    tail = jnp.zeros_like(masks[0])
    for mask, sig, other in zip(masks, picked, others):
        value = jnp.where(group == 0, 1.0, jnp.where(group == 1, other, jnp.where(group == 2, sig / total, 0.0)))
        tail = tail + mask * value
    pay_ref[:, :width] = normed.astype(BF)
    pay_ref[:, width:] = tail.astype(BF)
    lane = lax.broadcasted_iota(jnp.int32, keep_ref.shape, 1)
    columns = coefs + [s for share in shares for s in share] + [scale]
    kept = jnp.zeros(keep_ref.shape, F32)
    for i, column in enumerate(columns):
        kept = jnp.where(lane == i, column, kept)
    keep_ref[...] = kept


def gather_kernel(skipped, *refs):
    ins, out_ref = refs[skipped:-1], refs[-1]
    at = 0
    for r in ins:
        out_ref[at : at + r.shape[0], :] = r[...]
        at += r.shape[0]


def slot_places(tail, columns, step, count, capacity, my):
    tokens = tail.shape[0]
    lane_row = lax.broadcasted_iota(jnp.int32, (LANES, LANES), 0)
    lane_col = lax.broadcasted_iota(jnp.int32, (LANES, LANES), 1)
    lane = (step * (lane_col % GROUP)) ^ my
    lane = jnp.where(lane_col < GROUP, lane, lane + 2 * GROUP)
    live = (lane_col % GROUP < columns) & (lane_col < 2 * GROUP)
    order = ((lane_row == lane) & live).astype(F32).astype(BF)
    ordered = jnp.dot(tail, order, preferred_element_type=F32).astype(BF)
    row = lax.broadcasted_iota(jnp.int32, (tokens, tokens), 0)
    col = lax.broadcasted_iota(jnp.int32, (tokens, tokens), 1)
    eye = (row == col).astype(F32).astype(BF)
    before = ((row < col) & (row // count == col // count)).astype(F32).astype(BF)
    ordered_t = lax.dot_general(ordered, eye, ROWS_T, preferred_element_type=F32)
    place_t = lax.dot_general(ordered, before, ROWS_T, preferred_element_type=F32)[:GROUP, :]
    block = lax.broadcasted_iota(jnp.int32, (GROUP, tokens), 1) // count
    place_t = place_t + (block * capacity).astype(F32)
    return jnp.where(ordered_t[:GROUP, :] > 0.5, place_t, -1.0), ordered_t[GROUP : 2 * GROUP, :]


def selection(places, values, columns, rows):
    slot = lax.broadcasted_iota(jnp.int32, (rows, places.shape[1]), 0).astype(F32)
    picks = [jnp.where(places[m : m + 1, :] == slot, values[m : m + 1, :], 0.0) for m in range(columns)]
    return jnp.concatenate(picks, axis=0).astype(BF)


def pick_kernel(pieces, chunks, capacity, my_ref, cot_ref, token_ref, other_cot_ref, other_token_ref, *refs):
    cot_outs, outs = refs[:chunks], refs[chunks:]
    tokens, full = token_ref.shape
    width = full - LANES
    count = tokens // pieces
    cots = cot_ref.shape[0]
    near = pieces // 2
    my = my_ref[0]

    tail = jnp.concatenate([token_ref[:cots, width:], other_token_ref[:cots, width:]], axis=0)
    places, gates = slot_places(tail, chunks, 2, count, capacity, my)
    picks = selection(places, gates, chunks, 2 * near * capacity)
    cot_rows = jnp.concatenate([cot_ref[...], other_cot_ref[...]], axis=0)
    chosen = jnp.dot(picks, cot_rows, preferred_element_type=F32).astype(BF)
    for m, out in enumerate(cot_outs):
        out[...] = chosen[m * out.shape[0] : (m + 1) * out.shape[0], :]

    token_rows = jnp.concatenate([token_ref[...], other_token_ref[...]], axis=0)
    places, gates = slot_places(token_rows[:, width:], chunks, 2, count, capacity, my)
    picks = selection(places, jnp.ones_like(gates), chunks, 2 * pieces * capacity)
    chosen = jnp.dot(picks, token_rows, preferred_element_type=F32).astype(BF)
    for m, out in enumerate(outs):
        out[...] = chosen[m * out.shape[0] : (m + 1) * out.shape[0], :]


def back_pick_kernel(owners, count, capacity, my_ref, token_ref, out_ref):
    tail = token_ref[:, token_ref.shape[1] - LANES :]
    places, gates = slot_places(tail, owners, 1, count, capacity, my_ref[0])
    out_ref[...] = selection(places, jnp.ones_like(gates), owners, out_ref.shape[0] // owners)


def interleave(near, far, owners):
    share = near.shape[0] // owners
    return jnp.concatenate([r[d * share : (d + 1) * share, :] for d in range(owners) for r in (near, far)], axis=0)


def upstream_kernel(owners, near_ref, far_ref, weight_ref, out_ref):
    rows = jnp.concatenate([near_ref[...], far_ref[...]], axis=0)
    upstream = lax.dot_general(rows, weight_ref[...], COLS, preferred_element_type=F32)
    half = near_ref.shape[0]
    out_ref[...] = interleave(upstream[:half, :], upstream[half:, :], owners)


def expert_kernel(chunks, owners, tile, waits, my_ref, *refs):
    refs = refs[waits:]
    ins, refs = refs[:chunks], refs[chunks:]
    upstream_ref, weight_ref, router_ref = refs[:3]
    outs, (rows_ref, hidden_ref, grad_ref) = refs[3 : 3 + owners], refs[3 + owners :]
    slots, width = rows_ref.shape
    experts = router_ref.shape[0]
    rows = slots // owners
    token_rows = jnp.concatenate([r[:, :width] for r in ins], axis=0)
    rows_ref[...] = token_rows
    terms = jnp.zeros((slots, LANES), F32)
    for f in range(weight_ref.shape[1] // tile):
        part = slice(f * tile, (f + 1) * tile)
        preact = jnp.dot(token_rows, weight_ref[:, part], preferred_element_type=F32)
        upstream = upstream_ref[:, part]
        normal_cdf = 0.5 * (1.0 + lax.erf(preact * SQRT_HALF))
        normal_pdf = INV_ROOT_TWO_PI * jnp.exp(-0.5 * preact * preact)
        hidden = preact * normal_cdf
        products = hidden * upstream
        for k in range(tile // LANES):
            terms = terms + products[:, k * LANES : (k + 1) * LANES]
        grad_ref[:, part] = (upstream * (normal_cdf + preact * normal_pdf)).astype(BF)
        hidden_ref[:, part] = hidden.astype(BF)
    term = jnp.sum(terms, axis=1, keepdims=True)
    tail = jnp.concatenate([r[:, width:] for r in ins], axis=0).astype(F32)
    lane = lax.broadcasted_iota(jnp.int32, (slots, LANES), 1)
    mine = lane % GROUP == my_ref[0]
    other_gate = jnp.sum(jnp.where((lane // GROUP == 2) & ~mine, tail, 0.0), axis=1, keepdims=True)
    spread = jnp.where(lane // GROUP == 1, jnp.where(mine, tail, -tail), 0.0) * (term * other_gate)
    high = spread.astype(BF)
    low = (spread - high.astype(F32)).astype(BF)
    router = router_ref[...].astype(F32)
    blank = jnp.zeros((GROUP, width), F32)
    padded = [router] if experts == GROUP else [router, jnp.zeros((GROUP - experts, width), F32)]
    router = jnp.concatenate([blank, *padded, blank, blank], axis=0).astype(BF)
    back = lax.dot_general(grad_ref[...], weight_ref[...], COLS, preferred_element_type=F32)
    back = back + jnp.dot(high, router, preferred_element_type=F32) + jnp.dot(low, router, preferred_element_type=F32)
    back = back.astype(BF)
    for m, out in enumerate(outs):
        out[...] = back[m * rows : (m + 1) * rows, :]


def stack_kernel(owners, *refs):
    ins, outs = refs[:10], refs[10:]
    half = outs[0].shape[0] // 2
    for g in range(2):
        near_ref, far_ref, *others = ins[5 * g : 5 * g + 5]
        at = slice(g * half, (g + 1) * half)
        outs[0][at, :] = interleave(near_ref[...].astype(F32), far_ref[...].astype(F32), owners).astype(BF)
        for r, out in zip(others, outs[1:]):
            out[at, :] = r[...]


def combine_kernel(owners, pick_ref, *refs):
    ins, outs = refs[:owners], refs[owners:]
    stacked = jnp.concatenate([r[...] for r in ins], axis=0)
    back = lax.dot_general(pick_ref[...], stacked, ROWS_T, preferred_element_type=F32).astype(BF)
    count = outs[0].shape[0]
    for k, out in enumerate(outs):
        out[...] = back[k * count : (k + 1) * count, :]


def back_kernel(pieces, embed_ref, score_ref, gain_ref, tok_ref, keep_ref, cot_ref, *refs):
    parts, out_ref = refs[:pieces], refs[pieces]
    count, width = tok_ref.shape
    values = quartet_values(embed_ref[...], count)
    kept = keep_ref[...]
    column = [kept[:, i : i + 1] for i in range(17)]
    coefs = column[:4]
    shares = [column[4 + 3 * q : 7 + 3 * q] for q in range(4)]
    scale = column[16]
    normed_grad = parts[0][...].astype(F32)
    for part in parts[1:]:
        normed_grad = normed_grad + part[...].astype(F32)
    tokens = tok_ref[...]
    scaled = gain_ref[...] * normed_grad
    inner = jnp.mean(tokens * scaled, axis=1, keepdims=True)
    token_grad = cot_ref[...].astype(F32) + scale * scaled - tokens * (scale * scale * scale * inner)
    dots = [jnp.sum(token_grad * v, axis=1, keepdims=True) for v in values]
    pairs = [dots[0] + dots[1], dots[2] + dots[3]]
    four = 0.0625 * (pairs[0] + pairs[1])
    score_grads = []
    for q in range(4):
        share = shares[q]
        grads = (0.25 * dots[q], 0.125 * pairs[q // 2], four)
        average = share[0] * grads[0] + share[1] * grads[1] + share[2] * grads[2]
        score_grads.append([s * (g - average) for s, g in zip(share, grads)])
    all_four = 0.25 * (score_grads[0][2] + score_grads[1][2] + score_grads[2][2] + score_grads[3][2])
    weight = score_ref[...]
    ordered = []
    for q in range(4):
        pair = 0.5 * (score_grads[q][1] + score_grads[q ^ 1][1])
        slope = score_grads[q][0] + pair + all_four
        ordered.append((coefs[q] * token_grad + slope * weight).astype(BF))
    out_ref[...] = lax.dot_general(
        quartet_order(count), jnp.concatenate(ordered, axis=0), ROWS_T, preferred_element_type=F32
    ).astype(BF)


def per_device(byte_embed, score_weight, norm_gain, router, routes, expert_in, expert_out, cotangent):
    experts = router.shape[1]
    count = routes.shape[1]
    width = byte_embed.shape[2]
    full = width + LANES
    capacity = max(2, 3 * count // experts)
    pieces = lax.axis_size("seq")
    owners = lax.axis_size("exp")
    chunks = owners // 2
    rows = 2 * pieces * capacity
    slots = chunks * rows
    tokens = pieces * count
    hidden = expert_in.shape[2]
    tile = min(256, hidden)
    my = lax.axis_index("exp").astype(jnp.int32).reshape(1)
    embed = byte_embed[0]
    cot = cotangent[0]
    score_row = score_weight.reshape(1, width)
    gain_row = norm_gain.reshape(1, width)
    router_t = router.T
    routes_t = routes[0].T
    weight_in = expert_in[0]
    weight_out = expert_out[0]

    def shape(*dims, dtype=BF):
        return jax.ShapeDtypeStruct(dims, dtype)

    def over_seq(value, k):
        return lax.ppermute(value, "seq", [(i, i ^ k) for i in range(pieces)])

    def over_exp(values, step):
        moved = list(values)
        for m in sorted(range(1, len(values)), key=lambda m: (m & (2 // step - 1), -m)):
            moved[m] = lax.ppermute(values[m], "exp", [(i, i ^ (m * step)) for i in range(owners)])
        return moved

    def over_cores(value):
        return lax.ppermute(value, "exp", [(i, i ^ 1) for i in range(owners)])

    half = pieces // 2
    places = list(range(0, pieces, 2)) + list(range(1, pieces, 2))
    front_args = (embed, score_row, gain_row, router_t, routes_t)
    cot_far = [over_seq(cot, k) for k in places[1:half]]
    pay, tok, keep = call(
        front_kernel,
        "front",
        (shape(count, full), shape(count, width, dtype=F32), shape(count, LANES, dtype=F32)),
        front_args,
        us=2.0,
        scratch=[pltpu.VMEM(a.shape, a.dtype) for a in front_args]
        + [pltpu.VMEM((count, LANES), F32), pltpu.SemaphoreType.DMA((len(front_args),))],
        limit=56,
        held=False,
    )
    held_cot = call(functools.partial(gather_kernel, 0), "hold_cot", shape(count, width), (cot,), us=1.0)
    cot_near = call(
        functools.partial(gather_kernel, 0), "cot_near", shape(half * count, width), (held_cot, *cot_far), us=5.0
    )
    held = call(functools.partial(gather_kernel, 0), "hold_own", shape(count, full), (pay,), us=1.0)
    held_out = call(functools.partial(gather_kernel, 0), "hold_weight", shape(hidden, width), (weight_out,), us=2.0)
    token_near = call(
        functools.partial(gather_kernel, 1),
        "token_near",
        shape(tokens, full),
        (cot_near, held, *[over_seq(pay, k) for k in places[1:]]),
    )
    chosen = call(
        functools.partial(pick_kernel, pieces, chunks, capacity),
        "pick",
        [shape(rows // 2, width)] * chunks + [shape(rows, full)] * chunks,
        (my, cot_near, token_near, over_cores(cot_near), over_cores(token_near)),
        scalars=1,
        limit=16,
    )
    back_pick = call(
        functools.partial(back_pick_kernel, owners, count, capacity),
        "back_pick",
        shape(slots, tokens),
        (my, token_near),
        us=1.0,
        scalars=1,
        limit=16,
    )
    cot_chunks = over_exp(chosen[:chunks], 2)
    token_chunks = over_exp(chosen[chunks:], 2)
    order = [0, *range(chunks - 1, 0, -1)]
    stacked, back_rows = [], [None] * owners
    groups = (order[: chunks // 2], order[chunks // 2 :])
    part = slots // 2
    near, far, upstream = [], [], []
    for group in groups:
        cot_a = call(
            functools.partial(gather_kernel, 0), "cot_slots", shape(part // 2, width), [cot_chunks[m] for m in group]
        )
        near.append(cot_a)
        far.append(over_seq(cot_a, 1))
    for cot_a, cot_b in zip(near, far):
        upstream.append(
            call(
                functools.partial(upstream_kernel, chunks),
                "upstream",
                shape(part, hidden, dtype=F32),
                (cot_a, cot_b, held_out),
                limit=16,
            )
        )
    for g, group in enumerate(groups):
        shares = 2 * len(group)
        waits = upstream[1:] if g == 0 else []
        *outs, token_rows, hidden_rows, hidden_grad = call(
            functools.partial(expert_kernel, len(group), shares, tile, len(waits)),
            "expert",
            [shape(rows // 2, width)] * shares + [shape(part, width), shape(part, hidden), shape(part, hidden)],
            (my, *waits, *[token_chunks[m] for m in group], upstream[g], weight_in, router_t),
            scalars=1,
            limit=24,
        )
        for i, out in enumerate(outs):
            back_rows[2 * group[i // 2] + i % 2] = out
        stacked += [near[g], far[g], hidden_rows, token_rows, hidden_grad]
    cot_slots, hidden_rows, token_slots, hidden_grad = call(
        functools.partial(stack_kernel, chunks),
        "stack",
        (shape(slots, width), shape(slots, hidden), shape(slots, width), shape(slots, hidden)),
        stacked,
        limit=16,
    )
    grad_out = lax.dot_general(hidden_rows, cot_slots, ROWS_T, preferred_element_type=F32)
    grad_in = lax.dot_general(token_slots, hidden_grad, ROWS_T, preferred_element_type=F32)
    *returned, grad_out = lax.optimization_barrier((*over_exp(back_rows, 1), grad_out))
    partial_rows = call(
        functools.partial(combine_kernel, owners),
        "combine",
        [shape(count, width)] * pieces,
        (back_pick, *returned),
        limit=16,
    )
    parts = [partial_rows[0]] + [over_seq(partial_rows[i], places[i]) for i in range(pieces - 1, 0, -1)]
    embed_grad = call(
        functools.partial(back_kernel, pieces),
        "back",
        shape(4 * count, width),
        (embed, score_row, gain_row, tok, keep, cot, *parts),
    )
    return (embed_grad[None], grad_in[None], grad_out[None])


def solution(mesh):
    in_specs = (
        P("exp", "seq", None),
        P(),
        P(),
        P(),
        P("exp", "seq", None),
        P("exp", None, "seq"),
        P("exp", "seq", None),
        P("exp", "seq", None),
    )
    out_specs = (P("exp", "seq", None), P("exp", None, "seq"), P("exp", "seq", None))
    return jax.shard_map(
        per_device, mesh=mesh, in_specs=in_specs, out_specs=out_specs, check_vma=False
    )
```

time: 69.5 us -> 65.2 us (0.938)
  waiting for transfers between devices: 26.9 us -> 14.9 us
  starting transfers between devices: 22.9 us -> 28.4 us
  Pallas kernels: 11.1 us -> 12.3 us
  local copies, waits for them, and re-layouts: 0.96 us -> 1.8 us
    ppermute x9 -> x13, waiting for transfers between devices: 10.3 us -> 5.11 us  [over_exp(): lax.ppermute(values[m], 'exp', [(i, i ^ m * step) for i in range(owners)])]
    ppermute x7 -> x9, waiting for transfers between devices: 13.2 us -> 8.58 us  [over_seq(): return lax.ppermute(value, 'seq', [(i, i ^ k) for i in range(pieces)])]
    ppermute x9 -> x13, starting transfers between devices: 10.6 us -> 15.2 us  [over_exp(): lax.ppermute(values[m], 'exp', [(i, i ^ m * step) for i in range(owners)])]
    ppermute x2, waiting for transfers between devices: 3.33 us -> 1.26 us  [over_cores(): return lax.ppermute(value, 'exp', [(i, i ^ 1) for i in range(owners)])]
    pallas_call x11 -> x17, Pallas kernels: 11.1 us -> 12.3 us  [call(): pl.pallas_call(body, name=name, out_shape=outs, in_specs=[smem] * scalars...]
    unnamed x22, local copies, waits for them, and re-layouts: 0.96 us -> 1.8 us
    ppermute x7 -> x9, starting transfers between devices: 12.2 us -> 12.7 us  [over_seq(): return lax.ppermute(value, 'seq', [(i, i ^ k) for i in range(pieces)])]
  transfers between devices with their start and end apart: 18 -> 24, of which waited for: 13 -> 9; matrix products, arithmetic and copies ran while one was open for 10% -> 10% of each run, Pallas kernels for 2% -> 10%
where the time goes in v3:
time: 65.2 us; the launch traced here: 65 us
  starting transfers between devices  28.4 us (44%)
  waiting for transfers between devices  14.9 us (23%)
  Pallas kernels  12.3 us (19%)
  matrix products  6.61 us (10%)
  local copies, waits for them, and re-layouts  1.8 us (3%)
  between operations  0.91 us (1%)
    ppermute x13, starting transfers between devices, over_exp(): lax.ppermute(values[m], 'exp', [(i, i ^ m * step) for i in range(owners)])  15.2 us
    ppermute x9, starting transfers between devices, over_seq(): return lax.ppermute(value, 'seq', [(i, i ^ k) for i in range(pieces)])  12.7 us
    pallas_call x17, Pallas kernels, call(): pl.pallas_call(body, name=name, out_shape=outs, in_specs=[smem] * scalars...  12.3 us
    ppermute x9, waiting for transfers between devices, over_seq(): return lax.ppermute(value, 'seq', [(i, i ^ k) for i in range(pieces)])  8.58 us
    ppermute x13, waiting for transfers between devices, over_exp(): lax.ppermute(values[m], 'exp', [(i, i ^ m * step) for i in range(owners)])  5.11 us
    dot_general x1, matrix products, per_device(): lax.dot_general(hidden_rows, cot_slots, ROWS_T, preferred_element_type=F32)  3.3 us
    dot_general x1, matrix products, per_device(): lax.dot_general(token_slots, hidden_grad, ROWS_T, preferred_element_type=...  3.3 us
    unnamed x22, local copies, waits for them, and re-layouts  1.8 us
  transfers between devices with their start and end apart: 24, of which 9 were waited for; matrix products, arithmetic and copies ran while one was open for 10% of the time, Pallas kernels for 10%

profile of v3, /device:TPU:0, one launch (start us, length us, event | category | flops | bytes accessed | tf_op | source)
XLA Modules:
  0.0 65.0 jit_solution(10813200887481613366)
XLA Ops:
  0.6 2.8 %front.1 = (bf16[32,1152]{1,0:T(8,128)(2,1)}, f32[32,1024]{1,0:T(8,128)}, f32[32,128]{1,0:T(8,128)}) custom-call(bf16[128,1024]{1,0:T(8,128)(2,1)} %bitcast.22, f32[1,1024]{1,0:T(1,128)} %bitcast.30, f32[1,1024]{1,0:T(1,128)} %bitcast.32, bf16[8,1024]{1,0:T(8,128)(2,1)} %bitcast.27, s32[2,32]{1,0:T(2,128)} %bitcast.36), custom_call_target="tpu_custom_call" | custom-call | bytes 6000000 | tf_op jit(solution)/shard_map/front/pallas_call | solution.py:26
  3.4 5.1 %collective-permute-start.3 = (bf16[32,1152]{1,0:T(8,128)(2,1)}, bf16[32,1152]{1,0:T(8,128)(2,1)S(1)}, u32[]{:S(2)}, u32[]{:S(2)}) collective-permute-start(bf16[32,1152]{1,0:T(8,128)(2,1)} %get-tuple-element.47.refs_0_), channel_id=1, source_target_pairs={{0,24},{8,16},{16,8},{24,0},{1,25},{9,17},{17,9},{25,1},{2,26},{10... | collective-permute-start | bytes 221192 | tf_op jit(solution)/shard_map/ppermute | solution.py:327
  8.5 0.6 collective-permute-start.1
  9.2 2.3 %collective-permute-start = (bf16[32,1024]{1,0:T(8,128)(2,1)}, bf16[32,1024]{1,0:T(8,128)(2,1)S(1)}, u32[]{:S(2)}, u32[]{:S(2)}) collective-permute-start(bf16[32,1024]{1,0:T(8,128)(2,1)} %bitcast.24), channel_id=1, source_target_pairs={{0,16},{8,24},{16,0},{24,8},{1,17},{9,25},{17,1},{25,9},{2,18},{10... | collective-permute-start | bytes 196616 | tf_op jit(solution)/shard_map/ppermute | solution.py:327
  11.5 0.9 %copy-done.3 = bf16[1,32,1024]{2,1,0:T(8,128)(2,1)S(1)} copy-done((bf16[1,32,1024]{2,1,0:T(8,128)(2,1)S(1)}, bf16[1,32,1024]{2,1,0:T(8,128)(2,1)}, u32[]{:S(2)}) %copy-start.3) | copy-done | bytes 65560
  12.3 0.9 %copy-done.7 = bf16[32,1152]{1,0:T(8,128)(2,1)S(1)} copy-done((bf16[32,1152]{1,0:T(8,128)(2,1)S(1)}, bf16[32,1152]{1,0:T(8,128)(2,1)}, u32[]{:S(2)}) %copy-start.7) | copy-done | bytes 73752
  13.2 4.6 %collective-permute-done.refs_1_ = bf16[32,1024]{1,0:T(8,128)(2,1)S(1)} collective-permute-done((bf16[32,1024]{1,0:T(8,128)(2,1)}, bf16[32,1024]{1,0:T(8,128)(2,1)S(1)}, u32[]{:S(2)}, u32[]{:S(2)}) %collective-permute-start) | collective-permute-done | bytes 65568 | tf_op jit(solution)/shard_map/ppermute | solution.py:327
  17.9 0.1 collective-permute-start.5
  18.0 0.5 collective-permute-start.4
  18.5 1.3 %collective-permute-done.4.other_cot_ref = bf16[64,1024]{1,0:T(8,128)(2,1)S(1)} collective-permute-done((bf16[64,1024]{1,0:T(8,128)(2,1)S(1)}, bf16[64,1024]{1,0:T(8,128)(2,1)S(1)}, u32[]{:S(2)}, u32[]{:S(2)}) %collective-permute-start.4) | collective-permute-done | bytes 131104 | tf_op jit(solution)/shard_map/ppermute | solution.py:336
  19.7 1.2 %pick.1 = (bf16[48,1024]{1,0:T(8,128)(2,1)S(1)}, bf16[48,1024]{1,0:T(8,128)(2,1)S(1)}, bf16[48,1024]{1,0:T(8,128)(2,1)S(1)}, bf16[48,1024]{1,0:T(8,128)(2,1)S(1)...) custom-call(s32[1]{0:T(128)} %bitcast.7.my_ref, ...), custom_call_target="tpu_custom_call" | custom-call | tf_op jit(solution)/shard_map/pick/pallas_call | solution.py:26
  20.9 1.6 %collective-permute-start.6 = (bf16[48,1024]{1,0:T(8,128)(2,1)S(1)}, bf16[48,1024]{1,0:T(8,128)(2,1)S(1)}, u32[]{:S(2)}, u32[]{:S(2)}) collective-permute-start(bf16[48,1024]{1,0:T(8,128)(2,1)S(1)} %get-tuple-element.48), channel_id=1, source_target_pairs={{0,4},{1,5},{2,6},{3,7},{4,0},{5,1},{6,2},{7,3},{8,12},{9,13},{10,... | collective-permute-start | bytes 294920 | tf_op jit(solution)/shard_map/ppermute | solution.py:332
  22.5 1.5 %collective-permute-start.7 = (bf16[48,1024]{1,0:T(8,128)(2,1)S(1)}, bf16[48,1024]{1,0:T(8,128)(2,1)S(1)}, u32[]{:S(2)}, u32[]{:S(2)}) collective-permute-start(bf16[48,1024]{1,0:T(8,128)(2,1)S(1)} %get-tuple-element.49), channel_id=1, source_target_pairs={{0,2},{1,3},{2,0},{3,1},{4,6},{5,7},{6,4},{7,5},{8,10},{9,11},{10,... | collective-permute-start | bytes 294920 | tf_op jit(solution)/shard_map/ppermute | solution.py:332
  24.0 0.5 collective-permute-start.10
  24.4 2.4 %collective-permute-start.9 = (bf16[96,1152]{1,0:T(8,128)(2,1)S(1)}, bf16[96,1152]{1,0:T(8,128)(2,1)S(1)}, u32[]{:S(2)}, u32[]{:S(2)}) collective-permute-start(bf16[96,1152]{1,0:T(8,128)(2,1)S(1)} %get-tuple-element.51), channel_id=1, source_target_pairs={{0,6},{1,7},{2,4},{3,5},{4,2},{5,3},{6,0},{7,1},{8,14},{9,15},{10,... | collective-permute-start | bytes 663560 | tf_op jit(solution)/shard_map/ppermute | solution.py:332
  26.9 1.2 %collective-permute-done.7.refs_1_ = bf16[48,1024]{1,0:T(8,128)(2,1)S(1)} collective-permute-done((bf16[48,1024]{1,0:T(8,128)(2,1)S(1)}, bf16[48,1024]{1,0:T(8,128)(2,1)S(1)}, u32[]{:S(2)}, u32[]{:S(2)}) %collective-permute-start.7) | collective-permute-done | bytes 98336 | tf_op jit(solution)/shard_map/ppermute | solution.py:332
  28.1 0.1 collective-permute-start.8
  28.2 2.4 %collective-permute-done.10.refs_1_ = bf16[48,1024]{1,0:T(8,128)(2,1)S(1)} collective-permute-done((bf16[48,1024]{1,0:T(8,128)(2,1)S(1)}, bf16[48,1024]{1,0:T(8,128)(2,1)S(1)}, u32[]{:S(2)}, u32[]{:S(2)}) %collective-permute-start.10) | collective-permute-done | bytes 98336 | tf_op jit(solution)/shard_map/ppermute | solution.py:332
  30.6 0.1 collective-permute-start.11
  30.7 1.1 %collective-permute-start.13 = (bf16[96,1152]{1,0:T(8,128)(2,1)S(1)}, bf16[96,1152]{1,0:T(8,128)(2,1)S(1)}, u32[]{:S(2)}, u32[]{:S(2)}) collective-permute-start(bf16[96,1152]{1,0:T(8,128)(2,1)S(1)} %get-tuple-element.56), channel_id=1, source_target_pairs={{0,4},{1,5},{2,6},{3,7},{4,0},{5,1},{6,2},{7,3},{8,12},{9,13},{10,... | collective-permute-start | bytes 663560 | tf_op jit(solution)/shard_map/ppermute | solution.py:332
  31.8 1.5 %collective-permute-start.14 = (bf16[96,1152]{1,0:T(8,128)(2,1)S(1)}, bf16[96,1152]{1,0:T(8,128)(2,1)S(1)}, u32[]{:S(2)}, u32[]{:S(2)}) collective-permute-start(bf16[96,1152]{1,0:T(8,128)(2,1)S(1)} %get-tuple-element.57), channel_id=1, source_target_pairs={{0,2},{1,3},{2,0},{3,1},{4,6},{5,7},{6,4},{7,5},{8,10},{9,11},{10,... | collective-permute-start | bytes 663560 | tf_op jit(solution)/shard_map/ppermute | solution.py:332
  33.4 0.1 hold_weight.1.weight_ref
  33.5 0.0 copy-start
  33.5 0.0 copy-start.5
  33.5 1.4 %collective-permute-done.8.far_ref.refs_6_ = bf16[96,1024]{1,0:T(8,128)(2,1)S(1)} collective-permute-done((bf16[96,1024]{1,0:T(8,128)(2,1)S(1)}, bf16[96,1024]{1,0:T(8,128)(2,1)S(1)}, u32[]{:S(2)}, u32[]{:S(2)}) %collective-permute-start.8) | collective-permute-done | bytes 196640 | tf_op jit(solution)/shard_map/ppermute | solution.py:327
  34.9 0.8 %upstream.2.refs_0_.refs_2_ = f32[192,1024]{1,0:T(8,128)S(1)} custom-call(bf16[96,1024]{1,0:T(8,128)(2,1)S(1)} %cot_slots.2.near_ref.refs_5_, bf16[96,1024]{1,0:T(8,128)(2,1)S(1)} %collective-permute-done.8.far_ref.refs_6_, bf16[1024,1024]{1,0:T(8,128)(2,1)S(1)} %hold_weight.1.weight_ref), custom_call_target="tpu_custom_call" | custom-call | tf_op jit(solution)/shard_map/upstream/pallas_call | solution.py:26
  35.8 1.3 %collective-permute-done.11.far_ref.refs_1_ = bf16[96,1024]{1,0:T(8,128)(2,1)S(1)} collective-permute-done((bf16[96,1024]{1,0:T(8,128)(2,1)S(1)}, bf16[96,1024]{1,0:T(8,128)(2,1)S(1)}, u32[]{:S(2)}, u32[]{:S(2)}) %collective-permute-start.11) | collective-permute-done | bytes 196640 | tf_op jit(solution)/shard_map/ppermute | solution.py:327
  37.0 0.8 %upstream.3.refs_3_ = f32[192,1024]{1,0:T(8,128)S(1)} custom-call(bf16[96,1024]{1,0:T(8,128)(2,1)S(1)} %cot_slots.3.near_ref.refs_0_, bf16[96,1024]{1,0:T(8,128)(2,1)S(1)} %collective-permute-done.11.far_ref.refs_1_, bf16[1024,1024]{1,0:T(8,128)(2,1)S(1)} %hold_weight.1.weight_ref), custom_call_target="tpu_custom_call" | custom-call | tf_op jit(solution)/shard_map/upstream/pallas_call | solution.py:26
  37.9 2.0 %expert.2 = (bf16[48,1024]{1,0:T(8,128)(2,1)S(1)}, bf16[48,1024]{1,0:T(8,128)(2,1)S(1)}, bf16[48,1024]{1,0:T(8,128)(2,1)S(1)}, bf16[48,1024]{1,0:T(8,128)(2,1)S(...) custom-call(s32[1]{0:T(128)} %bitcast.7.my_ref, ...), custom_call_target="tpu_custom_call" | custom-call | tf_op jit(solution)/shard_map/expert/pallas_call | solution.py:26
  39.9 0.1 collective-permute-start.12
  40.0 2.3 %collective-permute-start.19 = (bf16[48,1024]{1,0:T(8,128)(2,1)S(1)}, bf16[48,1024]{1,0:T(8,128)(2,1)S(1)}, u32[]{:S(2)}, u32[]{:S(2)}) collective-permute-start(bf16[48,1024]{1,0:T(8,128)(2,1)S(1)} %get-tuple-element.62), channel_id=1, source_target_pairs={{0,6},{1,7},{2,4},{3,5},{4,2},{5,3},{6,0},{7,1},{8,14},{9,15},{10,... | collective-permute-start | bytes 294920 | tf_op jit(solution)/shard_map/ppermute | solution.py:332
  42.2 0.3 back_pick.1.pick_ref
  42.6 0.6 collective-permute-start.20
  43.2 2.0 %expert.3 = (bf16[48,1024]{1,0:T(8,128)(2,1)S(1)}, bf16[48,1024]{1,0:T(8,128)(2,1)S(1)}, bf16[48,1024]{1,0:T(8,128)(2,1)S(1)}, bf16[48,1024]{1,0:T(8,128)(2,1)S(...) custom-call(s32[1]{0:T(128)} %bitcast.7.my_ref, ...), custom_call_target="tpu_custom_call" | custom-call | tf_op jit(solution)/shard_map/expert/pallas_call | solution.py:26
  45.1 1.8 %collective-permute-start.15 = (bf16[48,1024]{1,0:T(8,128)(2,1)S(1)}, bf16[48,1024]{1,0:T(8,128)(2,1)S(1)}, u32[]{:S(2)}, u32[]{:S(2)}) collective-permute-start(bf16[48,1024]{1,0:T(8,128)(2,1)S(1)} %get-tuple-element.58), channel_id=1, source_target_pairs={{0,2},{1,3},{2,0},{3,1},{4,6},{5,7},{6,4},{7,5},{8,10},{9,11},{10,... | collective-permute-start | bytes 294920 | tf_op jit(solution)/shard_map/ppermute | solution.py:332
  47.0 0.0 collective-permute-start.16
  47.0 0.2 stack.1
  47.2 1.1 %collective-permute-start.17 = (bf16[48,1024]{1,0:T(8,128)(2,1)S(1)}, bf16[48,1024]{1,0:T(8,128)(2,1)S(1)}, u32[]{:S(2)}, u32[]{:S(2)}) collective-permute-start(bf16[48,1024]{1,0:T(8,128)(2,1)S(1)} %get-tuple-element.60), channel_id=1, source_target_pairs={{0,4},{1,5},{2,6},{3,7},{4,0},{5,1},{6,2},{7,3},{8,12},{9,13},{10,... | collective-permute-start | bytes 294920 | tf_op jit(solution)/shard_map/ppermute | solution.py:332
  48.3 0.7 %collective-permute-start.18 = (bf16[48,1024]{1,0:T(8,128)(2,1)S(1)}, bf16[48,1024]{1,0:T(8,128)(2,1)S(1)}, u32[]{:S(2)}, u32[]{:S(2)}) collective-permute-start(bf16[48,1024]{1,0:T(8,128)(2,1)S(1)} %get-tuple-element.61), channel_id=1, source_target_pairs={{0,5},{1,4},{2,7},{3,6},{4,1},{5,0},{6,3},{7,2},{8,13},{9,12},{10,... | collective-permute-start | bytes 294920 | tf_op jit(solution)/shard_map/ppermute | solution.py:332
  49.0 3.3 %fusion = f32[1024,1024]{1,0:T(8,128)} fusion(bf16[384,1024]{1,0:T(8,128)(2,1)S(1)} %get-tuple-element.70, bf16[384,1024]{1,0:T(8,128)(2,1)S(1)} %get-tuple-element.71), kind=kOutput, calls=%fused_computation.1 | convolution fusion | flops 805306368 | bytes 5767168 | tf_op jit(solution)/shard_map/dot_general | solution.py:426
  52.4 0.6 collective-permute-done.17.refs_4_
  52.9 0.9 %collective-permute-done.18.refs_5_ = bf16[48,1024]{1,0:T(8,128)(2,1)S(1)} collective-permute-done((bf16[48,1024]{1,0:T(8,128)(2,1)S(1)}, bf16[48,1024]{1,0:T(8,128)(2,1)S(1)}, u32[]{:S(2)}, u32[]{:S(2)}) %collective-permute-start.18) | collective-permute-done | bytes 98336 | tf_op jit(solution)/shard_map/ppermute | solution.py:332
  53.9 0.3 combine.1
  54.2 2.8 %collective-permute-start.21 = (bf16[32,1024]{1,0:T(8,128)(2,1)S(1)}, bf16[32,1024]{1,0:T(8,128)(2,1)S(1)}, u32[]{:S(2)}, u32[]{:S(2)}) collective-permute-start(bf16[32,1024]{1,0:T(8,128)(2,1)S(1)} %get-tuple-element.81), channel_id=1, source_target_pairs={{0,24},{8,16},{16,8},{24,0},{1,25},{9,17},{17,9},{25,1},{2,26},{10... | collective-permute-start | bytes 196616 | tf_op jit(solution)/shard_map/ppermute | solution.py:327
  57.0 1.7 %collective-permute-start.23 = (bf16[32,1024]{1,0:T(8,128)(2,1)S(1)}, bf16[32,1024]{1,0:T(8,128)(2,1)S(1)}, u32[]{:S(2)}, u32[]{:S(2)}) collective-permute-start(bf16[32,1024]{1,0:T(8,128)(2,1)S(1)} %get-tuple-element.83), channel_id=1, source_target_pairs={{0,16},{8,24},{16,0},{24,8},{1,17},{9,25},{17,1},{25,9},{2,18},{10... | collective-permute-start | bytes 196616 | tf_op jit(solution)/shard_map/ppermute | solution.py:327
  58.6 3.3 %convolution_bitcast_fusion = f32[1,1024,1024]{2,1,0:T(8,128)} fusion(bf16[384,1024]{1,0:T(8,128)(2,1)S(1)} %get-tuple-element.84, bf16[384,1024]{1,0:T(8,128)(2,1)S(1)} %get-tuple-element.85), kind=kOutput, calls=%fused_computation | convolution fusion | flops 805306368 | bytes 5767168 | tf_op jit(solution)/shard_map/dot_general | solution.py:427
  62.0 1.3 %collective-permute-done.22.refs_2_ = bf16[32,1024]{1,0:T(8,128)(2,1)S(1)} collective-permute-done((bf16[32,1024]{1,0:T(8,128)(2,1)S(1)}, bf16[32,1024]{1,0:T(8,128)(2,1)S(1)}, u32[]{:S(2)}, u32[]{:S(2)}) %collective-permute-start.22) | collective-permute-done | bytes 65568 | tf_op jit(solution)/shard_map/ppermute | solution.py:327
  63.3 1.6 %back.1 = bf16[128,1024]{1,0:T(8,128)(2,1)} custom-call(bf16[128,1024]{1,0:T(8,128)(2,1)S(1)} %bitcast.23, f32[1,1024]{1,0:T(1,128)S(1)} %bitcast.31, f32[1,1024]{1,0:T(1,128)S(1)} %bitcast.33, f32[32,1024]{1,0:T(8,128)S(1)} %copy-done.6, f32[32,128]{1,0:T(8,128)S(1)} %copy-done.8, bf16[32,1024]{1,0:T(8,128)(2,1)S(1)} %bitcast.26, ...), custom_call_target="tpu_custom_call" | custom-call | tf_op jit(solution)/shard_map/back/pallas_call | solution.py:26
  (41 shorter events, 0.2 us)
Async XLA Ops:
  0.6 32.7 %copy-start.1 = (bf16[1,1024,1024]{2,1,0:T(8,128)(2,1)S(1)}, bf16[1,1024,1024]{2,1,0:T(8,128)(2,1)}, u32[]{:S(2)}) copy-start(bf16[1,1024,1024]{2,1,0:T(8,128)(2,1)} %param.14) | copy-start | bytes 6291460
  3.4 14.4 %collective-permute-start.3 = (bf16[32,1152]{1,0:T(8,128)(2,1)}, bf16[32,1152]{1,0:T(8,128)(2,1)S(1)}, u32[]{:S(2)}, u32[]{:S(2)}) collective-permute-start(bf16[32,1152]{1,0:T(8,128)(2,1)} %get-tuple-element.47.refs_0_), channel_id=1, source_target_pairs={{0,24},{8,16},{16,8},{24,0},{1,25},{9,17},{17,9},{25,1},{2,26},{10... | collective-permute-start | bytes 221192 | tf_op jit(solution)/shard_map/ppermute | solution.py:327
  8.5 9.3 %collective-permute-start.2 = (bf16[32,1152]{1,0:T(8,128)(2,1)}, bf16[32,1152]{1,0:T(8,128)(2,1)S(1)}, u32[]{:S(2)}, u32[]{:S(2)}) collective-permute-start(bf16[32,1152]{1,0:T(8,128)(2,1)} %get-tuple-element.47.refs_0_), channel_id=1, source_target_pairs={{0,8},{8,0},{16,24},{24,16},{1,9},{9,1},{17,25},{25,17},{2,10},{10... | collective-permute-start | bytes 221192 | tf_op jit(solution)/shard_map/ppermute | solution.py:327
  8.5 9.3 %collective-permute-start.1 = (bf16[32,1152]{1,0:T(8,128)(2,1)}, bf16[32,1152]{1,0:T(8,128)(2,1)S(1)}, u32[]{:S(2)}, u32[]{:S(2)}) collective-permute-start(bf16[32,1152]{1,0:T(8,128)(2,1)} %get-tuple-element.47.refs_0_), channel_id=1, source_target_pairs={{0,16},{8,24},{16,0},{24,8},{1,17},{9,25},{17,1},{25,9},{2,18},{10... | collective-permute-start | bytes 221192 | tf_op jit(solution)/shard_map/ppermute | solution.py:327
  9.2 8.6 %collective-permute-start = (bf16[32,1024]{1,0:T(8,128)(2,1)}, bf16[32,1024]{1,0:T(8,128)(2,1)S(1)}, u32[]{:S(2)}, u32[]{:S(2)}) collective-permute-start(bf16[32,1024]{1,0:T(8,128)(2,1)} %bitcast.24), channel_id=1, source_target_pairs={{0,16},{8,24},{16,0},{24,8},{1,17},{9,25},{17,1},{25,9},{2,18},{10... | collective-permute-start | bytes 196616 | tf_op jit(solution)/shard_map/ppermute | solution.py:327
  11.5 0.9 %copy-start.3 = (bf16[1,32,1024]{2,1,0:T(8,128)(2,1)S(1)}, bf16[1,32,1024]{2,1,0:T(8,128)(2,1)}, u32[]{:S(2)}) copy-start(bf16[1,32,1024]{2,1,0:T(8,128)(2,1)} %param.15) | copy-start | bytes 196612
  12.3 0.9 %copy-start.7 = (bf16[32,1152]{1,0:T(8,128)(2,1)S(1)}, bf16[32,1152]{1,0:T(8,128)(2,1)}, u32[]{:S(2)}) copy-start(bf16[32,1152]{1,0:T(8,128)(2,1)} %get-tuple-element.47.refs_0_) | copy-start | bytes 221188
  17.9 1.8 %collective-permute-start.5 = (bf16[128,1152]{1,0:T(8,128)(2,1)S(1)}, bf16[128,1152]{1,0:T(8,128)(2,1)S(1)}, u32[]{:S(2)}, u32[]{:S(2)}) collective-permute-start(bf16[128,1152]{1,0:T(8,128)(2,1)S(1)} %token_near.1.token_ref), channel_id=1, source_target_pairs={{0,1},{1,0},{2,3},{3,2},{4,5},{5,4},{6,7},{7,6},{8,9},{9,8},{10,11... | collective-permute-start | bytes 884744 | tf_op jit(solution)/shard_map/ppermute | solution.py:336
  18.0 1.8 %collective-permute-start.4 = (bf16[64,1024]{1,0:T(8,128)(2,1)S(1)}, bf16[64,1024]{1,0:T(8,128)(2,1)S(1)}, u32[]{:S(2)}, u32[]{:S(2)}) collective-permute-start(bf16[64,1024]{1,0:T(8,128)(2,1)S(1)} %cot_near.1.refs_0_.cot_ref), channel_id=1, source_target_pairs={{0,1},{1,0},{2,3},{3,2},{4,5},{5,4},{6,7},{7,6},{8,9},{9,8},{10,11... | collective-permute-start | bytes 393224 | tf_op jit(solution)/shard_map/ppermute | solution.py:336
  20.9 6.0 %collective-permute-start.6 = (bf16[48,1024]{1,0:T(8,128)(2,1)S(1)}, bf16[48,1024]{1,0:T(8,128)(2,1)S(1)}, u32[]{:S(2)}, u32[]{:S(2)}) collective-permute-start(bf16[48,1024]{1,0:T(8,128)(2,1)S(1)} %get-tuple-element.48), channel_id=1, source_target_pairs={{0,4},{1,5},{2,6},{3,7},{4,0},{5,1},{6,2},{7,3},{8,12},{9,13},{10,... | collective-permute-start | bytes 294920 | tf_op jit(solution)/shard_map/ppermute | solution.py:332
  22.5 5.6 %collective-permute-start.7 = (bf16[48,1024]{1,0:T(8,128)(2,1)S(1)}, bf16[48,1024]{1,0:T(8,128)(2,1)S(1)}, u32[]{:S(2)}, u32[]{:S(2)}) collective-permute-start(bf16[48,1024]{1,0:T(8,128)(2,1)S(1)} %get-tuple-element.49), channel_id=1, source_target_pairs={{0,2},{1,3},{2,0},{3,1},{4,6},{5,7},{6,4},{7,5},{8,10},{9,11},{10,... | collective-permute-start | bytes 294920 | tf_op jit(solution)/shard_map/ppermute | solution.py:332
  24.0 6.6 %collective-permute-start.10 = (bf16[48,1024]{1,0:T(8,128)(2,1)S(1)}, bf16[48,1024]{1,0:T(8,128)(2,1)S(1)}, u32[]{:S(2)}, u32[]{:S(2)}) collective-permute-start(bf16[48,1024]{1,0:T(8,128)(2,1)S(1)} %get-tuple-element.53), channel_id=1, source_target_pairs={{0,6},{1,7},{2,4},{3,5},{4,2},{5,3},{6,0},{7,1},{8,14},{9,15},{10,... | collective-permute-start | bytes 294920 | tf_op jit(solution)/shard_map/ppermute | solution.py:332
  24.4 13.4 %collective-permute-start.9 = (bf16[96,1152]{1,0:T(8,128)(2,1)S(1)}, bf16[96,1152]{1,0:T(8,128)(2,1)S(1)}, u32[]{:S(2)}, u32[]{:S(2)}) collective-permute-start(bf16[96,1152]{1,0:T(8,128)(2,1)S(1)} %get-tuple-element.51), channel_id=1, source_target_pairs={{0,6},{1,7},{2,4},{3,5},{4,2},{5,3},{6,0},{7,1},{8,14},{9,15},{10,... | collective-permute-start | bytes 663560 | tf_op jit(solution)/shard_map/ppermute | solution.py:332
  28.1 6.8 %collective-permute-start.8 = (bf16[96,1024]{1,0:T(8,128)(2,1)S(1)}, bf16[96,1024]{1,0:T(8,128)(2,1)S(1)}, u32[]{:S(2)}, u32[]{:S(2)}) collective-permute-start(bf16[96,1024]{1,0:T(8,128)(2,1)S(1)} %cot_slots.2.near_ref.refs_5_), channel_id=1, source_target_pairs={{0,8},{8,0},{16,24},{24,16},{1,9},{9,1},{17,25},{25,17},{2,10},{10... | collective-permute-start | bytes 589832 | tf_op jit(solution)/shard_map/ppermute | solution.py:327
  30.6 6.4 %collective-permute-start.11 = (bf16[96,1024]{1,0:T(8,128)(2,1)S(1)}, bf16[96,1024]{1,0:T(8,128)(2,1)S(1)}, u32[]{:S(2)}, u32[]{:S(2)}) collective-permute-start(bf16[96,1024]{1,0:T(8,128)(2,1)S(1)} %cot_slots.3.near_ref.refs_0_), channel_id=1, source_target_pairs={{0,8},{8,0},{16,24},{24,16},{1,9},{9,1},{17,25},{25,17},{2,10},{10... | collective-permute-start | bytes 589832 | tf_op jit(solution)/shard_map/ppermute | solution.py:327
  30.7 12.4 %collective-permute-start.13 = (bf16[96,1152]{1,0:T(8,128)(2,1)S(1)}, bf16[96,1152]{1,0:T(8,128)(2,1)S(1)}, u32[]{:S(2)}, u32[]{:S(2)}) collective-permute-start(bf16[96,1152]{1,0:T(8,128)(2,1)S(1)} %get-tuple-element.56), channel_id=1, source_target_pairs={{0,4},{1,5},{2,6},{3,7},{4,0},{5,1},{6,2},{7,3},{8,12},{9,13},{10,... | collective-permute-start | bytes 663560 | tf_op jit(solution)/shard_map/ppermute | solution.py:332
  31.8 11.3 %collective-permute-start.14 = (bf16[96,1152]{1,0:T(8,128)(2,1)S(1)}, bf16[96,1152]{1,0:T(8,128)(2,1)S(1)}, u32[]{:S(2)}, u32[]{:S(2)}) collective-permute-start(bf16[96,1152]{1,0:T(8,128)(2,1)S(1)} %get-tuple-element.57), channel_id=1, source_target_pairs={{0,2},{1,3},{2,0},{3,1},{4,6},{5,7},{6,4},{7,5},{8,10},{9,11},{10,... | collective-permute-start | bytes 663560 | tf_op jit(solution)/shard_map/ppermute | solution.py:332
  33.5 4.4 %copy-start = (bf16[1,1024,1024]{2,1,0:T(8,128)(2,1)S(1)}, bf16[1,1024,1024]{2,1,0:T(8,128)(2,1)}, u32[]{:S(2)}) copy-start(bf16[1,1024,1024]{2,1,0:T(8,128)(2,1)} %param.13) | copy-start | bytes 6291460
  33.5 4.4 %copy-start.5 = (bf16[1024,8]{0,1:T(8,128)(2,1)S(1)}, bf16[1024,8]{0,1:T(8,128)(2,1)}, u32[]{:S(2)}) copy-start(bf16[1024,8]{0,1:T(8,128)(2,1)} %param.11) | copy-start | bytes 49156
  39.9 7.3 %collective-permute-start.12 = (bf16[48,1024]{1,0:T(8,128)(2,1)S(1)}, bf16[48,1024]{1,0:T(8,128)(2,1)S(1)}, u32[]{:S(2)}, u32[]{:S(2)}) collective-permute-start(bf16[48,1024]{1,0:T(8,128)(2,1)S(1)} %get-tuple-element.55), channel_id=1, source_target_pairs={{0,1},{1,0},{2,3},{3,2},{4,5},{5,4},{6,7},{7,6},{8,9},{9,8},{10,11... | collective-permute-start | bytes 294920 | tf_op jit(solution)/shard_map/ppermute | solution.py:332
  40.0 8.3 %collective-permute-start.19 = (bf16[48,1024]{1,0:T(8,128)(2,1)S(1)}, bf16[48,1024]{1,0:T(8,128)(2,1)S(1)}, u32[]{:S(2)}, u32[]{:S(2)}) collective-permute-start(bf16[48,1024]{1,0:T(8,128)(2,1)S(1)} %get-tuple-element.62), channel_id=1, source_target_pairs={{0,6},{1,7},{2,4},{3,5},{4,2},{5,3},{6,0},{7,1},{8,14},{9,15},{10,... | collective-permute-start | bytes 294920 | tf_op jit(solution)/shard_map/ppermute | solution.py:332
  42.6 9.7 %collective-permute-start.20 = (bf16[48,1024]{1,0:T(8,128)(2,1)S(1)}, bf16[48,1024]{1,0:T(8,128)(2,1)S(1)}, u32[]{:S(2)}, u32[]{:S(2)}) collective-permute-start(bf16[48,1024]{1,0:T(8,128)(2,1)S(1)} %get-tuple-element.63), channel_id=1, source_target_pairs={{0,7},{1,6},{2,5},{3,4},{4,3},{5,2},{6,1},{7,0},{8,15},{9,14},{10,... | collective-permute-start | bytes 294920 | tf_op jit(solution)/shard_map/ppermute | solution.py:332
  45.1 7.2 %collective-permute-start.15 = (bf16[48,1024]{1,0:T(8,128)(2,1)S(1)}, bf16[48,1024]{1,0:T(8,128)(2,1)S(1)}, u32[]{:S(2)}, u32[]{:S(2)}) collective-permute-start(bf16[48,1024]{1,0:T(8,128)(2,1)S(1)} %get-tuple-element.58), channel_id=1, source_target_pairs={{0,2},{1,3},{2,0},{3,1},{4,6},{5,7},{6,4},{7,5},{8,10},{9,11},{10,... | collective-permute-start | bytes 294920 | tf_op jit(solution)/shard_map/ppermute | solution.py:332
  47.0 5.4 %collective-permute-start.16 = (bf16[48,1024]{1,0:T(8,128)(2,1)S(1)}, bf16[48,1024]{1,0:T(8,128)(2,1)S(1)}, u32[]{:S(2)}, u32[]{:S(2)}) collective-permute-start(bf16[48,1024]{1,0:T(8,128)(2,1)S(1)} %get-tuple-element.59), channel_id=1, source_target_pairs={{0,3},{1,2},{2,1},{3,0},{4,7},{5,6},{6,5},{7,4},{8,11},{9,10},{10,... | collective-permute-start | bytes 294920 | tf_op jit(solution)/shard_map/ppermute | solution.py:332
  47.2 5.7 %collective-permute-start.17 = (bf16[48,1024]{1,0:T(8,128)(2,1)S(1)}, bf16[48,1024]{1,0:T(8,128)(2,1)S(1)}, u32[]{:S(2)}, u32[]{:S(2)}) collective-permute-start(bf16[48,1024]{1,0:T(8,128)(2,1)S(1)} %get-tuple-element.60), channel_id=1, source_target_pairs={{0,4},{1,5},{2,6},{3,7},{4,0},{5,1},{6,2},{7,3},{8,12},{9,13},{10,... | collective-permute-start | bytes 294920 | tf_op jit(solution)/shard_map/ppermute | solution.py:332
  48.3 5.6 %collective-permute-start.18 = (bf16[48,1024]{1,0:T(8,128)(2,1)S(1)}, bf16[48,1024]{1,0:T(8,128)(2,1)S(1)}, u32[]{:S(2)}, u32[]{:S(2)}) collective-permute-start(bf16[48,1024]{1,0:T(8,128)(2,1)S(1)} %get-tuple-element.61), channel_id=1, source_target_pairs={{0,5},{1,4},{2,7},{3,6},{4,1},{5,0},{6,3},{7,2},{8,13},{9,12},{10,... | collective-permute-start | bytes 294920 | tf_op jit(solution)/shard_map/ppermute | solution.py:332
  52.3 11.0 %copy-start.2 = (bf16[1,128,1024]{2,1,0:T(8,128)(2,1)S(1)}, bf16[1,128,1024]{2,1,0:T(8,128)(2,1)}, u32[]{:S(2)}) copy-start(bf16[1,128,1024]{2,1,0:T(8,128)(2,1)} %param.8) | copy-start | bytes 786436
  52.3 11.0 %copy-start.4 = (bf16[1,32,1024]{2,1,0:T(8,128)(2,1)S(1)}, bf16[1,32,1024]{2,1,0:T(8,128)(2,1)}, u32[]{:S(2)}) copy-start(bf16[1,32,1024]{2,1,0:T(8,128)(2,1)} %param.15) | copy-start | bytes 196612
  52.3 11.0 %copy-start.6 = (f32[32,1024]{1,0:T(8,128)S(1)}, f32[32,1024]{1,0:T(8,128)}, u32[]{:S(2)}) copy-start(f32[32,1024]{1,0:T(8,128)} %get-tuple-element.45.tok_ref) | copy-start | bytes 393220
  52.3 11.0 %copy-start.8 = (f32[32,128]{1,0:T(8,128)S(1)}, f32[32,128]{1,0:T(8,128)}, u32[]{:S(2)}) copy-start(f32[32,128]{1,0:T(8,128)} %get-tuple-element.46.keep_ref) | copy-start | bytes 49156
  52.3 11.0 %copy-start.9 = (f32[1024]{0:T(1024)S(1)}, f32[1024]{0:T(1024)}, u32[]{:S(2)}) copy-start(f32[1024]{0:T(1024)} %param.9) | copy-start | bytes 12292
  52.3 11.0 %copy-start.10 = (f32[1024]{0:T(1024)S(1)}, f32[1024]{0:T(1024)}, u32[]{:S(2)}) copy-start(f32[1024]{0:T(1024)} %param.10) | copy-start | bytes 12292
  54.2 7.8 %collective-permute-start.21 = (bf16[32,1024]{1,0:T(8,128)(2,1)S(1)}, bf16[32,1024]{1,0:T(8,128)(2,1)S(1)}, u32[]{:S(2)}, u32[]{:S(2)}) collective-permute-start(bf16[32,1024]{1,0:T(8,128)(2,1)S(1)} %get-tuple-element.81), channel_id=1, source_target_pairs={{0,24},{8,16},{16,8},{24,0},{1,25},{9,17},{17,9},{25,1},{2,26},{10... | collective-permute-start | bytes 196616 | tf_op jit(solution)/shard_map/ppermute | solution.py:327
  57.0 6.3 %collective-permute-start.22 = (bf16[32,1024]{1,0:T(8,128)(2,1)S(1)}, bf16[32,1024]{1,0:T(8,128)(2,1)S(1)}, u32[]{:S(2)}, u32[]{:S(2)}) collective-permute-start(bf16[32,1024]{1,0:T(8,128)(2,1)S(1)} %get-tuple-element.82), channel_id=1, source_target_pairs={{0,8},{8,0},{16,24},{24,16},{1,9},{9,1},{17,25},{25,17},{2,10},{10... | collective-permute-start | bytes 196616 | tf_op jit(solution)/shard_map/ppermute | solution.py:327
  57.0 6.3 %collective-permute-start.23 = (bf16[32,1024]{1,0:T(8,128)(2,1)S(1)}, bf16[32,1024]{1,0:T(8,128)(2,1)S(1)}, u32[]{:S(2)}, u32[]{:S(2)}) collective-permute-start(bf16[32,1024]{1,0:T(8,128)(2,1)S(1)} %get-tuple-element.83), channel_id=1, source_target_pairs={{0,16},{8,24},{16,0},{24,8},{1,17},{9,25},{17,1},{25,9},{2,18},{10... | collective-permute-start | bytes 196616 | tf_op jit(solution)/shard_map/ppermute | solution.py:327

commit v4 on v3

--- a/solution.py
+++ b/solution.py
@@ -128,11 +128,11 @@
         at += r.shape[0]
 
 
-def slot_places(tail, columns, step, count, capacity, my):
+def slot_places(tail, columns, count, capacity, my):
     tokens = tail.shape[0]
     lane_row = lax.broadcasted_iota(jnp.int32, (LANES, LANES), 0)
     lane_col = lax.broadcasted_iota(jnp.int32, (LANES, LANES), 1)
-    lane = (step * (lane_col % GROUP)) ^ my
+    lane = (2 * (lane_col % GROUP)) ^ my
     lane = jnp.where(lane_col < GROUP, lane, lane + 2 * GROUP)
     live = (lane_col % GROUP < columns) & (lane_col < 2 * GROUP)
     order = ((lane_row == lane) & live).astype(F32).astype(BF)
@@ -155,7 +155,7 @@
 
 
 def pick_kernel(pieces, chunks, capacity, my_ref, cot_ref, token_ref, other_cot_ref, other_token_ref, *refs):
-    cot_outs, outs = refs[:chunks], refs[chunks:]
+    cot_outs, outs, pick_ref = refs[:chunks], refs[chunks : 2 * chunks], refs[2 * chunks]
     tokens, full = token_ref.shape
     width = full - LANES
     count = tokens // pieces
@@ -164,7 +164,7 @@
     my = my_ref[0]
 
     tail = jnp.concatenate([token_ref[:cots, width:], other_token_ref[:cots, width:]], axis=0)
-    places, gates = slot_places(tail, chunks, 2, count, capacity, my)
+    places, gates = slot_places(tail, chunks, count, capacity, my)
     picks = selection(places, gates, chunks, 2 * near * capacity)
     cot_rows = jnp.concatenate([cot_ref[...], other_cot_ref[...]], axis=0)
     chosen = jnp.dot(picks, cot_rows, preferred_element_type=F32).astype(BF)
@@ -172,17 +172,12 @@
         out[...] = chosen[m * out.shape[0] : (m + 1) * out.shape[0], :]
 
     token_rows = jnp.concatenate([token_ref[...], other_token_ref[...]], axis=0)
-    places, gates = slot_places(token_rows[:, width:], chunks, 2, count, capacity, my)
+    places, gates = slot_places(token_rows[:, width:], chunks, count, capacity, my)
     picks = selection(places, jnp.ones_like(gates), chunks, 2 * pieces * capacity)
+    pick_ref[...] = picks
     chosen = jnp.dot(picks, token_rows, preferred_element_type=F32).astype(BF)
     for m, out in enumerate(outs):
         out[...] = chosen[m * out.shape[0] : (m + 1) * out.shape[0], :]
-
-
-def back_pick_kernel(owners, count, capacity, my_ref, token_ref, out_ref):
-    tail = token_ref[:, token_ref.shape[1] - LANES :]
-    places, gates = slot_places(tail, owners, 1, count, capacity, my_ref[0])
-    out_ref[...] = selection(places, jnp.ones_like(gates), owners, out_ref.shape[0] // owners)
 
 
 def interleave(near, far, owners):
@@ -197,14 +192,14 @@
     out_ref[...] = interleave(upstream[:half, :], upstream[half:, :], owners)
 
 
-def expert_kernel(chunks, owners, tile, waits, my_ref, *refs):
+def expert_kernel(chunks, tile, waits, my_ref, *refs):
     refs = refs[waits:]
     ins, refs = refs[:chunks], refs[chunks:]
     upstream_ref, weight_ref, router_ref = refs[:3]
-    outs, (rows_ref, hidden_ref, grad_ref) = refs[3 : 3 + owners], refs[3 + owners :]
+    outs, (rows_ref, hidden_ref, grad_ref) = refs[3 : 3 + chunks], refs[3 + chunks :]
     slots, width = rows_ref.shape
     experts = router_ref.shape[0]
-    rows = slots // owners
+    rows = slots // chunks
     token_rows = jnp.concatenate([r[:, :width] for r in ins], axis=0)
     rows_ref[...] = token_rows
     terms = jnp.zeros((slots, LANES), F32)
@@ -240,21 +235,27 @@
 
 
 def stack_kernel(owners, *refs):
-    ins, outs = refs[:10], refs[10:]
-    half = outs[0].shape[0] // 2
-    for g in range(2):
-        near_ref, far_ref, *others = ins[5 * g : 5 * g + 5]
-        at = slice(g * half, (g + 1) * half)
-        outs[0][at, :] = interleave(near_ref[...].astype(F32), far_ref[...].astype(F32), owners).astype(BF)
-        for r, out in zip(others, outs[1:]):
-            out[at, :] = r[...]
-
-
-def combine_kernel(owners, pick_ref, *refs):
-    ins, outs = refs[:owners], refs[owners:]
-    stacked = jnp.concatenate([r[...] for r in ins], axis=0)
-    back = lax.dot_general(pick_ref[...], stacked, ROWS_T, preferred_element_type=F32).astype(BF)
+    ins, outs = refs[:-4], refs[-4:]
+    cots = [interleave(a[...].astype(F32), b[...].astype(F32), owners) for a, b in zip(ins[::5], ins[1::5])]
+    outs[0][...] = jnp.concatenate(cots, axis=0).astype(BF)
+    for i, out in enumerate(outs[1:]):
+        out[...] = jnp.concatenate([r[...] for r in ins[2 + i :: 5]], axis=0)
+
+
+def combine_other_kernel(pick_ref, *refs):
+    ins, out_ref = refs[:-1], refs[-1]
+    tokens = out_ref.shape[0]
+    rows = jnp.concatenate([r[...] for r in ins], axis=0)
+    out_ref[...] = lax.dot_general(pick_ref[:, tokens:], rows, ROWS_T, preferred_element_type=F32).astype(BF)
+
+
+def combine_own_kernel(chunks, pick_ref, *refs):
+    ins, other_ref, outs = refs[:chunks], refs[chunks], refs[chunks + 1 :]
+    tokens = other_ref.shape[0]
     count = outs[0].shape[0]
+    rows = jnp.concatenate([r[...] for r in ins], axis=0)
+    back = lax.dot_general(pick_ref[:, :tokens], rows, ROWS_T, preferred_element_type=F32)
+    back = (back + other_ref[...].astype(F32)).astype(BF)
     for k, out in enumerate(outs):
         out[...] = back[k * count : (k + 1) * count, :]
 
@@ -362,27 +363,17 @@
         shape(tokens, full),
         (cot_near, held, *[over_seq(pay, k) for k in places[1:]]),
     )
-    chosen = call(
+    *chosen, pick = call(
         functools.partial(pick_kernel, pieces, chunks, capacity),
         "pick",
-        [shape(rows // 2, width)] * chunks + [shape(rows, full)] * chunks,
+        [shape(rows // 2, width)] * chunks + [shape(rows, full)] * chunks + [shape(slots, 2 * tokens)],
         (my, cot_near, token_near, over_cores(cot_near), over_cores(token_near)),
         scalars=1,
         limit=16,
     )
-    back_pick = call(
-        functools.partial(back_pick_kernel, owners, count, capacity),
-        "back_pick",
-        shape(slots, tokens),
-        (my, token_near),
-        us=1.0,
-        scalars=1,
-        limit=16,
-    )
     cot_chunks = over_exp(chosen[:chunks], 2)
     token_chunks = over_exp(chosen[chunks:], 2)
     order = [0, *range(chunks - 1, 0, -1)]
-    stacked, back_rows = [], [None] * owners
     groups = (order[: chunks // 2], order[chunks // 2 :])
     part = slots // 2
     near, far, upstream = [], [], []
@@ -402,19 +393,19 @@
                 limit=16,
             )
         )
+    stacked, back_rows = [], [None] * chunks
     for g, group in enumerate(groups):
-        shares = 2 * len(group)
         waits = upstream[1:] if g == 0 else []
         *outs, token_rows, hidden_rows, hidden_grad = call(
-            functools.partial(expert_kernel, len(group), shares, tile, len(waits)),
+            functools.partial(expert_kernel, len(group), tile, len(waits)),
             "expert",
-            [shape(rows // 2, width)] * shares + [shape(part, width), shape(part, hidden), shape(part, hidden)],
+            [shape(rows, width)] * len(group) + [shape(part, width), shape(part, hidden), shape(part, hidden)],
             (my, *waits, *[token_chunks[m] for m in group], upstream[g], weight_in, router_t),
             scalars=1,
             limit=24,
         )
-        for i, out in enumerate(outs):
-            back_rows[2 * group[i // 2] + i % 2] = out
+        for m, out in zip(group, outs):
+            back_rows[m] = out
         stacked += [near[g], far[g], hidden_rows, token_rows, hidden_grad]
     cot_slots, hidden_rows, token_slots, hidden_grad = call(
         functools.partial(stack_kernel, chunks),
@@ -425,12 +416,14 @@
     )
     grad_out = lax.dot_general(hidden_rows, cot_slots, ROWS_T, preferred_element_type=F32)
     grad_in = lax.dot_general(token_slots, hidden_grad, ROWS_T, preferred_element_type=F32)
-    *returned, grad_out = lax.optimization_barrier((*over_exp(back_rows, 1), grad_out))
+    returned = over_exp(back_rows, 2)
+    *returned, grad_out = lax.optimization_barrier((*returned, grad_out))
+    other_rows = call(combine_other_kernel, "combine_other", shape(tokens, width), (pick, *returned), limit=16)
     partial_rows = call(
-        functools.partial(combine_kernel, owners),
-        "combine",
+        functools.partial(combine_own_kernel, chunks),
+        "combine_own",
         [shape(count, width)] * pieces,
-        (back_pick, *returned),
+        (pick, *returned, over_cores(other_rows)),
         limit=16,
     )
     parts = [partial_rows[0]] + [over_seq(partial_rows[i], places[i]) for i in range(pieces - 1, 0, -1)]

time: 65.2 us -> 64.3 us (0.986)
  starting transfers between devices: 28.4 us -> 24 us
  waiting for transfers between devices: 14.9 us -> 18.5 us
    ppermute x13 -> x9, starting transfers between devices: 15.2 us -> 10.7 us  [over_exp(): lax.ppermute(values[m], 'exp', [(i, i ^ m * step) for i in range(owners)])]
    ppermute x9, waiting for transfers between devices: 8.58 us -> 11.3 us  [over_seq(): return lax.ppermute(value, 'seq', [(i, i ^ k) for i in range(pieces)])]
    ppermute x2 -> x3, waiting for transfers between devices: 1.26 us -> 2.78 us  [over_cores(): return lax.ppermute(value, 'exp', [(i, i ^ 1) for i in range(owners)])]
    ppermute x13 -> x9, waiting for transfers between devices: 5.11 us -> 4.42 us  [over_exp(): lax.ppermute(values[m], 'exp', [(i, i ^ m * step) for i in range(owners)])]
  transfers between devices with their start and end apart: 24 -> 21, of which waited for: 9 -> 10; matrix products, arithmetic and copies ran while one was open for 10% -> 10% of each run, Pallas kernels for 10% -> 9%
where the time goes in v4:
time: 64.3 us; the launch traced here: 64.1 us
  starting transfers between devices  24 us (37%)
  waiting for transfers between devices  18.5 us (29%)
  Pallas kernels  12.3 us (19%)
  matrix products  6.61 us (10%)
  local copies, waits for them, and re-layouts  1.8 us (3%)
  between operations  0.88 us (1%)
    ppermute x9, starting transfers between devices, over_seq(): return lax.ppermute(value, 'seq', [(i, i ^ k) for i in range(pieces)])  12.7 us
    pallas_call x17, Pallas kernels, call(): pl.pallas_call(body, name=name, out_shape=outs, in_specs=[smem] * scalars...  12.3 us
    ppermute x9, waiting for transfers between devices, over_seq(): return lax.ppermute(value, 'seq', [(i, i ^ k) for i in range(pieces)])  11.3 us
    ppermute x9, starting transfers between devices, over_exp(): lax.ppermute(values[m], 'exp', [(i, i ^ m * step) for i in range(owners)])  10.7 us
    ppermute x9, waiting for transfers between devices, over_exp(): lax.ppermute(values[m], 'exp', [(i, i ^ m * step) for i in range(owners)])  4.42 us
    dot_general x1, matrix products, per_device(): lax.dot_general(hidden_rows, cot_slots, ROWS_T, preferred_element_type=F32)  3.3 us
    dot_general x1, matrix products, per_device(): lax.dot_general(token_slots, hidden_grad, ROWS_T, preferred_element_type=...  3.3 us
    ppermute x3, waiting for transfers between devices, over_cores(): return lax.ppermute(value, 'exp', [(i, i ^ 1) for i in range(owners)])  2.78 us
  transfers between devices with their start and end apart: 21, of which 10 were waited for; matrix products, arithmetic and copies ran while one was open for 10% of the time, Pallas kernels for 9%

profile of v4, /device:TPU:0, one launch (start us, length us, event | category | flops | bytes accessed | tf_op | source)
XLA Modules:
  0.0 64.1 jit_solution(14443071724795348771)
XLA Ops:
  0.6 2.8 %front.1 = (bf16[32,1152]{1,0:T(8,128)(2,1)}, f32[32,1024]{1,0:T(8,128)}, f32[32,128]{1,0:T(8,128)}) custom-call(bf16[128,1024]{1,0:T(8,128)(2,1)} %bitcast.22, f32[1,1024]{1,0:T(1,128)} %bitcast.30, f32[1,1024]{1,0:T(1,128)} %bitcast.32, bf16[8,1024]{1,0:T(8,128)(2,1)} %bitcast.27, s32[2,32]{1,0:T(2,128)} %bitcast.36), custom_call_target="tpu_custom_call" | custom-call | bytes 6000000 | tf_op jit(solution)/shard_map/front/pallas_call | solution.py:26
  3.4 5.1 %collective-permute-start.3 = (bf16[32,1152]{1,0:T(8,128)(2,1)}, bf16[32,1152]{1,0:T(8,128)(2,1)S(1)}, u32[]{:S(2)}, u32[]{:S(2)}) collective-permute-start(bf16[32,1152]{1,0:T(8,128)(2,1)} %get-tuple-element.40.refs_0_), channel_id=1, source_target_pairs={{0,24},{8,16},{16,8},{24,0},{1,25},{9,17},{17,9},{25,1},{2,26},{10... | collective-permute-start | bytes 221192 | tf_op jit(solution)/shard_map/ppermute | solution.py:328
  8.5 0.6 collective-permute-start.1
  9.2 2.3 %collective-permute-start = (bf16[32,1024]{1,0:T(8,128)(2,1)}, bf16[32,1024]{1,0:T(8,128)(2,1)S(1)}, u32[]{:S(2)}, u32[]{:S(2)}) collective-permute-start(bf16[32,1024]{1,0:T(8,128)(2,1)} %bitcast.24), channel_id=1, source_target_pairs={{0,16},{8,24},{16,0},{24,8},{1,17},{9,25},{17,1},{25,9},{2,18},{10... | collective-permute-start | bytes 196616 | tf_op jit(solution)/shard_map/ppermute | solution.py:328
  11.5 0.9 %copy-done.3 = bf16[1,32,1024]{2,1,0:T(8,128)(2,1)S(1)} copy-done((bf16[1,32,1024]{2,1,0:T(8,128)(2,1)S(1)}, bf16[1,32,1024]{2,1,0:T(8,128)(2,1)}, u32[]{:S(2)}) %copy-start.3) | copy-done | bytes 65560
  12.3 0.9 %copy-done.7 = bf16[32,1152]{1,0:T(8,128)(2,1)S(1)} copy-done((bf16[32,1152]{1,0:T(8,128)(2,1)S(1)}, bf16[32,1152]{1,0:T(8,128)(2,1)}, u32[]{:S(2)}) %copy-start.7) | copy-done | bytes 73752
  13.2 4.6 %collective-permute-done.refs_1_ = bf16[32,1024]{1,0:T(8,128)(2,1)S(1)} collective-permute-done((bf16[32,1024]{1,0:T(8,128)(2,1)}, bf16[32,1024]{1,0:T(8,128)(2,1)S(1)}, u32[]{:S(2)}, u32[]{:S(2)}) %collective-permute-start) | collective-permute-done | bytes 65568 | tf_op jit(solution)/shard_map/ppermute | solution.py:328
  17.9 0.1 collective-permute-start.5
  18.0 0.5 collective-permute-start.4
  18.5 1.3 %collective-permute-done.4.other_cot_ref = bf16[64,1024]{1,0:T(8,128)(2,1)S(1)} collective-permute-done((bf16[64,1024]{1,0:T(8,128)(2,1)S(1)}, bf16[64,1024]{1,0:T(8,128)(2,1)S(1)}, u32[]{:S(2)}, u32[]{:S(2)}) %collective-permute-start.4) | collective-permute-done | bytes 131104 | tf_op jit(solution)/shard_map/ppermute | solution.py:337
  19.7 1.2 %pick.1 = (bf16[48,1024]{1,0:T(8,128)(2,1)S(1)}, bf16[48,1024]{1,0:T(8,128)(2,1)S(1)}, bf16[48,1024]{1,0:T(8,128)(2,1)S(1)}, bf16[48,1024]{1,0:T(8,128)(2,1)S(1)...) custom-call(s32[1]{0:T(128)} %bitcast.7.my_ref, ...), custom_call_target="tpu_custom_call" | custom-call | tf_op jit(solution)/shard_map/pick/pallas_call | solution.py:26
  20.9 1.6 %collective-permute-start.6 = (bf16[48,1024]{1,0:T(8,128)(2,1)S(1)}, bf16[48,1024]{1,0:T(8,128)(2,1)S(1)}, u32[]{:S(2)}, u32[]{:S(2)}) collective-permute-start(bf16[48,1024]{1,0:T(8,128)(2,1)S(1)} %get-tuple-element.42), channel_id=1, source_target_pairs={{0,4},{1,5},{2,6},{3,7},{4,0},{5,1},{6,2},{7,3},{8,12},{9,13},{10,... | collective-permute-start | bytes 294920 | tf_op jit(solution)/shard_map/ppermute | solution.py:333
  22.5 1.5 %collective-permute-start.7 = (bf16[48,1024]{1,0:T(8,128)(2,1)S(1)}, bf16[48,1024]{1,0:T(8,128)(2,1)S(1)}, u32[]{:S(2)}, u32[]{:S(2)}) collective-permute-start(bf16[48,1024]{1,0:T(8,128)(2,1)S(1)} %get-tuple-element.43), channel_id=1, source_target_pairs={{0,2},{1,3},{2,0},{3,1},{4,6},{5,7},{6,4},{7,5},{8,10},{9,11},{10,... | collective-permute-start | bytes 294920 | tf_op jit(solution)/shard_map/ppermute | solution.py:333
  24.0 0.5 collective-permute-start.10
  24.4 2.4 %collective-permute-start.9 = (bf16[96,1152]{1,0:T(8,128)(2,1)S(1)}, bf16[96,1152]{1,0:T(8,128)(2,1)S(1)}, u32[]{:S(2)}, u32[]{:S(2)}) collective-permute-start(bf16[96,1152]{1,0:T(8,128)(2,1)S(1)} %get-tuple-element.45), channel_id=1, source_target_pairs={{0,6},{1,7},{2,4},{3,5},{4,2},{5,3},{6,0},{7,1},{8,14},{9,15},{10,... | collective-permute-start | bytes 663560 | tf_op jit(solution)/shard_map/ppermute | solution.py:333
  26.9 0.5 collective-permute-start.12
  27.4 0.5 collective-permute-start.13
  27.9 0.2 collective-permute-done.7.refs_1_
  28.1 0.1 collective-permute-start.8
  28.2 2.5 %collective-permute-done.10.refs_1_ = bf16[48,1024]{1,0:T(8,128)(2,1)S(1)} collective-permute-done((bf16[48,1024]{1,0:T(8,128)(2,1)S(1)}, bf16[48,1024]{1,0:T(8,128)(2,1)S(1)}, u32[]{:S(2)}, u32[]{:S(2)}) %collective-permute-start.10) | collective-permute-done | bytes 98336 | tf_op jit(solution)/shard_map/ppermute | solution.py:333
  30.7 0.1 collective-permute-start.11
  30.8 0.1 hold_weight.1.weight_ref
  30.9 0.0 copy-start
  31.0 0.0 copy-start.5
  31.0 4.4 %collective-permute-done.8.far_ref.refs_6_ = bf16[96,1024]{1,0:T(8,128)(2,1)S(1)} collective-permute-done((bf16[96,1024]{1,0:T(8,128)(2,1)S(1)}, bf16[96,1024]{1,0:T(8,128)(2,1)S(1)}, u32[]{:S(2)}, u32[]{:S(2)}) %collective-permute-start.8) | collective-permute-done | bytes 196640 | tf_op jit(solution)/shard_map/ppermute | solution.py:328
  35.4 0.8 %upstream.2.refs_0_.refs_2_ = f32[192,1024]{1,0:T(8,128)S(1)} custom-call(bf16[96,1024]{1,0:T(8,128)(2,1)S(1)} %cot_slots.2.near_ref.refs_5_, bf16[96,1024]{1,0:T(8,128)(2,1)S(1)} %collective-permute-done.8.far_ref.refs_6_, bf16[1024,1024]{1,0:T(8,128)(2,1)S(1)} %hold_weight.1.weight_ref), custom_call_target="tpu_custom_call" | custom-call | tf_op jit(solution)/shard_map/upstream/pallas_call | solution.py:26
  36.2 1.3 %collective-permute-done.11.far_ref.refs_1_ = bf16[96,1024]{1,0:T(8,128)(2,1)S(1)} collective-permute-done((bf16[96,1024]{1,0:T(8,128)(2,1)S(1)}, bf16[96,1024]{1,0:T(8,128)(2,1)S(1)}, u32[]{:S(2)}, u32[]{:S(2)}) %collective-permute-start.11) | collective-permute-done | bytes 196640 | tf_op jit(solution)/shard_map/ppermute | solution.py:328
  37.5 0.8 %upstream.3.refs_3_ = f32[192,1024]{1,0:T(8,128)S(1)} custom-call(bf16[96,1024]{1,0:T(8,128)(2,1)S(1)} %cot_slots.3.near_ref.refs_0_, bf16[96,1024]{1,0:T(8,128)(2,1)S(1)} %collective-permute-done.11.far_ref.refs_1_, bf16[1024,1024]{1,0:T(8,128)(2,1)S(1)} %hold_weight.1.weight_ref), custom_call_target="tpu_custom_call" | custom-call | tf_op jit(solution)/shard_map/upstream/pallas_call | solution.py:26
  38.4 2.0 %expert.2 = (bf16[96,1024]{1,0:T(8,128)(2,1)S(1)}, bf16[96,1024]{1,0:T(8,128)(2,1)S(1)}, bf16[192,1024]{1,0:T(8,128)(2,1)S(1)}, bf16[192,1024]{1,0:T(8,128)(2,1)S(1)}, bf16[192,1024]{1,0:T(8,128)(2,1)S(1)}) custom-call(s32[1]{0:T(128)} %bitcast.7.my_ref, f32[192,1024]{1,0:T(8,128)S(1)} %upstream.2.refs_0_.refs_2_, ...), custom_call_target="tpu_custom_call" | custom-call | tf_op jit(solution)/shard_map/expert/pallas_call | solution.py:26
  40.4 2.5 %collective-permute-start.16 = (bf16[96,1024]{1,0:T(8,128)(2,1)S(1)}, bf16[96,1024]{1,0:T(8,128)(2,1)S(1)}, u32[]{:S(2)}, u32[]{:S(2)}) collective-permute-start(bf16[96,1024]{1,0:T(8,128)(2,1)S(1)} %get-tuple-element.53), channel_id=1, source_target_pairs={{0,6},{1,7},{2,4},{3,5},{4,2},{5,3},{6,0},{7,1},{8,14},{9,15},{10,... | collective-permute-start | bytes 589832 | tf_op jit(solution)/shard_map/ppermute | solution.py:333
  42.9 2.0 %expert.3 = (bf16[96,1024]{1,0:T(8,128)(2,1)S(1)}, bf16[96,1024]{1,0:T(8,128)(2,1)S(1)}, bf16[192,1024]{1,0:T(8,128)(2,1)S(1)}, bf16[192,1024]{1,0:T(8,128)(2,1)S(1)}, bf16[192,1024]{1,0:T(8,128)(2,1)S(1)}) custom-call(s32[1]{0:T(128)} %bitcast.7.my_ref, bf16[96,1152]{1,0:T(8,128)(2,1)S(1)} %collective-permute-done.12.refs_0_, ...), custom_call_target="tpu_custom_call" | custom-call | tf_op jit(solution)/shard_map/expert/pallas_call | solution.py:26
  44.9 0.6 collective-permute-start.14
  45.5 0.5 collective-permute-start.15
  46.0 0.2 stack.1
  46.2 3.3 %fusion = f32[1024,1024]{1,0:T(8,128)} fusion(bf16[384,1024]{1,0:T(8,128)(2,1)S(1)} %get-tuple-element.60, bf16[384,1024]{1,0:T(8,128)(2,1)S(1)} %get-tuple-element.61), kind=kOutput, calls=%fused_computation.1 | convolution fusion | flops 805306368 | bytes 5767168 | tf_op jit(solution)/shard_map/dot_general | solution.py:417
  49.5 1.6 %collective-permute-done.14.refs_1_ = bf16[96,1024]{1,0:T(8,128)(2,1)S(1)} collective-permute-done((bf16[96,1024]{1,0:T(8,128)(2,1)S(1)}, bf16[96,1024]{1,0:T(8,128)(2,1)S(1)}, u32[]{:S(2)}, u32[]{:S(2)}) %collective-permute-start.14) | collective-permute-done | bytes 196640 | tf_op jit(solution)/shard_map/ppermute | solution.py:333
  51.1 0.2 collective-permute-done.15.refs_2_
  51.3 0.0 copy-start.9
  51.3 0.0 copy-start.10
  51.3 0.3 combine_other.1
  51.7 0.1 collective-permute-start.17
  51.7 1.5 %collective-permute-done.17.refs_4_ = bf16[128,1024]{1,0:T(8,128)(2,1)S(1)} collective-permute-done((bf16[128,1024]{1,0:T(8,128)(2,1)S(1)}, bf16[128,1024]{1,0:T(8,128)(2,1)S(1)}, u32[]{:S(2)}, u32[]{:S(2)}) %collective-permute-start.17) | collective-permute-done | bytes 262176 | tf_op jit(solution)/shard_map/ppermute | solution.py:337
  53.3 0.3 combine_own.1
  53.6 2.8 %collective-permute-start.18 = (bf16[32,1024]{1,0:T(8,128)(2,1)S(1)}, bf16[32,1024]{1,0:T(8,128)(2,1)S(1)}, u32[]{:S(2)}, u32[]{:S(2)}) collective-permute-start(bf16[32,1024]{1,0:T(8,128)(2,1)S(1)} %get-tuple-element.67), channel_id=1, source_target_pairs={{0,24},{8,16},{16,8},{24,0},{1,25},{9,17},{17,9},{25,1},{2,26},{10... | collective-permute-start | bytes 196616 | tf_op jit(solution)/shard_map/ppermute | solution.py:328
  56.4 1.7 %collective-permute-start.20 = (bf16[32,1024]{1,0:T(8,128)(2,1)S(1)}, bf16[32,1024]{1,0:T(8,128)(2,1)S(1)}, u32[]{:S(2)}, u32[]{:S(2)}) collective-permute-start(bf16[32,1024]{1,0:T(8,128)(2,1)S(1)} %get-tuple-element.69), channel_id=1, source_target_pairs={{0,16},{8,24},{16,0},{24,8},{1,17},{9,25},{17,1},{25,9},{2,18},{10... | collective-permute-start | bytes 196616 | tf_op jit(solution)/shard_map/ppermute | solution.py:328
  58.1 3.3 %convolution_bitcast_fusion = f32[1,1024,1024]{2,1,0:T(8,128)} fusion(bf16[384,1024]{1,0:T(8,128)(2,1)S(1)} %get-tuple-element.70, bf16[384,1024]{1,0:T(8,128)(2,1)S(1)} %get-tuple-element.71), kind=kOutput, calls=%fused_computation | convolution fusion | flops 805306368 | bytes 5767168 | tf_op jit(solution)/shard_map/dot_general | solution.py:418
  61.4 1.0 %collective-permute-done.19.refs_2_ = bf16[32,1024]{1,0:T(8,128)(2,1)S(1)} collective-permute-done((bf16[32,1024]{1,0:T(8,128)(2,1)S(1)}, bf16[32,1024]{1,0:T(8,128)(2,1)S(1)}, u32[]{:S(2)}, u32[]{:S(2)}) %collective-permute-start.19) | collective-permute-done | bytes 65568 | tf_op jit(solution)/shard_map/ppermute | solution.py:328
  62.5 1.6 %back.1 = bf16[128,1024]{1,0:T(8,128)(2,1)} custom-call(bf16[128,1024]{1,0:T(8,128)(2,1)S(1)} %bitcast.23, f32[1,1024]{1,0:T(1,128)S(1)} %bitcast.31, f32[1,1024]{1,0:T(1,128)S(1)} %bitcast.33, f32[32,1024]{1,0:T(8,128)S(1)} %copy-done.6, f32[32,128]{1,0:T(8,128)S(1)} %copy-done.8, bf16[32,1024]{1,0:T(8,128)(2,1)S(1)} %bitcast.26, ...), custom_call_target="tpu_custom_call" | custom-call | tf_op jit(solution)/shard_map/back/pallas_call | solution.py:26
  (35 shorter events, 0.1 us)
Async XLA Ops:
  0.6 30.2 %copy-start.1 = (bf16[1,1024,1024]{2,1,0:T(8,128)(2,1)S(1)}, bf16[1,1024,1024]{2,1,0:T(8,128)(2,1)}, u32[]{:S(2)}) copy-start(bf16[1,1024,1024]{2,1,0:T(8,128)(2,1)} %param.14) | copy-start | bytes 6291460
  3.4 14.4 %collective-permute-start.3 = (bf16[32,1152]{1,0:T(8,128)(2,1)}, bf16[32,1152]{1,0:T(8,128)(2,1)S(1)}, u32[]{:S(2)}, u32[]{:S(2)}) collective-permute-start(bf16[32,1152]{1,0:T(8,128)(2,1)} %get-tuple-element.40.refs_0_), channel_id=1, source_target_pairs={{0,24},{8,16},{16,8},{24,0},{1,25},{9,17},{17,9},{25,1},{2,26},{10... | collective-permute-start | bytes 221192 | tf_op jit(solution)/shard_map/ppermute | solution.py:328
  8.5 9.3 %collective-permute-start.2 = (bf16[32,1152]{1,0:T(8,128)(2,1)}, bf16[32,1152]{1,0:T(8,128)(2,1)S(1)}, u32[]{:S(2)}, u32[]{:S(2)}) collective-permute-start(bf16[32,1152]{1,0:T(8,128)(2,1)} %get-tuple-element.40.refs_0_), channel_id=1, source_target_pairs={{0,8},{8,0},{16,24},{24,16},{1,9},{9,1},{17,25},{25,17},{2,10},{10... | collective-permute-start | bytes 221192 | tf_op jit(solution)/shard_map/ppermute | solution.py:328
  8.5 9.3 %collective-permute-start.1 = (bf16[32,1152]{1,0:T(8,128)(2,1)}, bf16[32,1152]{1,0:T(8,128)(2,1)S(1)}, u32[]{:S(2)}, u32[]{:S(2)}) collective-permute-start(bf16[32,1152]{1,0:T(8,128)(2,1)} %get-tuple-element.40.refs_0_), channel_id=1, source_target_pairs={{0,16},{8,24},{16,0},{24,8},{1,17},{9,25},{17,1},{25,9},{2,18},{10... | collective-permute-start | bytes 221192 | tf_op jit(solution)/shard_map/ppermute | solution.py:328
  9.2 8.6 %collective-permute-start = (bf16[32,1024]{1,0:T(8,128)(2,1)}, bf16[32,1024]{1,0:T(8,128)(2,1)S(1)}, u32[]{:S(2)}, u32[]{:S(2)}) collective-permute-start(bf16[32,1024]{1,0:T(8,128)(2,1)} %bitcast.24), channel_id=1, source_target_pairs={{0,16},{8,24},{16,0},{24,8},{1,17},{9,25},{17,1},{25,9},{2,18},{10... | collective-permute-start | bytes 196616 | tf_op jit(solution)/shard_map/ppermute | solution.py:328
  11.5 0.9 %copy-start.3 = (bf16[1,32,1024]{2,1,0:T(8,128)(2,1)S(1)}, bf16[1,32,1024]{2,1,0:T(8,128)(2,1)}, u32[]{:S(2)}) copy-start(bf16[1,32,1024]{2,1,0:T(8,128)(2,1)} %param.15) | copy-start | bytes 196612
  12.3 0.9 %copy-start.7 = (bf16[32,1152]{1,0:T(8,128)(2,1)S(1)}, bf16[32,1152]{1,0:T(8,128)(2,1)}, u32[]{:S(2)}) copy-start(bf16[32,1152]{1,0:T(8,128)(2,1)} %get-tuple-element.40.refs_0_) | copy-start | bytes 221188
  17.9 1.8 %collective-permute-start.5 = (bf16[128,1152]{1,0:T(8,128)(2,1)S(1)}, bf16[128,1152]{1,0:T(8,128)(2,1)S(1)}, u32[]{:S(2)}, u32[]{:S(2)}) collective-permute-start(bf16[128,1152]{1,0:T(8,128)(2,1)S(1)} %token_near.1.token_ref), channel_id=1, source_target_pairs={{0,1},{1,0},{2,3},{3,2},{4,5},{5,4},{6,7},{7,6},{8,9},{9,8},{10,11... | collective-permute-start | bytes 884744 | tf_op jit(solution)/shard_map/ppermute | solution.py:337
  18.0 1.8 %collective-permute-start.4 = (bf16[64,1024]{1,0:T(8,128)(2,1)S(1)}, bf16[64,1024]{1,0:T(8,128)(2,1)S(1)}, u32[]{:S(2)}, u32[]{:S(2)}) collective-permute-start(bf16[64,1024]{1,0:T(8,128)(2,1)S(1)} %cot_near.1.refs_0_.cot_ref), channel_id=1, source_target_pairs={{0,1},{1,0},{2,3},{3,2},{4,5},{5,4},{6,7},{7,6},{8,9},{9,8},{10,11... | collective-permute-start | bytes 393224 | tf_op jit(solution)/shard_map/ppermute | solution.py:337
  20.9 6.5 %collective-permute-start.6 = (bf16[48,1024]{1,0:T(8,128)(2,1)S(1)}, bf16[48,1024]{1,0:T(8,128)(2,1)S(1)}, u32[]{:S(2)}, u32[]{:S(2)}) collective-permute-start(bf16[48,1024]{1,0:T(8,128)(2,1)S(1)} %get-tuple-element.42), channel_id=1, source_target_pairs={{0,4},{1,5},{2,6},{3,7},{4,0},{5,1},{6,2},{7,3},{8,12},{9,13},{10,... | collective-permute-start | bytes 294920 | tf_op jit(solution)/shard_map/ppermute | solution.py:333
  22.5 5.6 %collective-permute-start.7 = (bf16[48,1024]{1,0:T(8,128)(2,1)S(1)}, bf16[48,1024]{1,0:T(8,128)(2,1)S(1)}, u32[]{:S(2)}, u32[]{:S(2)}) collective-permute-start(bf16[48,1024]{1,0:T(8,128)(2,1)S(1)} %get-tuple-element.43), channel_id=1, source_target_pairs={{0,2},{1,3},{2,0},{3,1},{4,6},{5,7},{6,4},{7,5},{8,10},{9,11},{10,... | collective-permute-start | bytes 294920 | tf_op jit(solution)/shard_map/ppermute | solution.py:333
  24.0 6.7 %collective-permute-start.10 = (bf16[48,1024]{1,0:T(8,128)(2,1)S(1)}, bf16[48,1024]{1,0:T(8,128)(2,1)S(1)}, u32[]{:S(2)}, u32[]{:S(2)}) collective-permute-start(bf16[48,1024]{1,0:T(8,128)(2,1)S(1)} %get-tuple-element.47), channel_id=1, source_target_pairs={{0,6},{1,7},{2,4},{3,5},{4,2},{5,3},{6,0},{7,1},{8,14},{9,15},{10,... | collective-permute-start | bytes 294920 | tf_op jit(solution)/shard_map/ppermute | solution.py:333
  24.4 13.9 %collective-permute-start.9 = (bf16[96,1152]{1,0:T(8,128)(2,1)S(1)}, bf16[96,1152]{1,0:T(8,128)(2,1)S(1)}, u32[]{:S(2)}, u32[]{:S(2)}) collective-permute-start(bf16[96,1152]{1,0:T(8,128)(2,1)S(1)} %get-tuple-element.45), channel_id=1, source_target_pairs={{0,6},{1,7},{2,4},{3,5},{4,2},{5,3},{6,0},{7,1},{8,14},{9,15},{10,... | collective-permute-start | bytes 663560 | tf_op jit(solution)/shard_map/ppermute | solution.py:333
  26.9 16.0 %collective-permute-start.12 = (bf16[96,1152]{1,0:T(8,128)(2,1)S(1)}, bf16[96,1152]{1,0:T(8,128)(2,1)S(1)}, u32[]{:S(2)}, u32[]{:S(2)}) collective-permute-start(bf16[96,1152]{1,0:T(8,128)(2,1)S(1)} %get-tuple-element.49), channel_id=1, source_target_pairs={{0,4},{1,5},{2,6},{3,7},{4,0},{5,1},{6,2},{7,3},{8,12},{9,13},{10,... | collective-permute-start | bytes 663560 | tf_op jit(solution)/shard_map/ppermute | solution.py:333
  27.4 15.5 %collective-permute-start.13 = (bf16[96,1152]{1,0:T(8,128)(2,1)S(1)}, bf16[96,1152]{1,0:T(8,128)(2,1)S(1)}, u32[]{:S(2)}, u32[]{:S(2)}) collective-permute-start(bf16[96,1152]{1,0:T(8,128)(2,1)S(1)} %get-tuple-element.50), channel_id=1, source_target_pairs={{0,2},{1,3},{2,0},{3,1},{4,6},{5,7},{6,4},{7,5},{8,10},{9,11},{10,... | collective-permute-start | bytes 663560 | tf_op jit(solution)/shard_map/ppermute | solution.py:333
  28.1 7.3 %collective-permute-start.8 = (bf16[96,1024]{1,0:T(8,128)(2,1)S(1)}, bf16[96,1024]{1,0:T(8,128)(2,1)S(1)}, u32[]{:S(2)}, u32[]{:S(2)}) collective-permute-start(bf16[96,1024]{1,0:T(8,128)(2,1)S(1)} %cot_slots.2.near_ref.refs_5_), channel_id=1, source_target_pairs={{0,8},{8,0},{16,24},{24,16},{1,9},{9,1},{17,25},{25,17},{2,10},{10... | collective-permute-start | bytes 589832 | tf_op jit(solution)/shard_map/ppermute | solution.py:328
  30.7 6.8 %collective-permute-start.11 = (bf16[96,1024]{1,0:T(8,128)(2,1)S(1)}, bf16[96,1024]{1,0:T(8,128)(2,1)S(1)}, u32[]{:S(2)}, u32[]{:S(2)}) collective-permute-start(bf16[96,1024]{1,0:T(8,128)(2,1)S(1)} %cot_slots.3.near_ref.refs_0_), channel_id=1, source_target_pairs={{0,8},{8,0},{16,24},{24,16},{1,9},{9,1},{17,25},{25,17},{2,10},{10... | collective-permute-start | bytes 589832 | tf_op jit(solution)/shard_map/ppermute | solution.py:328
  30.9 7.4 %copy-start = (bf16[1,1024,1024]{2,1,0:T(8,128)(2,1)S(1)}, bf16[1,1024,1024]{2,1,0:T(8,128)(2,1)}, u32[]{:S(2)}) copy-start(bf16[1,1024,1024]{2,1,0:T(8,128)(2,1)} %param.13) | copy-start | bytes 6291460
  31.0 7.4 %copy-start.5 = (bf16[1024,8]{0,1:T(8,128)(2,1)S(1)}, bf16[1024,8]{0,1:T(8,128)(2,1)}, u32[]{:S(2)}) copy-start(bf16[1024,8]{0,1:T(8,128)(2,1)} %param.11) | copy-start | bytes 49156
  40.4 9.1 %collective-permute-start.16 = (bf16[96,1024]{1,0:T(8,128)(2,1)S(1)}, bf16[96,1024]{1,0:T(8,128)(2,1)S(1)}, u32[]{:S(2)}, u32[]{:S(2)}) collective-permute-start(bf16[96,1024]{1,0:T(8,128)(2,1)S(1)} %get-tuple-element.53), channel_id=1, source_target_pairs={{0,6},{1,7},{2,4},{3,5},{4,2},{5,3},{6,0},{7,1},{8,14},{9,15},{10,... | collective-permute-start | bytes 589832 | tf_op jit(solution)/shard_map/ppermute | solution.py:333
  44.9 6.2 %collective-permute-start.14 = (bf16[96,1024]{1,0:T(8,128)(2,1)S(1)}, bf16[96,1024]{1,0:T(8,128)(2,1)S(1)}, u32[]{:S(2)}, u32[]{:S(2)}) collective-permute-start(bf16[96,1024]{1,0:T(8,128)(2,1)S(1)} %get-tuple-element.51), channel_id=1, source_target_pairs={{0,2},{1,3},{2,0},{3,1},{4,6},{5,7},{6,4},{7,5},{8,10},{9,11},{10,... | collective-permute-start | bytes 589832 | tf_op jit(solution)/shard_map/ppermute | solution.py:333
  45.5 5.8 %collective-permute-start.15 = (bf16[96,1024]{1,0:T(8,128)(2,1)S(1)}, bf16[96,1024]{1,0:T(8,128)(2,1)S(1)}, u32[]{:S(2)}, u32[]{:S(2)}) collective-permute-start(bf16[96,1024]{1,0:T(8,128)(2,1)S(1)} %get-tuple-element.52), channel_id=1, source_target_pairs={{0,4},{1,5},{2,6},{3,7},{4,0},{5,1},{6,2},{7,3},{8,12},{9,13},{10,... | collective-permute-start | bytes 589832 | tf_op jit(solution)/shard_map/ppermute | solution.py:333
  51.3 11.1 %copy-start.2 = (bf16[1,128,1024]{2,1,0:T(8,128)(2,1)S(1)}, bf16[1,128,1024]{2,1,0:T(8,128)(2,1)}, u32[]{:S(2)}) copy-start(bf16[1,128,1024]{2,1,0:T(8,128)(2,1)} %param.8) | copy-start | bytes 786436
  51.3 11.1 %copy-start.4 = (bf16[1,32,1024]{2,1,0:T(8,128)(2,1)S(1)}, bf16[1,32,1024]{2,1,0:T(8,128)(2,1)}, u32[]{:S(2)}) copy-start(bf16[1,32,1024]{2,1,0:T(8,128)(2,1)} %param.15) | copy-start | bytes 196612
  51.3 11.1 %copy-start.6 = (f32[32,1024]{1,0:T(8,128)S(1)}, f32[32,1024]{1,0:T(8,128)}, u32[]{:S(2)}) copy-start(f32[32,1024]{1,0:T(8,128)} %get-tuple-element.38.tok_ref) | copy-start | bytes 393220
  51.3 11.1 %copy-start.8 = (f32[32,128]{1,0:T(8,128)S(1)}, f32[32,128]{1,0:T(8,128)}, u32[]{:S(2)}) copy-start(f32[32,128]{1,0:T(8,128)} %get-tuple-element.39.keep_ref) | copy-start | bytes 49156
  51.3 11.1 %copy-start.9 = (f32[1024]{0:T(1024)S(1)}, f32[1024]{0:T(1024)}, u32[]{:S(2)}) copy-start(f32[1024]{0:T(1024)} %param.9) | copy-start | bytes 12292
  51.3 11.1 %copy-start.10 = (f32[1024]{0:T(1024)S(1)}, f32[1024]{0:T(1024)}, u32[]{:S(2)}) copy-start(f32[1024]{0:T(1024)} %param.10) | copy-start | bytes 12292
  51.7 1.6 %collective-permute-start.17 = (bf16[128,1024]{1,0:T(8,128)(2,1)S(1)}, bf16[128,1024]{1,0:T(8,128)(2,1)S(1)}, u32[]{:S(2)}, u32[]{:S(2)}) collective-permute-start(bf16[128,1024]{1,0:T(8,128)(2,1)S(1)} %combine_other.1), channel_id=1, source_target_pairs={{0,1},{1,0},{2,3},{3,2},{4,5},{5,4},{6,7},{7,6},{8,9},{9,8},{10,11... | collective-permute-start | bytes 786440 | tf_op jit(solution)/shard_map/ppermute | solution.py:337
  53.6 7.8 %collective-permute-start.18 = (bf16[32,1024]{1,0:T(8,128)(2,1)S(1)}, bf16[32,1024]{1,0:T(8,128)(2,1)S(1)}, u32[]{:S(2)}, u32[]{:S(2)}) collective-permute-start(bf16[32,1024]{1,0:T(8,128)(2,1)S(1)} %get-tuple-element.67), channel_id=1, source_target_pairs={{0,24},{8,16},{16,8},{24,0},{1,25},{9,17},{17,9},{25,1},{2,26},{10... | collective-permute-start | bytes 196616 | tf_op jit(solution)/shard_map/ppermute | solution.py:328
  56.4 6.0 %collective-permute-start.19 = (bf16[32,1024]{1,0:T(8,128)(2,1)S(1)}, bf16[32,1024]{1,0:T(8,128)(2,1)S(1)}, u32[]{:S(2)}, u32[]{:S(2)}) collective-permute-start(bf16[32,1024]{1,0:T(8,128)(2,1)S(1)} %get-tuple-element.68), channel_id=1, source_target_pairs={{0,8},{8,0},{16,24},{24,16},{1,9},{9,1},{17,25},{25,17},{2,10},{10... | collective-permute-start | bytes 196616 | tf_op jit(solution)/shard_map/ppermute | solution.py:328
  56.4 6.0 %collective-permute-start.20 = (bf16[32,1024]{1,0:T(8,128)(2,1)S(1)}, bf16[32,1024]{1,0:T(8,128)(2,1)S(1)}, u32[]{:S(2)}, u32[]{:S(2)}) collective-permute-start(bf16[32,1024]{1,0:T(8,128)(2,1)S(1)} %get-tuple-element.69), channel_id=1, source_target_pairs={{0,16},{8,24},{16,0},{24,8},{1,17},{9,25},{17,1},{25,9},{2,18},{10... | collective-permute-start | bytes 196616 | tf_op jit(solution)/shard_map/ppermute | solution.py:328

commit v5 on v4

--- a/solution.py
+++ b/solution.py
@@ -70,32 +70,39 @@
     return shares
 
 
-def front_kernel(*refs):
-    far, outs, near, logit, arrived = refs[:5], refs[5:8], refs[8:13], refs[13], refs[14]
-    copies = [pltpu.make_async_copy(a, b, arrived.at[i]) for i, (a, b) in enumerate(zip(far, near))]
-    for copy in copies:
-        copy.start()
-    embed_ref, score_ref, gain_ref, router_ref, routes_ref = near
-    pay_ref, tok_ref, keep_ref = outs
-    for copy in copies:
-        copy.wait()
-    count, width = tok_ref.shape
-    experts = router_ref.shape[0]
-    values = quartet_values(embed_ref[...], count)
-    shares = quartet_scores(values, score_ref[...])
+def pooled(values, weight):
+    shares = quartet_scores(values, weight)
     whole = 0.25 * (shares[0][2] + shares[1][2] + shares[2][2] + shares[3][2])
     coefs = []
     for q in range(4):
         pair = 0.5 * (shares[q][1] + shares[q ^ 1][1])
         coefs.append(0.25 * (shares[q][0] + pair + whole))
     tokens = coefs[0] * values[0] + coefs[1] * values[1] + coefs[2] * values[2] + coefs[3] * values[3]
-    tok_ref[...] = tokens
     scale = lax.rsqrt(jnp.mean(tokens * tokens, axis=1, keepdims=True) + 1e-06)
+    return shares, coefs, tokens, scale
+
+
+def front_kernel(*refs):
+    far, pay_ref, near, logit, arrived = refs[:5], refs[5], refs[6:11], refs[11], refs[12]
+    copies = [pltpu.make_async_copy(a, b, arrived.at[i]) for i, (a, b) in enumerate(zip(far, near))]
+    for copy in copies:
+        copy.start()
+    embed_ref, score_ref, gain_ref, router_ref, routes_ref = near
+    for copy in copies:
+        copy.wait()
+    count = pay_ref.shape[0]
+    experts, width = router_ref.shape
+    _, _, tokens, scale = pooled(quartet_values(embed_ref[...], count), score_ref[...])
     normed = tokens * scale * gain_ref[...]
+    high = normed.astype(BF)
+    rest = normed - high.astype(F32)
+    middle = rest.astype(BF)
+    low = (rest - middle.astype(F32)).astype(BF)
+    products = lax.dot_general(
+        jnp.concatenate([high, middle, low], axis=0), router_ref[...], COLS, preferred_element_type=F32
+    )
     logit[...] = jnp.zeros_like(logit)
-    logit[:, :experts] = lax.dot_general(
-        normed, router_ref[...].astype(F32), COLS, precision=HIGHEST, preferred_element_type=F32
-    )
+    logit[:, :experts] = products[:count, :] + (products[count : 2 * count, :] + products[2 * count :, :])
     logits = logit[...]
     sigmoid = 1.0 / (1.0 + jnp.exp(-logits))
     rest = 1.0 / (1.0 + jnp.exp(logits))
@@ -110,14 +117,24 @@
     for mask, sig, other in zip(masks, picked, others):
         value = jnp.where(group == 0, 1.0, jnp.where(group == 1, other, jnp.where(group == 2, sig / total, 0.0)))
         tail = tail + mask * value
-    pay_ref[:, :width] = normed.astype(BF)
+    pay_ref[:, :width] = high
     pay_ref[:, width:] = tail.astype(BF)
+
+
+def keep_kernel(embed_ref, score_ref, tok_ref, keep_ref):
+    count = tok_ref.shape[0]
+    shares, coefs, tokens, scale = pooled(quartet_values(embed_ref[...], count), score_ref[...])
+    tok_ref[...] = tokens
+    columns = coefs + [s for share in shares for s in share] + [scale]
     lane = lax.broadcasted_iota(jnp.int32, keep_ref.shape, 1)
-    columns = coefs + [s for share in shares for s in share] + [scale]
     kept = jnp.zeros(keep_ref.shape, F32)
     for i, column in enumerate(columns):
         kept = jnp.where(lane == i, column, kept)
     keep_ref[...] = kept
+
+
+def transpose_kernel(in_ref, out_ref):
+    out_ref[...] = in_ref[...].T
 
 
 def gather_kernel(skipped, *refs):
@@ -185,38 +202,44 @@
     return jnp.concatenate([r[d * share : (d + 1) * share, :] for d in range(owners) for r in (near, far)], axis=0)
 
 
-def upstream_kernel(owners, near_ref, far_ref, weight_ref, out_ref):
+def upstream_kernel(owners, waits, *refs):
+    near_ref, far_ref, weight_ref, out_ref = refs[waits:]
     rows = jnp.concatenate([near_ref[...], far_ref[...]], axis=0)
-    upstream = lax.dot_general(rows, weight_ref[...], COLS, preferred_element_type=F32)
+    upstream = jnp.dot(rows, weight_ref[...], preferred_element_type=F32)
     half = near_ref.shape[0]
     out_ref[...] = interleave(upstream[:half, :], upstream[half:, :], owners)
 
 
-def expert_kernel(chunks, tile, waits, my_ref, *refs):
+def hidden_kernel(chunks, tile, waits, *refs):
     refs = refs[waits:]
-    ins, refs = refs[:chunks], refs[chunks:]
-    upstream_ref, weight_ref, router_ref = refs[:3]
-    outs, (rows_ref, hidden_ref, grad_ref) = refs[3 : 3 + chunks], refs[3 + chunks :]
-    slots, width = rows_ref.shape
-    experts = router_ref.shape[0]
-    rows = slots // chunks
+    ins, (weight_ref, rows_ref, tail_ref, hidden_ref, slope_ref) = refs[:chunks], refs[chunks:]
+    width = rows_ref.shape[1]
     token_rows = jnp.concatenate([r[:, :width] for r in ins], axis=0)
     rows_ref[...] = token_rows
-    terms = jnp.zeros((slots, LANES), F32)
+    tail_ref[...] = jnp.concatenate([r[:, width:] for r in ins], axis=0)
     for f in range(weight_ref.shape[1] // tile):
         part = slice(f * tile, (f + 1) * tile)
         preact = jnp.dot(token_rows, weight_ref[:, part], preferred_element_type=F32)
-        upstream = upstream_ref[:, part]
         normal_cdf = 0.5 * (1.0 + lax.erf(preact * SQRT_HALF))
         normal_pdf = INV_ROOT_TWO_PI * jnp.exp(-0.5 * preact * preact)
-        hidden = preact * normal_cdf
-        products = hidden * upstream
-        for k in range(tile // LANES):
-            terms = terms + products[:, k * LANES : (k + 1) * LANES]
-        grad_ref[:, part] = (upstream * (normal_cdf + preact * normal_pdf)).astype(BF)
-        hidden_ref[:, part] = hidden.astype(BF)
+        hidden_ref[:, part] = (preact * normal_cdf).astype(BF)
+        slope_ref[:, part] = normal_cdf + preact * normal_pdf
+
+
+def grad_kernel(chunks, waits, my_ref, *refs):
+    hidden_ref, slope_ref, tail_ref, upstream_ref, weight_ref, router_ref = refs[waits : waits + 6]
+    outs, grad_ref = refs[waits + 6 : -1], refs[-1]
+    slots = hidden_ref.shape[0]
+    experts, width = router_ref.shape
+    rows = slots // chunks
+    terms = jnp.zeros((slots, LANES), F32)
+    for k in range(hidden_ref.shape[1] // LANES):
+        part = slice(k * LANES, (k + 1) * LANES)
+        upstream = upstream_ref[:, part]
+        terms = terms + hidden_ref[:, part].astype(F32) * upstream
+        grad_ref[:, part] = (upstream * slope_ref[:, part]).astype(BF)
     term = jnp.sum(terms, axis=1, keepdims=True)
-    tail = jnp.concatenate([r[:, width:] for r in ins], axis=0).astype(F32)
+    tail = tail_ref[...].astype(F32)
     lane = lax.broadcasted_iota(jnp.int32, (slots, LANES), 1)
     mine = lane % GROUP == my_ref[0]
     other_gate = jnp.sum(jnp.where((lane // GROUP == 2) & ~mine, tail, 0.0), axis=1, keepdims=True)
@@ -227,7 +250,7 @@
     blank = jnp.zeros((GROUP, width), F32)
     padded = [router] if experts == GROUP else [router, jnp.zeros((GROUP - experts, width), F32)]
     router = jnp.concatenate([blank, *padded, blank, blank], axis=0).astype(BF)
-    back = lax.dot_general(grad_ref[...], weight_ref[...], COLS, preferred_element_type=F32)
+    back = jnp.dot(grad_ref[...], weight_ref[...], preferred_element_type=F32)
     back = back + jnp.dot(high, router, preferred_element_type=F32) + jnp.dot(low, router, preferred_element_type=F32)
     back = back.astype(BF)
     for m, out in enumerate(outs):
@@ -340,10 +363,10 @@
     places = list(range(0, pieces, 2)) + list(range(1, pieces, 2))
     front_args = (embed, score_row, gain_row, router_t, routes_t)
     cot_far = [over_seq(cot, k) for k in places[1:half]]
-    pay, tok, keep = call(
+    pay = call(
         front_kernel,
         "front",
-        (shape(count, full), shape(count, width, dtype=F32), shape(count, LANES, dtype=F32)),
+        shape(count, full),
         front_args,
         us=2.0,
         scratch=[pltpu.VMEM(a.shape, a.dtype) for a in front_args]
@@ -351,12 +374,20 @@
         limit=56,
         held=False,
     )
+    tok, keep = call(
+        keep_kernel,
+        "keep",
+        (shape(count, width, dtype=F32), shape(count, LANES, dtype=F32)),
+        (embed, score_row),
+        us=2.0,
+    )
     held_cot = call(functools.partial(gather_kernel, 0), "hold_cot", shape(count, width), (cot,), us=1.0)
     cot_near = call(
         functools.partial(gather_kernel, 0), "cot_near", shape(half * count, width), (held_cot, *cot_far), us=5.0
     )
     held = call(functools.partial(gather_kernel, 0), "hold_own", shape(count, full), (pay,), us=1.0)
-    held_out = call(functools.partial(gather_kernel, 0), "hold_weight", shape(hidden, width), (weight_out,), us=2.0)
+    in_across = call(transpose_kernel, "across", shape(hidden, width), (weight_in,), us=2.0, limit=16)
+    out_across = call(transpose_kernel, "across", shape(width, hidden), (weight_out,), us=2.0, limit=16)
     token_near = call(
         functools.partial(gather_kernel, 1),
         "token_near",
@@ -383,26 +414,40 @@
         )
         near.append(cot_a)
         far.append(over_seq(cot_a, 1))
+    hiddens, upstream = [], []
     for cot_a, cot_b in zip(near, far):
         upstream.append(
             call(
-                functools.partial(upstream_kernel, chunks),
+                functools.partial(upstream_kernel, chunks, 0),
                 "upstream",
                 shape(part, hidden, dtype=F32),
-                (cot_a, cot_b, held_out),
+                (cot_a, cot_b, out_across),
                 limit=16,
+            )
+        )
+    for g, group in enumerate(groups):
+        waits = upstream[1:] if g else []
+        hiddens.append(
+            call(
+                functools.partial(hidden_kernel, len(group), tile, len(waits)),
+                "hidden",
+                (shape(part, width), shape(part, LANES), shape(part, hidden), shape(part, hidden, dtype=F32)),
+                (*waits, *[token_chunks[m] for m in group], weight_in),
+                limit=16,
+                us=1.0,
             )
         )
     stacked, back_rows = [], [None] * chunks
     for g, group in enumerate(groups):
         waits = upstream[1:] if g == 0 else []
-        *outs, token_rows, hidden_rows, hidden_grad = call(
-            functools.partial(expert_kernel, len(group), tile, len(waits)),
-            "expert",
-            [shape(rows, width)] * len(group) + [shape(part, width), shape(part, hidden), shape(part, hidden)],
-            (my, *waits, *[token_chunks[m] for m in group], upstream[g], weight_in, router_t),
+        token_rows, tail, hidden_rows, slope = hiddens[g]
+        *outs, hidden_grad = call(
+            functools.partial(grad_kernel, len(group), len(waits)),
+            "grads",
+            [shape(rows, width)] * len(group) + [shape(part, hidden)],
+            (my, *waits, hidden_rows, slope, tail, upstream[g], in_across, router_t),
             scalars=1,
-            limit=24,
+            limit=16,
         )
         for m, out in zip(group, outs):
             back_rows[m] = out

time: 64.3 us -> 62.8 us (0.977)
  waiting for transfers between devices: 18.5 us -> 16.6 us
    ppermute x9, waiting for transfers between devices: 11.3 us -> 6.34 us  [over_seq(): return lax.ppermute(value, 'seq', [(i, i ^ k) for i in range(pieces)])]
    ppermute x9, waiting for transfers between devices: 4.42 us -> 7.98 us  [over_exp(): lax.ppermute(values[m], 'exp', [(i, i ^ m * step) for i in range(owners)])]
    pallas_call x17 -> x21, Pallas kernels: 12.3 us -> 12.7 us  [call(): pl.pallas_call(body, name=name, out_shape=outs, in_specs=[smem] * scalars...]
    unnamed x22 -> x18, local copies, waits for them, and re-layouts: 1.8 us -> 1.79 us
  transfers between devices with their start and end apart: 21 -> 21, of which waited for: 10 -> 10; matrix products, arithmetic and copies ran while one was open for 10% -> 11% of each run, Pallas kernels for 9% -> 11%
where the time goes in v5:
time: 62.8 us; the launch traced here: 62.6 us
  starting transfers between devices  24 us (38%)
  waiting for transfers between devices  16.6 us (26%)
  Pallas kernels  12.7 us (20%)
  matrix products  6.61 us (11%)
  local copies, waits for them, and re-layouts  1.79 us (3%)
  between operations  0.88 us (1%)
    pallas_call x21, Pallas kernels, call(): pl.pallas_call(body, name=name, out_shape=outs, in_specs=[smem] * scalars...  12.7 us
    ppermute x9, starting transfers between devices, over_seq(): return lax.ppermute(value, 'seq', [(i, i ^ k) for i in range(pieces)])  12.7 us
    ppermute x9, starting transfers between devices, over_exp(): lax.ppermute(values[m], 'exp', [(i, i ^ m * step) for i in range(owners)])  10.7 us
    ppermute x9, waiting for transfers between devices, over_exp(): lax.ppermute(values[m], 'exp', [(i, i ^ m * step) for i in range(owners)])  7.98 us
    ppermute x9, waiting for transfers between devices, over_seq(): return lax.ppermute(value, 'seq', [(i, i ^ k) for i in range(pieces)])  6.34 us
    dot_general x1, matrix products, per_device(): lax.dot_general(hidden_rows, cot_slots, ROWS_T, preferred_element_type=F32)  3.31 us
    dot_general x1, matrix products, per_device(): lax.dot_general(token_slots, hidden_grad, ROWS_T, preferred_element_type=...  3.3 us
    ppermute x3, waiting for transfers between devices, over_cores(): return lax.ppermute(value, 'exp', [(i, i ^ 1) for i in range(owners)])  2.28 us
  transfers between devices with their start and end apart: 21, of which 10 were waited for; matrix products, arithmetic and copies ran while one was open for 11% of the time, Pallas kernels for 11%

profile of v5, /device:TPU:0, one launch (start us, length us, event | category | flops | bytes accessed | tf_op | source)
XLA Modules:
  0.0 62.6 jit_solution(8917159118544295738)
XLA Ops:
  0.6 2.6 %front.1.refs_0_ = bf16[32,1152]{1,0:T(8,128)(2,1)} custom-call(bf16[128,1024]{1,0:T(8,128)(2,1)} %bitcast.22, f32[1,1024]{1,0:T(1,128)} %bitcast.32, f32[1,1024]{1,0:T(1,128)} %bitcast.35, bf16[8,1024]{1,0:T(8,128)(2,1)} %bitcast.29, s32[2,32]{1,0:T(2,128)} %bitcast.39), custom_call_target="tpu_custom_call" | custom-call | bytes 6000000 | tf_op jit(solution)/shard_map/front/pallas_call | solution.py:26
  3.3 5.1 %collective-permute-start.3 = (bf16[32,1152]{1,0:T(8,128)(2,1)}, bf16[32,1152]{1,0:T(8,128)(2,1)S(1)}, u32[]{:S(2)}, u32[]{:S(2)}) collective-permute-start(bf16[32,1152]{1,0:T(8,128)(2,1)} %front.1.refs_0_), channel_id=1, source_target_pairs={{0,24},{8,16},{16,8},{24,0},{1,25},{9,17},{17,9},{25,1},{2,26},{10... | collective-permute-start | bytes 221192 | tf_op jit(solution)/shard_map/ppermute | solution.py:351
  8.4 0.6 %collective-permute-start.1 = (bf16[32,1152]{1,0:T(8,128)(2,1)}, bf16[32,1152]{1,0:T(8,128)(2,1)S(1)}, u32[]{:S(2)}, u32[]{:S(2)}) collective-permute-start(bf16[32,1152]{1,0:T(8,128)(2,1)} %front.1.refs_0_), channel_id=1, source_target_pairs={{0,16},{8,24},{16,0},{24,8},{1,17},{9,25},{17,1},{25,9},{2,18},{10... | collective-permute-start | bytes 221192 | tf_op jit(solution)/shard_map/ppermute | solution.py:351
  9.0 2.3 %collective-permute-start = (bf16[32,1024]{1,0:T(8,128)(2,1)}, bf16[32,1024]{1,0:T(8,128)(2,1)S(1)}, u32[]{:S(2)}, u32[]{:S(2)}) collective-permute-start(bf16[32,1024]{1,0:T(8,128)(2,1)} %bitcast.26), channel_id=1, source_target_pairs={{0,16},{8,24},{16,0},{24,8},{1,17},{9,25},{17,1},{25,9},{2,18},{10... | collective-permute-start | bytes 196616 | tf_op jit(solution)/shard_map/ppermute | solution.py:351
  11.3 0.9 %copy-done.4 = bf16[1,32,1024]{2,1,0:T(8,128)(2,1)S(1)} copy-done((bf16[1,32,1024]{2,1,0:T(8,128)(2,1)S(1)}, bf16[1,32,1024]{2,1,0:T(8,128)(2,1)}, u32[]{:S(2)}) %copy-start.4) | copy-done | bytes 65560
  12.2 0.9 %copy-done.3 = bf16[32,1152]{1,0:T(8,128)(2,1)S(1)} copy-done((bf16[32,1152]{1,0:T(8,128)(2,1)S(1)}, bf16[32,1152]{1,0:T(8,128)(2,1)}, u32[]{:S(2)}) %copy-start.3) | copy-done | bytes 73752
  13.1 4.6 %collective-permute-done.refs_1_ = bf16[32,1024]{1,0:T(8,128)(2,1)S(1)} collective-permute-done((bf16[32,1024]{1,0:T(8,128)(2,1)}, bf16[32,1024]{1,0:T(8,128)(2,1)S(1)}, u32[]{:S(2)}, u32[]{:S(2)}) %collective-permute-start) | collective-permute-done | bytes 65568 | tf_op jit(solution)/shard_map/ppermute | solution.py:351
  17.8 0.1 collective-permute-start.5
  17.8 0.5 collective-permute-start.4
  18.3 1.3 %collective-permute-done.4.other_cot_ref = bf16[64,1024]{1,0:T(8,128)(2,1)S(1)} collective-permute-done((bf16[64,1024]{1,0:T(8,128)(2,1)S(1)}, bf16[64,1024]{1,0:T(8,128)(2,1)S(1)}, u32[]{:S(2)}, u32[]{:S(2)}) %collective-permute-start.4) | collective-permute-done | bytes 131104 | tf_op jit(solution)/shard_map/ppermute | solution.py:360
  19.6 1.1 %pick.1 = (bf16[48,1024]{1,0:T(8,128)(2,1)S(1)}, bf16[48,1024]{1,0:T(8,128)(2,1)S(1)}, bf16[48,1024]{1,0:T(8,128)(2,1)S(1)}, bf16[48,1024]{1,0:T(8,128)(2,1)S(1)...) custom-call(s32[1]{0:T(128)} %bitcast.4.my_ref, ...), custom_call_target="tpu_custom_call" | custom-call | tf_op jit(solution)/shard_map/pick/pallas_call | solution.py:26
  20.7 1.6 %collective-permute-start.6 = (bf16[48,1024]{1,0:T(8,128)(2,1)S(1)}, bf16[48,1024]{1,0:T(8,128)(2,1)S(1)}, u32[]{:S(2)}, u32[]{:S(2)}) collective-permute-start(bf16[48,1024]{1,0:T(8,128)(2,1)S(1)} %get-tuple-element.44), channel_id=1, source_target_pairs={{0,4},{1,5},{2,6},{3,7},{4,0},{5,1},{6,2},{7,3},{8,12},{9,13},{10,... | collective-permute-start | bytes 294920 | tf_op jit(solution)/shard_map/ppermute | solution.py:356
  22.3 1.5 %collective-permute-start.7 = (bf16[48,1024]{1,0:T(8,128)(2,1)S(1)}, bf16[48,1024]{1,0:T(8,128)(2,1)S(1)}, u32[]{:S(2)}, u32[]{:S(2)}) collective-permute-start(bf16[48,1024]{1,0:T(8,128)(2,1)S(1)} %get-tuple-element.45), channel_id=1, source_target_pairs={{0,2},{1,3},{2,0},{3,1},{4,6},{5,7},{6,4},{7,5},{8,10},{9,11},{10,... | collective-permute-start | bytes 294920 | tf_op jit(solution)/shard_map/ppermute | solution.py:356
  23.8 0.5 collective-permute-start.10
  24.3 2.5 %collective-permute-start.9 = (bf16[96,1152]{1,0:T(8,128)(2,1)S(1)}, bf16[96,1152]{1,0:T(8,128)(2,1)S(1)}, u32[]{:S(2)}, u32[]{:S(2)}) collective-permute-start(bf16[96,1152]{1,0:T(8,128)(2,1)S(1)} %get-tuple-element.47), channel_id=1, source_target_pairs={{0,6},{1,7},{2,4},{3,5},{4,2},{5,3},{6,0},{7,1},{8,14},{9,15},{10,... | collective-permute-start | bytes 663560 | tf_op jit(solution)/shard_map/ppermute | solution.py:356
  26.8 0.5 collective-permute-start.12
  27.3 0.5 collective-permute-start.13
  27.8 0.2 collective-permute-done.7.refs_1_
  28.0 0.1 collective-permute-start.8
  28.1 2.5 %collective-permute-done.10.refs_1_ = bf16[48,1024]{1,0:T(8,128)(2,1)S(1)} collective-permute-done((bf16[48,1024]{1,0:T(8,128)(2,1)S(1)}, bf16[48,1024]{1,0:T(8,128)(2,1)S(1)}, u32[]{:S(2)}, u32[]{:S(2)}) %collective-permute-start.10) | collective-permute-done | bytes 98336 | tf_op jit(solution)/shard_map/ppermute | solution.py:356
  30.6 0.1 collective-permute-start.11
  30.7 0.6 %across.3.refs_5_.refs_4_ = bf16[1024,1024]{1,0:T(8,128)(2,1)S(1)} custom-call(bf16[1024,1024]{1,0:T(8,128)(2,1)S(1)} %bitcast.19), custom_call_target="tpu_custom_call" | custom-call | bytes 6000000 | tf_op jit(solution)/shard_map/across/pallas_call | solution.py:26
  31.3 0.6 %across.2.refs_2_ = bf16[1024,1024]{1,0:T(8,128)(2,1)S(1)} custom-call(bf16[1024,1024]{1,0:T(8,128)(2,1)S(1)} %bitcast.25), custom_call_target="tpu_custom_call" | custom-call | bytes 6000000 | tf_op jit(solution)/shard_map/across/pallas_call | solution.py:26
  32.0 3.3 %collective-permute-done.9.refs_1_ = bf16[96,1152]{1,0:T(8,128)(2,1)S(1)} collective-permute-done((bf16[96,1152]{1,0:T(8,128)(2,1)S(1)}, bf16[96,1152]{1,0:T(8,128)(2,1)S(1)}, u32[]{:S(2)}, u32[]{:S(2)}) %collective-permute-start.9) | collective-permute-done | bytes 221216 | tf_op jit(solution)/shard_map/ppermute | solution.py:356
  35.2 0.8 %hidden.2 = (bf16[192,1024]{1,0:T(8,128)(2,1)S(1)}, bf16[192,128]{1,0:T(8,128)(2,1)S(1)}, bf16[192,1024]{1,0:T(8,128)(2,1)S(1)}, f32[192,1024]{1,0:T(8,128)S(1)}) custom-call(bf16[96,1152]{1,0:T(8,128)(2,1)S(1)} %get-tuple-element.46.refs_0_, bf16[96,1152]{1,0:T(8,128)(2,1)S(1)} %collective-permute-done.9.refs_1_, bf16[1024,1024]{1,0:T(8,128)(2,1)S(1)} %bitcast.20), custom_call_target="tpu_custom_call" | custom-call | bytes 3000000 | tf_op jit(solution)/shard_map/hidden/pallas_call | solution.py:26
  36.1 0.6 upstream.2.refs_0_.refs_3_
  36.7 0.7 %collective-permute-done.11.refs_1_ = bf16[96,1024]{1,0:T(8,128)(2,1)S(1)} collective-permute-done((bf16[96,1024]{1,0:T(8,128)(2,1)S(1)}, bf16[96,1024]{1,0:T(8,128)(2,1)S(1)}, u32[]{:S(2)}, u32[]{:S(2)}) %collective-permute-start.11) | collective-permute-done | bytes 196640 | tf_op jit(solution)/shard_map/ppermute | solution.py:351
  37.4 0.6 upstream.3.refs_4_
  38.0 0.9 %grads.2 = (bf16[96,1024]{1,0:T(8,128)(2,1)S(1)}, bf16[96,1024]{1,0:T(8,128)(2,1)S(1)}, bf16[192,1024]{1,0:T(8,128)(2,1)S(1)}) custom-call(s32[1]{0:T(128)} %bitcast.4.my_ref, f32[192,1024]{1,0:T(8,128)S(1)} %upstream.2.refs_0_.refs_3_, bf16[192,1024]{1,0:T(8,128)(2,1)S(1)} %get-tuple-element.48.refs_1_.refs_2_, f32[192,1024]{1,0:T(8,128)S(1)} %get-tuple-element.49.refs_2_, ...), custom_call_target="tpu_custom_call" | custom-call | tf_op jit(solution)/shard_map/grads/pallas_call | solution.py:26
  38.9 2.5 %collective-permute-start.16 = (bf16[96,1024]{1,0:T(8,128)(2,1)S(1)}, bf16[96,1024]{1,0:T(8,128)(2,1)S(1)}, u32[]{:S(2)}, u32[]{:S(2)}) collective-permute-start(bf16[96,1024]{1,0:T(8,128)(2,1)S(1)} %get-tuple-element.61), channel_id=1, source_target_pairs={{0,6},{1,7},{2,4},{3,5},{4,2},{5,3},{6,0},{7,1},{8,14},{9,15},{10,... | collective-permute-start | bytes 589832 | tf_op jit(solution)/shard_map/ppermute | solution.py:356
  41.4 0.8 %hidden.3 = (bf16[192,1024]{1,0:T(8,128)(2,1)S(1)}, bf16[192,128]{1,0:T(8,128)(2,1)S(1)}, bf16[192,1024]{1,0:T(8,128)(2,1)S(1)}, f32[192,1024]{1,0:T(8,128)S(1)}) custom-call(f32[192,1024]{1,0:T(8,128)S(1)} %upstream.2.refs_0_.refs_3_, bf16[96,1152]{1,0:T(8,128)(2,1)S(1)} %collective-permute-done.12.refs_1_, ...), custom_call_target="tpu_custom_call" | custom-call | bytes 3000000 | tf_op jit(solution)/shard_map/hidden/pallas_call | solution.py:26
  42.2 0.9 %grads.3 = (bf16[96,1024]{1,0:T(8,128)(2,1)S(1)}, bf16[96,1024]{1,0:T(8,128)(2,1)S(1)}, bf16[192,1024]{1,0:T(8,128)(2,1)S(1)}) custom-call(s32[1]{0:T(128)} %bitcast.4.my_ref, bf16[192,1024]{1,0:T(8,128)(2,1)S(1)} %get-tuple-element.56.refs_0_.refs_7_, f32[192,1024]{1,0:T(8,128)S(1)} %get-tuple-element.57.refs_1_, ...), custom_call_target="tpu_custom_call" | custom-call | tf_op jit(solution)/shard_map/grads/pallas_call | solution.py:26
  43.1 0.6 collective-permute-start.14
  43.7 0.5 collective-permute-start.15
  44.3 0.2 stack.1
  44.5 3.3 %fusion = f32[1024,1024]{1,0:T(8,128)} fusion(bf16[384,1024]{1,0:T(8,128)(2,1)S(1)} %get-tuple-element.66, bf16[384,1024]{1,0:T(8,128)(2,1)S(1)} %get-tuple-element.67), kind=kOutput, calls=%fused_computation.1 | convolution fusion | flops 805306368 | bytes 5767168 | tf_op jit(solution)/shard_map/dot_general | solution.py:462
  47.8 1.6 %collective-permute-done.14.refs_1_ = bf16[96,1024]{1,0:T(8,128)(2,1)S(1)} collective-permute-done((bf16[96,1024]{1,0:T(8,128)(2,1)S(1)}, bf16[96,1024]{1,0:T(8,128)(2,1)S(1)}, u32[]{:S(2)}, u32[]{:S(2)}) %collective-permute-start.14) | collective-permute-done | bytes 196640 | tf_op jit(solution)/shard_map/ppermute | solution.py:356
  49.4 0.5 collective-permute-done.15.refs_2_
  49.9 0.3 combine_other.1
  50.2 0.1 collective-permute-start.17
  50.3 0.5 keep.1
  50.8 1.0 %collective-permute-done.17.refs_4_ = bf16[128,1024]{1,0:T(8,128)(2,1)S(1)} collective-permute-done((bf16[128,1024]{1,0:T(8,128)(2,1)S(1)}, bf16[128,1024]{1,0:T(8,128)(2,1)S(1)}, u32[]{:S(2)}, u32[]{:S(2)}) %collective-permute-start.17) | collective-permute-done | bytes 262176 | tf_op jit(solution)/shard_map/ppermute | solution.py:360
  51.8 0.3 combine_own.1
  52.1 2.8 %collective-permute-start.18 = (bf16[32,1024]{1,0:T(8,128)(2,1)S(1)}, bf16[32,1024]{1,0:T(8,128)(2,1)S(1)}, u32[]{:S(2)}, u32[]{:S(2)}) collective-permute-start(bf16[32,1024]{1,0:T(8,128)(2,1)S(1)} %get-tuple-element.73), channel_id=1, source_target_pairs={{0,24},{8,16},{16,8},{24,0},{1,25},{9,17},{17,9},{25,1},{2,26},{10... | collective-permute-start | bytes 196616 | tf_op jit(solution)/shard_map/ppermute | solution.py:351
  55.0 1.6 %collective-permute-start.20 = (bf16[32,1024]{1,0:T(8,128)(2,1)S(1)}, bf16[32,1024]{1,0:T(8,128)(2,1)S(1)}, u32[]{:S(2)}, u32[]{:S(2)}) collective-permute-start(bf16[32,1024]{1,0:T(8,128)(2,1)S(1)} %get-tuple-element.75), channel_id=1, source_target_pairs={{0,16},{8,24},{16,0},{24,8},{1,17},{9,25},{17,1},{25,9},{2,18},{10... | collective-permute-start | bytes 196616 | tf_op jit(solution)/shard_map/ppermute | solution.py:351
  56.6 3.3 %convolution_bitcast_fusion = f32[1,1024,1024]{2,1,0:T(8,128)} fusion(bf16[384,1024]{1,0:T(8,128)(2,1)S(1)} %get-tuple-element.76, bf16[384,1024]{1,0:T(8,128)(2,1)S(1)} %get-tuple-element.77), kind=kOutput, calls=%fused_computation | convolution fusion | flops 805306368 | bytes 5767168 | tf_op jit(solution)/shard_map/dot_general | solution.py:463
  59.9 1.1 %collective-permute-done.19.refs_2_ = bf16[32,1024]{1,0:T(8,128)(2,1)S(1)} collective-permute-done((bf16[32,1024]{1,0:T(8,128)(2,1)S(1)}, bf16[32,1024]{1,0:T(8,128)(2,1)S(1)}, u32[]{:S(2)}, u32[]{:S(2)}) %collective-permute-start.19) | collective-permute-done | bytes 65568 | tf_op jit(solution)/shard_map/ppermute | solution.py:351
  60.9 1.6 %back.1 = bf16[128,1024]{1,0:T(8,128)(2,1)} custom-call(bf16[128,1024]{1,0:T(8,128)(2,1)S(1)} %bitcast.24, f32[1,1024]{1,0:T(1,128)S(1)} %bitcast.34, f32[1,1024]{1,0:T(1,128)S(1)} %bitcast.36, f32[32,1024]{1,0:T(8,128)S(1)} %get-tuple-element.41.tok_ref, f32[32,128]{1,0:T(8,128)S(1)} %get-tuple-element.42.keep_ref, bf16[32,1024]{1,0:T(8,128)(2,1)S(1)} %bitcast.28, ...), custom_call_target="tpu_custom_call" | custom-call | tf_op jit(solution)/shard_map/back/pallas_call | solution.py:26
  (35 shorter events, 0.1 us)
Async XLA Ops:
  0.6 30.0 %copy-start = (bf16[1,1024,1024]{2,1,0:T(8,128)(2,1)S(1)}, bf16[1,1024,1024]{2,1,0:T(8,128)(2,1)}, u32[]{:S(2)}) copy-start(bf16[1,1024,1024]{2,1,0:T(8,128)(2,1)} %param.13) | copy-start | bytes 6291460
  3.3 14.4 %collective-permute-start.3 = (bf16[32,1152]{1,0:T(8,128)(2,1)}, bf16[32,1152]{1,0:T(8,128)(2,1)S(1)}, u32[]{:S(2)}, u32[]{:S(2)}) collective-permute-start(bf16[32,1152]{1,0:T(8,128)(2,1)} %front.1.refs_0_), channel_id=1, source_target_pairs={{0,24},{8,16},{16,8},{24,0},{1,25},{9,17},{17,9},{25,1},{2,26},{10... | collective-permute-start | bytes 221192 | tf_op jit(solution)/shard_map/ppermute | solution.py:351
  8.4 9.3 %collective-permute-start.2 = (bf16[32,1152]{1,0:T(8,128)(2,1)}, bf16[32,1152]{1,0:T(8,128)(2,1)S(1)}, u32[]{:S(2)}, u32[]{:S(2)}) collective-permute-start(bf16[32,1152]{1,0:T(8,128)(2,1)} %front.1.refs_0_), channel_id=1, source_target_pairs={{0,8},{8,0},{16,24},{24,16},{1,9},{9,1},{17,25},{25,17},{2,10},{10... | collective-permute-start | bytes 221192 | tf_op jit(solution)/shard_map/ppermute | solution.py:351
  8.4 9.3 %collective-permute-start.1 = (bf16[32,1152]{1,0:T(8,128)(2,1)}, bf16[32,1152]{1,0:T(8,128)(2,1)S(1)}, u32[]{:S(2)}, u32[]{:S(2)}) collective-permute-start(bf16[32,1152]{1,0:T(8,128)(2,1)} %front.1.refs_0_), channel_id=1, source_target_pairs={{0,16},{8,24},{16,0},{24,8},{1,17},{9,25},{17,1},{25,9},{2,18},{10... | collective-permute-start | bytes 221192 | tf_op jit(solution)/shard_map/ppermute | solution.py:351
  9.0 8.6 %collective-permute-start = (bf16[32,1024]{1,0:T(8,128)(2,1)}, bf16[32,1024]{1,0:T(8,128)(2,1)S(1)}, u32[]{:S(2)}, u32[]{:S(2)}) collective-permute-start(bf16[32,1024]{1,0:T(8,128)(2,1)} %bitcast.26), channel_id=1, source_target_pairs={{0,16},{8,24},{16,0},{24,8},{1,17},{9,25},{17,1},{25,9},{2,18},{10... | collective-permute-start | bytes 196616 | tf_op jit(solution)/shard_map/ppermute | solution.py:351
  11.3 0.9 %copy-start.4 = (bf16[1,32,1024]{2,1,0:T(8,128)(2,1)S(1)}, bf16[1,32,1024]{2,1,0:T(8,128)(2,1)}, u32[]{:S(2)}) copy-start(bf16[1,32,1024]{2,1,0:T(8,128)(2,1)} %param.15) | copy-start | bytes 196612
  12.2 0.9 %copy-start.3 = (bf16[32,1152]{1,0:T(8,128)(2,1)S(1)}, bf16[32,1152]{1,0:T(8,128)(2,1)}, u32[]{:S(2)}) copy-start(bf16[32,1152]{1,0:T(8,128)(2,1)} %front.1.refs_0_) | copy-start | bytes 221188
  17.8 1.8 %collective-permute-start.5 = (bf16[128,1152]{1,0:T(8,128)(2,1)S(1)}, bf16[128,1152]{1,0:T(8,128)(2,1)S(1)}, u32[]{:S(2)}, u32[]{:S(2)}) collective-permute-start(bf16[128,1152]{1,0:T(8,128)(2,1)S(1)} %token_near.1.token_ref), channel_id=1, source_target_pairs={{0,1},{1,0},{2,3},{3,2},{4,5},{5,4},{6,7},{7,6},{8,9},{9,8},{10,11... | collective-permute-start | bytes 884744 | tf_op jit(solution)/shard_map/ppermute | solution.py:360
  17.8 1.8 %collective-permute-start.4 = (bf16[64,1024]{1,0:T(8,128)(2,1)S(1)}, bf16[64,1024]{1,0:T(8,128)(2,1)S(1)}, u32[]{:S(2)}, u32[]{:S(2)}) collective-permute-start(bf16[64,1024]{1,0:T(8,128)(2,1)S(1)} %cot_near.1.refs_0_.cot_ref), channel_id=1, source_target_pairs={{0,1},{1,0},{2,3},{3,2},{4,5},{5,4},{6,7},{7,6},{8,9},{9,8},{10,11... | collective-permute-start | bytes 393224 | tf_op jit(solution)/shard_map/ppermute | solution.py:360
  18.3 13.0 %copy-start.2 = (bf16[1,1024,1024]{2,1,0:T(8,128)(2,1)S(1)}, bf16[1,1024,1024]{2,1,0:T(8,128)(2,1)}, u32[]{:S(2)}) copy-start(bf16[1,1024,1024]{2,1,0:T(8,128)(2,1)} %param.14) | copy-start | bytes 6291460
  20.7 6.5 %collective-permute-start.6 = (bf16[48,1024]{1,0:T(8,128)(2,1)S(1)}, bf16[48,1024]{1,0:T(8,128)(2,1)S(1)}, u32[]{:S(2)}, u32[]{:S(2)}) collective-permute-start(bf16[48,1024]{1,0:T(8,128)(2,1)S(1)} %get-tuple-element.44), channel_id=1, source_target_pairs={{0,4},{1,5},{2,6},{3,7},{4,0},{5,1},{6,2},{7,3},{8,12},{9,13},{10,... | collective-permute-start | bytes 294920 | tf_op jit(solution)/shard_map/ppermute | solution.py:356
  22.3 5.6 %collective-permute-start.7 = (bf16[48,1024]{1,0:T(8,128)(2,1)S(1)}, bf16[48,1024]{1,0:T(8,128)(2,1)S(1)}, u32[]{:S(2)}, u32[]{:S(2)}) collective-permute-start(bf16[48,1024]{1,0:T(8,128)(2,1)S(1)} %get-tuple-element.45), channel_id=1, source_target_pairs={{0,2},{1,3},{2,0},{3,1},{4,6},{5,7},{6,4},{7,5},{8,10},{9,11},{10,... | collective-permute-start | bytes 294920 | tf_op jit(solution)/shard_map/ppermute | solution.py:356
  23.8 6.7 %collective-permute-start.10 = (bf16[48,1024]{1,0:T(8,128)(2,1)S(1)}, bf16[48,1024]{1,0:T(8,128)(2,1)S(1)}, u32[]{:S(2)}, u32[]{:S(2)}) collective-permute-start(bf16[48,1024]{1,0:T(8,128)(2,1)S(1)} %get-tuple-element.52), channel_id=1, source_target_pairs={{0,6},{1,7},{2,4},{3,5},{4,2},{5,3},{6,0},{7,1},{8,14},{9,15},{10,... | collective-permute-start | bytes 294920 | tf_op jit(solution)/shard_map/ppermute | solution.py:356
  24.3 10.9 %collective-permute-start.9 = (bf16[96,1152]{1,0:T(8,128)(2,1)S(1)}, bf16[96,1152]{1,0:T(8,128)(2,1)S(1)}, u32[]{:S(2)}, u32[]{:S(2)}) collective-permute-start(bf16[96,1152]{1,0:T(8,128)(2,1)S(1)} %get-tuple-element.47), channel_id=1, source_target_pairs={{0,6},{1,7},{2,4},{3,5},{4,2},{5,3},{6,0},{7,1},{8,14},{9,15},{10,... | collective-permute-start | bytes 663560 | tf_op jit(solution)/shard_map/ppermute | solution.py:356
  26.8 14.6 %collective-permute-start.12 = (bf16[96,1152]{1,0:T(8,128)(2,1)S(1)}, bf16[96,1152]{1,0:T(8,128)(2,1)S(1)}, u32[]{:S(2)}, u32[]{:S(2)}) collective-permute-start(bf16[96,1152]{1,0:T(8,128)(2,1)S(1)} %get-tuple-element.54), channel_id=1, source_target_pairs={{0,4},{1,5},{2,6},{3,7},{4,0},{5,1},{6,2},{7,3},{8,12},{9,13},{10,... | collective-permute-start | bytes 663560 | tf_op jit(solution)/shard_map/ppermute | solution.py:356
  27.3 14.1 %collective-permute-start.13 = (bf16[96,1152]{1,0:T(8,128)(2,1)S(1)}, bf16[96,1152]{1,0:T(8,128)(2,1)S(1)}, u32[]{:S(2)}, u32[]{:S(2)}) collective-permute-start(bf16[96,1152]{1,0:T(8,128)(2,1)S(1)} %get-tuple-element.55), channel_id=1, source_target_pairs={{0,2},{1,3},{2,0},{3,1},{4,6},{5,7},{6,4},{7,5},{8,10},{9,11},{10,... | collective-permute-start | bytes 663560 | tf_op jit(solution)/shard_map/ppermute | solution.py:356
  28.0 8.1 %collective-permute-start.8 = (bf16[96,1024]{1,0:T(8,128)(2,1)S(1)}, bf16[96,1024]{1,0:T(8,128)(2,1)S(1)}, u32[]{:S(2)}, u32[]{:S(2)}) collective-permute-start(bf16[96,1024]{1,0:T(8,128)(2,1)S(1)} %cot_slots.2.refs_0_.refs_5_), channel_id=1, source_target_pairs={{0,8},{8,0},{16,24},{24,16},{1,9},{9,1},{17,25},{25,17},{2,10},{10... | collective-permute-start | bytes 589832 | tf_op jit(solution)/shard_map/ppermute | solution.py:351
  30.6 6.8 %collective-permute-start.11 = (bf16[96,1024]{1,0:T(8,128)(2,1)S(1)}, bf16[96,1024]{1,0:T(8,128)(2,1)S(1)}, u32[]{:S(2)}, u32[]{:S(2)}) collective-permute-start(bf16[96,1024]{1,0:T(8,128)(2,1)S(1)} %cot_slots.3.refs_0_), channel_id=1, source_target_pairs={{0,8},{8,0},{16,24},{24,16},{1,9},{9,1},{17,25},{25,17},{2,10},{10... | collective-permute-start | bytes 589832 | tf_op jit(solution)/shard_map/ppermute | solution.py:351
  35.2 2.7 %copy-start.6 = (bf16[1024,8]{0,1:T(8,128)(2,1)S(1)}, bf16[1024,8]{0,1:T(8,128)(2,1)}, u32[]{:S(2)}) copy-start(bf16[1024,8]{0,1:T(8,128)(2,1)} %param.11) | copy-start | bytes 49156
  38.9 8.9 %collective-permute-start.16 = (bf16[96,1024]{1,0:T(8,128)(2,1)S(1)}, bf16[96,1024]{1,0:T(8,128)(2,1)S(1)}, u32[]{:S(2)}, u32[]{:S(2)}) collective-permute-start(bf16[96,1024]{1,0:T(8,128)(2,1)S(1)} %get-tuple-element.61), channel_id=1, source_target_pairs={{0,6},{1,7},{2,4},{3,5},{4,2},{5,3},{6,0},{7,1},{8,14},{9,15},{10,... | collective-permute-start | bytes 589832 | tf_op jit(solution)/shard_map/ppermute | solution.py:356
  43.1 6.2 %collective-permute-start.14 = (bf16[96,1024]{1,0:T(8,128)(2,1)S(1)}, bf16[96,1024]{1,0:T(8,128)(2,1)S(1)}, u32[]{:S(2)}, u32[]{:S(2)}) collective-permute-start(bf16[96,1024]{1,0:T(8,128)(2,1)S(1)} %get-tuple-element.59), channel_id=1, source_target_pairs={{0,2},{1,3},{2,0},{3,1},{4,6},{5,7},{6,4},{7,5},{8,10},{9,11},{10,... | collective-permute-start | bytes 589832 | tf_op jit(solution)/shard_map/ppermute | solution.py:356
  43.7 6.1 %collective-permute-start.15 = (bf16[96,1024]{1,0:T(8,128)(2,1)S(1)}, bf16[96,1024]{1,0:T(8,128)(2,1)S(1)}, u32[]{:S(2)}, u32[]{:S(2)}) collective-permute-start(bf16[96,1024]{1,0:T(8,128)(2,1)S(1)} %get-tuple-element.60), channel_id=1, source_target_pairs={{0,4},{1,5},{2,6},{3,7},{4,0},{5,1},{6,2},{7,3},{8,12},{9,13},{10,... | collective-permute-start | bytes 589832 | tf_op jit(solution)/shard_map/ppermute | solution.py:356
  44.5 5.8 %copy-start.1 = (bf16[1,128,1024]{2,1,0:T(8,128)(2,1)S(1)}, bf16[1,128,1024]{2,1,0:T(8,128)(2,1)}, u32[]{:S(2)}) copy-start(bf16[1,128,1024]{2,1,0:T(8,128)(2,1)} %param.8) | copy-start | bytes 786436
  44.5 5.8 %copy-start.7 = (f32[1024]{0:T(1024)S(1)}, f32[1024]{0:T(1024)}, u32[]{:S(2)}) copy-start(f32[1024]{0:T(1024)} %param.9) | copy-start | bytes 12292
  49.9 11.1 %copy-start.5 = (bf16[1,32,1024]{2,1,0:T(8,128)(2,1)S(1)}, bf16[1,32,1024]{2,1,0:T(8,128)(2,1)}, u32[]{:S(2)}) copy-start(bf16[1,32,1024]{2,1,0:T(8,128)(2,1)} %param.15) | copy-start | bytes 196612
  49.9 11.1 %copy-start.8 = (f32[1024]{0:T(1024)S(1)}, f32[1024]{0:T(1024)}, u32[]{:S(2)}) copy-start(f32[1024]{0:T(1024)} %param.10) | copy-start | bytes 12292
  50.2 1.6 %collective-permute-start.17 = (bf16[128,1024]{1,0:T(8,128)(2,1)S(1)}, bf16[128,1024]{1,0:T(8,128)(2,1)S(1)}, u32[]{:S(2)}, u32[]{:S(2)}) collective-permute-start(bf16[128,1024]{1,0:T(8,128)(2,1)S(1)} %combine_other.1), channel_id=1, source_target_pairs={{0,1},{1,0},{2,3},{3,2},{4,5},{5,4},{6,7},{7,6},{8,9},{9,8},{10,11... | collective-permute-start | bytes 786440 | tf_op jit(solution)/shard_map/ppermute | solution.py:360
  52.1 7.8 %collective-permute-start.18 = (bf16[32,1024]{1,0:T(8,128)(2,1)S(1)}, bf16[32,1024]{1,0:T(8,128)(2,1)S(1)}, u32[]{:S(2)}, u32[]{:S(2)}) collective-permute-start(bf16[32,1024]{1,0:T(8,128)(2,1)S(1)} %get-tuple-element.73), channel_id=1, source_target_pairs={{0,24},{8,16},{16,8},{24,0},{1,25},{9,17},{17,9},{25,1},{2,26},{10... | collective-permute-start | bytes 196616 | tf_op jit(solution)/shard_map/ppermute | solution.py:351
  55.0 6.0 %collective-permute-start.19 = (bf16[32,1024]{1,0:T(8,128)(2,1)S(1)}, bf16[32,1024]{1,0:T(8,128)(2,1)S(1)}, u32[]{:S(2)}, u32[]{:S(2)}) collective-permute-start(bf16[32,1024]{1,0:T(8,128)(2,1)S(1)} %get-tuple-element.74), channel_id=1, source_target_pairs={{0,8},{8,0},{16,24},{24,16},{1,9},{9,1},{17,25},{25,17},{2,10},{10... | collective-permute-start | bytes 196616 | tf_op jit(solution)/shard_map/ppermute | solution.py:351
  55.0 6.0 %collective-permute-start.20 = (bf16[32,1024]{1,0:T(8,128)(2,1)S(1)}, bf16[32,1024]{1,0:T(8,128)(2,1)S(1)}, u32[]{:S(2)}, u32[]{:S(2)}) collective-permute-start(bf16[32,1024]{1,0:T(8,128)(2,1)S(1)} %get-tuple-element.75), channel_id=1, source_target_pairs={{0,16},{8,24},{16,0},{24,8},{1,17},{9,25},{17,1},{25,9},{2,18},{10... | collective-permute-start | bytes 196616 | tf_op jit(solution)/shard_map/ppermute | solution.py:351

commit v6 on v5

--- a/solution.py
+++ b/solution.py
@@ -22,7 +22,7 @@
 def call(body, name, outs, args, us=0.0, scratch=(), limit=8, scalars=0, held=True):
     vmem = pl.BlockSpec(memory_space=pltpu.VMEM)
     smem = pl.BlockSpec(memory_space=pltpu.SMEM)
-    rest = vmem if held else pl.BlockSpec(memory_space=pltpu.HBM)
+    rest = vmem if held else pl.BlockSpec()
     return pl.pallas_call(
         body,
         name=name,
@@ -82,14 +82,7 @@
     return shares, coefs, tokens, scale
 
 
-def front_kernel(*refs):
-    far, pay_ref, near, logit, arrived = refs[:5], refs[5], refs[6:11], refs[11], refs[12]
-    copies = [pltpu.make_async_copy(a, b, arrived.at[i]) for i, (a, b) in enumerate(zip(far, near))]
-    for copy in copies:
-        copy.start()
-    embed_ref, score_ref, gain_ref, router_ref, routes_ref = near
-    for copy in copies:
-        copy.wait()
+def front_kernel(embed_ref, score_ref, gain_ref, router_ref, routes_ref, pay_ref, logit):
     count = pay_ref.shape[0]
     experts, width = router_ref.shape
     _, _, tokens, scale = pooled(quartet_values(embed_ref[...], count), score_ref[...])
@@ -147,22 +140,21 @@
 
 def slot_places(tail, columns, count, capacity, my):
     tokens = tail.shape[0]
-    lane_row = lax.broadcasted_iota(jnp.int32, (LANES, LANES), 0)
-    lane_col = lax.broadcasted_iota(jnp.int32, (LANES, LANES), 1)
-    lane = (2 * (lane_col % GROUP)) ^ my
-    lane = jnp.where(lane_col < GROUP, lane, lane + 2 * GROUP)
-    live = (lane_col % GROUP < columns) & (lane_col < 2 * GROUP)
-    order = ((lane_row == lane) & live).astype(F32).astype(BF)
-    ordered = jnp.dot(tail, order, preferred_element_type=F32).astype(BF)
+    at = lax.broadcasted_iota(jnp.int32, (LANES, LANES), 0)
+    lane = lax.broadcasted_iota(jnp.int32, (LANES, LANES), 1)
+    named_lane = (2 * (at % GROUP)) ^ my
+    named_lane = jnp.where(at < GROUP, named_lane, named_lane + 2 * GROUP)
+    live = (at % GROUP < columns) & (at < 2 * GROUP)
+    order = ((lane == named_lane) & live).astype(F32).astype(BF)
     row = lax.broadcasted_iota(jnp.int32, (tokens, tokens), 0)
     col = lax.broadcasted_iota(jnp.int32, (tokens, tokens), 1)
-    eye = (row == col).astype(F32).astype(BF)
     before = ((row < col) & (row // count == col // count)).astype(F32).astype(BF)
-    ordered_t = lax.dot_general(ordered, eye, ROWS_T, preferred_element_type=F32)
-    place_t = lax.dot_general(ordered, before, ROWS_T, preferred_element_type=F32)[:GROUP, :]
+    ordered_t = lax.dot_general(order, tail, COLS, preferred_element_type=F32)
+    named_t = ordered_t[:GROUP, :]
+    place_t = jnp.dot(named_t.astype(BF), before, preferred_element_type=F32)
     block = lax.broadcasted_iota(jnp.int32, (GROUP, tokens), 1) // count
     place_t = place_t + (block * capacity).astype(F32)
-    return jnp.where(ordered_t[:GROUP, :] > 0.5, place_t, -1.0), ordered_t[GROUP : 2 * GROUP, :]
+    return jnp.where(named_t > 0.5, place_t, -1.0), ordered_t[GROUP : 2 * GROUP, :]
 
 
 def selection(places, values, columns, rows):
@@ -171,28 +163,27 @@
     return jnp.concatenate(picks, axis=0).astype(BF)
 
 
-def pick_kernel(pieces, chunks, capacity, my_ref, cot_ref, token_ref, other_cot_ref, other_token_ref, *refs):
-    cot_outs, outs, pick_ref = refs[:chunks], refs[chunks : 2 * chunks], refs[2 * chunks]
+def cot_pick_kernel(pieces, capacity, my_ref, cot_ref, token_ref, other_cot_ref, other_token_ref, *outs):
     tokens, full = token_ref.shape
     width = full - LANES
     count = tokens // pieces
     cots = cot_ref.shape[0]
-    near = pieces // 2
-    my = my_ref[0]
-
     tail = jnp.concatenate([token_ref[:cots, width:], other_token_ref[:cots, width:]], axis=0)
-    places, gates = slot_places(tail, chunks, count, capacity, my)
-    picks = selection(places, gates, chunks, 2 * near * capacity)
+    places, gates = slot_places(tail, len(outs), count, capacity, my_ref[0])
+    picks = selection(places, gates, len(outs), 2 * (pieces // 2) * capacity)
     cot_rows = jnp.concatenate([cot_ref[...], other_cot_ref[...]], axis=0)
     chosen = jnp.dot(picks, cot_rows, preferred_element_type=F32).astype(BF)
-    for m, out in enumerate(cot_outs):
+    for m, out in enumerate(outs):
         out[...] = chosen[m * out.shape[0] : (m + 1) * out.shape[0], :]
 
-    token_rows = jnp.concatenate([token_ref[...], other_token_ref[...]], axis=0)
-    places, gates = slot_places(token_rows[:, width:], chunks, count, capacity, my)
-    picks = selection(places, jnp.ones_like(gates), chunks, 2 * pieces * capacity)
-    pick_ref[...] = picks
-    chosen = jnp.dot(picks, token_rows, preferred_element_type=F32).astype(BF)
+
+def token_pick_kernel(pieces, capacity, waits, my_ref, *refs):
+    token_ref, other_token_ref, *outs, pick_ref = refs[waits:]
+    tokens, full = token_ref.shape
+    rows = jnp.concatenate([token_ref[...], other_token_ref[...]], axis=0)
+    places, gates = slot_places(rows[:, full - LANES :], len(outs), tokens // pieces, capacity, my_ref[0])
+    pick_ref[...] = selection(places, jnp.ones_like(gates), len(outs), 2 * pieces * capacity)
+    chosen = jnp.dot(pick_ref[...], rows, preferred_element_type=F32).astype(BF)
     for m, out in enumerate(outs):
         out[...] = chosen[m * out.shape[0] : (m + 1) * out.shape[0], :]
 
@@ -369,8 +360,7 @@
         shape(count, full),
         front_args,
         us=2.0,
-        scratch=[pltpu.VMEM(a.shape, a.dtype) for a in front_args]
-        + [pltpu.VMEM((count, LANES), F32), pltpu.SemaphoreType.DMA((len(front_args),))],
+        scratch=[pltpu.VMEM((count, LANES), F32)],
         limit=56,
         held=False,
     )
@@ -394,16 +384,25 @@
         shape(tokens, full),
         (cot_near, held, *[over_seq(pay, k) for k in places[1:]]),
     )
-    *chosen, pick = call(
-        functools.partial(pick_kernel, pieces, chunks, capacity),
-        "pick",
-        [shape(rows // 2, width)] * chunks + [shape(rows, full)] * chunks + [shape(slots, 2 * tokens)],
-        (my, cot_near, token_near, over_cores(cot_near), over_cores(token_near)),
+    cot_other, token_other = over_cores(cot_near), over_cores(token_near)
+    cot_chosen = call(
+        functools.partial(cot_pick_kernel, pieces, capacity),
+        "cot_pick",
+        [shape(rows // 2, width)] * chunks,
+        (my, cot_near, token_near, cot_other, token_other),
         scalars=1,
         limit=16,
     )
-    cot_chunks = over_exp(chosen[:chunks], 2)
-    token_chunks = over_exp(chosen[chunks:], 2)
+    cot_chunks = over_exp(cot_chosen, 2)
+    *chosen, pick = call(
+        functools.partial(token_pick_kernel, pieces, capacity, 1),
+        "token_pick",
+        [shape(rows, full)] * chunks + [shape(slots, 2 * tokens)],
+        (my, cot_chosen[0], token_near, token_other),
+        scalars=1,
+        limit=16,
+    )
+    token_chunks = over_exp(chosen, 2)
     order = [0, *range(chunks - 1, 0, -1)]
     groups = (order[: chunks // 2], order[chunks // 2 :])
     part = slots // 2

time: 62.8 us -> 62.7 us (level)
    ppermute x9, waiting for transfers between devices: 7.98 us -> 7.03 us  [over_exp(): lax.ppermute(values[m], 'exp', [(i, i ^ m * step) for i in range(owners)])]
    ppermute x9, waiting for transfers between devices: 6.34 us -> 7.06 us  [over_seq(): return lax.ppermute(value, 'seq', [(i, i ^ k) for i in range(pieces)])]
    pallas_call x21 -> x22, Pallas kernels: 12.7 us -> 12.7 us  [call(): pl.pallas_call(body, name=name, out_shape=outs, in_specs=[smem] * scalars...]
  transfers between devices with their start and end apart: 21 -> 21, of which waited for: 10 -> 9; matrix products, arithmetic and copies ran while one was open for 11% -> 11% of each run, Pallas kernels for 11% -> 12%
where the time goes in v6:
time: 62.7 us; the launch traced here: 62.5 us
  starting transfers between devices  24.1 us (38%)
  waiting for transfers between devices  16.4 us (26%)
  Pallas kernels  12.7 us (20%)
  matrix products  6.61 us (11%)
  local copies, waits for them, and re-layouts  1.79 us (3%)
  between operations  0.88 us (1%)
    pallas_call x22, Pallas kernels, call(): pl.pallas_call(body, name=name, out_shape=outs, in_specs=[smem] * scalars...  12.7 us
    ppermute x9, starting transfers between devices, over_seq(): return lax.ppermute(value, 'seq', [(i, i ^ k) for i in range(pieces)])  12.7 us
    ppermute x9, starting transfers between devices, over_exp(): lax.ppermute(values[m], 'exp', [(i, i ^ m * step) for i in range(owners)])  10.7 us
    ppermute x9, waiting for transfers between devices, over_seq(): return lax.ppermute(value, 'seq', [(i, i ^ k) for i in range(pieces)])  7.06 us
    ppermute x9, waiting for transfers between devices, over_exp(): lax.ppermute(values[m], 'exp', [(i, i ^ m * step) for i in range(owners)])  7.03 us
    dot_general x1, matrix products, per_device(): lax.dot_general(hidden_rows, cot_slots, ROWS_T, preferred_element_type=F32)  3.31 us
    dot_general x1, matrix products, per_device(): lax.dot_general(token_slots, hidden_grad, ROWS_T, preferred_element_type=...  3.3 us
    ppermute x3, waiting for transfers between devices, over_cores(): return lax.ppermute(value, 'exp', [(i, i ^ 1) for i in range(owners)])  2.28 us
  transfers between devices with their start and end apart: 21, of which 9 were waited for; matrix products, arithmetic and copies ran while one was open for 11% of the time, Pallas kernels for 12%

profile of v6, /device:TPU:0, one launch (start us, length us, event | category | flops | bytes accessed | tf_op | source)
XLA Modules:
  0.0 62.5 jit_solution(11585926081930132075)
XLA Ops:
  0.6 2.6 %front.1.refs_0_ = bf16[32,1152]{1,0:T(8,128)(2,1)} custom-call(bf16[128,1024]{1,0:T(8,128)(2,1)} %bitcast.22, f32[1,1024]{1,0:T(1,128)} %bitcast.32, f32[1,1024]{1,0:T(1,128)} %bitcast.35, bf16[8,1024]{1,0:T(8,128)(2,1)} %bitcast.29, s32[2,32]{1,0:T(2,128)} %bitcast.39), custom_call_target="tpu_custom_call" | custom-call | bytes 6000000 | tf_op jit(solution)/shard_map/front/pallas_call | solution.py:26
  3.3 5.0 %collective-permute-start.3 = (bf16[32,1152]{1,0:T(8,128)(2,1)}, bf16[32,1152]{1,0:T(8,128)(2,1)S(1)}, u32[]{:S(2)}, u32[]{:S(2)}) collective-permute-start(bf16[32,1152]{1,0:T(8,128)(2,1)} %front.1.refs_0_), channel_id=1, source_target_pairs={{0,24},{8,16},{16,8},{24,0},{1,25},{9,17},{17,9},{25,1},{2,26},{10... | collective-permute-start | bytes 221192 | tf_op jit(solution)/shard_map/ppermute | solution.py:342
  8.3 0.6 collective-permute-start.1
  8.9 2.4 %collective-permute-start = (bf16[32,1024]{1,0:T(8,128)(2,1)}, bf16[32,1024]{1,0:T(8,128)(2,1)S(1)}, u32[]{:S(2)}, u32[]{:S(2)}) collective-permute-start(bf16[32,1024]{1,0:T(8,128)(2,1)} %bitcast.26), channel_id=1, source_target_pairs={{0,16},{8,24},{16,0},{24,8},{1,17},{9,25},{17,1},{25,9},{2,18},{10... | collective-permute-start | bytes 196616 | tf_op jit(solution)/shard_map/ppermute | solution.py:342
  11.2 0.9 %copy-done.4 = bf16[1,32,1024]{2,1,0:T(8,128)(2,1)S(1)} copy-done((bf16[1,32,1024]{2,1,0:T(8,128)(2,1)S(1)}, bf16[1,32,1024]{2,1,0:T(8,128)(2,1)}, u32[]{:S(2)}) %copy-start.4) | copy-done | bytes 65560
  12.1 0.9 %copy-done.3 = bf16[32,1152]{1,0:T(8,128)(2,1)S(1)} copy-done((bf16[32,1152]{1,0:T(8,128)(2,1)S(1)}, bf16[32,1152]{1,0:T(8,128)(2,1)}, u32[]{:S(2)}) %copy-start.3) | copy-done | bytes 73752
  13.0 4.6 %collective-permute-done.refs_1_ = bf16[32,1024]{1,0:T(8,128)(2,1)S(1)} collective-permute-done((bf16[32,1024]{1,0:T(8,128)(2,1)}, bf16[32,1024]{1,0:T(8,128)(2,1)S(1)}, u32[]{:S(2)}, u32[]{:S(2)}) %collective-permute-start) | collective-permute-done | bytes 65568 | tf_op jit(solution)/shard_map/ppermute | solution.py:342
  17.7 0.1 collective-permute-start.5
  17.7 0.5 collective-permute-start.4
  18.2 1.3 %collective-permute-done.4.other_cot_ref = bf16[64,1024]{1,0:T(8,128)(2,1)S(1)} collective-permute-done((bf16[64,1024]{1,0:T(8,128)(2,1)S(1)}, bf16[64,1024]{1,0:T(8,128)(2,1)S(1)}, u32[]{:S(2)}, u32[]{:S(2)}) %collective-permute-start.4) | collective-permute-done | bytes 131104 | tf_op jit(solution)/shard_map/ppermute | solution.py:351
  19.5 0.5 cot_pick.1
  20.0 1.6 %collective-permute-start.6 = (bf16[48,1024]{1,0:T(8,128)(2,1)S(1)}, bf16[48,1024]{1,0:T(8,128)(2,1)S(1)}, u32[]{:S(2)}, u32[]{:S(2)}) collective-permute-start(bf16[48,1024]{1,0:T(8,128)(2,1)S(1)} %get-tuple-element.45), channel_id=1, source_target_pairs={{0,4},{1,5},{2,6},{3,7},{4,0},{5,1},{6,2},{7,3},{8,12},{9,13},{10,... | collective-permute-start | bytes 294920 | tf_op jit(solution)/shard_map/ppermute | solution.py:347
  21.6 1.5 %collective-permute-start.7 = (bf16[48,1024]{1,0:T(8,128)(2,1)S(1)}, bf16[48,1024]{1,0:T(8,128)(2,1)S(1)}, u32[]{:S(2)}, u32[]{:S(2)}) collective-permute-start(bf16[48,1024]{1,0:T(8,128)(2,1)S(1)} %get-tuple-element.46), channel_id=1, source_target_pairs={{0,2},{1,3},{2,0},{3,1},{4,6},{5,7},{6,4},{7,5},{8,10},{9,11},{10,... | collective-permute-start | bytes 294920 | tf_op jit(solution)/shard_map/ppermute | solution.py:347
  23.1 0.5 collective-permute-start.10
  23.6 0.7 %token_pick.1 = (bf16[96,1152]{1,0:T(8,128)(2,1)S(1)}, bf16[96,1152]{1,0:T(8,128)(2,1)S(1)}, bf16[96,1152]{1,0:T(8,128)(2,1)S(1)}, bf16[96,1152]{1,0:T(8,128)(2,1)S(1)}, bf16[384,256]{1,0:T(8,128)(2,1)S(1)}) custom-call(s32[1]{0:T(128)} %bitcast.4.my_ref, bf16[48,1024]{1,0:T(8,128)(2,1)S(1)} %get-tuple-element.43.refs_0_, ...), custom_call_target="tpu_custom_call" | custom-call | tf_op jit(solution)/shard_map/token_pick/pallas_call | solution.py:26
  24.2 2.5 %collective-permute-start.9 = (bf16[96,1152]{1,0:T(8,128)(2,1)S(1)}, bf16[96,1152]{1,0:T(8,128)(2,1)S(1)}, u32[]{:S(2)}, u32[]{:S(2)}) collective-permute-start(bf16[96,1152]{1,0:T(8,128)(2,1)S(1)} %get-tuple-element.48), channel_id=1, source_target_pairs={{0,6},{1,7},{2,4},{3,5},{4,2},{5,3},{6,0},{7,1},{8,14},{9,15},{10,... | collective-permute-start | bytes 663560 | tf_op jit(solution)/shard_map/ppermute | solution.py:347
  26.8 0.5 collective-permute-start.12
  27.3 0.5 collective-permute-start.13
  27.8 0.1 collective-permute-start.8
  27.9 1.9 %collective-permute-done.10.refs_1_ = bf16[48,1024]{1,0:T(8,128)(2,1)S(1)} collective-permute-done((bf16[48,1024]{1,0:T(8,128)(2,1)S(1)}, bf16[48,1024]{1,0:T(8,128)(2,1)S(1)}, u32[]{:S(2)}, u32[]{:S(2)}) %collective-permute-start.10) | collective-permute-done | bytes 98336 | tf_op jit(solution)/shard_map/ppermute | solution.py:347
  29.8 0.2 collective-permute-start.11
  30.0 0.6 %across.3.refs_5_.refs_4_ = bf16[1024,1024]{1,0:T(8,128)(2,1)S(1)} custom-call(bf16[1024,1024]{1,0:T(8,128)(2,1)S(1)} %bitcast.19), custom_call_target="tpu_custom_call" | custom-call | bytes 6000000 | tf_op jit(solution)/shard_map/across/pallas_call | solution.py:26
  30.6 0.6 %across.2.refs_2_ = bf16[1024,1024]{1,0:T(8,128)(2,1)S(1)} custom-call(bf16[1024,1024]{1,0:T(8,128)(2,1)S(1)} %bitcast.25), custom_call_target="tpu_custom_call" | custom-call | bytes 6000000 | tf_op jit(solution)/shard_map/across/pallas_call | solution.py:26
  31.3 3.2 %collective-permute-done.9.refs_1_ = bf16[96,1152]{1,0:T(8,128)(2,1)S(1)} collective-permute-done((bf16[96,1152]{1,0:T(8,128)(2,1)S(1)}, bf16[96,1152]{1,0:T(8,128)(2,1)S(1)}, u32[]{:S(2)}, u32[]{:S(2)}) %collective-permute-start.9) | collective-permute-done | bytes 221216 | tf_op jit(solution)/shard_map/ppermute | solution.py:347
  34.5 0.8 %hidden.2 = (bf16[192,1024]{1,0:T(8,128)(2,1)S(1)}, bf16[192,128]{1,0:T(8,128)(2,1)S(1)}, bf16[192,1024]{1,0:T(8,128)(2,1)S(1)}, f32[192,1024]{1,0:T(8,128)S(1)}) custom-call(bf16[96,1152]{1,0:T(8,128)(2,1)S(1)} %get-tuple-element.47.refs_0_, bf16[96,1152]{1,0:T(8,128)(2,1)S(1)} %collective-permute-done.9.refs_1_, bf16[1024,1024]{1,0:T(8,128)(2,1)S(1)} %bitcast.20), custom_call_target="tpu_custom_call" | custom-call | bytes 3000000 | tf_op jit(solution)/shard_map/hidden/pallas_call | solution.py:26
  35.4 0.6 upstream.2.refs_0_.refs_3_
  36.0 1.4 %collective-permute-done.11.refs_1_ = bf16[96,1024]{1,0:T(8,128)(2,1)S(1)} collective-permute-done((bf16[96,1024]{1,0:T(8,128)(2,1)S(1)}, bf16[96,1024]{1,0:T(8,128)(2,1)S(1)}, u32[]{:S(2)}, u32[]{:S(2)}) %collective-permute-start.11) | collective-permute-done | bytes 196640 | tf_op jit(solution)/shard_map/ppermute | solution.py:342
  37.4 0.6 upstream.3.refs_4_
  38.0 0.9 %grads.2 = (bf16[96,1024]{1,0:T(8,128)(2,1)S(1)}, bf16[96,1024]{1,0:T(8,128)(2,1)S(1)}, bf16[192,1024]{1,0:T(8,128)(2,1)S(1)}) custom-call(s32[1]{0:T(128)} %bitcast.4.my_ref, f32[192,1024]{1,0:T(8,128)S(1)} %upstream.2.refs_0_.refs_3_, bf16[192,1024]{1,0:T(8,128)(2,1)S(1)} %get-tuple-element.49.refs_1_.refs_2_, f32[192,1024]{1,0:T(8,128)S(1)} %get-tuple-element.50.refs_2_, ...), custom_call_target="tpu_custom_call" | custom-call | tf_op jit(solution)/shard_map/grads/pallas_call | solution.py:26
  38.9 2.5 %collective-permute-start.16 = (bf16[96,1024]{1,0:T(8,128)(2,1)S(1)}, bf16[96,1024]{1,0:T(8,128)(2,1)S(1)}, u32[]{:S(2)}, u32[]{:S(2)}) collective-permute-start(bf16[96,1024]{1,0:T(8,128)(2,1)S(1)} %get-tuple-element.61), channel_id=1, source_target_pairs={{0,6},{1,7},{2,4},{3,5},{4,2},{5,3},{6,0},{7,1},{8,14},{9,15},{10,... | collective-permute-start | bytes 589832 | tf_op jit(solution)/shard_map/ppermute | solution.py:347
  41.4 0.8 %hidden.3 = (bf16[192,1024]{1,0:T(8,128)(2,1)S(1)}, bf16[192,128]{1,0:T(8,128)(2,1)S(1)}, bf16[192,1024]{1,0:T(8,128)(2,1)S(1)}, f32[192,1024]{1,0:T(8,128)S(1)}) custom-call(f32[192,1024]{1,0:T(8,128)S(1)} %upstream.2.refs_0_.refs_3_, bf16[96,1152]{1,0:T(8,128)(2,1)S(1)} %collective-permute-done.12.refs_1_, ...), custom_call_target="tpu_custom_call" | custom-call | bytes 3000000 | tf_op jit(solution)/shard_map/hidden/pallas_call | solution.py:26
  42.2 0.9 %grads.3 = (bf16[96,1024]{1,0:T(8,128)(2,1)S(1)}, bf16[96,1024]{1,0:T(8,128)(2,1)S(1)}, bf16[192,1024]{1,0:T(8,128)(2,1)S(1)}) custom-call(s32[1]{0:T(128)} %bitcast.4.my_ref, bf16[192,1024]{1,0:T(8,128)(2,1)S(1)} %get-tuple-element.56.refs_0_.refs_7_, f32[192,1024]{1,0:T(8,128)S(1)} %get-tuple-element.57.refs_1_, ...), custom_call_target="tpu_custom_call" | custom-call | tf_op jit(solution)/shard_map/grads/pallas_call | solution.py:26
  43.1 0.6 collective-permute-start.14
  43.7 0.5 collective-permute-start.15
  44.3 0.2 stack.1
  44.5 3.3 %fusion = f32[1024,1024]{1,0:T(8,128)} fusion(bf16[384,1024]{1,0:T(8,128)(2,1)S(1)} %get-tuple-element.66, bf16[384,1024]{1,0:T(8,128)(2,1)S(1)} %get-tuple-element.67), kind=kOutput, calls=%fused_computation.1 | convolution fusion | flops 805306368 | bytes 5767168 | tf_op jit(solution)/shard_map/dot_general | solution.py:461
  47.8 1.6 %collective-permute-done.14.refs_1_ = bf16[96,1024]{1,0:T(8,128)(2,1)S(1)} collective-permute-done((bf16[96,1024]{1,0:T(8,128)(2,1)S(1)}, bf16[96,1024]{1,0:T(8,128)(2,1)S(1)}, u32[]{:S(2)}, u32[]{:S(2)}) %collective-permute-start.14) | collective-permute-done | bytes 196640 | tf_op jit(solution)/shard_map/ppermute | solution.py:347
  49.4 0.4 collective-permute-done.15.refs_2_
  49.7 0.3 combine_other.1
  50.1 0.1 collective-permute-start.17
  50.2 0.5 keep.1
  50.6 1.0 %collective-permute-done.17.refs_4_ = bf16[128,1024]{1,0:T(8,128)(2,1)S(1)} collective-permute-done((bf16[128,1024]{1,0:T(8,128)(2,1)S(1)}, bf16[128,1024]{1,0:T(8,128)(2,1)S(1)}, u32[]{:S(2)}, u32[]{:S(2)}) %collective-permute-start.17) | collective-permute-done | bytes 262176 | tf_op jit(solution)/shard_map/ppermute | solution.py:351
  51.7 0.3 combine_own.1
  52.0 2.8 %collective-permute-start.18 = (bf16[32,1024]{1,0:T(8,128)(2,1)S(1)}, bf16[32,1024]{1,0:T(8,128)(2,1)S(1)}, u32[]{:S(2)}, u32[]{:S(2)}) collective-permute-start(bf16[32,1024]{1,0:T(8,128)(2,1)S(1)} %get-tuple-element.73), channel_id=1, source_target_pairs={{0,24},{8,16},{16,8},{24,0},{1,25},{9,17},{17,9},{25,1},{2,26},{10... | collective-permute-start | bytes 196616 | tf_op jit(solution)/shard_map/ppermute | solution.py:342
  54.8 1.7 %collective-permute-start.20 = (bf16[32,1024]{1,0:T(8,128)(2,1)S(1)}, bf16[32,1024]{1,0:T(8,128)(2,1)S(1)}, u32[]{:S(2)}, u32[]{:S(2)}) collective-permute-start(bf16[32,1024]{1,0:T(8,128)(2,1)S(1)} %get-tuple-element.75), channel_id=1, source_target_pairs={{0,16},{8,24},{16,0},{24,8},{1,17},{9,25},{17,1},{25,9},{2,18},{10... | collective-permute-start | bytes 196616 | tf_op jit(solution)/shard_map/ppermute | solution.py:342
  56.4 3.3 %convolution_bitcast_fusion = f32[1,1024,1024]{2,1,0:T(8,128)} fusion(bf16[384,1024]{1,0:T(8,128)(2,1)S(1)} %get-tuple-element.76, bf16[384,1024]{1,0:T(8,128)(2,1)S(1)} %get-tuple-element.77), kind=kOutput, calls=%fused_computation | convolution fusion | flops 805306368 | bytes 5767168 | tf_op jit(solution)/shard_map/dot_general | solution.py:462
  59.7 1.1 %collective-permute-done.19.refs_2_ = bf16[32,1024]{1,0:T(8,128)(2,1)S(1)} collective-permute-done((bf16[32,1024]{1,0:T(8,128)(2,1)S(1)}, bf16[32,1024]{1,0:T(8,128)(2,1)S(1)}, u32[]{:S(2)}, u32[]{:S(2)}) %collective-permute-start.19) | collective-permute-done | bytes 65568 | tf_op jit(solution)/shard_map/ppermute | solution.py:342
  60.8 1.6 %back.1 = bf16[128,1024]{1,0:T(8,128)(2,1)} custom-call(bf16[128,1024]{1,0:T(8,128)(2,1)S(1)} %bitcast.24, f32[1,1024]{1,0:T(1,128)S(1)} %bitcast.34, f32[1,1024]{1,0:T(1,128)S(1)} %bitcast.36, f32[32,1024]{1,0:T(8,128)S(1)} %get-tuple-element.41.tok_ref, f32[32,128]{1,0:T(8,128)S(1)} %get-tuple-element.42.keep_ref, bf16[32,1024]{1,0:T(8,128)(2,1)S(1)} %bitcast.28, ...), custom_call_target="tpu_custom_call" | custom-call | tf_op jit(solution)/shard_map/back/pallas_call | solution.py:26
  (36 shorter events, 0.1 us)
Async XLA Ops:
  0.6 29.4 %copy-start = (bf16[1,1024,1024]{2,1,0:T(8,128)(2,1)S(1)}, bf16[1,1024,1024]{2,1,0:T(8,128)(2,1)}, u32[]{:S(2)}) copy-start(bf16[1,1024,1024]{2,1,0:T(8,128)(2,1)} %param.13) | copy-start | bytes 6291460
  3.3 14.3 %collective-permute-start.3 = (bf16[32,1152]{1,0:T(8,128)(2,1)}, bf16[32,1152]{1,0:T(8,128)(2,1)S(1)}, u32[]{:S(2)}, u32[]{:S(2)}) collective-permute-start(bf16[32,1152]{1,0:T(8,128)(2,1)} %front.1.refs_0_), channel_id=1, source_target_pairs={{0,24},{8,16},{16,8},{24,0},{1,25},{9,17},{17,9},{25,1},{2,26},{10... | collective-permute-start | bytes 221192 | tf_op jit(solution)/shard_map/ppermute | solution.py:342
  8.3 9.3 %collective-permute-start.2 = (bf16[32,1152]{1,0:T(8,128)(2,1)}, bf16[32,1152]{1,0:T(8,128)(2,1)S(1)}, u32[]{:S(2)}, u32[]{:S(2)}) collective-permute-start(bf16[32,1152]{1,0:T(8,128)(2,1)} %front.1.refs_0_), channel_id=1, source_target_pairs={{0,8},{8,0},{16,24},{24,16},{1,9},{9,1},{17,25},{25,17},{2,10},{10... | collective-permute-start | bytes 221192 | tf_op jit(solution)/shard_map/ppermute | solution.py:342
  8.3 9.3 %collective-permute-start.1 = (bf16[32,1152]{1,0:T(8,128)(2,1)}, bf16[32,1152]{1,0:T(8,128)(2,1)S(1)}, u32[]{:S(2)}, u32[]{:S(2)}) collective-permute-start(bf16[32,1152]{1,0:T(8,128)(2,1)} %front.1.refs_0_), channel_id=1, source_target_pairs={{0,16},{8,24},{16,0},{24,8},{1,17},{9,25},{17,1},{25,9},{2,18},{10... | collective-permute-start | bytes 221192 | tf_op jit(solution)/shard_map/ppermute | solution.py:342
  8.9 8.7 %collective-permute-start = (bf16[32,1024]{1,0:T(8,128)(2,1)}, bf16[32,1024]{1,0:T(8,128)(2,1)S(1)}, u32[]{:S(2)}, u32[]{:S(2)}) collective-permute-start(bf16[32,1024]{1,0:T(8,128)(2,1)} %bitcast.26), channel_id=1, source_target_pairs={{0,16},{8,24},{16,0},{24,8},{1,17},{9,25},{17,1},{25,9},{2,18},{10... | collective-permute-start | bytes 196616 | tf_op jit(solution)/shard_map/ppermute | solution.py:342
  11.2 0.9 %copy-start.4 = (bf16[1,32,1024]{2,1,0:T(8,128)(2,1)S(1)}, bf16[1,32,1024]{2,1,0:T(8,128)(2,1)}, u32[]{:S(2)}) copy-start(bf16[1,32,1024]{2,1,0:T(8,128)(2,1)} %param.15) | copy-start | bytes 196612
  12.1 0.9 %copy-start.3 = (bf16[32,1152]{1,0:T(8,128)(2,1)S(1)}, bf16[32,1152]{1,0:T(8,128)(2,1)}, u32[]{:S(2)}) copy-start(bf16[32,1152]{1,0:T(8,128)(2,1)} %front.1.refs_0_) | copy-start | bytes 221188
  17.7 1.8 %collective-permute-start.5 = (bf16[128,1152]{1,0:T(8,128)(2,1)S(1)}, bf16[128,1152]{1,0:T(8,128)(2,1)S(1)}, u32[]{:S(2)}, u32[]{:S(2)}) collective-permute-start(bf16[128,1152]{1,0:T(8,128)(2,1)S(1)} %token_near.1.token_ref.refs_1_), channel_id=1, source_target_pairs={{0,1},{1,0},{2,3},{3,2},{4,5},{5,4},{6,7},{7,6},{8,9},{9,8},{10,11... | collective-permute-start | bytes 884744 | tf_op jit(solution)/shard_map/ppermute | solution.py:351
  17.7 1.8 %collective-permute-start.4 = (bf16[64,1024]{1,0:T(8,128)(2,1)S(1)}, bf16[64,1024]{1,0:T(8,128)(2,1)S(1)}, u32[]{:S(2)}, u32[]{:S(2)}) collective-permute-start(bf16[64,1024]{1,0:T(8,128)(2,1)S(1)} %cot_near.1.refs_0_.cot_ref), channel_id=1, source_target_pairs={{0,1},{1,0},{2,3},{3,2},{4,5},{5,4},{6,7},{7,6},{8,9},{9,8},{10,11... | collective-permute-start | bytes 393224 | tf_op jit(solution)/shard_map/ppermute | solution.py:351
  18.2 12.4 %copy-start.2 = (bf16[1,1024,1024]{2,1,0:T(8,128)(2,1)S(1)}, bf16[1,1024,1024]{2,1,0:T(8,128)(2,1)}, u32[]{:S(2)}) copy-start(bf16[1,1024,1024]{2,1,0:T(8,128)(2,1)} %param.14) | copy-start | bytes 6291460
  20.0 7.3 %collective-permute-start.6 = (bf16[48,1024]{1,0:T(8,128)(2,1)S(1)}, bf16[48,1024]{1,0:T(8,128)(2,1)S(1)}, u32[]{:S(2)}, u32[]{:S(2)}) collective-permute-start(bf16[48,1024]{1,0:T(8,128)(2,1)S(1)} %get-tuple-element.45), channel_id=1, source_target_pairs={{0,4},{1,5},{2,6},{3,7},{4,0},{5,1},{6,2},{7,3},{8,12},{9,13},{10,... | collective-permute-start | bytes 294920 | tf_op jit(solution)/shard_map/ppermute | solution.py:347
  21.6 6.2 %collective-permute-start.7 = (bf16[48,1024]{1,0:T(8,128)(2,1)S(1)}, bf16[48,1024]{1,0:T(8,128)(2,1)S(1)}, u32[]{:S(2)}, u32[]{:S(2)}) collective-permute-start(bf16[48,1024]{1,0:T(8,128)(2,1)S(1)} %get-tuple-element.46), channel_id=1, source_target_pairs={{0,2},{1,3},{2,0},{3,1},{4,6},{5,7},{6,4},{7,5},{8,10},{9,11},{10,... | collective-permute-start | bytes 294920 | tf_op jit(solution)/shard_map/ppermute | solution.py:347
  23.1 6.7 %collective-permute-start.10 = (bf16[48,1024]{1,0:T(8,128)(2,1)S(1)}, bf16[48,1024]{1,0:T(8,128)(2,1)S(1)}, u32[]{:S(2)}, u32[]{:S(2)}) collective-permute-start(bf16[48,1024]{1,0:T(8,128)(2,1)S(1)} %get-tuple-element.52), channel_id=1, source_target_pairs={{0,6},{1,7},{2,4},{3,5},{4,2},{5,3},{6,0},{7,1},{8,14},{9,15},{10,... | collective-permute-start | bytes 294920 | tf_op jit(solution)/shard_map/ppermute | solution.py:347
  24.2 10.3 %collective-permute-start.9 = (bf16[96,1152]{1,0:T(8,128)(2,1)S(1)}, bf16[96,1152]{1,0:T(8,128)(2,1)S(1)}, u32[]{:S(2)}, u32[]{:S(2)}) collective-permute-start(bf16[96,1152]{1,0:T(8,128)(2,1)S(1)} %get-tuple-element.48), channel_id=1, source_target_pairs={{0,6},{1,7},{2,4},{3,5},{4,2},{5,3},{6,0},{7,1},{8,14},{9,15},{10,... | collective-permute-start | bytes 663560 | tf_op jit(solution)/shard_map/ppermute | solution.py:347
  26.8 14.6 %collective-permute-start.12 = (bf16[96,1152]{1,0:T(8,128)(2,1)S(1)}, bf16[96,1152]{1,0:T(8,128)(2,1)S(1)}, u32[]{:S(2)}, u32[]{:S(2)}) collective-permute-start(bf16[96,1152]{1,0:T(8,128)(2,1)S(1)} %get-tuple-element.54), channel_id=1, source_target_pairs={{0,4},{1,5},{2,6},{3,7},{4,0},{5,1},{6,2},{7,3},{8,12},{9,13},{10,... | collective-permute-start | bytes 663560 | tf_op jit(solution)/shard_map/ppermute | solution.py:347
  27.3 14.1 %collective-permute-start.13 = (bf16[96,1152]{1,0:T(8,128)(2,1)S(1)}, bf16[96,1152]{1,0:T(8,128)(2,1)S(1)}, u32[]{:S(2)}, u32[]{:S(2)}) collective-permute-start(bf16[96,1152]{1,0:T(8,128)(2,1)S(1)} %get-tuple-element.55), channel_id=1, source_target_pairs={{0,2},{1,3},{2,0},{3,1},{4,6},{5,7},{6,4},{7,5},{8,10},{9,11},{10,... | collective-permute-start | bytes 663560 | tf_op jit(solution)/shard_map/ppermute | solution.py:347
  27.8 7.5 %collective-permute-start.8 = (bf16[96,1024]{1,0:T(8,128)(2,1)S(1)}, bf16[96,1024]{1,0:T(8,128)(2,1)S(1)}, u32[]{:S(2)}, u32[]{:S(2)}) collective-permute-start(bf16[96,1024]{1,0:T(8,128)(2,1)S(1)} %cot_slots.2.refs_0_.refs_5_), channel_id=1, source_target_pairs={{0,8},{8,0},{16,24},{24,16},{1,9},{9,1},{17,25},{25,17},{2,10},{10... | collective-permute-start | bytes 589832 | tf_op jit(solution)/shard_map/ppermute | solution.py:342
  29.8 7.5 %collective-permute-start.11 = (bf16[96,1024]{1,0:T(8,128)(2,1)S(1)}, bf16[96,1024]{1,0:T(8,128)(2,1)S(1)}, u32[]{:S(2)}, u32[]{:S(2)}) collective-permute-start(bf16[96,1024]{1,0:T(8,128)(2,1)S(1)} %cot_slots.3.refs_0_), channel_id=1, source_target_pairs={{0,8},{8,0},{16,24},{24,16},{1,9},{9,1},{17,25},{25,17},{2,10},{10... | collective-permute-start | bytes 589832 | tf_op jit(solution)/shard_map/ppermute | solution.py:342
  34.5 3.5 %copy-start.6 = (bf16[1024,8]{0,1:T(8,128)(2,1)S(1)}, bf16[1024,8]{0,1:T(8,128)(2,1)}, u32[]{:S(2)}) copy-start(bf16[1024,8]{0,1:T(8,128)(2,1)} %param.11) | copy-start | bytes 49156
  38.9 8.9 %collective-permute-start.16 = (bf16[96,1024]{1,0:T(8,128)(2,1)S(1)}, bf16[96,1024]{1,0:T(8,128)(2,1)S(1)}, u32[]{:S(2)}, u32[]{:S(2)}) collective-permute-start(bf16[96,1024]{1,0:T(8,128)(2,1)S(1)} %get-tuple-element.61), channel_id=1, source_target_pairs={{0,6},{1,7},{2,4},{3,5},{4,2},{5,3},{6,0},{7,1},{8,14},{9,15},{10,... | collective-permute-start | bytes 589832 | tf_op jit(solution)/shard_map/ppermute | solution.py:347
  43.1 6.2 %collective-permute-start.14 = (bf16[96,1024]{1,0:T(8,128)(2,1)S(1)}, bf16[96,1024]{1,0:T(8,128)(2,1)S(1)}, u32[]{:S(2)}, u32[]{:S(2)}) collective-permute-start(bf16[96,1024]{1,0:T(8,128)(2,1)S(1)} %get-tuple-element.59), channel_id=1, source_target_pairs={{0,2},{1,3},{2,0},{3,1},{4,6},{5,7},{6,4},{7,5},{8,10},{9,11},{10,... | collective-permute-start | bytes 589832 | tf_op jit(solution)/shard_map/ppermute | solution.py:347
  43.7 6.0 %collective-permute-start.15 = (bf16[96,1024]{1,0:T(8,128)(2,1)S(1)}, bf16[96,1024]{1,0:T(8,128)(2,1)S(1)}, u32[]{:S(2)}, u32[]{:S(2)}) collective-permute-start(bf16[96,1024]{1,0:T(8,128)(2,1)S(1)} %get-tuple-element.60), channel_id=1, source_target_pairs={{0,4},{1,5},{2,6},{3,7},{4,0},{5,1},{6,2},{7,3},{8,12},{9,13},{10,... | collective-permute-start | bytes 589832 | tf_op jit(solution)/shard_map/ppermute | solution.py:347
  44.5 5.7 %copy-start.1 = (bf16[1,128,1024]{2,1,0:T(8,128)(2,1)S(1)}, bf16[1,128,1024]{2,1,0:T(8,128)(2,1)}, u32[]{:S(2)}) copy-start(bf16[1,128,1024]{2,1,0:T(8,128)(2,1)} %param.8) | copy-start | bytes 786436
  44.5 5.7 %copy-start.7 = (f32[1024]{0:T(1024)S(1)}, f32[1024]{0:T(1024)}, u32[]{:S(2)}) copy-start(f32[1024]{0:T(1024)} %param.9) | copy-start | bytes 12292
  49.7 11.1 %copy-start.5 = (bf16[1,32,1024]{2,1,0:T(8,128)(2,1)S(1)}, bf16[1,32,1024]{2,1,0:T(8,128)(2,1)}, u32[]{:S(2)}) copy-start(bf16[1,32,1024]{2,1,0:T(8,128)(2,1)} %param.15) | copy-start | bytes 196612
  49.7 11.1 %copy-start.8 = (f32[1024]{0:T(1024)S(1)}, f32[1024]{0:T(1024)}, u32[]{:S(2)}) copy-start(f32[1024]{0:T(1024)} %param.10) | copy-start | bytes 12292
  50.1 1.6 %collective-permute-start.17 = (bf16[128,1024]{1,0:T(8,128)(2,1)S(1)}, bf16[128,1024]{1,0:T(8,128)(2,1)S(1)}, u32[]{:S(2)}, u32[]{:S(2)}) collective-permute-start(bf16[128,1024]{1,0:T(8,128)(2,1)S(1)} %combine_other.1), channel_id=1, source_target_pairs={{0,1},{1,0},{2,3},{3,2},{4,5},{5,4},{6,7},{7,6},{8,9},{9,8},{10,11... | collective-permute-start | bytes 786440 | tf_op jit(solution)/shard_map/ppermute | solution.py:351
  52.0 7.8 %collective-permute-start.18 = (bf16[32,1024]{1,0:T(8,128)(2,1)S(1)}, bf16[32,1024]{1,0:T(8,128)(2,1)S(1)}, u32[]{:S(2)}, u32[]{:S(2)}) collective-permute-start(bf16[32,1024]{1,0:T(8,128)(2,1)S(1)} %get-tuple-element.73), channel_id=1, source_target_pairs={{0,24},{8,16},{16,8},{24,0},{1,25},{9,17},{17,9},{25,1},{2,26},{10... | collective-permute-start | bytes 196616 | tf_op jit(solution)/shard_map/ppermute | solution.py:342
  54.8 6.0 %collective-permute-start.19 = (bf16[32,1024]{1,0:T(8,128)(2,1)S(1)}, bf16[32,1024]{1,0:T(8,128)(2,1)S(1)}, u32[]{:S(2)}, u32[]{:S(2)}) collective-permute-start(bf16[32,1024]{1,0:T(8,128)(2,1)S(1)} %get-tuple-element.74), channel_id=1, source_target_pairs={{0,8},{8,0},{16,24},{24,16},{1,9},{9,1},{17,25},{25,17},{2,10},{10... | collective-permute-start | bytes 196616 | tf_op jit(solution)/shard_map/ppermute | solution.py:342
  54.8 6.0 %collective-permute-start.20 = (bf16[32,1024]{1,0:T(8,128)(2,1)S(1)}, bf16[32,1024]{1,0:T(8,128)(2,1)S(1)}, u32[]{:S(2)}, u32[]{:S(2)}) collective-permute-start(bf16[32,1024]{1,0:T(8,128)(2,1)S(1)} %get-tuple-element.75), channel_id=1, source_target_pairs={{0,16},{8,24},{16,0},{24,8},{1,17},{9,25},{17,1},{25,9},{2,18},{10... | collective-permute-start | bytes 196616 | tf_op jit(solution)/shard_map/ppermute | solution.py:342

commit v7 on v6

--- a/solution.py
+++ b/solution.py
@@ -114,9 +114,11 @@
     pay_ref[:, width:] = tail.astype(BF)
 
 
-def keep_kernel(embed_ref, score_ref, tok_ref, keep_ref):
+def keep_kernel(embed_ref, score_ref, values_ref, tok_ref, keep_ref):
     count = tok_ref.shape[0]
-    shares, coefs, tokens, scale = pooled(quartet_values(embed_ref[...], count), score_ref[...])
+    values = quartet_values(embed_ref[...], count)
+    values_ref[...] = jnp.concatenate([v.astype(BF) for v in values], axis=0)
+    shares, coefs, tokens, scale = pooled(values, score_ref[...])
     tok_ref[...] = tokens
     columns = coefs + [s for share in shares for s in share] + [scale]
     lane = lax.broadcasted_iota(jnp.int32, keep_ref.shape, 1)
@@ -163,25 +165,36 @@
     return jnp.concatenate(picks, axis=0).astype(BF)
 
 
-def cot_pick_kernel(pieces, capacity, my_ref, cot_ref, token_ref, other_cot_ref, other_token_ref, *outs):
-    tokens, full = token_ref.shape
-    width = full - LANES
-    count = tokens // pieces
-    cots = cot_ref.shape[0]
-    tail = jnp.concatenate([token_ref[:cots, width:], other_token_ref[:cots, width:]], axis=0)
+def near_kernel(cots, *refs):
+    ins, out_ref = refs[:-1], refs[-1]
+    count, width = ins[0].shape
+    for i, r in enumerate(ins):
+        at = slice(i * count, (i + 1) * count)
+        if i < cots:
+            out_ref[at, :width] = r[...]
+            out_ref[at, width:] = jnp.zeros((count, out_ref.shape[1] - width), BF)
+        else:
+            out_ref[at, :] = r[...]
+
+
+def cot_pick_kernel(near, count, capacity, my_ref, own_ref, other_ref, *outs):
+    cots = near * count
+    width = own_ref.shape[1] - LANES
+    tail = jnp.concatenate([r[cots : 2 * cots, width:] for r in (own_ref, other_ref)], axis=0)
     places, gates = slot_places(tail, len(outs), count, capacity, my_ref[0])
-    picks = selection(places, gates, len(outs), 2 * (pieces // 2) * capacity)
-    cot_rows = jnp.concatenate([cot_ref[...], other_cot_ref[...]], axis=0)
+    picks = selection(places, gates, len(outs), 2 * near * capacity)
+    cot_rows = jnp.concatenate([r[:cots, :width] for r in (own_ref, other_ref)], axis=0)
     chosen = jnp.dot(picks, cot_rows, preferred_element_type=F32).astype(BF)
     for m, out in enumerate(outs):
         out[...] = chosen[m * out.shape[0] : (m + 1) * out.shape[0], :]
 
 
-def token_pick_kernel(pieces, capacity, waits, my_ref, *refs):
-    token_ref, other_token_ref, *outs, pick_ref = refs[waits:]
-    tokens, full = token_ref.shape
-    rows = jnp.concatenate([token_ref[...], other_token_ref[...]], axis=0)
-    places, gates = slot_places(rows[:, full - LANES :], len(outs), tokens // pieces, capacity, my_ref[0])
+def token_pick_kernel(near, count, capacity, waits, my_ref, *refs):
+    own_ref, other_ref, *outs, pick_ref = refs[waits:]
+    full = own_ref.shape[1]
+    pieces = 2 * near
+    rows = jnp.concatenate([r[near * count :, :] for r in (own_ref, other_ref)], axis=0)
+    places, gates = slot_places(rows[:, full - LANES :], len(outs), count, capacity, my_ref[0])
     pick_ref[...] = selection(places, jnp.ones_like(gates), len(outs), 2 * pieces * capacity)
     chosen = jnp.dot(pick_ref[...], rows, preferred_element_type=F32).astype(BF)
     for m, out in enumerate(outs):
@@ -274,10 +287,10 @@
         out[...] = back[k * count : (k + 1) * count, :]
 
 
-def back_kernel(pieces, embed_ref, score_ref, gain_ref, tok_ref, keep_ref, cot_ref, *refs):
+def back_kernel(pieces, ordered_ref, score_ref, gain_ref, tok_ref, keep_ref, cot_ref, *refs):
     parts, out_ref = refs[:pieces], refs[pieces]
     count, width = tok_ref.shape
-    values = quartet_values(embed_ref[...], count)
+    values = [ordered_ref[q * count : (q + 1) * count, :].astype(F32) for q in range(4)]
     kept = keep_ref[...]
     column = [kept[:, i : i + 1] for i in range(17)]
     coefs = column[:4]
@@ -364,41 +377,38 @@
         limit=56,
         held=False,
     )
-    tok, keep = call(
+    ordered, tok, keep = call(
         keep_kernel,
         "keep",
-        (shape(count, width, dtype=F32), shape(count, LANES, dtype=F32)),
+        (shape(4 * count, width), shape(count, width, dtype=F32), shape(count, LANES, dtype=F32)),
         (embed, score_row),
         us=2.0,
     )
     held_cot = call(functools.partial(gather_kernel, 0), "hold_cot", shape(count, width), (cot,), us=1.0)
-    cot_near = call(
-        functools.partial(gather_kernel, 0), "cot_near", shape(half * count, width), (held_cot, *cot_far), us=5.0
-    )
     held = call(functools.partial(gather_kernel, 0), "hold_own", shape(count, full), (pay,), us=1.0)
     in_across = call(transpose_kernel, "across", shape(hidden, width), (weight_in,), us=2.0, limit=16)
     out_across = call(transpose_kernel, "across", shape(width, hidden), (weight_out,), us=2.0, limit=16)
-    token_near = call(
-        functools.partial(gather_kernel, 1),
-        "token_near",
-        shape(tokens, full),
-        (cot_near, held, *[over_seq(pay, k) for k in places[1:]]),
-    )
-    cot_other, token_other = over_cores(cot_near), over_cores(token_near)
+    near = call(
+        functools.partial(near_kernel, half),
+        "near",
+        shape(half * count + tokens, full),
+        (held_cot, *cot_far, held, *[over_seq(pay, k) for k in places[1:]]),
+    )
+    other = over_cores(near)
     cot_chosen = call(
-        functools.partial(cot_pick_kernel, pieces, capacity),
+        functools.partial(cot_pick_kernel, half, count, capacity),
         "cot_pick",
         [shape(rows // 2, width)] * chunks,
-        (my, cot_near, token_near, cot_other, token_other),
+        (my, near, other),
         scalars=1,
         limit=16,
     )
     cot_chunks = over_exp(cot_chosen, 2)
     *chosen, pick = call(
-        functools.partial(token_pick_kernel, pieces, capacity, 1),
+        functools.partial(token_pick_kernel, half, count, capacity, 1),
         "token_pick",
         [shape(rows, full)] * chunks + [shape(slots, 2 * tokens)],
-        (my, cot_chosen[0], token_near, token_other),
+        (my, cot_chosen[0], near, other),
         scalars=1,
         limit=16,
     )
@@ -475,7 +485,7 @@
         functools.partial(back_kernel, pieces),
         "back",
         shape(4 * count, width),
-        (embed, score_row, gain_row, tok, keep, cot, *parts),
+        (ordered, score_row, gain_row, tok, keep, cot, *parts),
     )
     return (embed_grad[None], grad_in[None], grad_out[None])
 

time: 62.7 us -> 62.6 us (level)
    ppermute x3 -> x2, waiting for transfers between devices: 2.28 us -> 2.79 us  [over_cores(): return lax.ppermute(value, 'exp', [(i, i ^ 1) for i in range(owners)])]
    pallas_call x22 -> x21, Pallas kernels: 12.7 us -> 12.7 us  [call(): pl.pallas_call(body, name=name, out_shape=outs, in_specs=[smem] * scalars...]
  transfers between devices with their start and end apart: 21 -> 20, of which waited for: 9 -> 9; matrix products, arithmetic and copies ran while one was open for 11% -> 11% of each run, Pallas kernels for 12% -> 12%
where the time goes in v7:
time: 62.6 us; the launch traced here: 62.4 us
  starting transfers between devices  23.6 us (38%)
  waiting for transfers between devices  16.9 us (27%)
  Pallas kernels  12.7 us (20%)
  matrix products  6.61 us (11%)
  local copies, waits for them, and re-layouts  1.79 us (3%)
  between operations  0.87 us (1%)
    ppermute x9, starting transfers between devices, over_seq(): return lax.ppermute(value, 'seq', [(i, i ^ k) for i in range(pieces)])  12.7 us
    pallas_call x21, Pallas kernels, call(): pl.pallas_call(body, name=name, out_shape=outs, in_specs=[smem] * scalars...  12.7 us
    ppermute x9, starting transfers between devices, over_exp(): lax.ppermute(values[m], 'exp', [(i, i ^ m * step) for i in range(owners)])  10.7 us
    ppermute x9, waiting for transfers between devices, over_seq(): return lax.ppermute(value, 'seq', [(i, i ^ k) for i in range(pieces)])  7.08 us
    ppermute x9, waiting for transfers between devices, over_exp(): lax.ppermute(values[m], 'exp', [(i, i ^ m * step) for i in range(owners)])  7.02 us
    dot_general x1, matrix products, per_device(): lax.dot_general(hidden_rows, cot_slots, ROWS_T, preferred_element_type=F32)  3.31 us
    dot_general x1, matrix products, per_device(): lax.dot_general(token_slots, hidden_grad, ROWS_T, preferred_element_type=...  3.3 us
    ppermute x2, waiting for transfers between devices, over_cores(): return lax.ppermute(value, 'exp', [(i, i ^ 1) for i in range(owners)])  2.79 us
  transfers between devices with their start and end apart: 20, of which 9 were waited for; matrix products, arithmetic and copies ran while one was open for 11% of the time, Pallas kernels for 12%

profile of v7, /device:TPU:0, one launch (start us, length us, event | category | flops | bytes accessed | tf_op | source)
XLA Modules:
  0.0 62.4 jit_solution(12933999246991800696)
XLA Ops:
  0.6 2.6 %front.1.refs_0_ = bf16[32,1152]{1,0:T(8,128)(2,1)} custom-call(bf16[128,1024]{1,0:T(8,128)(2,1)} %bitcast.23, f32[1,1024]{1,0:T(1,128)} %bitcast.31, f32[1,1024]{1,0:T(1,128)} %bitcast.34, bf16[8,1024]{1,0:T(8,128)(2,1)} %bitcast.28, s32[2,32]{1,0:T(2,128)} %bitcast.38), custom_call_target="tpu_custom_call" | custom-call | bytes 6000000 | tf_op jit(solution)/shard_map/front/pallas_call | solution.py:26
  3.3 5.0 %collective-permute-start.3 = (bf16[32,1152]{1,0:T(8,128)(2,1)}, bf16[32,1152]{1,0:T(8,128)(2,1)S(1)}, u32[]{:S(2)}, u32[]{:S(2)}) collective-permute-start(bf16[32,1152]{1,0:T(8,128)(2,1)} %front.1.refs_0_), channel_id=1, source_target_pairs={{0,24},{8,16},{16,8},{24,0},{1,25},{9,17},{17,9},{25,1},{2,26},{10... | collective-permute-start | bytes 221192 | tf_op jit(solution)/shard_map/ppermute | solution.py:355
  8.3 0.6 collective-permute-start.1
  8.9 2.4 %collective-permute-start = (bf16[32,1024]{1,0:T(8,128)(2,1)}, bf16[32,1024]{1,0:T(8,128)(2,1)S(1)}, u32[]{:S(2)}, u32[]{:S(2)}) collective-permute-start(bf16[32,1024]{1,0:T(8,128)(2,1)} %bitcast.25), channel_id=1, source_target_pairs={{0,16},{8,24},{16,0},{24,8},{1,17},{9,25},{17,1},{25,9},{2,18},{10... | collective-permute-start | bytes 196616 | tf_op jit(solution)/shard_map/ppermute | solution.py:355
  11.2 0.9 %copy-done.4 = bf16[1,32,1024]{2,1,0:T(8,128)(2,1)S(1)} copy-done((bf16[1,32,1024]{2,1,0:T(8,128)(2,1)S(1)}, bf16[1,32,1024]{2,1,0:T(8,128)(2,1)}, u32[]{:S(2)}) %copy-start.4) | copy-done | bytes 65560
  12.1 0.9 %copy-done.3 = bf16[32,1152]{1,0:T(8,128)(2,1)S(1)} copy-done((bf16[32,1152]{1,0:T(8,128)(2,1)S(1)}, bf16[32,1152]{1,0:T(8,128)(2,1)}, u32[]{:S(2)}) %copy-start.3) | copy-done | bytes 73752
  13.0 4.6 %collective-permute-done.refs_1_ = bf16[32,1024]{1,0:T(8,128)(2,1)S(1)} collective-permute-done((bf16[32,1024]{1,0:T(8,128)(2,1)}, bf16[32,1024]{1,0:T(8,128)(2,1)S(1)}, u32[]{:S(2)}, u32[]{:S(2)}) %collective-permute-start) | collective-permute-done | bytes 65568 | tf_op jit(solution)/shard_map/ppermute | solution.py:355
  17.6 0.1 collective-permute-start.4
  17.7 0.0 copy-start.1
  17.7 1.8 %collective-permute-done.4.other_ref.refs_2_ = bf16[192,1152]{1,0:T(8,128)(2,1)S(1)} collective-permute-done((bf16[192,1152]{1,0:T(8,128)(2,1)S(1)}, bf16[192,1152]{1,0:T(8,128)(2,1)S(1)}, u32[]{:S(2)}, u32[]{:S(2)}) %collective-permute-start.4) | collective-permute-done | bytes 442400 | tf_op jit(solution)/shard_map/ppermute | solution.py:364
  19.5 0.5 cot_pick.1
  20.0 1.6 %collective-permute-start.5 = (bf16[48,1024]{1,0:T(8,128)(2,1)S(1)}, bf16[48,1024]{1,0:T(8,128)(2,1)S(1)}, u32[]{:S(2)}, u32[]{:S(2)}) collective-permute-start(bf16[48,1024]{1,0:T(8,128)(2,1)S(1)} %get-tuple-element.47), channel_id=1, source_target_pairs={{0,4},{1,5},{2,6},{3,7},{4,0},{5,1},{6,2},{7,3},{8,12},{9,13},{10,... | collective-permute-start | bytes 294920 | tf_op jit(solution)/shard_map/ppermute | solution.py:360
  21.6 1.5 %collective-permute-start.6 = (bf16[48,1024]{1,0:T(8,128)(2,1)S(1)}, bf16[48,1024]{1,0:T(8,128)(2,1)S(1)}, u32[]{:S(2)}, u32[]{:S(2)}) collective-permute-start(bf16[48,1024]{1,0:T(8,128)(2,1)S(1)} %get-tuple-element.48), channel_id=1, source_target_pairs={{0,2},{1,3},{2,0},{3,1},{4,6},{5,7},{6,4},{7,5},{8,10},{9,11},{10,... | collective-permute-start | bytes 294920 | tf_op jit(solution)/shard_map/ppermute | solution.py:360
  23.1 0.5 collective-permute-start.9
  23.6 0.7 %token_pick.1 = (bf16[96,1152]{1,0:T(8,128)(2,1)S(1)}, bf16[96,1152]{1,0:T(8,128)(2,1)S(1)}, bf16[96,1152]{1,0:T(8,128)(2,1)S(1)}, bf16[96,1152]{1,0:T(8,128)(2,1)S(1)}, bf16[384,256]{1,0:T(8,128)(2,1)S(1)}) custom-call(s32[1]{0:T(128)} %bitcast.4.my_ref, bf16[48,1024]{1,0:T(8,128)(2,1)S(1)} %get-tuple-element.45.refs_0_, ...), custom_call_target="tpu_custom_call" | custom-call | tf_op jit(solution)/shard_map/token_pick/pallas_call | solution.py:26
  24.2 2.5 %collective-permute-start.8 = (bf16[96,1152]{1,0:T(8,128)(2,1)S(1)}, bf16[96,1152]{1,0:T(8,128)(2,1)S(1)}, u32[]{:S(2)}, u32[]{:S(2)}) collective-permute-start(bf16[96,1152]{1,0:T(8,128)(2,1)S(1)} %get-tuple-element.50), channel_id=1, source_target_pairs={{0,6},{1,7},{2,4},{3,5},{4,2},{5,3},{6,0},{7,1},{8,14},{9,15},{10,... | collective-permute-start | bytes 663560 | tf_op jit(solution)/shard_map/ppermute | solution.py:360
  26.8 0.5 collective-permute-start.11
  27.3 0.5 collective-permute-start.12
  27.8 0.1 collective-permute-start.7
  27.9 1.9 %collective-permute-done.9.refs_1_ = bf16[48,1024]{1,0:T(8,128)(2,1)S(1)} collective-permute-done((bf16[48,1024]{1,0:T(8,128)(2,1)S(1)}, bf16[48,1024]{1,0:T(8,128)(2,1)S(1)}, u32[]{:S(2)}, u32[]{:S(2)}) %collective-permute-start.9) | collective-permute-done | bytes 98336 | tf_op jit(solution)/shard_map/ppermute | solution.py:360
  29.8 0.2 collective-permute-start.10
  30.0 0.6 %across.3.refs_5_.refs_4_ = bf16[1024,1024]{1,0:T(8,128)(2,1)S(1)} custom-call(bf16[1024,1024]{1,0:T(8,128)(2,1)S(1)} %bitcast.19), custom_call_target="tpu_custom_call" | custom-call | bytes 6000000 | tf_op jit(solution)/shard_map/across/pallas_call | solution.py:26
  30.6 0.6 %across.2.refs_2_ = bf16[1024,1024]{1,0:T(8,128)(2,1)S(1)} custom-call(bf16[1024,1024]{1,0:T(8,128)(2,1)S(1)} %bitcast.22), custom_call_target="tpu_custom_call" | custom-call | bytes 6000000 | tf_op jit(solution)/shard_map/across/pallas_call | solution.py:26
  31.3 3.2 %collective-permute-done.8.refs_1_ = bf16[96,1152]{1,0:T(8,128)(2,1)S(1)} collective-permute-done((bf16[96,1152]{1,0:T(8,128)(2,1)S(1)}, bf16[96,1152]{1,0:T(8,128)(2,1)S(1)}, u32[]{:S(2)}, u32[]{:S(2)}) %collective-permute-start.8) | collective-permute-done | bytes 221216 | tf_op jit(solution)/shard_map/ppermute | solution.py:360
  34.5 0.8 %hidden.2 = (bf16[192,1024]{1,0:T(8,128)(2,1)S(1)}, bf16[192,128]{1,0:T(8,128)(2,1)S(1)}, bf16[192,1024]{1,0:T(8,128)(2,1)S(1)}, f32[192,1024]{1,0:T(8,128)S(1)}) custom-call(bf16[96,1152]{1,0:T(8,128)(2,1)S(1)} %get-tuple-element.49.refs_0_, bf16[96,1152]{1,0:T(8,128)(2,1)S(1)} %collective-permute-done.8.refs_1_, bf16[1024,1024]{1,0:T(8,128)(2,1)S(1)} %bitcast.20), custom_call_target="tpu_custom_call" | custom-call | bytes 3000000 | tf_op jit(solution)/shard_map/hidden/pallas_call | solution.py:26
  35.3 0.6 upstream.2.refs_0_.refs_3_
  35.9 1.4 %collective-permute-done.10.refs_1_ = bf16[96,1024]{1,0:T(8,128)(2,1)S(1)} collective-permute-done((bf16[96,1024]{1,0:T(8,128)(2,1)S(1)}, bf16[96,1024]{1,0:T(8,128)(2,1)S(1)}, u32[]{:S(2)}, u32[]{:S(2)}) %collective-permute-start.10) | collective-permute-done | bytes 196640 | tf_op jit(solution)/shard_map/ppermute | solution.py:355
  37.4 0.6 upstream.3.refs_4_
  38.0 0.9 %grads.2 = (bf16[96,1024]{1,0:T(8,128)(2,1)S(1)}, bf16[96,1024]{1,0:T(8,128)(2,1)S(1)}, bf16[192,1024]{1,0:T(8,128)(2,1)S(1)}) custom-call(s32[1]{0:T(128)} %bitcast.4.my_ref, f32[192,1024]{1,0:T(8,128)S(1)} %upstream.2.refs_0_.refs_3_, bf16[192,1024]{1,0:T(8,128)(2,1)S(1)} %get-tuple-element.51.refs_1_.refs_2_, f32[192,1024]{1,0:T(8,128)S(1)} %get-tuple-element.52.refs_2_, ...), custom_call_target="tpu_custom_call" | custom-call | tf_op jit(solution)/shard_map/grads/pallas_call | solution.py:26
  38.9 2.5 %collective-permute-start.15 = (bf16[96,1024]{1,0:T(8,128)(2,1)S(1)}, bf16[96,1024]{1,0:T(8,128)(2,1)S(1)}, u32[]{:S(2)}, u32[]{:S(2)}) collective-permute-start(bf16[96,1024]{1,0:T(8,128)(2,1)S(1)} %get-tuple-element.63), channel_id=1, source_target_pairs={{0,6},{1,7},{2,4},{3,5},{4,2},{5,3},{6,0},{7,1},{8,14},{9,15},{10,... | collective-permute-start | bytes 589832 | tf_op jit(solution)/shard_map/ppermute | solution.py:360
  41.4 0.8 %hidden.3 = (bf16[192,1024]{1,0:T(8,128)(2,1)S(1)}, bf16[192,128]{1,0:T(8,128)(2,1)S(1)}, bf16[192,1024]{1,0:T(8,128)(2,1)S(1)}, f32[192,1024]{1,0:T(8,128)S(1)}) custom-call(f32[192,1024]{1,0:T(8,128)S(1)} %upstream.2.refs_0_.refs_3_, bf16[96,1152]{1,0:T(8,128)(2,1)S(1)} %collective-permute-done.11.refs_1_, ...), custom_call_target="tpu_custom_call" | custom-call | bytes 3000000 | tf_op jit(solution)/shard_map/hidden/pallas_call | solution.py:26
  42.2 0.9 %grads.3 = (bf16[96,1024]{1,0:T(8,128)(2,1)S(1)}, bf16[96,1024]{1,0:T(8,128)(2,1)S(1)}, bf16[192,1024]{1,0:T(8,128)(2,1)S(1)}) custom-call(s32[1]{0:T(128)} %bitcast.4.my_ref, bf16[192,1024]{1,0:T(8,128)(2,1)S(1)} %get-tuple-element.58.refs_0_.refs_7_, f32[192,1024]{1,0:T(8,128)S(1)} %get-tuple-element.59.refs_1_, ...), custom_call_target="tpu_custom_call" | custom-call | tf_op jit(solution)/shard_map/grads/pallas_call | solution.py:26
  43.1 0.6 collective-permute-start.13
  43.8 0.5 collective-permute-start.14
  44.3 0.2 stack.1
  44.5 3.3 %fusion = f32[1024,1024]{1,0:T(8,128)} fusion(bf16[384,1024]{1,0:T(8,128)(2,1)S(1)} %get-tuple-element.68, bf16[384,1024]{1,0:T(8,128)(2,1)S(1)} %get-tuple-element.69), kind=kOutput, calls=%fused_computation.1 | convolution fusion | flops 805306368 | bytes 5767168 | tf_op jit(solution)/shard_map/dot_general | solution.py:471
  47.8 1.6 %collective-permute-done.13.refs_1_ = bf16[96,1024]{1,0:T(8,128)(2,1)S(1)} collective-permute-done((bf16[96,1024]{1,0:T(8,128)(2,1)S(1)}, bf16[96,1024]{1,0:T(8,128)(2,1)S(1)}, u32[]{:S(2)}, u32[]{:S(2)}) %collective-permute-start.13) | collective-permute-done | bytes 196640 | tf_op jit(solution)/shard_map/ppermute | solution.py:360
  49.4 0.3 collective-permute-done.14.refs_2_
  49.7 0.3 combine_other.1
  50.0 0.1 collective-permute-start.16
  50.1 0.5 keep.1
  50.6 1.0 %collective-permute-done.16.refs_4_ = bf16[128,1024]{1,0:T(8,128)(2,1)S(1)} collective-permute-done((bf16[128,1024]{1,0:T(8,128)(2,1)S(1)}, bf16[128,1024]{1,0:T(8,128)(2,1)S(1)}, u32[]{:S(2)}, u32[]{:S(2)}) %collective-permute-start.16) | collective-permute-done | bytes 262176 | tf_op jit(solution)/shard_map/ppermute | solution.py:364
  51.6 0.3 combine_own.1
  52.0 2.8 %collective-permute-start.17 = (bf16[32,1024]{1,0:T(8,128)(2,1)S(1)}, bf16[32,1024]{1,0:T(8,128)(2,1)S(1)}, u32[]{:S(2)}, u32[]{:S(2)}) collective-permute-start(bf16[32,1024]{1,0:T(8,128)(2,1)S(1)} %get-tuple-element.75), channel_id=1, source_target_pairs={{0,24},{8,16},{16,8},{24,0},{1,25},{9,17},{17,9},{25,1},{2,26},{10... | collective-permute-start | bytes 196616 | tf_op jit(solution)/shard_map/ppermute | solution.py:355
  54.8 1.6 %collective-permute-start.19 = (bf16[32,1024]{1,0:T(8,128)(2,1)S(1)}, bf16[32,1024]{1,0:T(8,128)(2,1)S(1)}, u32[]{:S(2)}, u32[]{:S(2)}) collective-permute-start(bf16[32,1024]{1,0:T(8,128)(2,1)S(1)} %get-tuple-element.77), channel_id=1, source_target_pairs={{0,16},{8,24},{16,0},{24,8},{1,17},{9,25},{17,1},{25,9},{2,18},{10... | collective-permute-start | bytes 196616 | tf_op jit(solution)/shard_map/ppermute | solution.py:355
  56.4 3.3 %convolution_bitcast_fusion = f32[1,1024,1024]{2,1,0:T(8,128)} fusion(bf16[384,1024]{1,0:T(8,128)(2,1)S(1)} %get-tuple-element.78, bf16[384,1024]{1,0:T(8,128)(2,1)S(1)} %get-tuple-element.79), kind=kOutput, calls=%fused_computation | convolution fusion | flops 805306368 | bytes 5767168 | tf_op jit(solution)/shard_map/dot_general | solution.py:472
  59.7 1.1 %collective-permute-done.18.refs_2_ = bf16[32,1024]{1,0:T(8,128)(2,1)S(1)} collective-permute-done((bf16[32,1024]{1,0:T(8,128)(2,1)S(1)}, bf16[32,1024]{1,0:T(8,128)(2,1)S(1)}, u32[]{:S(2)}, u32[]{:S(2)}) %collective-permute-start.18) | collective-permute-done | bytes 65568 | tf_op jit(solution)/shard_map/ppermute | solution.py:355
  60.8 1.6 %back.1 = bf16[128,1024]{1,0:T(8,128)(2,1)} custom-call(bf16[128,1024]{1,0:T(8,128)(2,1)S(1)} %get-tuple-element.42.ordered_ref, f32[1,1024]{1,0:T(1,128)S(1)} %bitcast.33, f32[1,1024]{1,0:T(1,128)S(1)} %bitcast.35, f32[32,1024]{1,0:T(8,128)S(1)} %get-tuple-element.43.tok_ref, f32[32,128]{1,0:T(8,128)S(1)} %get-tuple-element.44.keep_ref, ...), custom_call_target="tpu_custom_call" | custom-call | tf_op jit(solution)/shard_map/back/pallas_call | solution.py:26
  (33 shorter events, 0.1 us)
Async XLA Ops:
  0.6 29.4 %copy-start = (bf16[1,1024,1024]{2,1,0:T(8,128)(2,1)S(1)}, bf16[1,1024,1024]{2,1,0:T(8,128)(2,1)}, u32[]{:S(2)}) copy-start(bf16[1,1024,1024]{2,1,0:T(8,128)(2,1)} %param.13) | copy-start | bytes 6291460
  3.3 14.3 %collective-permute-start.3 = (bf16[32,1152]{1,0:T(8,128)(2,1)}, bf16[32,1152]{1,0:T(8,128)(2,1)S(1)}, u32[]{:S(2)}, u32[]{:S(2)}) collective-permute-start(bf16[32,1152]{1,0:T(8,128)(2,1)} %front.1.refs_0_), channel_id=1, source_target_pairs={{0,24},{8,16},{16,8},{24,0},{1,25},{9,17},{17,9},{25,1},{2,26},{10... | collective-permute-start | bytes 221192 | tf_op jit(solution)/shard_map/ppermute | solution.py:355
  8.3 9.3 %collective-permute-start.2 = (bf16[32,1152]{1,0:T(8,128)(2,1)}, bf16[32,1152]{1,0:T(8,128)(2,1)S(1)}, u32[]{:S(2)}, u32[]{:S(2)}) collective-permute-start(bf16[32,1152]{1,0:T(8,128)(2,1)} %front.1.refs_0_), channel_id=1, source_target_pairs={{0,8},{8,0},{16,24},{24,16},{1,9},{9,1},{17,25},{25,17},{2,10},{10... | collective-permute-start | bytes 221192 | tf_op jit(solution)/shard_map/ppermute | solution.py:355
  8.3 9.3 %collective-permute-start.1 = (bf16[32,1152]{1,0:T(8,128)(2,1)}, bf16[32,1152]{1,0:T(8,128)(2,1)S(1)}, u32[]{:S(2)}, u32[]{:S(2)}) collective-permute-start(bf16[32,1152]{1,0:T(8,128)(2,1)} %front.1.refs_0_), channel_id=1, source_target_pairs={{0,16},{8,24},{16,0},{24,8},{1,17},{9,25},{17,1},{25,9},{2,18},{10... | collective-permute-start | bytes 221192 | tf_op jit(solution)/shard_map/ppermute | solution.py:355
  8.9 8.7 %collective-permute-start = (bf16[32,1024]{1,0:T(8,128)(2,1)}, bf16[32,1024]{1,0:T(8,128)(2,1)S(1)}, u32[]{:S(2)}, u32[]{:S(2)}) collective-permute-start(bf16[32,1024]{1,0:T(8,128)(2,1)} %bitcast.25), channel_id=1, source_target_pairs={{0,16},{8,24},{16,0},{24,8},{1,17},{9,25},{17,1},{25,9},{2,18},{10... | collective-permute-start | bytes 196616 | tf_op jit(solution)/shard_map/ppermute | solution.py:355
  11.2 0.9 %copy-start.4 = (bf16[1,32,1024]{2,1,0:T(8,128)(2,1)S(1)}, bf16[1,32,1024]{2,1,0:T(8,128)(2,1)}, u32[]{:S(2)}) copy-start(bf16[1,32,1024]{2,1,0:T(8,128)(2,1)} %param.15) | copy-start | bytes 196612
  12.1 0.9 %copy-start.3 = (bf16[32,1152]{1,0:T(8,128)(2,1)S(1)}, bf16[32,1152]{1,0:T(8,128)(2,1)}, u32[]{:S(2)}) copy-start(bf16[32,1152]{1,0:T(8,128)(2,1)} %front.1.refs_0_) | copy-start | bytes 221188
  17.6 1.9 %collective-permute-start.4 = (bf16[192,1152]{1,0:T(8,128)(2,1)S(1)}, bf16[192,1152]{1,0:T(8,128)(2,1)S(1)}, u32[]{:S(2)}, u32[]{:S(2)}) collective-permute-start(bf16[192,1152]{1,0:T(8,128)(2,1)S(1)} %near.1.own_ref.refs_1_), channel_id=1, source_target_pairs={{0,1},{1,0},{2,3},{3,2},{4,5},{5,4},{6,7},{7,6},{8,9},{9,8},{10,11... | collective-permute-start | bytes 1327112 | tf_op jit(solution)/shard_map/ppermute | solution.py:364
  17.7 12.9 %copy-start.1 = (bf16[1,1024,1024]{2,1,0:T(8,128)(2,1)S(1)}, bf16[1,1024,1024]{2,1,0:T(8,128)(2,1)}, u32[]{:S(2)}) copy-start(bf16[1,1024,1024]{2,1,0:T(8,128)(2,1)} %param.14) | copy-start | bytes 6291460
  20.0 7.3 %collective-permute-start.5 = (bf16[48,1024]{1,0:T(8,128)(2,1)S(1)}, bf16[48,1024]{1,0:T(8,128)(2,1)S(1)}, u32[]{:S(2)}, u32[]{:S(2)}) collective-permute-start(bf16[48,1024]{1,0:T(8,128)(2,1)S(1)} %get-tuple-element.47), channel_id=1, source_target_pairs={{0,4},{1,5},{2,6},{3,7},{4,0},{5,1},{6,2},{7,3},{8,12},{9,13},{10,... | collective-permute-start | bytes 294920 | tf_op jit(solution)/shard_map/ppermute | solution.py:360
  21.6 6.2 %collective-permute-start.6 = (bf16[48,1024]{1,0:T(8,128)(2,1)S(1)}, bf16[48,1024]{1,0:T(8,128)(2,1)S(1)}, u32[]{:S(2)}, u32[]{:S(2)}) collective-permute-start(bf16[48,1024]{1,0:T(8,128)(2,1)S(1)} %get-tuple-element.48), channel_id=1, source_target_pairs={{0,2},{1,3},{2,0},{3,1},{4,6},{5,7},{6,4},{7,5},{8,10},{9,11},{10,... | collective-permute-start | bytes 294920 | tf_op jit(solution)/shard_map/ppermute | solution.py:360
  23.1 6.7 %collective-permute-start.9 = (bf16[48,1024]{1,0:T(8,128)(2,1)S(1)}, bf16[48,1024]{1,0:T(8,128)(2,1)S(1)}, u32[]{:S(2)}, u32[]{:S(2)}) collective-permute-start(bf16[48,1024]{1,0:T(8,128)(2,1)S(1)} %get-tuple-element.54), channel_id=1, source_target_pairs={{0,6},{1,7},{2,4},{3,5},{4,2},{5,3},{6,0},{7,1},{8,14},{9,15},{10,... | collective-permute-start | bytes 294920 | tf_op jit(solution)/shard_map/ppermute | solution.py:360
  24.2 10.3 %collective-permute-start.8 = (bf16[96,1152]{1,0:T(8,128)(2,1)S(1)}, bf16[96,1152]{1,0:T(8,128)(2,1)S(1)}, u32[]{:S(2)}, u32[]{:S(2)}) collective-permute-start(bf16[96,1152]{1,0:T(8,128)(2,1)S(1)} %get-tuple-element.50), channel_id=1, source_target_pairs={{0,6},{1,7},{2,4},{3,5},{4,2},{5,3},{6,0},{7,1},{8,14},{9,15},{10,... | collective-permute-start | bytes 663560 | tf_op jit(solution)/shard_map/ppermute | solution.py:360
  26.8 14.6 %collective-permute-start.11 = (bf16[96,1152]{1,0:T(8,128)(2,1)S(1)}, bf16[96,1152]{1,0:T(8,128)(2,1)S(1)}, u32[]{:S(2)}, u32[]{:S(2)}) collective-permute-start(bf16[96,1152]{1,0:T(8,128)(2,1)S(1)} %get-tuple-element.56), channel_id=1, source_target_pairs={{0,4},{1,5},{2,6},{3,7},{4,0},{5,1},{6,2},{7,3},{8,12},{9,13},{10,... | collective-permute-start | bytes 663560 | tf_op jit(solution)/shard_map/ppermute | solution.py:360
  27.3 14.1 %collective-permute-start.12 = (bf16[96,1152]{1,0:T(8,128)(2,1)S(1)}, bf16[96,1152]{1,0:T(8,128)(2,1)S(1)}, u32[]{:S(2)}, u32[]{:S(2)}) collective-permute-start(bf16[96,1152]{1,0:T(8,128)(2,1)S(1)} %get-tuple-element.57), channel_id=1, source_target_pairs={{0,2},{1,3},{2,0},{3,1},{4,6},{5,7},{6,4},{7,5},{8,10},{9,11},{10,... | collective-permute-start | bytes 663560 | tf_op jit(solution)/shard_map/ppermute | solution.py:360
  27.8 7.5 %collective-permute-start.7 = (bf16[96,1024]{1,0:T(8,128)(2,1)S(1)}, bf16[96,1024]{1,0:T(8,128)(2,1)S(1)}, u32[]{:S(2)}, u32[]{:S(2)}) collective-permute-start(bf16[96,1024]{1,0:T(8,128)(2,1)S(1)} %cot_slots.2.refs_0_.refs_5_), channel_id=1, source_target_pairs={{0,8},{8,0},{16,24},{24,16},{1,9},{9,1},{17,25},{25,17},{2,10},{10... | collective-permute-start | bytes 589832 | tf_op jit(solution)/shard_map/ppermute | solution.py:355
  29.8 7.5 %collective-permute-start.10 = (bf16[96,1024]{1,0:T(8,128)(2,1)S(1)}, bf16[96,1024]{1,0:T(8,128)(2,1)S(1)}, u32[]{:S(2)}, u32[]{:S(2)}) collective-permute-start(bf16[96,1024]{1,0:T(8,128)(2,1)S(1)} %cot_slots.3.refs_0_), channel_id=1, source_target_pairs={{0,8},{8,0},{16,24},{24,16},{1,9},{9,1},{17,25},{25,17},{2,10},{10... | collective-permute-start | bytes 589832 | tf_op jit(solution)/shard_map/ppermute | solution.py:355
  34.5 3.5 %copy-start.6 = (bf16[1024,8]{0,1:T(8,128)(2,1)S(1)}, bf16[1024,8]{0,1:T(8,128)(2,1)}, u32[]{:S(2)}) copy-start(bf16[1024,8]{0,1:T(8,128)(2,1)} %param.11) | copy-start | bytes 49156
  38.9 8.9 %collective-permute-start.15 = (bf16[96,1024]{1,0:T(8,128)(2,1)S(1)}, bf16[96,1024]{1,0:T(8,128)(2,1)S(1)}, u32[]{:S(2)}, u32[]{:S(2)}) collective-permute-start(bf16[96,1024]{1,0:T(8,128)(2,1)S(1)} %get-tuple-element.63), channel_id=1, source_target_pairs={{0,6},{1,7},{2,4},{3,5},{4,2},{5,3},{6,0},{7,1},{8,14},{9,15},{10,... | collective-permute-start | bytes 589832 | tf_op jit(solution)/shard_map/ppermute | solution.py:360
  43.1 6.2 %collective-permute-start.13 = (bf16[96,1024]{1,0:T(8,128)(2,1)S(1)}, bf16[96,1024]{1,0:T(8,128)(2,1)S(1)}, u32[]{:S(2)}, u32[]{:S(2)}) collective-permute-start(bf16[96,1024]{1,0:T(8,128)(2,1)S(1)} %get-tuple-element.61), channel_id=1, source_target_pairs={{0,2},{1,3},{2,0},{3,1},{4,6},{5,7},{6,4},{7,5},{8,10},{9,11},{10,... | collective-permute-start | bytes 589832 | tf_op jit(solution)/shard_map/ppermute | solution.py:360
  43.8 6.0 %collective-permute-start.14 = (bf16[96,1024]{1,0:T(8,128)(2,1)S(1)}, bf16[96,1024]{1,0:T(8,128)(2,1)S(1)}, u32[]{:S(2)}, u32[]{:S(2)}) collective-permute-start(bf16[96,1024]{1,0:T(8,128)(2,1)S(1)} %get-tuple-element.62), channel_id=1, source_target_pairs={{0,4},{1,5},{2,6},{3,7},{4,0},{5,1},{6,2},{7,3},{8,12},{9,13},{10,... | collective-permute-start | bytes 589832 | tf_op jit(solution)/shard_map/ppermute | solution.py:360
  44.5 5.7 %copy-start.2 = (bf16[1,128,1024]{2,1,0:T(8,128)(2,1)S(1)}, bf16[1,128,1024]{2,1,0:T(8,128)(2,1)}, u32[]{:S(2)}) copy-start(bf16[1,128,1024]{2,1,0:T(8,128)(2,1)} %param.8) | copy-start | bytes 786436
  44.5 5.7 %copy-start.7 = (f32[1024]{0:T(1024)S(1)}, f32[1024]{0:T(1024)}, u32[]{:S(2)}) copy-start(f32[1024]{0:T(1024)} %param.9) | copy-start | bytes 12292
  49.7 11.1 %copy-start.5 = (bf16[1,32,1024]{2,1,0:T(8,128)(2,1)S(1)}, bf16[1,32,1024]{2,1,0:T(8,128)(2,1)}, u32[]{:S(2)}) copy-start(bf16[1,32,1024]{2,1,0:T(8,128)(2,1)} %param.15) | copy-start | bytes 196612
  49.7 11.1 %copy-start.8 = (f32[1024]{0:T(1024)S(1)}, f32[1024]{0:T(1024)}, u32[]{:S(2)}) copy-start(f32[1024]{0:T(1024)} %param.10) | copy-start | bytes 12292
  50.0 1.6 %collective-permute-start.16 = (bf16[128,1024]{1,0:T(8,128)(2,1)S(1)}, bf16[128,1024]{1,0:T(8,128)(2,1)S(1)}, u32[]{:S(2)}, u32[]{:S(2)}) collective-permute-start(bf16[128,1024]{1,0:T(8,128)(2,1)S(1)} %combine_other.1), channel_id=1, source_target_pairs={{0,1},{1,0},{2,3},{3,2},{4,5},{5,4},{6,7},{7,6},{8,9},{9,8},{10,11... | collective-permute-start | bytes 786440 | tf_op jit(solution)/shard_map/ppermute | solution.py:364
  52.0 7.8 %collective-permute-start.17 = (bf16[32,1024]{1,0:T(8,128)(2,1)S(1)}, bf16[32,1024]{1,0:T(8,128)(2,1)S(1)}, u32[]{:S(2)}, u32[]{:S(2)}) collective-permute-start(bf16[32,1024]{1,0:T(8,128)(2,1)S(1)} %get-tuple-element.75), channel_id=1, source_target_pairs={{0,24},{8,16},{16,8},{24,0},{1,25},{9,17},{17,9},{25,1},{2,26},{10... | collective-permute-start | bytes 196616 | tf_op jit(solution)/shard_map/ppermute | solution.py:355
  54.8 6.0 %collective-permute-start.18 = (bf16[32,1024]{1,0:T(8,128)(2,1)S(1)}, bf16[32,1024]{1,0:T(8,128)(2,1)S(1)}, u32[]{:S(2)}, u32[]{:S(2)}) collective-permute-start(bf16[32,1024]{1,0:T(8,128)(2,1)S(1)} %get-tuple-element.76), channel_id=1, source_target_pairs={{0,8},{8,0},{16,24},{24,16},{1,9},{9,1},{17,25},{25,17},{2,10},{10... | collective-permute-start | bytes 196616 | tf_op jit(solution)/shard_map/ppermute | solution.py:355
  54.8 6.0 %collective-permute-start.19 = (bf16[32,1024]{1,0:T(8,128)(2,1)S(1)}, bf16[32,1024]{1,0:T(8,128)(2,1)S(1)}, u32[]{:S(2)}, u32[]{:S(2)}) collective-permute-start(bf16[32,1024]{1,0:T(8,128)(2,1)S(1)} %get-tuple-element.77), channel_id=1, source_target_pairs={{0,16},{8,24},{16,0},{24,8},{1,17},{9,25},{17,1},{25,9},{2,18},{10... | collective-permute-start | bytes 196616 | tf_op jit(solution)/shard_map/ppermute | solution.py:355

commit v8 on v6

--- a/solution.py
+++ b/solution.py
@@ -260,7 +260,7 @@
     ins, out_ref = refs[:-1], refs[-1]
     tokens = out_ref.shape[0]
     rows = jnp.concatenate([r[...] for r in ins], axis=0)
-    out_ref[...] = lax.dot_general(pick_ref[:, tokens:], rows, ROWS_T, preferred_element_type=F32).astype(BF)
+    out_ref[...] = jnp.dot(pick_ref[tokens:, :], rows, preferred_element_type=F32).astype(BF)
 
 
 def combine_own_kernel(chunks, pick_ref, *refs):
@@ -268,7 +268,7 @@
     tokens = other_ref.shape[0]
     count = outs[0].shape[0]
     rows = jnp.concatenate([r[...] for r in ins], axis=0)
-    back = lax.dot_general(pick_ref[:, :tokens], rows, ROWS_T, preferred_element_type=F32)
+    back = jnp.dot(pick_ref[:tokens, :], rows, preferred_element_type=F32)
     back = (back + other_ref[...].astype(F32)).astype(BF)
     for k, out in enumerate(outs):
         out[...] = back[k * count : (k + 1) * count, :]
@@ -403,6 +403,7 @@
         limit=16,
     )
     token_chunks = over_exp(chosen, 2)
+    pick_across = call(transpose_kernel, "across", shape(2 * tokens, slots), (pick,), us=1.0)
     order = [0, *range(chunks - 1, 0, -1)]
     groups = (order[: chunks // 2], order[chunks // 2 :])
     part = slots // 2
@@ -462,12 +463,12 @@
     grad_in = lax.dot_general(token_slots, hidden_grad, ROWS_T, preferred_element_type=F32)
     returned = over_exp(back_rows, 2)
     *returned, grad_out = lax.optimization_barrier((*returned, grad_out))
-    other_rows = call(combine_other_kernel, "combine_other", shape(tokens, width), (pick, *returned), limit=16)
+    other_rows = call(combine_other_kernel, "combine_other", shape(tokens, width), (pick_across, *returned), limit=16)
     partial_rows = call(
         functools.partial(combine_own_kernel, chunks),
         "combine_own",
         [shape(count, width)] * pieces,
-        (pick, *returned, over_cores(other_rows)),
+        (pick_across, *returned, over_cores(other_rows)),
         limit=16,
     )
     parts = [partial_rows[0]] + [over_seq(partial_rows[i], places[i]) for i in range(pieces - 1, 0, -1)]

time: 62.7 us -> 62.6 us (level)
    pallas_call x22 -> x23, Pallas kernels: 12.7 us -> 12.8 us  [call(): pl.pallas_call(body, name=name, out_shape=outs, in_specs=[smem] * scalars...]
where the time goes in v8:
time: 62.6 us; the launch traced here: 62.4 us
  starting transfers between devices  24.1 us (38%)
  waiting for transfers between devices  16.3 us (26%)
  Pallas kernels  12.8 us (20%)
  matrix products  6.61 us (11%)
  local copies, waits for them, and re-layouts  1.79 us (3%)
  between operations  0.89 us (1%)
    pallas_call x23, Pallas kernels, call(): pl.pallas_call(body, name=name, out_shape=outs, in_specs=[smem] * scalars...  12.8 us
    ppermute x9, starting transfers between devices, over_seq(): return lax.ppermute(value, 'seq', [(i, i ^ k) for i in range(pieces)])  12.7 us
    ppermute x9, starting transfers between devices, over_exp(): lax.ppermute(values[m], 'exp', [(i, i ^ m * step) for i in range(owners)])  10.7 us
    ppermute x9, waiting for transfers between devices, over_seq(): return lax.ppermute(value, 'seq', [(i, i ^ k) for i in range(pieces)])  7.08 us
    ppermute x9, waiting for transfers between devices, over_exp(): lax.ppermute(values[m], 'exp', [(i, i ^ m * step) for i in range(owners)])  6.92 us
    dot_general x1, matrix products, per_device(): lax.dot_general(hidden_rows, cot_slots, ROWS_T, preferred_element_type=F32)  3.31 us
    dot_general x1, matrix products, per_device(): lax.dot_general(token_slots, hidden_grad, ROWS_T, preferred_element_type=...  3.3 us
    ppermute x3, waiting for transfers between devices, over_cores(): return lax.ppermute(value, 'exp', [(i, i ^ 1) for i in range(owners)])  2.28 us
  transfers between devices with their start and end apart: 21, of which 9 were waited for; matrix products, arithmetic and copies ran while one was open for 11% of the time, Pallas kernels for 12%

profile of v8, /device:TPU:0, one launch (start us, length us, event | category | flops | bytes accessed | tf_op | source)
XLA Modules:
  0.0 62.4 jit_solution(8340687899771193574)
XLA Ops:
  0.6 2.6 %front.1.refs_0_ = bf16[32,1152]{1,0:T(8,128)(2,1)} custom-call(bf16[128,1024]{1,0:T(8,128)(2,1)} %bitcast.22, f32[1,1024]{1,0:T(1,128)} %bitcast.32, f32[1,1024]{1,0:T(1,128)} %bitcast.35, bf16[8,1024]{1,0:T(8,128)(2,1)} %bitcast.29, s32[2,32]{1,0:T(2,128)} %bitcast.39), custom_call_target="tpu_custom_call" | custom-call | bytes 6000000 | tf_op jit(solution)/shard_map/front/pallas_call | solution.py:26
  3.3 5.0 %collective-permute-start.3 = (bf16[32,1152]{1,0:T(8,128)(2,1)}, bf16[32,1152]{1,0:T(8,128)(2,1)S(1)}, u32[]{:S(2)}, u32[]{:S(2)}) collective-permute-start(bf16[32,1152]{1,0:T(8,128)(2,1)} %front.1.refs_0_), channel_id=1, source_target_pairs={{0,24},{8,16},{16,8},{24,0},{1,25},{9,17},{17,9},{25,1},{2,26},{10... | collective-permute-start | bytes 221192 | tf_op jit(solution)/shard_map/ppermute | solution.py:342
  8.3 0.6 collective-permute-start.1
  8.9 2.4 %collective-permute-start = (bf16[32,1024]{1,0:T(8,128)(2,1)}, bf16[32,1024]{1,0:T(8,128)(2,1)S(1)}, u32[]{:S(2)}, u32[]{:S(2)}) collective-permute-start(bf16[32,1024]{1,0:T(8,128)(2,1)} %bitcast.26), channel_id=1, source_target_pairs={{0,16},{8,24},{16,0},{24,8},{1,17},{9,25},{17,1},{25,9},{2,18},{10... | collective-permute-start | bytes 196616 | tf_op jit(solution)/shard_map/ppermute | solution.py:342
  11.2 0.9 %copy-done.4 = bf16[1,32,1024]{2,1,0:T(8,128)(2,1)S(1)} copy-done((bf16[1,32,1024]{2,1,0:T(8,128)(2,1)S(1)}, bf16[1,32,1024]{2,1,0:T(8,128)(2,1)}, u32[]{:S(2)}) %copy-start.4) | copy-done | bytes 65560
  12.1 0.9 %copy-done.3 = bf16[32,1152]{1,0:T(8,128)(2,1)S(1)} copy-done((bf16[32,1152]{1,0:T(8,128)(2,1)S(1)}, bf16[32,1152]{1,0:T(8,128)(2,1)}, u32[]{:S(2)}) %copy-start.3) | copy-done | bytes 73752
  13.0 4.6 %collective-permute-done.refs_1_ = bf16[32,1024]{1,0:T(8,128)(2,1)S(1)} collective-permute-done((bf16[32,1024]{1,0:T(8,128)(2,1)}, bf16[32,1024]{1,0:T(8,128)(2,1)S(1)}, u32[]{:S(2)}, u32[]{:S(2)}) %collective-permute-start) | collective-permute-done | bytes 65568 | tf_op jit(solution)/shard_map/ppermute | solution.py:342
  17.7 0.1 collective-permute-start.5
  17.7 0.5 collective-permute-start.4
  18.2 1.3 %collective-permute-done.4.other_cot_ref = bf16[64,1024]{1,0:T(8,128)(2,1)S(1)} collective-permute-done((bf16[64,1024]{1,0:T(8,128)(2,1)S(1)}, bf16[64,1024]{1,0:T(8,128)(2,1)S(1)}, u32[]{:S(2)}, u32[]{:S(2)}) %collective-permute-start.4) | collective-permute-done | bytes 131104 | tf_op jit(solution)/shard_map/ppermute | solution.py:351
  19.5 0.5 cot_pick.1
  20.0 1.6 %collective-permute-start.6 = (bf16[48,1024]{1,0:T(8,128)(2,1)S(1)}, bf16[48,1024]{1,0:T(8,128)(2,1)S(1)}, u32[]{:S(2)}, u32[]{:S(2)}) collective-permute-start(bf16[48,1024]{1,0:T(8,128)(2,1)S(1)} %get-tuple-element.45), channel_id=1, source_target_pairs={{0,4},{1,5},{2,6},{3,7},{4,0},{5,1},{6,2},{7,3},{8,12},{9,13},{10,... | collective-permute-start | bytes 294920 | tf_op jit(solution)/shard_map/ppermute | solution.py:347
  21.6 1.5 %collective-permute-start.7 = (bf16[48,1024]{1,0:T(8,128)(2,1)S(1)}, bf16[48,1024]{1,0:T(8,128)(2,1)S(1)}, u32[]{:S(2)}, u32[]{:S(2)}) collective-permute-start(bf16[48,1024]{1,0:T(8,128)(2,1)S(1)} %get-tuple-element.46), channel_id=1, source_target_pairs={{0,2},{1,3},{2,0},{3,1},{4,6},{5,7},{6,4},{7,5},{8,10},{9,11},{10,... | collective-permute-start | bytes 294920 | tf_op jit(solution)/shard_map/ppermute | solution.py:347
  23.1 0.5 collective-permute-start.10
  23.6 0.7 %token_pick.1 = (bf16[96,1152]{1,0:T(8,128)(2,1)S(1)}, bf16[96,1152]{1,0:T(8,128)(2,1)S(1)}, bf16[96,1152]{1,0:T(8,128)(2,1)S(1)}, bf16[96,1152]{1,0:T(8,128)(2,1)S(1)}, bf16[384,256]{1,0:T(8,128)(2,1)S(1)}) custom-call(s32[1]{0:T(128)} %bitcast.4.my_ref, bf16[48,1024]{1,0:T(8,128)(2,1)S(1)} %get-tuple-element.43.refs_0_, ...), custom_call_target="tpu_custom_call" | custom-call | tf_op jit(solution)/shard_map/token_pick/pallas_call | solution.py:26
  24.2 2.5 %collective-permute-start.9 = (bf16[96,1152]{1,0:T(8,128)(2,1)S(1)}, bf16[96,1152]{1,0:T(8,128)(2,1)S(1)}, u32[]{:S(2)}, u32[]{:S(2)}) collective-permute-start(bf16[96,1152]{1,0:T(8,128)(2,1)S(1)} %get-tuple-element.48), channel_id=1, source_target_pairs={{0,6},{1,7},{2,4},{3,5},{4,2},{5,3},{6,0},{7,1},{8,14},{9,15},{10,... | collective-permute-start | bytes 663560 | tf_op jit(solution)/shard_map/ppermute | solution.py:347
  26.8 0.5 collective-permute-start.12
  27.3 0.5 collective-permute-start.13
  27.8 0.1 collective-permute-start.8
  27.9 1.9 %collective-permute-done.10.refs_1_ = bf16[48,1024]{1,0:T(8,128)(2,1)S(1)} collective-permute-done((bf16[48,1024]{1,0:T(8,128)(2,1)S(1)}, bf16[48,1024]{1,0:T(8,128)(2,1)S(1)}, u32[]{:S(2)}, u32[]{:S(2)}) %collective-permute-start.10) | collective-permute-done | bytes 98336 | tf_op jit(solution)/shard_map/ppermute | solution.py:347
  29.8 0.2 collective-permute-start.11
  30.0 0.6 %across.5.refs_5_.refs_4_ = bf16[1024,1024]{1,0:T(8,128)(2,1)S(1)} custom-call(bf16[1024,1024]{1,0:T(8,128)(2,1)S(1)} %bitcast.19), custom_call_target="tpu_custom_call" | custom-call | bytes 6000000 | tf_op jit(solution)/shard_map/across/pallas_call | solution.py:26
  30.6 0.6 %across.4.refs_2_ = bf16[1024,1024]{1,0:T(8,128)(2,1)S(1)} custom-call(bf16[1024,1024]{1,0:T(8,128)(2,1)S(1)} %bitcast.25), custom_call_target="tpu_custom_call" | custom-call | bytes 6000000 | tf_op jit(solution)/shard_map/across/pallas_call | solution.py:26
  31.3 0.1 across.3.pick_ref
  31.4 3.1 %collective-permute-done.9.refs_1_ = bf16[96,1152]{1,0:T(8,128)(2,1)S(1)} collective-permute-done((bf16[96,1152]{1,0:T(8,128)(2,1)S(1)}, bf16[96,1152]{1,0:T(8,128)(2,1)S(1)}, u32[]{:S(2)}, u32[]{:S(2)}) %collective-permute-start.9) | collective-permute-done | bytes 221216 | tf_op jit(solution)/shard_map/ppermute | solution.py:347
  34.5 0.8 %hidden.2 = (bf16[192,1024]{1,0:T(8,128)(2,1)S(1)}, bf16[192,128]{1,0:T(8,128)(2,1)S(1)}, bf16[192,1024]{1,0:T(8,128)(2,1)S(1)}, f32[192,1024]{1,0:T(8,128)S(1)}) custom-call(bf16[96,1152]{1,0:T(8,128)(2,1)S(1)} %get-tuple-element.47.refs_0_, bf16[96,1152]{1,0:T(8,128)(2,1)S(1)} %collective-permute-done.9.refs_1_, bf16[1024,1024]{1,0:T(8,128)(2,1)S(1)} %bitcast.20), custom_call_target="tpu_custom_call" | custom-call | bytes 3000000 | tf_op jit(solution)/shard_map/hidden/pallas_call | solution.py:26
  35.3 0.6 upstream.2.refs_0_.refs_3_
  35.9 1.4 %collective-permute-done.11.refs_1_ = bf16[96,1024]{1,0:T(8,128)(2,1)S(1)} collective-permute-done((bf16[96,1024]{1,0:T(8,128)(2,1)S(1)}, bf16[96,1024]{1,0:T(8,128)(2,1)S(1)}, u32[]{:S(2)}, u32[]{:S(2)}) %collective-permute-start.11) | collective-permute-done | bytes 196640 | tf_op jit(solution)/shard_map/ppermute | solution.py:342
  37.4 0.6 upstream.3.refs_4_
  38.0 0.9 %grads.2 = (bf16[96,1024]{1,0:T(8,128)(2,1)S(1)}, bf16[96,1024]{1,0:T(8,128)(2,1)S(1)}, bf16[192,1024]{1,0:T(8,128)(2,1)S(1)}) custom-call(s32[1]{0:T(128)} %bitcast.4.my_ref, f32[192,1024]{1,0:T(8,128)S(1)} %upstream.2.refs_0_.refs_3_, bf16[192,1024]{1,0:T(8,128)(2,1)S(1)} %get-tuple-element.49.refs_1_.refs_2_, f32[192,1024]{1,0:T(8,128)S(1)} %get-tuple-element.50.refs_2_, ...), custom_call_target="tpu_custom_call" | custom-call | tf_op jit(solution)/shard_map/grads/pallas_call | solution.py:26
  38.9 2.5 %collective-permute-start.16 = (bf16[96,1024]{1,0:T(8,128)(2,1)S(1)}, bf16[96,1024]{1,0:T(8,128)(2,1)S(1)}, u32[]{:S(2)}, u32[]{:S(2)}) collective-permute-start(bf16[96,1024]{1,0:T(8,128)(2,1)S(1)} %get-tuple-element.61), channel_id=1, source_target_pairs={{0,6},{1,7},{2,4},{3,5},{4,2},{5,3},{6,0},{7,1},{8,14},{9,15},{10,... | collective-permute-start | bytes 589832 | tf_op jit(solution)/shard_map/ppermute | solution.py:347
  41.4 0.8 %hidden.3 = (bf16[192,1024]{1,0:T(8,128)(2,1)S(1)}, bf16[192,128]{1,0:T(8,128)(2,1)S(1)}, bf16[192,1024]{1,0:T(8,128)(2,1)S(1)}, f32[192,1024]{1,0:T(8,128)S(1)}) custom-call(f32[192,1024]{1,0:T(8,128)S(1)} %upstream.2.refs_0_.refs_3_, bf16[96,1152]{1,0:T(8,128)(2,1)S(1)} %collective-permute-done.12.refs_1_, ...), custom_call_target="tpu_custom_call" | custom-call | bytes 3000000 | tf_op jit(solution)/shard_map/hidden/pallas_call | solution.py:26
  42.2 0.9 %grads.3 = (bf16[96,1024]{1,0:T(8,128)(2,1)S(1)}, bf16[96,1024]{1,0:T(8,128)(2,1)S(1)}, bf16[192,1024]{1,0:T(8,128)(2,1)S(1)}) custom-call(s32[1]{0:T(128)} %bitcast.4.my_ref, bf16[192,1024]{1,0:T(8,128)(2,1)S(1)} %get-tuple-element.56.refs_0_.refs_7_, f32[192,1024]{1,0:T(8,128)S(1)} %get-tuple-element.57.refs_1_, ...), custom_call_target="tpu_custom_call" | custom-call | tf_op jit(solution)/shard_map/grads/pallas_call | solution.py:26
  43.1 0.6 collective-permute-start.14
  43.7 0.5 collective-permute-start.15
  44.3 0.2 stack.1
  44.5 3.3 %fusion = f32[1024,1024]{1,0:T(8,128)} fusion(bf16[384,1024]{1,0:T(8,128)(2,1)S(1)} %get-tuple-element.66, bf16[384,1024]{1,0:T(8,128)(2,1)S(1)} %get-tuple-element.67), kind=kOutput, calls=%fused_computation.1 | convolution fusion | flops 805306368 | bytes 5767168 | tf_op jit(solution)/shard_map/dot_general | solution.py:462
  47.8 1.6 %collective-permute-done.14.refs_1_ = bf16[96,1024]{1,0:T(8,128)(2,1)S(1)} collective-permute-done((bf16[96,1024]{1,0:T(8,128)(2,1)S(1)}, bf16[96,1024]{1,0:T(8,128)(2,1)S(1)}, u32[]{:S(2)}, u32[]{:S(2)}) %collective-permute-start.14) | collective-permute-done | bytes 196640 | tf_op jit(solution)/shard_map/ppermute | solution.py:347
  49.4 0.4 collective-permute-done.15.refs_2_
  49.7 0.3 combine_other.1
  50.1 0.5 keep.1
  50.6 1.0 %collective-permute-done.17.refs_4_ = bf16[128,1024]{1,0:T(8,128)(2,1)S(1)} collective-permute-done((bf16[128,1024]{1,0:T(8,128)(2,1)S(1)}, bf16[128,1024]{1,0:T(8,128)(2,1)S(1)}, u32[]{:S(2)}, u32[]{:S(2)}) %collective-permute-start.17) | collective-permute-done | bytes 262176 | tf_op jit(solution)/shard_map/ppermute | solution.py:351
  51.6 0.3 combine_own.1
  51.9 2.8 %collective-permute-start.18 = (bf16[32,1024]{1,0:T(8,128)(2,1)S(1)}, bf16[32,1024]{1,0:T(8,128)(2,1)S(1)}, u32[]{:S(2)}, u32[]{:S(2)}) collective-permute-start(bf16[32,1024]{1,0:T(8,128)(2,1)S(1)} %get-tuple-element.73), channel_id=1, source_target_pairs={{0,24},{8,16},{16,8},{24,0},{1,25},{9,17},{17,9},{25,1},{2,26},{10... | collective-permute-start | bytes 196616 | tf_op jit(solution)/shard_map/ppermute | solution.py:342
  54.8 1.6 %collective-permute-start.20 = (bf16[32,1024]{1,0:T(8,128)(2,1)S(1)}, bf16[32,1024]{1,0:T(8,128)(2,1)S(1)}, u32[]{:S(2)}, u32[]{:S(2)}) collective-permute-start(bf16[32,1024]{1,0:T(8,128)(2,1)S(1)} %get-tuple-element.75), channel_id=1, source_target_pairs={{0,16},{8,24},{16,0},{24,8},{1,17},{9,25},{17,1},{25,9},{2,18},{10... | collective-permute-start | bytes 196616 | tf_op jit(solution)/shard_map/ppermute | solution.py:342
  56.4 3.3 %convolution_bitcast_fusion = f32[1,1024,1024]{2,1,0:T(8,128)} fusion(bf16[384,1024]{1,0:T(8,128)(2,1)S(1)} %get-tuple-element.76, bf16[384,1024]{1,0:T(8,128)(2,1)S(1)} %get-tuple-element.77), kind=kOutput, calls=%fused_computation | convolution fusion | flops 805306368 | bytes 5767168 | tf_op jit(solution)/shard_map/dot_general | solution.py:463
  59.7 1.1 %collective-permute-done.19.refs_2_ = bf16[32,1024]{1,0:T(8,128)(2,1)S(1)} collective-permute-done((bf16[32,1024]{1,0:T(8,128)(2,1)S(1)}, bf16[32,1024]{1,0:T(8,128)(2,1)S(1)}, u32[]{:S(2)}, u32[]{:S(2)}) %collective-permute-start.19) | collective-permute-done | bytes 65568 | tf_op jit(solution)/shard_map/ppermute | solution.py:342
  60.8 1.6 %back.1 = bf16[128,1024]{1,0:T(8,128)(2,1)} custom-call(bf16[128,1024]{1,0:T(8,128)(2,1)S(1)} %bitcast.24, f32[1,1024]{1,0:T(1,128)S(1)} %bitcast.34, f32[1,1024]{1,0:T(1,128)S(1)} %bitcast.36, f32[32,1024]{1,0:T(8,128)S(1)} %get-tuple-element.41.tok_ref, f32[32,128]{1,0:T(8,128)S(1)} %get-tuple-element.42.keep_ref, bf16[32,1024]{1,0:T(8,128)(2,1)S(1)} %bitcast.28, ...), custom_call_target="tpu_custom_call" | custom-call | tf_op jit(solution)/shard_map/back/pallas_call | solution.py:26
  (37 shorter events, 0.2 us)
Async XLA Ops:
  0.6 29.4 %copy-start = (bf16[1,1024,1024]{2,1,0:T(8,128)(2,1)S(1)}, bf16[1,1024,1024]{2,1,0:T(8,128)(2,1)}, u32[]{:S(2)}) copy-start(bf16[1,1024,1024]{2,1,0:T(8,128)(2,1)} %param.13) | copy-start | bytes 6291460
  3.3 14.3 %collective-permute-start.3 = (bf16[32,1152]{1,0:T(8,128)(2,1)}, bf16[32,1152]{1,0:T(8,128)(2,1)S(1)}, u32[]{:S(2)}, u32[]{:S(2)}) collective-permute-start(bf16[32,1152]{1,0:T(8,128)(2,1)} %front.1.refs_0_), channel_id=1, source_target_pairs={{0,24},{8,16},{16,8},{24,0},{1,25},{9,17},{17,9},{25,1},{2,26},{10... | collective-permute-start | bytes 221192 | tf_op jit(solution)/shard_map/ppermute | solution.py:342
  8.3 9.3 %collective-permute-start.2 = (bf16[32,1152]{1,0:T(8,128)(2,1)}, bf16[32,1152]{1,0:T(8,128)(2,1)S(1)}, u32[]{:S(2)}, u32[]{:S(2)}) collective-permute-start(bf16[32,1152]{1,0:T(8,128)(2,1)} %front.1.refs_0_), channel_id=1, source_target_pairs={{0,8},{8,0},{16,24},{24,16},{1,9},{9,1},{17,25},{25,17},{2,10},{10... | collective-permute-start | bytes 221192 | tf_op jit(solution)/shard_map/ppermute | solution.py:342
  8.3 9.3 %collective-permute-start.1 = (bf16[32,1152]{1,0:T(8,128)(2,1)}, bf16[32,1152]{1,0:T(8,128)(2,1)S(1)}, u32[]{:S(2)}, u32[]{:S(2)}) collective-permute-start(bf16[32,1152]{1,0:T(8,128)(2,1)} %front.1.refs_0_), channel_id=1, source_target_pairs={{0,16},{8,24},{16,0},{24,8},{1,17},{9,25},{17,1},{25,9},{2,18},{10... | collective-permute-start | bytes 221192 | tf_op jit(solution)/shard_map/ppermute | solution.py:342
  8.9 8.7 %collective-permute-start = (bf16[32,1024]{1,0:T(8,128)(2,1)}, bf16[32,1024]{1,0:T(8,128)(2,1)S(1)}, u32[]{:S(2)}, u32[]{:S(2)}) collective-permute-start(bf16[32,1024]{1,0:T(8,128)(2,1)} %bitcast.26), channel_id=1, source_target_pairs={{0,16},{8,24},{16,0},{24,8},{1,17},{9,25},{17,1},{25,9},{2,18},{10... | collective-permute-start | bytes 196616 | tf_op jit(solution)/shard_map/ppermute | solution.py:342
  11.2 0.9 %copy-start.4 = (bf16[1,32,1024]{2,1,0:T(8,128)(2,1)S(1)}, bf16[1,32,1024]{2,1,0:T(8,128)(2,1)}, u32[]{:S(2)}) copy-start(bf16[1,32,1024]{2,1,0:T(8,128)(2,1)} %param.15) | copy-start | bytes 196612
  12.1 0.9 %copy-start.3 = (bf16[32,1152]{1,0:T(8,128)(2,1)S(1)}, bf16[32,1152]{1,0:T(8,128)(2,1)}, u32[]{:S(2)}) copy-start(bf16[32,1152]{1,0:T(8,128)(2,1)} %front.1.refs_0_) | copy-start | bytes 221188
  17.7 1.8 %collective-permute-start.5 = (bf16[128,1152]{1,0:T(8,128)(2,1)S(1)}, bf16[128,1152]{1,0:T(8,128)(2,1)S(1)}, u32[]{:S(2)}, u32[]{:S(2)}) collective-permute-start(bf16[128,1152]{1,0:T(8,128)(2,1)S(1)} %token_near.1.token_ref.refs_1_), channel_id=1, source_target_pairs={{0,1},{1,0},{2,3},{3,2},{4,5},{5,4},{6,7},{7,6},{8,9},{9,8},{10,11... | collective-permute-start | bytes 884744 | tf_op jit(solution)/shard_map/ppermute | solution.py:351
  17.7 1.8 %collective-permute-start.4 = (bf16[64,1024]{1,0:T(8,128)(2,1)S(1)}, bf16[64,1024]{1,0:T(8,128)(2,1)S(1)}, u32[]{:S(2)}, u32[]{:S(2)}) collective-permute-start(bf16[64,1024]{1,0:T(8,128)(2,1)S(1)} %cot_near.1.refs_0_.cot_ref), channel_id=1, source_target_pairs={{0,1},{1,0},{2,3},{3,2},{4,5},{5,4},{6,7},{7,6},{8,9},{9,8},{10,11... | collective-permute-start | bytes 393224 | tf_op jit(solution)/shard_map/ppermute | solution.py:351
  18.2 12.4 %copy-start.2 = (bf16[1,1024,1024]{2,1,0:T(8,128)(2,1)S(1)}, bf16[1,1024,1024]{2,1,0:T(8,128)(2,1)}, u32[]{:S(2)}) copy-start(bf16[1,1024,1024]{2,1,0:T(8,128)(2,1)} %param.14) | copy-start | bytes 6291460
  20.0 7.3 %collective-permute-start.6 = (bf16[48,1024]{1,0:T(8,128)(2,1)S(1)}, bf16[48,1024]{1,0:T(8,128)(2,1)S(1)}, u32[]{:S(2)}, u32[]{:S(2)}) collective-permute-start(bf16[48,1024]{1,0:T(8,128)(2,1)S(1)} %get-tuple-element.45), channel_id=1, source_target_pairs={{0,4},{1,5},{2,6},{3,7},{4,0},{5,1},{6,2},{7,3},{8,12},{9,13},{10,... | collective-permute-start | bytes 294920 | tf_op jit(solution)/shard_map/ppermute | solution.py:347
  21.6 6.2 %collective-permute-start.7 = (bf16[48,1024]{1,0:T(8,128)(2,1)S(1)}, bf16[48,1024]{1,0:T(8,128)(2,1)S(1)}, u32[]{:S(2)}, u32[]{:S(2)}) collective-permute-start(bf16[48,1024]{1,0:T(8,128)(2,1)S(1)} %get-tuple-element.46), channel_id=1, source_target_pairs={{0,2},{1,3},{2,0},{3,1},{4,6},{5,7},{6,4},{7,5},{8,10},{9,11},{10,... | collective-permute-start | bytes 294920 | tf_op jit(solution)/shard_map/ppermute | solution.py:347
  23.1 6.7 %collective-permute-start.10 = (bf16[48,1024]{1,0:T(8,128)(2,1)S(1)}, bf16[48,1024]{1,0:T(8,128)(2,1)S(1)}, u32[]{:S(2)}, u32[]{:S(2)}) collective-permute-start(bf16[48,1024]{1,0:T(8,128)(2,1)S(1)} %get-tuple-element.52), channel_id=1, source_target_pairs={{0,6},{1,7},{2,4},{3,5},{4,2},{5,3},{6,0},{7,1},{8,14},{9,15},{10,... | collective-permute-start | bytes 294920 | tf_op jit(solution)/shard_map/ppermute | solution.py:347
  24.2 10.3 %collective-permute-start.9 = (bf16[96,1152]{1,0:T(8,128)(2,1)S(1)}, bf16[96,1152]{1,0:T(8,128)(2,1)S(1)}, u32[]{:S(2)}, u32[]{:S(2)}) collective-permute-start(bf16[96,1152]{1,0:T(8,128)(2,1)S(1)} %get-tuple-element.48), channel_id=1, source_target_pairs={{0,6},{1,7},{2,4},{3,5},{4,2},{5,3},{6,0},{7,1},{8,14},{9,15},{10,... | collective-permute-start | bytes 663560 | tf_op jit(solution)/shard_map/ppermute | solution.py:347
  26.8 14.6 %collective-permute-start.12 = (bf16[96,1152]{1,0:T(8,128)(2,1)S(1)}, bf16[96,1152]{1,0:T(8,128)(2,1)S(1)}, u32[]{:S(2)}, u32[]{:S(2)}) collective-permute-start(bf16[96,1152]{1,0:T(8,128)(2,1)S(1)} %get-tuple-element.54), channel_id=1, source_target_pairs={{0,4},{1,5},{2,6},{3,7},{4,0},{5,1},{6,2},{7,3},{8,12},{9,13},{10,... | collective-permute-start | bytes 663560 | tf_op jit(solution)/shard_map/ppermute | solution.py:347
  27.3 14.1 %collective-permute-start.13 = (bf16[96,1152]{1,0:T(8,128)(2,1)S(1)}, bf16[96,1152]{1,0:T(8,128)(2,1)S(1)}, u32[]{:S(2)}, u32[]{:S(2)}) collective-permute-start(bf16[96,1152]{1,0:T(8,128)(2,1)S(1)} %get-tuple-element.55), channel_id=1, source_target_pairs={{0,2},{1,3},{2,0},{3,1},{4,6},{5,7},{6,4},{7,5},{8,10},{9,11},{10,... | collective-permute-start | bytes 663560 | tf_op jit(solution)/shard_map/ppermute | solution.py:347
  27.8 7.5 %collective-permute-start.8 = (bf16[96,1024]{1,0:T(8,128)(2,1)S(1)}, bf16[96,1024]{1,0:T(8,128)(2,1)S(1)}, u32[]{:S(2)}, u32[]{:S(2)}) collective-permute-start(bf16[96,1024]{1,0:T(8,128)(2,1)S(1)} %cot_slots.2.refs_0_.refs_5_), channel_id=1, source_target_pairs={{0,8},{8,0},{16,24},{24,16},{1,9},{9,1},{17,25},{25,17},{2,10},{10... | collective-permute-start | bytes 589832 | tf_op jit(solution)/shard_map/ppermute | solution.py:342
  29.8 7.5 %collective-permute-start.11 = (bf16[96,1024]{1,0:T(8,128)(2,1)S(1)}, bf16[96,1024]{1,0:T(8,128)(2,1)S(1)}, u32[]{:S(2)}, u32[]{:S(2)}) collective-permute-start(bf16[96,1024]{1,0:T(8,128)(2,1)S(1)} %cot_slots.3.refs_0_), channel_id=1, source_target_pairs={{0,8},{8,0},{16,24},{24,16},{1,9},{9,1},{17,25},{25,17},{2,10},{10... | collective-permute-start | bytes 589832 | tf_op jit(solution)/shard_map/ppermute | solution.py:342
  34.5 3.5 %copy-start.6 = (bf16[1024,8]{0,1:T(8,128)(2,1)S(1)}, bf16[1024,8]{0,1:T(8,128)(2,1)}, u32[]{:S(2)}) copy-start(bf16[1024,8]{0,1:T(8,128)(2,1)} %param.11) | copy-start | bytes 49156
  38.9 8.9 %collective-permute-start.16 = (bf16[96,1024]{1,0:T(8,128)(2,1)S(1)}, bf16[96,1024]{1,0:T(8,128)(2,1)S(1)}, u32[]{:S(2)}, u32[]{:S(2)}) collective-permute-start(bf16[96,1024]{1,0:T(8,128)(2,1)S(1)} %get-tuple-element.61), channel_id=1, source_target_pairs={{0,6},{1,7},{2,4},{3,5},{4,2},{5,3},{6,0},{7,1},{8,14},{9,15},{10,... | collective-permute-start | bytes 589832 | tf_op jit(solution)/shard_map/ppermute | solution.py:347
  43.1 6.2 %collective-permute-start.14 = (bf16[96,1024]{1,0:T(8,128)(2,1)S(1)}, bf16[96,1024]{1,0:T(8,128)(2,1)S(1)}, u32[]{:S(2)}, u32[]{:S(2)}) collective-permute-start(bf16[96,1024]{1,0:T(8,128)(2,1)S(1)} %get-tuple-element.59), channel_id=1, source_target_pairs={{0,2},{1,3},{2,0},{3,1},{4,6},{5,7},{6,4},{7,5},{8,10},{9,11},{10,... | collective-permute-start | bytes 589832 | tf_op jit(solution)/shard_map/ppermute | solution.py:347
  43.7 6.0 %collective-permute-start.15 = (bf16[96,1024]{1,0:T(8,128)(2,1)S(1)}, bf16[96,1024]{1,0:T(8,128)(2,1)S(1)}, u32[]{:S(2)}, u32[]{:S(2)}) collective-permute-start(bf16[96,1024]{1,0:T(8,128)(2,1)S(1)} %get-tuple-element.60), channel_id=1, source_target_pairs={{0,4},{1,5},{2,6},{3,7},{4,0},{5,1},{6,2},{7,3},{8,12},{9,13},{10,... | collective-permute-start | bytes 589832 | tf_op jit(solution)/shard_map/ppermute | solution.py:347
  44.5 5.6 %copy-start.1 = (bf16[1,128,1024]{2,1,0:T(8,128)(2,1)S(1)}, bf16[1,128,1024]{2,1,0:T(8,128)(2,1)}, u32[]{:S(2)}) copy-start(bf16[1,128,1024]{2,1,0:T(8,128)(2,1)} %param.8) | copy-start | bytes 786436
  44.5 5.6 %copy-start.7 = (f32[1024]{0:T(1024)S(1)}, f32[1024]{0:T(1024)}, u32[]{:S(2)}) copy-start(f32[1024]{0:T(1024)} %param.9) | copy-start | bytes 12292
  49.7 11.0 %copy-start.5 = (bf16[1,32,1024]{2,1,0:T(8,128)(2,1)S(1)}, bf16[1,32,1024]{2,1,0:T(8,128)(2,1)}, u32[]{:S(2)}) copy-start(bf16[1,32,1024]{2,1,0:T(8,128)(2,1)} %param.15) | copy-start | bytes 196612
  49.7 11.0 %copy-start.8 = (f32[1024]{0:T(1024)S(1)}, f32[1024]{0:T(1024)}, u32[]{:S(2)}) copy-start(f32[1024]{0:T(1024)} %param.10) | copy-start | bytes 12292
  50.0 1.6 %collective-permute-start.17 = (bf16[128,1024]{1,0:T(8,128)(2,1)S(1)}, bf16[128,1024]{1,0:T(8,128)(2,1)S(1)}, u32[]{:S(2)}, u32[]{:S(2)}) collective-permute-start(bf16[128,1024]{1,0:T(8,128)(2,1)S(1)} %combine_other.1), channel_id=1, source_target_pairs={{0,1},{1,0},{2,3},{3,2},{4,5},{5,4},{6,7},{7,6},{8,9},{9,8},{10,11... | collective-permute-start | bytes 786440 | tf_op jit(solution)/shard_map/ppermute | solution.py:351
  51.9 7.8 %collective-permute-start.18 = (bf16[32,1024]{1,0:T(8,128)(2,1)S(1)}, bf16[32,1024]{1,0:T(8,128)(2,1)S(1)}, u32[]{:S(2)}, u32[]{:S(2)}) collective-permute-start(bf16[32,1024]{1,0:T(8,128)(2,1)S(1)} %get-tuple-element.73), channel_id=1, source_target_pairs={{0,24},{8,16},{16,8},{24,0},{1,25},{9,17},{17,9},{25,1},{2,26},{10... | collective-permute-start | bytes 196616 | tf_op jit(solution)/shard_map/ppermute | solution.py:342
  54.8 6.0 %collective-permute-start.19 = (bf16[32,1024]{1,0:T(8,128)(2,1)S(1)}, bf16[32,1024]{1,0:T(8,128)(2,1)S(1)}, u32[]{:S(2)}, u32[]{:S(2)}) collective-permute-start(bf16[32,1024]{1,0:T(8,128)(2,1)S(1)} %get-tuple-element.74), channel_id=1, source_target_pairs={{0,8},{8,0},{16,24},{24,16},{1,9},{9,1},{17,25},{25,17},{2,10},{10... | collective-permute-start | bytes 196616 | tf_op jit(solution)/shard_map/ppermute | solution.py:342
  54.8 6.0 %collective-permute-start.20 = (bf16[32,1024]{1,0:T(8,128)(2,1)S(1)}, bf16[32,1024]{1,0:T(8,128)(2,1)S(1)}, u32[]{:S(2)}, u32[]{:S(2)}) collective-permute-start(bf16[32,1024]{1,0:T(8,128)(2,1)S(1)} %get-tuple-element.75), channel_id=1, source_target_pairs={{0,16},{8,24},{16,0},{24,8},{1,17},{9,25},{17,1},{25,9},{2,18},{10... | collective-permute-start | bytes 196616 | tf_op jit(solution)/shard_map/ppermute | solution.py:342

commit v9 on v6

--- a/solution.py
+++ b/solution.py
@@ -373,7 +373,7 @@
     )
     held_cot = call(functools.partial(gather_kernel, 0), "hold_cot", shape(count, width), (cot,), us=1.0)
     cot_near = call(
-        functools.partial(gather_kernel, 0), "cot_near", shape(half * count, width), (held_cot, *cot_far), us=5.0
+        functools.partial(gather_kernel, 0), "cot_near", shape(half * count, width), (held_cot, *cot_far), us=0.0
     )
     held = call(functools.partial(gather_kernel, 0), "hold_own", shape(count, full), (pay,), us=1.0)
     in_across = call(transpose_kernel, "across", shape(hidden, width), (weight_in,), us=2.0, limit=16)

time: 62.7 us -> 62.7 us (level)
  no operation moved by 1% of the time
where the time goes in v9:
time: 62.7 us; the launch traced here: 62.5 us
  starting transfers between devices  24.1 us (38%)
  waiting for transfers between devices  16.4 us (26%)
  Pallas kernels  12.7 us (20%)
  matrix products  6.61 us (11%)
  local copies, waits for them, and re-layouts  1.79 us (3%)
  between operations  0.88 us (1%)
    pallas_call x22, Pallas kernels, call(): pl.pallas_call(body, name=name, out_shape=outs, in_specs=[smem] * scalars...  12.7 us
    ppermute x9, starting transfers between devices, over_seq(): return lax.ppermute(value, 'seq', [(i, i ^ k) for i in range(pieces)])  12.7 us
    ppermute x9, starting transfers between devices, over_exp(): lax.ppermute(values[m], 'exp', [(i, i ^ m * step) for i in range(owners)])  10.7 us
    ppermute x9, waiting for transfers between devices, over_seq(): return lax.ppermute(value, 'seq', [(i, i ^ k) for i in range(pieces)])  7.06 us
    ppermute x9, waiting for transfers between devices, over_exp(): lax.ppermute(values[m], 'exp', [(i, i ^ m * step) for i in range(owners)])  7.03 us
    dot_general x1, matrix products, per_device(): lax.dot_general(hidden_rows, cot_slots, ROWS_T, preferred_element_type=F32)  3.31 us
    dot_general x1, matrix products, per_device(): lax.dot_general(token_slots, hidden_grad, ROWS_T, preferred_element_type=...  3.3 us
    ppermute x3, waiting for transfers between devices, over_cores(): return lax.ppermute(value, 'exp', [(i, i ^ 1) for i in range(owners)])  2.28 us
  transfers between devices with their start and end apart: 21, of which 9 were waited for; matrix products, arithmetic and copies ran while one was open for 11% of the time, Pallas kernels for 12%

profile of v9, /device:TPU:0, one launch (start us, length us, event | category | flops | bytes accessed | tf_op | source)
XLA Modules:
  0.0 62.5 jit_solution(11585926081930132075)
XLA Ops:
  0.6 2.6 %front.1.refs_0_ = bf16[32,1152]{1,0:T(8,128)(2,1)} custom-call(bf16[128,1024]{1,0:T(8,128)(2,1)} %bitcast.22, f32[1,1024]{1,0:T(1,128)} %bitcast.32, f32[1,1024]{1,0:T(1,128)} %bitcast.35, bf16[8,1024]{1,0:T(8,128)(2,1)} %bitcast.29, s32[2,32]{1,0:T(2,128)} %bitcast.39), custom_call_target="tpu_custom_call" | custom-call | bytes 6000000 | tf_op jit(solution)/shard_map/front/pallas_call | solution.py:26
  3.3 5.0 %collective-permute-start.3 = (bf16[32,1152]{1,0:T(8,128)(2,1)}, bf16[32,1152]{1,0:T(8,128)(2,1)S(1)}, u32[]{:S(2)}, u32[]{:S(2)}) collective-permute-start(bf16[32,1152]{1,0:T(8,128)(2,1)} %front.1.refs_0_), channel_id=1, source_target_pairs={{0,24},{8,16},{16,8},{24,0},{1,25},{9,17},{17,9},{25,1},{2,26},{10... | collective-permute-start | bytes 221192 | tf_op jit(solution)/shard_map/ppermute | solution.py:342
  8.3 0.6 collective-permute-start.1
  8.9 2.4 %collective-permute-start = (bf16[32,1024]{1,0:T(8,128)(2,1)}, bf16[32,1024]{1,0:T(8,128)(2,1)S(1)}, u32[]{:S(2)}, u32[]{:S(2)}) collective-permute-start(bf16[32,1024]{1,0:T(8,128)(2,1)} %bitcast.26), channel_id=1, source_target_pairs={{0,16},{8,24},{16,0},{24,8},{1,17},{9,25},{17,1},{25,9},{2,18},{10... | collective-permute-start | bytes 196616 | tf_op jit(solution)/shard_map/ppermute | solution.py:342
  11.2 0.9 %copy-done.4 = bf16[1,32,1024]{2,1,0:T(8,128)(2,1)S(1)} copy-done((bf16[1,32,1024]{2,1,0:T(8,128)(2,1)S(1)}, bf16[1,32,1024]{2,1,0:T(8,128)(2,1)}, u32[]{:S(2)}) %copy-start.4) | copy-done | bytes 65560
  12.1 0.9 %copy-done.3 = bf16[32,1152]{1,0:T(8,128)(2,1)S(1)} copy-done((bf16[32,1152]{1,0:T(8,128)(2,1)S(1)}, bf16[32,1152]{1,0:T(8,128)(2,1)}, u32[]{:S(2)}) %copy-start.3) | copy-done | bytes 73752
  13.0 4.6 %collective-permute-done.refs_1_ = bf16[32,1024]{1,0:T(8,128)(2,1)S(1)} collective-permute-done((bf16[32,1024]{1,0:T(8,128)(2,1)}, bf16[32,1024]{1,0:T(8,128)(2,1)S(1)}, u32[]{:S(2)}, u32[]{:S(2)}) %collective-permute-start) | collective-permute-done | bytes 65568 | tf_op jit(solution)/shard_map/ppermute | solution.py:342
  17.7 0.1 collective-permute-start.5
  17.7 0.5 collective-permute-start.4
  18.2 1.3 %collective-permute-done.4.other_cot_ref = bf16[64,1024]{1,0:T(8,128)(2,1)S(1)} collective-permute-done((bf16[64,1024]{1,0:T(8,128)(2,1)S(1)}, bf16[64,1024]{1,0:T(8,128)(2,1)S(1)}, u32[]{:S(2)}, u32[]{:S(2)}) %collective-permute-start.4) | collective-permute-done | bytes 131104 | tf_op jit(solution)/shard_map/ppermute | solution.py:351
  19.5 0.5 cot_pick.1
  20.0 1.6 %collective-permute-start.6 = (bf16[48,1024]{1,0:T(8,128)(2,1)S(1)}, bf16[48,1024]{1,0:T(8,128)(2,1)S(1)}, u32[]{:S(2)}, u32[]{:S(2)}) collective-permute-start(bf16[48,1024]{1,0:T(8,128)(2,1)S(1)} %get-tuple-element.45), channel_id=1, source_target_pairs={{0,4},{1,5},{2,6},{3,7},{4,0},{5,1},{6,2},{7,3},{8,12},{9,13},{10,... | collective-permute-start | bytes 294920 | tf_op jit(solution)/shard_map/ppermute | solution.py:347
  21.6 1.5 %collective-permute-start.7 = (bf16[48,1024]{1,0:T(8,128)(2,1)S(1)}, bf16[48,1024]{1,0:T(8,128)(2,1)S(1)}, u32[]{:S(2)}, u32[]{:S(2)}) collective-permute-start(bf16[48,1024]{1,0:T(8,128)(2,1)S(1)} %get-tuple-element.46), channel_id=1, source_target_pairs={{0,2},{1,3},{2,0},{3,1},{4,6},{5,7},{6,4},{7,5},{8,10},{9,11},{10,... | collective-permute-start | bytes 294920 | tf_op jit(solution)/shard_map/ppermute | solution.py:347
  23.1 0.5 collective-permute-start.10
  23.6 0.7 %token_pick.1 = (bf16[96,1152]{1,0:T(8,128)(2,1)S(1)}, bf16[96,1152]{1,0:T(8,128)(2,1)S(1)}, bf16[96,1152]{1,0:T(8,128)(2,1)S(1)}, bf16[96,1152]{1,0:T(8,128)(2,1)S(1)}, bf16[384,256]{1,0:T(8,128)(2,1)S(1)}) custom-call(s32[1]{0:T(128)} %bitcast.4.my_ref, bf16[48,1024]{1,0:T(8,128)(2,1)S(1)} %get-tuple-element.43.refs_0_, ...), custom_call_target="tpu_custom_call" | custom-call | tf_op jit(solution)/shard_map/token_pick/pallas_call | solution.py:26
  24.2 2.5 %collective-permute-start.9 = (bf16[96,1152]{1,0:T(8,128)(2,1)S(1)}, bf16[96,1152]{1,0:T(8,128)(2,1)S(1)}, u32[]{:S(2)}, u32[]{:S(2)}) collective-permute-start(bf16[96,1152]{1,0:T(8,128)(2,1)S(1)} %get-tuple-element.48), channel_id=1, source_target_pairs={{0,6},{1,7},{2,4},{3,5},{4,2},{5,3},{6,0},{7,1},{8,14},{9,15},{10,... | collective-permute-start | bytes 663560 | tf_op jit(solution)/shard_map/ppermute | solution.py:347
  26.8 0.5 collective-permute-start.12
  27.3 0.5 collective-permute-start.13
  27.8 0.1 collective-permute-start.8
  27.9 1.9 %collective-permute-done.10.refs_1_ = bf16[48,1024]{1,0:T(8,128)(2,1)S(1)} collective-permute-done((bf16[48,1024]{1,0:T(8,128)(2,1)S(1)}, bf16[48,1024]{1,0:T(8,128)(2,1)S(1)}, u32[]{:S(2)}, u32[]{:S(2)}) %collective-permute-start.10) | collective-permute-done | bytes 98336 | tf_op jit(solution)/shard_map/ppermute | solution.py:347
  29.8 0.2 collective-permute-start.11
  30.0 0.6 %across.3.refs_5_.refs_4_ = bf16[1024,1024]{1,0:T(8,128)(2,1)S(1)} custom-call(bf16[1024,1024]{1,0:T(8,128)(2,1)S(1)} %bitcast.19), custom_call_target="tpu_custom_call" | custom-call | bytes 6000000 | tf_op jit(solution)/shard_map/across/pallas_call | solution.py:26
  30.6 0.6 %across.2.refs_2_ = bf16[1024,1024]{1,0:T(8,128)(2,1)S(1)} custom-call(bf16[1024,1024]{1,0:T(8,128)(2,1)S(1)} %bitcast.25), custom_call_target="tpu_custom_call" | custom-call | bytes 6000000 | tf_op jit(solution)/shard_map/across/pallas_call | solution.py:26
  31.3 3.2 %collective-permute-done.9.refs_1_ = bf16[96,1152]{1,0:T(8,128)(2,1)S(1)} collective-permute-done((bf16[96,1152]{1,0:T(8,128)(2,1)S(1)}, bf16[96,1152]{1,0:T(8,128)(2,1)S(1)}, u32[]{:S(2)}, u32[]{:S(2)}) %collective-permute-start.9) | collective-permute-done | bytes 221216 | tf_op jit(solution)/shard_map/ppermute | solution.py:347
  34.5 0.8 %hidden.2 = (bf16[192,1024]{1,0:T(8,128)(2,1)S(1)}, bf16[192,128]{1,0:T(8,128)(2,1)S(1)}, bf16[192,1024]{1,0:T(8,128)(2,1)S(1)}, f32[192,1024]{1,0:T(8,128)S(1)}) custom-call(bf16[96,1152]{1,0:T(8,128)(2,1)S(1)} %get-tuple-element.47.refs_0_, bf16[96,1152]{1,0:T(8,128)(2,1)S(1)} %collective-permute-done.9.refs_1_, bf16[1024,1024]{1,0:T(8,128)(2,1)S(1)} %bitcast.20), custom_call_target="tpu_custom_call" | custom-call | bytes 3000000 | tf_op jit(solution)/shard_map/hidden/pallas_call | solution.py:26
  35.4 0.6 upstream.2.refs_0_.refs_3_
  36.0 1.4 %collective-permute-done.11.refs_1_ = bf16[96,1024]{1,0:T(8,128)(2,1)S(1)} collective-permute-done((bf16[96,1024]{1,0:T(8,128)(2,1)S(1)}, bf16[96,1024]{1,0:T(8,128)(2,1)S(1)}, u32[]{:S(2)}, u32[]{:S(2)}) %collective-permute-start.11) | collective-permute-done | bytes 196640 | tf_op jit(solution)/shard_map/ppermute | solution.py:342
  37.4 0.6 upstream.3.refs_4_
  38.0 0.9 %grads.2 = (bf16[96,1024]{1,0:T(8,128)(2,1)S(1)}, bf16[96,1024]{1,0:T(8,128)(2,1)S(1)}, bf16[192,1024]{1,0:T(8,128)(2,1)S(1)}) custom-call(s32[1]{0:T(128)} %bitcast.4.my_ref, f32[192,1024]{1,0:T(8,128)S(1)} %upstream.2.refs_0_.refs_3_, bf16[192,1024]{1,0:T(8,128)(2,1)S(1)} %get-tuple-element.49.refs_1_.refs_2_, f32[192,1024]{1,0:T(8,128)S(1)} %get-tuple-element.50.refs_2_, ...), custom_call_target="tpu_custom_call" | custom-call | tf_op jit(solution)/shard_map/grads/pallas_call | solution.py:26
  38.9 2.5 %collective-permute-start.16 = (bf16[96,1024]{1,0:T(8,128)(2,1)S(1)}, bf16[96,1024]{1,0:T(8,128)(2,1)S(1)}, u32[]{:S(2)}, u32[]{:S(2)}) collective-permute-start(bf16[96,1024]{1,0:T(8,128)(2,1)S(1)} %get-tuple-element.61), channel_id=1, source_target_pairs={{0,6},{1,7},{2,4},{3,5},{4,2},{5,3},{6,0},{7,1},{8,14},{9,15},{10,... | collective-permute-start | bytes 589832 | tf_op jit(solution)/shard_map/ppermute | solution.py:347
  41.4 0.8 %hidden.3 = (bf16[192,1024]{1,0:T(8,128)(2,1)S(1)}, bf16[192,128]{1,0:T(8,128)(2,1)S(1)}, bf16[192,1024]{1,0:T(8,128)(2,1)S(1)}, f32[192,1024]{1,0:T(8,128)S(1)}) custom-call(f32[192,1024]{1,0:T(8,128)S(1)} %upstream.2.refs_0_.refs_3_, bf16[96,1152]{1,0:T(8,128)(2,1)S(1)} %collective-permute-done.12.refs_1_, ...), custom_call_target="tpu_custom_call" | custom-call | bytes 3000000 | tf_op jit(solution)/shard_map/hidden/pallas_call | solution.py:26
  42.2 0.9 %grads.3 = (bf16[96,1024]{1,0:T(8,128)(2,1)S(1)}, bf16[96,1024]{1,0:T(8,128)(2,1)S(1)}, bf16[192,1024]{1,0:T(8,128)(2,1)S(1)}) custom-call(s32[1]{0:T(128)} %bitcast.4.my_ref, bf16[192,1024]{1,0:T(8,128)(2,1)S(1)} %get-tuple-element.56.refs_0_.refs_7_, f32[192,1024]{1,0:T(8,128)S(1)} %get-tuple-element.57.refs_1_, ...), custom_call_target="tpu_custom_call" | custom-call | tf_op jit(solution)/shard_map/grads/pallas_call | solution.py:26
  43.1 0.6 collective-permute-start.14
  43.7 0.5 collective-permute-start.15
  44.3 0.2 stack.1
  44.5 3.3 %fusion = f32[1024,1024]{1,0:T(8,128)} fusion(bf16[384,1024]{1,0:T(8,128)(2,1)S(1)} %get-tuple-element.66, bf16[384,1024]{1,0:T(8,128)(2,1)S(1)} %get-tuple-element.67), kind=kOutput, calls=%fused_computation.1 | convolution fusion | flops 805306368 | bytes 5767168 | tf_op jit(solution)/shard_map/dot_general | solution.py:461
  47.8 1.6 %collective-permute-done.14.refs_1_ = bf16[96,1024]{1,0:T(8,128)(2,1)S(1)} collective-permute-done((bf16[96,1024]{1,0:T(8,128)(2,1)S(1)}, bf16[96,1024]{1,0:T(8,128)(2,1)S(1)}, u32[]{:S(2)}, u32[]{:S(2)}) %collective-permute-start.14) | collective-permute-done | bytes 196640 | tf_op jit(solution)/shard_map/ppermute | solution.py:347
  49.4 0.4 collective-permute-done.15.refs_2_
  49.7 0.3 combine_other.1
  50.1 0.1 collective-permute-start.17
  50.2 0.5 keep.1
  50.6 1.0 %collective-permute-done.17.refs_4_ = bf16[128,1024]{1,0:T(8,128)(2,1)S(1)} collective-permute-done((bf16[128,1024]{1,0:T(8,128)(2,1)S(1)}, bf16[128,1024]{1,0:T(8,128)(2,1)S(1)}, u32[]{:S(2)}, u32[]{:S(2)}) %collective-permute-start.17) | collective-permute-done | bytes 262176 | tf_op jit(solution)/shard_map/ppermute | solution.py:351
  51.7 0.3 combine_own.1
  52.0 2.8 %collective-permute-start.18 = (bf16[32,1024]{1,0:T(8,128)(2,1)S(1)}, bf16[32,1024]{1,0:T(8,128)(2,1)S(1)}, u32[]{:S(2)}, u32[]{:S(2)}) collective-permute-start(bf16[32,1024]{1,0:T(8,128)(2,1)S(1)} %get-tuple-element.73), channel_id=1, source_target_pairs={{0,24},{8,16},{16,8},{24,0},{1,25},{9,17},{17,9},{25,1},{2,26},{10... | collective-permute-start | bytes 196616 | tf_op jit(solution)/shard_map/ppermute | solution.py:342
  54.8 1.7 %collective-permute-start.20 = (bf16[32,1024]{1,0:T(8,128)(2,1)S(1)}, bf16[32,1024]{1,0:T(8,128)(2,1)S(1)}, u32[]{:S(2)}, u32[]{:S(2)}) collective-permute-start(bf16[32,1024]{1,0:T(8,128)(2,1)S(1)} %get-tuple-element.75), channel_id=1, source_target_pairs={{0,16},{8,24},{16,0},{24,8},{1,17},{9,25},{17,1},{25,9},{2,18},{10... | collective-permute-start | bytes 196616 | tf_op jit(solution)/shard_map/ppermute | solution.py:342
  56.4 3.3 %convolution_bitcast_fusion = f32[1,1024,1024]{2,1,0:T(8,128)} fusion(bf16[384,1024]{1,0:T(8,128)(2,1)S(1)} %get-tuple-element.76, bf16[384,1024]{1,0:T(8,128)(2,1)S(1)} %get-tuple-element.77), kind=kOutput, calls=%fused_computation | convolution fusion | flops 805306368 | bytes 5767168 | tf_op jit(solution)/shard_map/dot_general | solution.py:462
  59.7 1.1 %collective-permute-done.19.refs_2_ = bf16[32,1024]{1,0:T(8,128)(2,1)S(1)} collective-permute-done((bf16[32,1024]{1,0:T(8,128)(2,1)S(1)}, bf16[32,1024]{1,0:T(8,128)(2,1)S(1)}, u32[]{:S(2)}, u32[]{:S(2)}) %collective-permute-start.19) | collective-permute-done | bytes 65568 | tf_op jit(solution)/shard_map/ppermute | solution.py:342
  60.8 1.6 %back.1 = bf16[128,1024]{1,0:T(8,128)(2,1)} custom-call(bf16[128,1024]{1,0:T(8,128)(2,1)S(1)} %bitcast.24, f32[1,1024]{1,0:T(1,128)S(1)} %bitcast.34, f32[1,1024]{1,0:T(1,128)S(1)} %bitcast.36, f32[32,1024]{1,0:T(8,128)S(1)} %get-tuple-element.41.tok_ref, f32[32,128]{1,0:T(8,128)S(1)} %get-tuple-element.42.keep_ref, bf16[32,1024]{1,0:T(8,128)(2,1)S(1)} %bitcast.28, ...), custom_call_target="tpu_custom_call" | custom-call | tf_op jit(solution)/shard_map/back/pallas_call | solution.py:26
  (36 shorter events, 0.1 us)
Async XLA Ops:
  0.6 29.4 %copy-start = (bf16[1,1024,1024]{2,1,0:T(8,128)(2,1)S(1)}, bf16[1,1024,1024]{2,1,0:T(8,128)(2,1)}, u32[]{:S(2)}) copy-start(bf16[1,1024,1024]{2,1,0:T(8,128)(2,1)} %param.13) | copy-start | bytes 6291460
  3.3 14.3 %collective-permute-start.3 = (bf16[32,1152]{1,0:T(8,128)(2,1)}, bf16[32,1152]{1,0:T(8,128)(2,1)S(1)}, u32[]{:S(2)}, u32[]{:S(2)}) collective-permute-start(bf16[32,1152]{1,0:T(8,128)(2,1)} %front.1.refs_0_), channel_id=1, source_target_pairs={{0,24},{8,16},{16,8},{24,0},{1,25},{9,17},{17,9},{25,1},{2,26},{10... | collective-permute-start | bytes 221192 | tf_op jit(solution)/shard_map/ppermute | solution.py:342
  8.3 9.3 %collective-permute-start.2 = (bf16[32,1152]{1,0:T(8,128)(2,1)}, bf16[32,1152]{1,0:T(8,128)(2,1)S(1)}, u32[]{:S(2)}, u32[]{:S(2)}) collective-permute-start(bf16[32,1152]{1,0:T(8,128)(2,1)} %front.1.refs_0_), channel_id=1, source_target_pairs={{0,8},{8,0},{16,24},{24,16},{1,9},{9,1},{17,25},{25,17},{2,10},{10... | collective-permute-start | bytes 221192 | tf_op jit(solution)/shard_map/ppermute | solution.py:342
  8.3 9.3 %collective-permute-start.1 = (bf16[32,1152]{1,0:T(8,128)(2,1)}, bf16[32,1152]{1,0:T(8,128)(2,1)S(1)}, u32[]{:S(2)}, u32[]{:S(2)}) collective-permute-start(bf16[32,1152]{1,0:T(8,128)(2,1)} %front.1.refs_0_), channel_id=1, source_target_pairs={{0,16},{8,24},{16,0},{24,8},{1,17},{9,25},{17,1},{25,9},{2,18},{10... | collective-permute-start | bytes 221192 | tf_op jit(solution)/shard_map/ppermute | solution.py:342
  8.9 8.7 %collective-permute-start = (bf16[32,1024]{1,0:T(8,128)(2,1)}, bf16[32,1024]{1,0:T(8,128)(2,1)S(1)}, u32[]{:S(2)}, u32[]{:S(2)}) collective-permute-start(bf16[32,1024]{1,0:T(8,128)(2,1)} %bitcast.26), channel_id=1, source_target_pairs={{0,16},{8,24},{16,0},{24,8},{1,17},{9,25},{17,1},{25,9},{2,18},{10... | collective-permute-start | bytes 196616 | tf_op jit(solution)/shard_map/ppermute | solution.py:342
  11.2 0.9 %copy-start.4 = (bf16[1,32,1024]{2,1,0:T(8,128)(2,1)S(1)}, bf16[1,32,1024]{2,1,0:T(8,128)(2,1)}, u32[]{:S(2)}) copy-start(bf16[1,32,1024]{2,1,0:T(8,128)(2,1)} %param.15) | copy-start | bytes 196612
  12.1 0.9 %copy-start.3 = (bf16[32,1152]{1,0:T(8,128)(2,1)S(1)}, bf16[32,1152]{1,0:T(8,128)(2,1)}, u32[]{:S(2)}) copy-start(bf16[32,1152]{1,0:T(8,128)(2,1)} %front.1.refs_0_) | copy-start | bytes 221188
  17.7 1.8 %collective-permute-start.5 = (bf16[128,1152]{1,0:T(8,128)(2,1)S(1)}, bf16[128,1152]{1,0:T(8,128)(2,1)S(1)}, u32[]{:S(2)}, u32[]{:S(2)}) collective-permute-start(bf16[128,1152]{1,0:T(8,128)(2,1)S(1)} %token_near.1.token_ref.refs_1_), channel_id=1, source_target_pairs={{0,1},{1,0},{2,3},{3,2},{4,5},{5,4},{6,7},{7,6},{8,9},{9,8},{10,11... | collective-permute-start | bytes 884744 | tf_op jit(solution)/shard_map/ppermute | solution.py:351
  17.7 1.8 %collective-permute-start.4 = (bf16[64,1024]{1,0:T(8,128)(2,1)S(1)}, bf16[64,1024]{1,0:T(8,128)(2,1)S(1)}, u32[]{:S(2)}, u32[]{:S(2)}) collective-permute-start(bf16[64,1024]{1,0:T(8,128)(2,1)S(1)} %cot_near.1.refs_0_.cot_ref), channel_id=1, source_target_pairs={{0,1},{1,0},{2,3},{3,2},{4,5},{5,4},{6,7},{7,6},{8,9},{9,8},{10,11... | collective-permute-start | bytes 393224 | tf_op jit(solution)/shard_map/ppermute | solution.py:351
  18.2 12.4 %copy-start.2 = (bf16[1,1024,1024]{2,1,0:T(8,128)(2,1)S(1)}, bf16[1,1024,1024]{2,1,0:T(8,128)(2,1)}, u32[]{:S(2)}) copy-start(bf16[1,1024,1024]{2,1,0:T(8,128)(2,1)} %param.14) | copy-start | bytes 6291460
  20.0 7.3 %collective-permute-start.6 = (bf16[48,1024]{1,0:T(8,128)(2,1)S(1)}, bf16[48,1024]{1,0:T(8,128)(2,1)S(1)}, u32[]{:S(2)}, u32[]{:S(2)}) collective-permute-start(bf16[48,1024]{1,0:T(8,128)(2,1)S(1)} %get-tuple-element.45), channel_id=1, source_target_pairs={{0,4},{1,5},{2,6},{3,7},{4,0},{5,1},{6,2},{7,3},{8,12},{9,13},{10,... | collective-permute-start | bytes 294920 | tf_op jit(solution)/shard_map/ppermute | solution.py:347
  21.6 6.2 %collective-permute-start.7 = (bf16[48,1024]{1,0:T(8,128)(2,1)S(1)}, bf16[48,1024]{1,0:T(8,128)(2,1)S(1)}, u32[]{:S(2)}, u32[]{:S(2)}) collective-permute-start(bf16[48,1024]{1,0:T(8,128)(2,1)S(1)} %get-tuple-element.46), channel_id=1, source_target_pairs={{0,2},{1,3},{2,0},{3,1},{4,6},{5,7},{6,4},{7,5},{8,10},{9,11},{10,... | collective-permute-start | bytes 294920 | tf_op jit(solution)/shard_map/ppermute | solution.py:347
  23.1 6.7 %collective-permute-start.10 = (bf16[48,1024]{1,0:T(8,128)(2,1)S(1)}, bf16[48,1024]{1,0:T(8,128)(2,1)S(1)}, u32[]{:S(2)}, u32[]{:S(2)}) collective-permute-start(bf16[48,1024]{1,0:T(8,128)(2,1)S(1)} %get-tuple-element.52), channel_id=1, source_target_pairs={{0,6},{1,7},{2,4},{3,5},{4,2},{5,3},{6,0},{7,1},{8,14},{9,15},{10,... | collective-permute-start | bytes 294920 | tf_op jit(solution)/shard_map/ppermute | solution.py:347
  24.2 10.3 %collective-permute-start.9 = (bf16[96,1152]{1,0:T(8,128)(2,1)S(1)}, bf16[96,1152]{1,0:T(8,128)(2,1)S(1)}, u32[]{:S(2)}, u32[]{:S(2)}) collective-permute-start(bf16[96,1152]{1,0:T(8,128)(2,1)S(1)} %get-tuple-element.48), channel_id=1, source_target_pairs={{0,6},{1,7},{2,4},{3,5},{4,2},{5,3},{6,0},{7,1},{8,14},{9,15},{10,... | collective-permute-start | bytes 663560 | tf_op jit(solution)/shard_map/ppermute | solution.py:347
  26.8 14.6 %collective-permute-start.12 = (bf16[96,1152]{1,0:T(8,128)(2,1)S(1)}, bf16[96,1152]{1,0:T(8,128)(2,1)S(1)}, u32[]{:S(2)}, u32[]{:S(2)}) collective-permute-start(bf16[96,1152]{1,0:T(8,128)(2,1)S(1)} %get-tuple-element.54), channel_id=1, source_target_pairs={{0,4},{1,5},{2,6},{3,7},{4,0},{5,1},{6,2},{7,3},{8,12},{9,13},{10,... | collective-permute-start | bytes 663560 | tf_op jit(solution)/shard_map/ppermute | solution.py:347
  27.3 14.1 %collective-permute-start.13 = (bf16[96,1152]{1,0:T(8,128)(2,1)S(1)}, bf16[96,1152]{1,0:T(8,128)(2,1)S(1)}, u32[]{:S(2)}, u32[]{:S(2)}) collective-permute-start(bf16[96,1152]{1,0:T(8,128)(2,1)S(1)} %get-tuple-element.55), channel_id=1, source_target_pairs={{0,2},{1,3},{2,0},{3,1},{4,6},{5,7},{6,4},{7,5},{8,10},{9,11},{10,... | collective-permute-start | bytes 663560 | tf_op jit(solution)/shard_map/ppermute | solution.py:347
  27.8 7.5 %collective-permute-start.8 = (bf16[96,1024]{1,0:T(8,128)(2,1)S(1)}, bf16[96,1024]{1,0:T(8,128)(2,1)S(1)}, u32[]{:S(2)}, u32[]{:S(2)}) collective-permute-start(bf16[96,1024]{1,0:T(8,128)(2,1)S(1)} %cot_slots.2.refs_0_.refs_5_), channel_id=1, source_target_pairs={{0,8},{8,0},{16,24},{24,16},{1,9},{9,1},{17,25},{25,17},{2,10},{10... | collective-permute-start | bytes 589832 | tf_op jit(solution)/shard_map/ppermute | solution.py:342
  29.8 7.5 %collective-permute-start.11 = (bf16[96,1024]{1,0:T(8,128)(2,1)S(1)}, bf16[96,1024]{1,0:T(8,128)(2,1)S(1)}, u32[]{:S(2)}, u32[]{:S(2)}) collective-permute-start(bf16[96,1024]{1,0:T(8,128)(2,1)S(1)} %cot_slots.3.refs_0_), channel_id=1, source_target_pairs={{0,8},{8,0},{16,24},{24,16},{1,9},{9,1},{17,25},{25,17},{2,10},{10... | collective-permute-start | bytes 589832 | tf_op jit(solution)/shard_map/ppermute | solution.py:342
  34.5 3.5 %copy-start.6 = (bf16[1024,8]{0,1:T(8,128)(2,1)S(1)}, bf16[1024,8]{0,1:T(8,128)(2,1)}, u32[]{:S(2)}) copy-start(bf16[1024,8]{0,1:T(8,128)(2,1)} %param.11) | copy-start | bytes 49156
  38.9 8.9 %collective-permute-start.16 = (bf16[96,1024]{1,0:T(8,128)(2,1)S(1)}, bf16[96,1024]{1,0:T(8,128)(2,1)S(1)}, u32[]{:S(2)}, u32[]{:S(2)}) collective-permute-start(bf16[96,1024]{1,0:T(8,128)(2,1)S(1)} %get-tuple-element.61), channel_id=1, source_target_pairs={{0,6},{1,7},{2,4},{3,5},{4,2},{5,3},{6,0},{7,1},{8,14},{9,15},{10,... | collective-permute-start | bytes 589832 | tf_op jit(solution)/shard_map/ppermute | solution.py:347
  43.1 6.2 %collective-permute-start.14 = (bf16[96,1024]{1,0:T(8,128)(2,1)S(1)}, bf16[96,1024]{1,0:T(8,128)(2,1)S(1)}, u32[]{:S(2)}, u32[]{:S(2)}) collective-permute-start(bf16[96,1024]{1,0:T(8,128)(2,1)S(1)} %get-tuple-element.59), channel_id=1, source_target_pairs={{0,2},{1,3},{2,0},{3,1},{4,6},{5,7},{6,4},{7,5},{8,10},{9,11},{10,... | collective-permute-start | bytes 589832 | tf_op jit(solution)/shard_map/ppermute | solution.py:347
  43.7 6.0 %collective-permute-start.15 = (bf16[96,1024]{1,0:T(8,128)(2,1)S(1)}, bf16[96,1024]{1,0:T(8,128)(2,1)S(1)}, u32[]{:S(2)}, u32[]{:S(2)}) collective-permute-start(bf16[96,1024]{1,0:T(8,128)(2,1)S(1)} %get-tuple-element.60), channel_id=1, source_target_pairs={{0,4},{1,5},{2,6},{3,7},{4,0},{5,1},{6,2},{7,3},{8,12},{9,13},{10,... | collective-permute-start | bytes 589832 | tf_op jit(solution)/shard_map/ppermute | solution.py:347
  44.5 5.7 %copy-start.1 = (bf16[1,128,1024]{2,1,0:T(8,128)(2,1)S(1)}, bf16[1,128,1024]{2,1,0:T(8,128)(2,1)}, u32[]{:S(2)}) copy-start(bf16[1,128,1024]{2,1,0:T(8,128)(2,1)} %param.8) | copy-start | bytes 786436
  44.5 5.7 %copy-start.7 = (f32[1024]{0:T(1024)S(1)}, f32[1024]{0:T(1024)}, u32[]{:S(2)}) copy-start(f32[1024]{0:T(1024)} %param.9) | copy-start | bytes 12292
  49.7 11.1 %copy-start.5 = (bf16[1,32,1024]{2,1,0:T(8,128)(2,1)S(1)}, bf16[1,32,1024]{2,1,0:T(8,128)(2,1)}, u32[]{:S(2)}) copy-start(bf16[1,32,1024]{2,1,0:T(8,128)(2,1)} %param.15) | copy-start | bytes 196612
  49.7 11.1 %copy-start.8 = (f32[1024]{0:T(1024)S(1)}, f32[1024]{0:T(1024)}, u32[]{:S(2)}) copy-start(f32[1024]{0:T(1024)} %param.10) | copy-start | bytes 12292
  50.1 1.6 %collective-permute-start.17 = (bf16[128,1024]{1,0:T(8,128)(2,1)S(1)}, bf16[128,1024]{1,0:T(8,128)(2,1)S(1)}, u32[]{:S(2)}, u32[]{:S(2)}) collective-permute-start(bf16[128,1024]{1,0:T(8,128)(2,1)S(1)} %combine_other.1), channel_id=1, source_target_pairs={{0,1},{1,0},{2,3},{3,2},{4,5},{5,4},{6,7},{7,6},{8,9},{9,8},{10,11... | collective-permute-start | bytes 786440 | tf_op jit(solution)/shard_map/ppermute | solution.py:351
  52.0 7.8 %collective-permute-start.18 = (bf16[32,1024]{1,0:T(8,128)(2,1)S(1)}, bf16[32,1024]{1,0:T(8,128)(2,1)S(1)}, u32[]{:S(2)}, u32[]{:S(2)}) collective-permute-start(bf16[32,1024]{1,0:T(8,128)(2,1)S(1)} %get-tuple-element.73), channel_id=1, source_target_pairs={{0,24},{8,16},{16,8},{24,0},{1,25},{9,17},{17,9},{25,1},{2,26},{10... | collective-permute-start | bytes 196616 | tf_op jit(solution)/shard_map/ppermute | solution.py:342
  54.8 6.0 %collective-permute-start.19 = (bf16[32,1024]{1,0:T(8,128)(2,1)S(1)}, bf16[32,1024]{1,0:T(8,128)(2,1)S(1)}, u32[]{:S(2)}, u32[]{:S(2)}) collective-permute-start(bf16[32,1024]{1,0:T(8,128)(2,1)S(1)} %get-tuple-element.74), channel_id=1, source_target_pairs={{0,8},{8,0},{16,24},{24,16},{1,9},{9,1},{17,25},{25,17},{2,10},{10... | collective-permute-start | bytes 196616 | tf_op jit(solution)/shard_map/ppermute | solution.py:342
  54.8 6.0 %collective-permute-start.20 = (bf16[32,1024]{1,0:T(8,128)(2,1)S(1)}, bf16[32,1024]{1,0:T(8,128)(2,1)S(1)}, u32[]{:S(2)}, u32[]{:S(2)}) collective-permute-start(bf16[32,1024]{1,0:T(8,128)(2,1)S(1)} %get-tuple-element.75), channel_id=1, source_target_pairs={{0,16},{8,24},{16,0},{24,8},{1,17},{9,25},{17,1},{25,9},{2,18},{10... | collective-permute-start | bytes 196616 | tf_op jit(solution)/shard_map/ppermute | solution.py:342
